TPU v7x, 32 devices: a whole 2x2x4 slice. The times are simulated.
32 devices in a mesh: gx: 8 (over z, x), gy: 4 (over y, core).
Axes of the slice: x: 2, y: 2, z: 4, core: 2. Of those that a mesh axis runs over, the one named last changes fastest.
Arguments:
- features: bfloat16 [128, 8, 8, 8, 128], P(('gx', 'gy')), may hold values from -6 to 6
- out_grad: bfloat16 [128, 8, 8, 8, 128], P(('gx', 'gy')), may hold values from -6 to 6
- kernel: bfloat16 [27, 128, 128], replicated, may hold values from -0.109375 to 0.109375
- voxel_mask: int32 [128, 512], P(('gx', 'gy')), may hold values from 0 to 1, as said below
- neighbours: int32 [128, 27], P(('gx', 'gy')), may hold values from 0 to 16, as said below
- face_sends: int32 [128, 2], P(('gx', 'gy')), may hold values from 0 to 4, as said below
- edge_sends: int32 [128, 1], P(('gx', 'gy')), may hold values from 0 to 4, as said below
Outputs:
- output: bfloat16 [128, 8, 8, 8, 128], P(('gx', 'gy'))
- input_grad: bfloat16 [128, 8, 8, 8, 128], P(('gx', 'gy'))
- weight_grad: float32 [27, 128, 128], replicated
Inputs may be any that keep to these rules, and one draw needn't show every extreme that they name: `voxel_mask`: zero in every voxel of a slot that holds no brick; in a slot that holds a brick each voxel is one or zero. neighbours[s, 9 (n_x + 1) + 3 (n_y + 1) + n_z + 1] is the index in the device's pool of the brick at brick offset n from slot s's brick, or 16 where that position lies outside the volume or holds no brick; the entry for offset (0,0,0) is the slot's own number; all other entries of a slot that holds no brick are 16. Each column of brick positions holds at most 1 bricks. `face_sends`: row 4 t + j lists, in increasing order, the device's slots whose bricks lie in its brick columns next to the side (-1,0), (1,0), (0,-1), (0,1) numbered j, then 4 for the rest. `edge_sends`: row 4 t + j lists, in increasing order, the device's slots whose bricks lie in its brick column at the corner (-1,-1), (-1,1), (1,-1), (1,1) numbered j, then 4 for the rest.
All inputs are finite; a program needn't handle non-finite values.
Results may differ from a plain program's by a relative error of at most 0.001.
Values may be sent and summed in bfloat16 or wider, within the bound.
No kernel may reach another device: no remote copies, remote signals or barrier semaphores. Data moves between devices by JAX's collectives and lax.ppermute only.
A program may use at most 192 MiB of HBM per device.

v0:
```python
import math

import jax
import jax.numpy as jnp
from jax import lax
from jax.experimental import pallas as pl
from jax.experimental.pallas import tpu as pltpu
from jax.sharding import PartitionSpec as P

FACES = ((-1, 0), (1, 0), (0, -1), (0, 1))
EDGES = ((-1, -1), (-1, 1), (1, -1), (1, 1))
C = 128
SLOTS = 4
FACE = 2
ZERO = SLOTS + 4 * FACE + 4
ROWS = 27 * C
VMEM_LIMIT = 50 * 1024 * 1024


def vmem():
    return pl.BlockSpec(memory_space=pltpu.VMEM)


def smem():
    return pl.BlockSpec(memory_space=pltpu.SMEM)


def mask_columns(mask_ref, s):
    m = mask_ref[...].astype(jnp.float32)
    pick = (lax.broadcasted_iota(jnp.int32, (SLOTS, C), 0) == s).astype(jnp.float32)
    return lax.dot_general(m, pick, (((0,), (0,)), ((), ())), preferred_element_type=jnp.float32)


def pack_kernel(face_ref, edge_ref, feat_ref, grad_ref, mask_ref, *refs):
    act_ref, grd_ref = refs[0:2]
    face_out = refs[2:6]
    edge_out = refs[6:10]
    full = refs[10]
    for s in range(SLOTS):
        rows = mask_columns(mask_ref, s)
        for f, (src, dst) in enumerate(((feat_ref, act_ref), (grad_ref, grd_ref))):
            masked = src[s].astype(jnp.float32) * rows
            full[f, s] = masked.reshape(8, 8, 8, C)
            dst[s] = masked.astype(jnp.bfloat16)
    for position, (ex, ey) in enumerate(FACES):
        for f in range(2):
            for r in range(FACE):
                entry = face_ref[position, r]
                slot = jnp.minimum(entry, SLOTS - 1)
                live = entry < SLOTS
                if ex != 0:
                    layer = full[f, slot, 7 if ex > 0 else 0]
                else:
                    layer = full[f, slot, :, 7 if ey > 0 else 0]
                layer = jnp.where(live, layer, 0.0)
                face_out[position][pl.ds((f * FACE + r) * 64, 64)] = layer.reshape(64, C).astype(jnp.bfloat16)
    for position, (ex, ey) in enumerate(EDGES):
        lines = []
        for f in range(2):
            entry = edge_ref[position, 0]
            slot = jnp.minimum(entry, SLOTS - 1)
            line = full[f, slot, 7 if ex > 0 else 0, 7 if ey > 0 else 0]
            lines.append(jnp.where(entry < SLOTS, line, 0.0))
        edge_out[position][...] = jnp.concatenate(lines, axis=0).astype(jnp.bfloat16)


def pack(features, out_grad, mask, face_sends, edge_sends):
    face = jax.ShapeDtypeStruct((2 * FACE * 64, C), jnp.bfloat16)
    edge = jax.ShapeDtypeStruct((16, C), jnp.bfloat16)
    brick = jax.ShapeDtypeStruct((SLOTS, 512, C), jnp.bfloat16)
    return pl.pallas_call(
        pack_kernel,
        out_shape=[brick, brick] + [face] * 4 + [edge] * 4,
        in_specs=[smem(), smem()] + [vmem()] * 3,
        out_specs=[vmem()] * 10,
        scratch_shapes=[pltpu.VMEM((2, SLOTS, 8, 8, 8, C), jnp.float32)],
        compiler_params=pltpu.CompilerParams(vmem_limit_bytes=VMEM_LIMIT),
        name="pack",
    )(face_sends, edge_sends, features, out_grad, mask)


def fill_layers(f, bricks, faces, edges, lx, ly, corners):
    zero_layer = jnp.zeros((8, 8, C), jnp.float32)
    for s in range(SLOTS):
        for side, at in ((0, 7), (1, 0)):
            lx[side, s] = bricks[s, pl.ds(64 * at, 64)].astype(jnp.float32).reshape(8, 8, C)
        whole = bricks[s].astype(jnp.float32).reshape(8, 8, 8, C)
        for side, at in ((0, 7), (1, 0)):
            ly[side, s] = whole[:, at]
    for side in range(2):
        for r in range(FACE):
            rows = pl.ds((f * FACE + r) * 64, 64)
            lx[side, SLOTS + r] = faces[side][rows].astype(jnp.float32).reshape(8, 8, C)
            ly[side, SLOTS + r] = faces[2 + side][rows].astype(jnp.float32).reshape(8, 8, C)
        lx[side, SLOTS + FACE] = zero_layer
        ly[side, SLOTS + FACE] = zero_layer
    for sx in range(2):
        for sy in range(2):
            ax = 0 if sx else 7
            ay = 0 if sy else 7
            c = 2 * sx + sy
            for s in range(SLOTS):
                corners[c, s] = lx[sx, s, ay]
            for r in range(FACE):
                corners[c, SLOTS + r] = lx[sx, SLOTS + r, ay]
                corners[c, SLOTS + FACE + r] = ly[sy, SLOTS + r, ax]
            corners[c, SLOTS + 2 * FACE] = edges[c][...].astype(jnp.float32)[8 * f : 8 * f + 8]
            corners[c, SLOTS + 2 * FACE + 1] = jnp.zeros((8, C), jnp.float32)


def build_columns(s, bricks, near, lx, ly, corners, wide, v):
    line = lax.broadcasted_iota(jnp.int32, (8, C), 0)

    def spread(cells, at_x, at_y, depth):
        if depth is None:
            keep = ((line >= 1), None, (line <= 6))
        else:
            same = depth == 0
            keep = (
                (same & (line >= 1)) | ((depth == -1) & (line == 0)),
                same & (line >= 0),
                (same & (line <= 6)) | ((depth == 1) & (line == 7)),
            )
        flat = cells.reshape(-1, 8, C)
        for k in range(3):
            moved = flat if k == 1 else pltpu.roll(flat, 1 if k == 0 else 7, 1)
            if keep[k] is not None:
                moved = jnp.where(keep[k][None], moved, 0.0)
            wide[k, at_x, at_y] = moved.reshape(cells.shape)

    def column(nx, ny):
        base = 9 * (nx + 1) + 3 * (ny + 1)
        low, mid, high = near[s, base], near[s, base + 1], near[s, base + 2]
        entry = jnp.minimum(jnp.minimum(low, mid), high)
        depth = jnp.where(low < ZERO, -1, jnp.where(high < ZERO, 1, 0))
        return entry, depth

    middle = pl.ds(1, 8)
    spread(bricks[s].astype(jnp.float32).reshape(8, 8, 8, C), middle, middle, None)
    for side, n in ((0, -1), (1, 1)):
        edge_at = pl.ds(0 if n < 0 else 9, 1)
        entry, depth = column(n, 0)
        place = jnp.where(entry < SLOTS, entry, jnp.clip(entry - FACE * side, 0, SLOTS + FACE))
        spread(lx[side, place].reshape(1, 8, 8, C), edge_at, middle, depth)
        entry, depth = column(0, n)
        place = jnp.where(entry < SLOTS, entry, jnp.clip(entry - FACE * (2 + side), 0, SLOTS + FACE))
        spread(ly[side, place].reshape(8, 1, 8, C), middle, edge_at, depth)
    for sx in range(2):
        for sy in range(2):
            entry, depth = column(2 * sx - 1, 2 * sy - 1)
            first_x = SLOTS + FACE * sx
            first_y = SLOTS + FACE * (2 + sy)
            own_edge = SLOTS + 4 * FACE + 2 * sx + sy
            in_x = (entry >= first_x) & (entry < first_x + FACE)
            in_y = (entry >= first_y) & (entry < first_y + FACE)
            place = jnp.where(entry == own_edge, SLOTS + 2 * FACE, SLOTS + 2 * FACE + 1)
            place = jnp.where(in_y, SLOTS + FACE + entry - first_y, place)
            place = jnp.where(in_x, SLOTS + entry - first_x, place)
            place = jnp.where(entry < SLOTS, entry, place)
            spread(corners[2 * sx + sy, place].reshape(1, 1, 8, C), pl.ds(9 * sx, 1), pl.ds(9 * sy, 1), depth)
    for y in range(3):
        for z in range(3):
            cells = wide[z, :, pl.ds(y, 8)].reshape(10, 64, C).astype(jnp.bfloat16)
            v[s, :, :, pl.ds((3 * y + z) * C, C)] = cells


def columns_scratch():
    return [
        pltpu.VMEM((2, SLOTS + FACE + 1, 8, 8, C), jnp.float32),
        pltpu.VMEM((2, SLOTS + FACE + 1, 8, 8, C), jnp.float32),
        pltpu.VMEM((4, SLOTS + 2 * FACE + 2, 8, C), jnp.float32),
        pltpu.VMEM((3, 10, 10, 8, C), jnp.float32),
        pltpu.VMEM((SLOTS, 10, 64, 9 * C), jnp.bfloat16),
    ]


def weight_kernel(parts, take, near, act, grd, *refs):
    faces, edges = refs[0:4], refs[4:8]
    out = refs[8]
    lx, ly, corners, wide, v, total = refs[9:]
    fill_layers(0, act, faces, edges, lx, ly, corners)

    def per_slot(s, carry):
        build_columns(s, act, near, lx, ly, corners, wide, v)
        return carry

    lax.fori_loop(0, SLOTS, per_slot, 0)
    rows = grd[...].reshape(SLOTS * 512, C)
    for x in range(3):
        for j in range(9):
            cells = v[:, pl.ds(x, 8), :, pl.ds(j * C, C)].reshape(SLOTS * 512, C)
            total[pl.ds((9 * x + j) * C, C)] = lax.dot_general(
                cells, rows, (((0,), (0,)), ((), ())), preferred_element_type=jnp.float32
            )
    if parts * take > ROWS:
        total[pl.ds(ROWS, parts * take - ROWS)] = jnp.zeros((parts * take - ROWS, C), jnp.float32)
    peak = jnp.max(jnp.abs(total[...]))
    power = jnp.clip(jnp.ceil(jnp.log2(jnp.full((8, C), peak))), -100.0, 100.0)
    scale = jnp.exp2(14.0 - power)
    held = out.shape[1]
    for p in range(parts):
        out[p, pl.ds(0, take)] = total[pl.ds(p * take, take)] * scale[0:1]
        out[p, pl.ds(take, held - take)] = jnp.broadcast_to(power[0:1], (held - take, C))


def weight_terms(parts, take, held, near, act, grd, faces, edges):
    return pl.pallas_call(
        lambda *refs: weight_kernel(parts, take, *refs),
        out_shape=jax.ShapeDtypeStruct((parts, held, C), jnp.float32),
        in_specs=[smem()] + [vmem()] * 10,
        out_specs=vmem(),
        scratch_shapes=columns_scratch() + [pltpu.VMEM((parts * take, C), jnp.float32)],
        compiler_params=pltpu.CompilerParams(vmem_limit_bytes=VMEM_LIMIT),
        cost_estimate=pl.CostEstimate(flops=2 * 2048 * ROWS * C, bytes_accessed=6 << 20, transcendentals=0),
        name="weight_terms",
    )(near, act, grd, *faces, *edges)


def products_kernel(near, mask_ref, kernel_ref, act, grd, *refs):
    faces, edges = refs[0:4], refs[4:8]
    outs = refs[8:10]
    lx, ly, corners, wide, v, flipped = refs[10:]
    for o in range(27):
        flipped[pl.ds((26 - o) * C, C)] = kernel_ref[pl.ds(o * C, C)].T
    for f, (bricks, weights) in enumerate(((act, kernel_ref), (grd, flipped))):
        fill_layers(f, bricks, faces, edges, lx, ly, corners)

        def per_slot(s, carry):
            build_columns(s, bricks, near, lx, ly, corners, wide, v)
            total = jnp.zeros((512, C), jnp.float32)
            for x in range(3):
                cells = v[s, pl.ds(x, 8)].reshape(512, 9 * C)
                total += jnp.dot(cells, weights[pl.ds(x * 9 * C, 9 * C)], preferred_element_type=jnp.float32)
            outs[f][s] = (total * mask_columns(mask_ref, s)).astype(jnp.bfloat16)
            return carry

        lax.fori_loop(0, SLOTS, per_slot, 0)


def products(near, mask, kernel, act, grd, faces, edges):
    brick = jax.ShapeDtypeStruct((SLOTS, 512, C), jnp.bfloat16)
    return pl.pallas_call(
        products_kernel,
        out_shape=[brick, brick],
        in_specs=[smem()] + [vmem()] * 12,
        out_specs=[vmem()] * 2,
        scratch_shapes=columns_scratch() + [pltpu.VMEM((ROWS, C), jnp.bfloat16)],
        compiler_params=pltpu.CompilerParams(vmem_limit_bytes=VMEM_LIMIT),
        cost_estimate=pl.CostEstimate(flops=4 * 2048 * ROWS * C, bytes_accessed=8 << 20, transcendentals=0),
        name="products",
    )(near, mask, kernel, act, grd, *faces, *edges)


def exchange(face_out, edge_out):
    size_x, size_y = lax.axis_size("gx"), lax.axis_size("gy")

    def moved(value, by_x, by_y):
        pairs = []
        for a in range(size_x):
            for b in range(size_y):
                if 0 <= a + by_x < size_x and 0 <= b + by_y < size_y:
                    pairs.append((a * size_y + b, (a + by_x) * size_y + b + by_y))
        return lax.ppermute(value, ("gx", "gy"), pairs)

    faces = [moved(face_out[p ^ 1], -ex, -ey) for p, (ex, ey) in enumerate(FACES)]
    edges = [moved(edge_out[3 - p], -ex, -ey) for p, (ex, ey) in enumerate(EDGES)]
    return faces, edges


def unscaled(blocks, take):
    wide = blocks.astype(jnp.float32)
    return wide[:, :take] * jnp.exp2(wide[:, take : take + 1] - 14.0)


def total_weights(terms, take):
    parts, held, _ = terms.shape
    arrived = lax.all_to_all(terms.astype(jnp.float16), ("gx", "gy"), 0, 0, tiled=True)
    mine = jnp.sum(unscaled(arrived, take), axis=0)
    power = jnp.clip(jnp.ceil(jnp.log2(jnp.max(jnp.abs(mine)))), -100.0, 100.0)
    scaled = jnp.concatenate(
        [mine * jnp.exp2(14.0 - power), jnp.full((held - take, C), power, jnp.float32)], axis=0
    ).astype(jnp.float16)
    copies = jnp.broadcast_to(scaled[None], (parts, held, C))
    gathered = lax.all_to_all(copies, ("gx", "gy"), 0, 0, tiled=True)
    return unscaled(gathered, take).reshape(parts * take, C)[:ROWS]


def local(features, out_grad, kernel, voxel_mask, neighbours, face_sends, edge_sends):
    parts = lax.axis_size("gx") * lax.axis_size("gy")
    take = -(-ROWS // parts)
    held = -(-(take + 1) // 16) * 16
    act, grd, *sends = pack(
        features.reshape(SLOTS, 512, C), out_grad.reshape(SLOTS, 512, C), voxel_mask, face_sends, edge_sends
    )
    faces, edges = exchange(sends[:4], sends[4:])
    terms = weight_terms(parts, take, held, neighbours, act, grd, faces, edges)
    weight = total_weights(terms, take)
    output, input_grad = products(
        neighbours, voxel_mask, kernel.reshape(ROWS, C), act, grd, faces, edges
    )
    scale = 1.0 / math.sqrt(parts * SLOTS * 512)
    shape = (SLOTS, 8, 8, 8, C)
    return (
        output.reshape(shape),
        input_grad.reshape(shape),
        (weight * scale).reshape(27, C, C),
    )


def solution(mesh):
    spec = P(("gx", "gy"))
    return jax.shard_map(
        local,
        mesh=mesh,
        in_specs=(spec, spec, P(), spec, spec, spec, spec),
        out_specs=(spec, spec, P()),
        check_vma=False,
    )
```

profile of v0, /device:TPU:0, one launch (start us, length us, event | category | flops | bytes accessed | tf_op | source)
XLA Modules:
  0.0 109.5 jit_solution(10135682704440645715)
XLA Ops:
  0.6 0.8 copy.12.face_ref
  1.4 0.7 copy.13.edge_ref
  2.1 0.0 copy-start
  2.1 1.0 copy-done
  3.2 0.0 copy-start.1
  3.2 1.0 copy-done.1
  4.2 0.0 copy-start.2
  4.2 0.7 copy-done.2
  4.9 1.1 %pack.1 = (bf16[4,512,128]{2,1,0:T(8,128)(2,1)S(1)}, bf16[4,512,128]{2,1,0:T(8,128)(2,1)S(1)}, bf16[256,128]{1,0:T(8,128)(2,1)S(1)}, bf16[256,128]{1,0:T(8,128)(...) custom-call(s32[4,2]{1,0:T(4,128)S(1)} %copy.12.face_ref, ...), custom_call_target="tpu_custom_call" | custom-call | tf_op jit(solution)/shard_map/pack/pallas_call | solution.py:71
  6.0 4.8 %collective-permute-start = (bf16[256,128]{1,0:T(8,128)(2,1)S(1)}, bf16[256,128]{1,0:T(8,128)(2,1)S(1)}, u32[]{:S(2)}, u32[]{:S(2)}) collective-permute-start(bf16[256,128]{1,0:T(8,128)(2,1)S(1)} %get-tuple-element.17), channel_id=1, source_target_pairs={{0,4},{1,5},{2,6},{3,7},{4,8},{5,9},{6,10},{7,11},{8,12},{9,13},{1... | collective-permute-start | bytes 196616 | tf_op jit(solution)/shard_map/ppermute | solution.py:263
  10.9 1.3 %collective-permute-start.1 = (bf16[256,128]{1,0:T(8,128)(2,1)S(1)}, bf16[256,128]{1,0:T(8,128)(2,1)S(1)}, u32[]{:S(2)}, u32[]{:S(2)}) collective-permute-start(bf16[256,128]{1,0:T(8,128)(2,1)S(1)} %get-tuple-element.18), channel_id=1, source_target_pairs={{4,0},{5,1},{6,2},{7,3},{8,4},{9,5},{10,6},{11,7},{12,8},{13,9},{1... | collective-permute-start | bytes 196616 | tf_op jit(solution)/shard_map/ppermute | solution.py:263
  12.2 1.5 %collective-permute-start.2 = (bf16[256,128]{1,0:T(8,128)(2,1)S(1)}, bf16[256,128]{1,0:T(8,128)(2,1)S(1)}, u32[]{:S(2)}, u32[]{:S(2)}) collective-permute-start(bf16[256,128]{1,0:T(8,128)(2,1)S(1)} %get-tuple-element.19), channel_id=1, source_target_pairs={{0,1},{1,2},{2,3},{4,5},{5,6},{6,7},{8,9},{9,10},{10,11},{12,13},{... | collective-permute-start | bytes 196616 | tf_op jit(solution)/shard_map/ppermute | solution.py:263
  13.7 1.3 %collective-permute-start.3 = (bf16[256,128]{1,0:T(8,128)(2,1)S(1)}, bf16[256,128]{1,0:T(8,128)(2,1)S(1)}, u32[]{:S(2)}, u32[]{:S(2)}) collective-permute-start(bf16[256,128]{1,0:T(8,128)(2,1)S(1)} %get-tuple-element.20), channel_id=1, source_target_pairs={{1,0},{2,1},{3,2},{5,4},{6,5},{7,6},{9,8},{10,9},{11,10},{13,12},{... | collective-permute-start | bytes 196616 | tf_op jit(solution)/shard_map/ppermute | solution.py:263
  15.0 6.9 %collective-permute-start.4 = (bf16[16,128]{1,0:T(8,128)(2,1)S(1)}, bf16[16,128]{1,0:T(8,128)(2,1)S(1)}, u32[]{:S(2)}, u32[]{:S(2)}) collective-permute-start(bf16[16,128]{1,0:T(8,128)(2,1)S(1)} %get-tuple-element.21), channel_id=1, source_target_pairs={{0,5},{1,6},{2,7},{4,9},{5,10},{6,11},{8,13},{9,14},{10,15},{12,17... | collective-permute-start | bytes 12296 | tf_op jit(solution)/shard_map/ppermute | solution.py:263
  21.8 1.3 %collective-permute-done.4.refs_4_.refs_7_ = bf16[16,128]{1,0:T(8,128)(2,1)S(1)} collective-permute-done((bf16[16,128]{1,0:T(8,128)(2,1)S(1)}, bf16[16,128]{1,0:T(8,128)(2,1)S(1)}, u32[]{:S(2)}, u32[]{:S(2)}) %collective-permute-start.4) | collective-permute-done | bytes 4128 | tf_op jit(solution)/shard_map/ppermute | solution.py:263
  23.1 0.6 collective-permute-start.5
  23.8 0.0 collective-permute-done.5.refs_5_.refs_8_
  23.8 0.7 collective-permute-start.6
  24.5 0.0 collective-permute-done.6.refs_6_.refs_9_
  24.5 1.3 %collective-permute-start.7 = (bf16[16,128]{1,0:T(8,128)(2,1)S(1)}, bf16[16,128]{1,0:T(8,128)(2,1)S(1)}, u32[]{:S(2)}, u32[]{:S(2)}) collective-permute-start(bf16[16,128]{1,0:T(8,128)(2,1)S(1)} %get-tuple-element.24), channel_id=1, source_target_pairs={{5,0},{6,1},{7,2},{9,4},{10,5},{11,6},{13,8},{14,9},{15,10},{17,12... | collective-permute-start | bytes 12296 | tf_op jit(solution)/shard_map/ppermute | solution.py:263
  25.8 15.2 %collective-permute-done.7.refs_7_.refs_10_ = bf16[16,128]{1,0:T(8,128)(2,1)S(1)} collective-permute-done((bf16[16,128]{1,0:T(8,128)(2,1)S(1)}, bf16[16,128]{1,0:T(8,128)(2,1)S(1)}, u32[]{:S(2)}, u32[]{:S(2)}) %collective-permute-start.7) | collective-permute-done | bytes 4128 | tf_op jit(solution)/shard_map/ppermute | solution.py:263
  41.0 0.0 collective-permute-done.refs_0_.refs_3_
  41.0 0.0 collective-permute-done.1.refs_1_.refs_4_
  41.0 0.0 collective-permute-done.2.refs_2_.refs_5_
  41.0 0.0 collective-permute-done.3.refs_3_.refs_6_
  41.0 0.0 copy-start.5
  41.0 0.7 copy-done.5
  41.7 5.9 %weight_terms.1 = f32[32,112,128]{2,1,0:T(8,128)S(1)} custom-call(s32[4,27]{1,0:T(4,128)S(1)} %copy-done.5, bf16[4,512,128]{2,1,0:T(8,128)(2,1)S(1)} %get-tuple-element.15.act.refs_1_, bf16[4,512,128]{2,1,0:T(8,128)(2,1)S(1)} %get-tuple-element.16.grd.refs_2_, bf16[256,128]{1,0:T(8,128)(2,1)S(1)} %collective-permute-done.refs_0_.refs_3_, ...), custom_call_target="tpu_custom_call" | custom-call | flops 1811939328 | bytes 6291456 | tf_op jit(solution)/shard_map/weight_terms/pallas_call | solution.py:207
  47.6 0.1 convert_element_type.10
  47.7 30.3 %all_to_all.10 = f16[32,112,128]{2,1,0:T(8,128)(2,1)S(1)} all-to-all(f16[32,112,128]{2,1,0:T(8,128)(2,1)S(1)} %convert_element_type.10), channel_id=1, replica_groups=mesh['gx'=8,'gy'=4] {'gx','gy'}, dimensions={0} | all-to-all | bytes 1835008 | tf_op jit(solution)/shard_map/all_to_all | solution.py:277
  78.0 0.1 convert_element_type.11
  78.2 0.2 fusion.1
  78.3 0.0 copy-start.3
  78.4 0.0 copy-start.4
  78.4 0.0 copy-start.6
  78.4 0.6 abs_reduce_fusion
  79.8 1.0 broadcast_in_dim.2
  80.8 3.6 %all-to-all-start.1 = ((f16[32,112,128]{2,1,0:T(8,128)(2,1)}), f16[32,112,128]{2,1,0:T(8,128)(2,1)S(1)}, u32[]{:S(2)}, u32[]{:S(2)}) async-start(f16[32,112,128]{2,1,0:T(8,128)(2,1)} %broadcast_in_dim.2), calls=%async_computation.1 | async-start | bytes 1835008 | tf_op jit(solution)/shard_map/all_to_all | solution.py:284
  84.4 0.0 copy-done.3
  84.5 0.0 copy-done.4
  84.5 0.0 copy-done.6
  84.5 10.9 %products.1 = (bf16[4,512,128]{2,1,0:T(8,128)(2,1)}, bf16[4,512,128]{2,1,0:T(8,128)(2,1)}) custom-call(s32[4,27]{1,0:T(4,128)S(1)} %copy-done.6, s32[4,512]{1,0:T(4,128)S(1)} %copy-done.3, bf16[3456,128]{1,0:T(8,128)(2,1)S(1)} %bitcast.9, bf16[4,512,128]{2,1,0:T(8,128)(2,1)S(1)} %get-tuple-element.15.act.refs_1_, ...), custom_call_target="tpu_custom_call" | custom-call | flops 3623878656 | bytes 8388608 | tf_op jit(solution)/shard_map/products/pallas_call | solution.py:242
  95.4 12.5 %all-to-all-done.1 = f16[32,112,128]{2,1,0:T(8,128)(2,1)S(1)} async-done(((f16[32,112,128]{2,1,0:T(8,128)(2,1)}), f16[32,112,128]{2,1,0:T(8,128)(2,1)S(1)}, u32[]{:S(2)}, u32[]{:S(2)}) %all-to-all-start.1) | async-done | bytes 917536 | tf_op jit(solution)/shard_map/all_to_all | solution.py:284
  107.9 0.1 convert_element_type.12
  108.0 0.1 fusion
  108.2 1.3 %mul.46 = f32[27,128,128]{2,1,0:T(8,128)} reshape(f32[32,108,128]{2,1,0:T(8,128)S(1)} %fusion) | data formatting | bytes 3538944 | tf_op jit(solution)/shard_map/mul | solution.py:306
  (4 shorter events, 0.1 us)
Async XLA Ops:
  2.1 1.0 copy-start
  3.2 1.0 copy-start.1
  4.2 0.7 copy-start.2
  6.0 35.0 %collective-permute-start = (bf16[256,128]{1,0:T(8,128)(2,1)S(1)}, bf16[256,128]{1,0:T(8,128)(2,1)S(1)}, u32[]{:S(2)}, u32[]{:S(2)}) collective-permute-start(bf16[256,128]{1,0:T(8,128)(2,1)S(1)} %get-tuple-element.17), channel_id=1, source_target_pairs={{0,4},{1,5},{2,6},{3,7},{4,8},{5,9},{6,10},{7,11},{8,12},{9,13},{1... | collective-permute-start | bytes 196616 | tf_op jit(solution)/shard_map/ppermute | solution.py:263
  10.9 30.1 %collective-permute-start.1 = (bf16[256,128]{1,0:T(8,128)(2,1)S(1)}, bf16[256,128]{1,0:T(8,128)(2,1)S(1)}, u32[]{:S(2)}, u32[]{:S(2)}) collective-permute-start(bf16[256,128]{1,0:T(8,128)(2,1)S(1)} %get-tuple-element.18), channel_id=1, source_target_pairs={{4,0},{5,1},{6,2},{7,3},{8,4},{9,5},{10,6},{11,7},{12,8},{13,9},{1... | collective-permute-start | bytes 196616 | tf_op jit(solution)/shard_map/ppermute | solution.py:263
  12.2 28.8 %collective-permute-start.2 = (bf16[256,128]{1,0:T(8,128)(2,1)S(1)}, bf16[256,128]{1,0:T(8,128)(2,1)S(1)}, u32[]{:S(2)}, u32[]{:S(2)}) collective-permute-start(bf16[256,128]{1,0:T(8,128)(2,1)S(1)} %get-tuple-element.19), channel_id=1, source_target_pairs={{0,1},{1,2},{2,3},{4,5},{5,6},{6,7},{8,9},{9,10},{10,11},{12,13},{... | collective-permute-start | bytes 196616 | tf_op jit(solution)/shard_map/ppermute | solution.py:263
  13.7 27.3 %collective-permute-start.3 = (bf16[256,128]{1,0:T(8,128)(2,1)S(1)}, bf16[256,128]{1,0:T(8,128)(2,1)S(1)}, u32[]{:S(2)}, u32[]{:S(2)}) collective-permute-start(bf16[256,128]{1,0:T(8,128)(2,1)S(1)} %get-tuple-element.20), channel_id=1, source_target_pairs={{1,0},{2,1},{3,2},{5,4},{6,5},{7,6},{9,8},{10,9},{11,10},{13,12},{... | collective-permute-start | bytes 196616 | tf_op jit(solution)/shard_map/ppermute | solution.py:263
  15.0 8.2 %collective-permute-start.4 = (bf16[16,128]{1,0:T(8,128)(2,1)S(1)}, bf16[16,128]{1,0:T(8,128)(2,1)S(1)}, u32[]{:S(2)}, u32[]{:S(2)}) collective-permute-start(bf16[16,128]{1,0:T(8,128)(2,1)S(1)} %get-tuple-element.21), channel_id=1, source_target_pairs={{0,5},{1,6},{2,7},{4,9},{5,10},{6,11},{8,13},{9,14},{10,15},{12,17... | collective-permute-start | bytes 12296 | tf_op jit(solution)/shard_map/ppermute | solution.py:263
  23.1 0.7 collective-permute-start.5
  23.8 0.7 collective-permute-start.6
  24.5 16.5 %collective-permute-start.7 = (bf16[16,128]{1,0:T(8,128)(2,1)S(1)}, bf16[16,128]{1,0:T(8,128)(2,1)S(1)}, u32[]{:S(2)}, u32[]{:S(2)}) collective-permute-start(bf16[16,128]{1,0:T(8,128)(2,1)S(1)} %get-tuple-element.24), channel_id=1, source_target_pairs={{5,0},{6,1},{7,2},{9,4},{10,5},{11,6},{13,8},{14,9},{15,10},{17,12... | collective-permute-start | bytes 12296 | tf_op jit(solution)/shard_map/ppermute | solution.py:263
  41.0 0.7 copy-start.5
  78.3 6.1 %copy-start.3 = (s32[4,512]{1,0:T(4,128)S(1)}, s32[4,512]{1,0:T(4,128)}, u32[]{:S(2)}) copy-start(s32[4,512]{1,0:T(4,128)} %mask_ref.3) | copy-start | bytes 24580
  78.4 6.1 %copy-start.4 = (bf16[27,128,128]{2,1,0:T(8,128)(2,1)S(1)}, bf16[27,128,128]{2,1,0:T(8,128)(2,1)}, u32[]{:S(2)}) copy-start(bf16[27,128,128]{2,1,0:T(8,128)(2,1)} %param.9) | copy-start | bytes 2654212
  78.4 6.1 %copy-start.6 = (s32[4,27]{1,0:T(4,128)S(1)}, s32[4,27]{1,0:T(4,128)}, u32[]{:S(2)}) copy-start(s32[4,27]{1,0:T(4,128)} %refs_0_.1) | copy-start | bytes 1300
  80.8 27.1 %all-to-all-start.1 = ((f16[32,112,128]{2,1,0:T(8,128)(2,1)}), f16[32,112,128]{2,1,0:T(8,128)(2,1)S(1)}, u32[]{:S(2)}, u32[]{:S(2)}) async-start(f16[32,112,128]{2,1,0:T(8,128)(2,1)} %broadcast_in_dim.2), calls=%async_computation.1 | async-start | bytes 1835008 | tf_op jit(solution)/shard_map/all_to_all | solution.py:284
where the time goes:
time: 110 us
  blocking collectives  30.3 us (28%)
  waiting for transfers between devices  29 us (26%)
  starting transfers between devices  22 us (20%)
  Pallas kernels  17.9 us (16%)
  local copies, waits for them, and re-layouts  7.36 us (7%)
  between operations  1.61 us (1%)
  other arithmetic  1.37 us (1%)
    all_to_all x1, blocking collectives, total_weights(): lax.all_to_all(terms.astype(jnp.float16), ('gx', 'gy'), 0, 0, tiled=True)  30.3 us
    ppermute x8, starting transfers between devices, moved(): return lax.ppermute(value, ('gx', 'gy'), pairs)  18.4 us
    ppermute x8, waiting for transfers between devices, moved(): return lax.ppermute(value, ('gx', 'gy'), pairs)  16.5 us
    all_to_all x1, waiting for transfers between devices, total_weights(): gathered = lax.all_to_all(copies, ('gx', 'gy'), 0, 0, tiled=True)  12.5 us
    pallas_call x1, Pallas kernels, products(): pl.pallas_call(products_kernel, out_shape=[brick, brick], in_specs=[smem(...  10.9 us
    pallas_call x1, Pallas kernels, weight_terms(): pl.pallas_call(lambda *refs: weight_kernel(parts, take, *refs), out_shape...  5.91 us
    unnamed x16, local copies, waits for them, and re-layouts  4.98 us
    all_to_all x1, starting transfers between devices, total_weights(): gathered = lax.all_to_all(copies, ('gx', 'gy'), 0, 0, tiled=True)  3.62 us
  transfers between devices with their start and end apart: 9, of which 3 were waited for; matrix products, arithmetic and copies ran while one was open for 0% of the time, Pallas kernels for 10%

commit v1 on v0

v1 whole, which is shorter than its diff:
```python
import math

import jax
import jax.numpy as jnp
from jax import lax
from jax.experimental import pallas as pl
from jax.experimental.pallas import tpu as pltpu
from jax.sharding import PartitionSpec as P

FACES = ((-1, 0), (1, 0), (0, -1), (0, 1))
EDGES = ((-1, -1), (-1, 1), (1, -1), (1, 1))
C = 128
SLOTS = 4
FACE = 2
ZERO = SLOTS + 4 * FACE + 4
ROWS = 27 * C
FACE_ROWS = 2 * FACE * 64
SEND_ROWS = FACE_ROWS + 32
HALF = ROWS // 2
VMEM_LIMIT = 50 * 1024 * 1024


def vmem():
    return pl.BlockSpec(memory_space=pltpu.VMEM)


def smem():
    return pl.BlockSpec(memory_space=pltpu.SMEM)


def mask_columns(mask_ref, s):
    m = mask_ref[...].astype(jnp.float32)
    pick = (lax.broadcasted_iota(jnp.int32, (SLOTS, C), 0) == s).astype(jnp.float32)
    return lax.dot_general(m, pick, (((0,), (0,)), ((), ())), preferred_element_type=jnp.float32)


def parity(axis):
    return lax.rem(lax.axis_index(axis), 2)


def side_of(k, odd):
    return 1 - odd if k == 0 else odd


def pack_kernel(face_ref, edge_ref, feat_hbm, grad_hbm, mask_hbm, act_ref, grd_ref, *refs):
    y_out, x_out = refs[0:2], refs[2:4]
    raw, mask_ref, full, sems = refs[4:]
    copies = [
        pltpu.make_async_copy(mask_hbm, mask_ref, sems.at[0]),
        pltpu.make_async_copy(feat_hbm, raw.at[0], sems.at[1]),
        pltpu.make_async_copy(grad_hbm, raw.at[1], sems.at[2]),
    ]
    for copy in copies:
        copy.start()
    for copy in copies:
        copy.wait()
    for s in range(SLOTS):
        rows = mask_columns(mask_ref, s)
        for f, dst in enumerate((act_ref, grd_ref)):
            masked = raw[f, s].astype(jnp.float32) * rows
            full[f, s] = masked.reshape(8, 8, 8, C)
            dst[s] = masked.astype(jnp.bfloat16)
    for axis, outs in enumerate((x_out, y_out)):
        odd = parity("gy" if axis else "gx")
        for k in range(2):
            side = side_of(k, odd)
            for f in range(2):
                for r in range(FACE):
                    entry = face_ref[r, 2 * axis + side]
                    slot = jnp.clip(entry, 0, SLOTS - 1)
                    layer = full[f, slot, :, 7 * side] if axis else full[f, slot, 7 * side]
                    layer = jnp.where(entry < SLOTS, layer, 0.0)
                    outs[k][pl.ds((f * FACE + r) * 64, 64)] = layer.reshape(64, C).astype(jnp.bfloat16)
            for far in range(2):
                if axis == 0:
                    outs[k][pl.ds(FACE_ROWS + 16 * far, 16)] = jnp.zeros((16, C), jnp.bfloat16)
                    continue
                entry = edge_ref[0, 2 * far + side]
                slot = jnp.clip(entry, 0, SLOTS - 1)
                lines = [full[f, slot, 7 * far, 7 * side] for f in range(2)]
                lines = jnp.where(entry < SLOTS, jnp.concatenate(lines, axis=0), 0.0)
                outs[k][pl.ds(FACE_ROWS + 16 * far, 16)] = lines.astype(jnp.bfloat16)


def pack(features, out_grad, mask, face_sends, edge_sends):
    send = jax.ShapeDtypeStruct((SEND_ROWS, C), jnp.bfloat16)
    brick = jax.ShapeDtypeStruct((SLOTS, 512, C), jnp.bfloat16)
    return pl.pallas_call(
        pack_kernel,
        out_shape=[brick, brick] + [send] * 4,
        in_specs=[smem(), smem()] + [pl.BlockSpec(memory_space=pl.ANY)] * 3,
        out_specs=[vmem()] * 6,
        scratch_shapes=[
            pltpu.VMEM((2, SLOTS, 512, C), jnp.bfloat16),
            pltpu.VMEM((SLOTS, 512), jnp.int32),
            pltpu.VMEM((2, SLOTS, 8, 8, 8, C), jnp.float32),
            pltpu.SemaphoreType.DMA((3,)),
        ],
        compiler_params=pltpu.CompilerParams(vmem_limit_bytes=VMEM_LIMIT),
        name="pack",
    )(face_sends.T, edge_sends.T, features, out_grad, mask)


def forward_kernel(x0, x1, y0, y1, out0, out1):
    odd_x, odd_y = parity("gx"), parity("gy")
    for k, out in enumerate((out0, out1)):
        far = side_of(k, odd_x)
        for j, came in enumerate((y0, y1)):
            source = side_of(j, odd_y)
            rows = came[pl.ds(pl.multiple_of(FACE_ROWS + 16 * far, 16), 16)]
            out[pl.ds(pl.multiple_of(FACE_ROWS + 16 * source, 16), 16)] = rows
        out[pl.ds(0, FACE_ROWS)] = (x0, x1)[k][pl.ds(0, FACE_ROWS)]


def forward_corners(x_send, y_came):
    send = jax.ShapeDtypeStruct((SEND_ROWS, C), jnp.bfloat16)
    return pl.pallas_call(
        forward_kernel,
        out_shape=[send] * 2,
        in_specs=[vmem()] * 4,
        out_specs=[vmem()] * 2,
        compiler_params=pltpu.CompilerParams(vmem_limit_bytes=VMEM_LIMIT),
        name="forward_corners",
    )(*x_send, *y_came)


def fill_layers(f, bricks, x_came, y_came, lx, ly, corners):
    odd_x, odd_y = parity("gx"), parity("gy")
    zero_layer = jnp.zeros((8, 8, C), jnp.float32)
    for s in range(SLOTS):
        whole = bricks[s].astype(jnp.float32).reshape(8, 8, 8, C)
        for side, at in ((0, 7), (1, 0)):
            lx[side, s] = whole[at]
            ly[side, s] = whole[:, at]
    for came, odd, dst in ((x_came, odd_x, lx), (y_came, odd_y, ly)):
        for k in range(2):
            side = side_of(k, odd)
            for r in range(FACE):
                rows = came[k][pl.ds((f * FACE + r) * 64, 64)]
                dst[side, SLOTS + r] = rows.astype(jnp.float32).reshape(8, 8, C)
            dst[k, SLOTS + FACE] = zero_layer
    for k in range(2):
        side = side_of(k, odd_x)
        for j in range(2):
            rows = x_came[k][pl.ds(FACE_ROWS + 16 * j, 16)].astype(jnp.float32)
            corners[2 * side + j, SLOTS + 2 * FACE] = rows[8 * f : 8 * f + 8]
    for sx in range(2):
        for sy in range(2):
            ax = 0 if sx else 7
            ay = 0 if sy else 7
            c = 2 * sx + sy
            for s in range(SLOTS):
                corners[c, s] = lx[sx, s, ay]
            for r in range(FACE):
                corners[c, SLOTS + r] = lx[sx, SLOTS + r, ay]
                corners[c, SLOTS + FACE + r] = ly[sy, SLOTS + r, ax]
            corners[c, SLOTS + 2 * FACE + 1] = jnp.zeros((8, C), jnp.float32)


def build_columns(s, bricks, near, lx, ly, corners, wide, v):
    line = lax.broadcasted_iota(jnp.int32, (8, C), 0)

    def spread(cells, at_x, at_y, depth):
        if depth is None:
            keep = ((line >= 1), None, (line <= 6))
        else:
            same = depth == 0
            keep = (
                (same & (line >= 1)) | ((depth == -1) & (line == 0)),
                same & (line >= 0),
                (same & (line <= 6)) | ((depth == 1) & (line == 7)),
            )
        flat = cells.reshape(-1, 8, C)
        for k in range(3):
            moved = flat if k == 1 else pltpu.roll(flat, 1 if k == 0 else 7, 1)
            if keep[k] is not None:
                moved = jnp.where(keep[k][None], moved, 0.0)
            wide[k, at_x, at_y] = moved.reshape(cells.shape)

    def column(nx, ny):
        base = 9 * (nx + 1) + 3 * (ny + 1)
        low, mid, high = near[s, base], near[s, base + 1], near[s, base + 2]
        entry = jnp.minimum(jnp.minimum(low, mid), high)
        depth = jnp.where(low < ZERO, -1, jnp.where(high < ZERO, 1, 0))
        return entry, depth

    middle = pl.ds(1, 8)
    spread(bricks[s].astype(jnp.float32).reshape(8, 8, 8, C), middle, middle, None)
    for side, n in ((0, -1), (1, 1)):
        edge_at = pl.ds(0 if n < 0 else 9, 1)
        entry, depth = column(n, 0)
        place = jnp.where(entry < SLOTS, entry, jnp.clip(entry - FACE * side, 0, SLOTS + FACE))
        spread(lx[side, place].reshape(1, 8, 8, C), edge_at, middle, depth)
        entry, depth = column(0, n)
        place = jnp.where(entry < SLOTS, entry, jnp.clip(entry - FACE * (2 + side), 0, SLOTS + FACE))
        spread(ly[side, place].reshape(8, 1, 8, C), middle, edge_at, depth)
    for sx in range(2):
        for sy in range(2):
            entry, depth = column(2 * sx - 1, 2 * sy - 1)
            first_x = SLOTS + FACE * sx
            first_y = SLOTS + FACE * (2 + sy)
            own_edge = SLOTS + 4 * FACE + 2 * sx + sy
            in_x = (entry >= first_x) & (entry < first_x + FACE)
            in_y = (entry >= first_y) & (entry < first_y + FACE)
            place = jnp.where(entry == own_edge, SLOTS + 2 * FACE, SLOTS + 2 * FACE + 1)
            place = jnp.where(in_y, SLOTS + FACE + entry - first_y, place)
            place = jnp.where(in_x, SLOTS + entry - first_x, place)
            place = jnp.where(entry < SLOTS, entry, place)
            spread(corners[2 * sx + sy, place].reshape(1, 1, 8, C), pl.ds(9 * sx, 1), pl.ds(9 * sy, 1), depth)
    for y in range(3):
        for z in range(3):
            cells = wide[z, :, pl.ds(y, 8)].reshape(10, 64, C).astype(jnp.bfloat16)
            v[s, :, :, pl.ds((3 * y + z) * C, C)] = cells


def columns_scratch():
    return [
        pltpu.VMEM((2, SLOTS + FACE + 1, 8, 8, C), jnp.float32),
        pltpu.VMEM((2, SLOTS + FACE + 1, 8, 8, C), jnp.float32),
        pltpu.VMEM((4, SLOTS + 2 * FACE + 2, 8, C), jnp.float32),
        pltpu.VMEM((3, 10, 10, 8, C), jnp.float32),
        pltpu.VMEM((SLOTS, 10, 64, 9 * C), jnp.bfloat16),
    ]


def weight_kernel(near, act, grd, x0, x1, y0, y1, keep, send, lx, ly, corners, wide, v, total):
    fill_layers(0, act, (x0, x1), (y0, y1), lx, ly, corners)

    def per_slot(s, carry):
        build_columns(s, act, near, lx, ly, corners, wide, v)
        return carry

    lax.fori_loop(0, SLOTS, per_slot, 0)
    rows = grd[...].reshape(SLOTS * 512, C)
    for x in range(3):
        for j in range(9):
            cells = v[:, pl.ds(x, 8), :, pl.ds(j * C, C)].reshape(SLOTS * 512, C)
            total[pl.ds((9 * x + j) * C, C)] = lax.dot_general(
                cells, rows, (((0,), (0,)), ((), ())), preferred_element_type=jnp.float32
            )
    core = parity("gy")
    keep[...] = total[pl.ds(pl.multiple_of(core * HALF, 8), HALF)]
    send[...] = total[pl.ds(pl.multiple_of((1 - core) * HALF, 8), HALF)]


def weight_terms(near, act, grd, x_came, y_came):
    half = jax.ShapeDtypeStruct((HALF, C), jnp.float32)
    return pl.pallas_call(
        weight_kernel,
        out_shape=[half, half],
        in_specs=[smem()] + [vmem()] * 6,
        out_specs=[vmem()] * 2,
        scratch_shapes=columns_scratch() + [pltpu.VMEM((ROWS, C), jnp.float32)],
        compiler_params=pltpu.CompilerParams(vmem_limit_bytes=VMEM_LIMIT),
        cost_estimate=pl.CostEstimate(flops=2 * 2048 * ROWS * C, bytes_accessed=6 << 20, transcendentals=0),
        name="weight_terms",
    )(near, act, grd, *x_came, *y_came)


def power_of(values):
    peak = jnp.max(jnp.abs(values))
    return jnp.clip(jnp.ceil(jnp.log2(jnp.full((8, C), peak))), -100.0, 100.0)[0:1]


def merge_kernel(groups, take, keep, came, out, total):
    held = out.shape[1]
    total[pl.ds(0, HALF)] = keep[...] + came[...]
    if groups * take > HALF:
        total[pl.ds(HALF, groups * take - HALF)] = jnp.zeros((groups * take - HALF, C), jnp.float32)
    power = power_of(total[...])
    scale = jnp.exp2(14.0 - power)
    for p in range(groups):
        out[p, pl.ds(0, take)] = total[pl.ds(p * take, take)] * scale
        out[p, pl.ds(take, held - take)] = jnp.broadcast_to(power, (held - take, C))


def merge(groups, take, held, keep, came):
    return pl.pallas_call(
        lambda *refs: merge_kernel(groups, take, *refs),
        out_shape=jax.ShapeDtypeStruct((groups, held, C), jnp.float32),
        in_specs=[vmem()] * 2,
        out_specs=vmem(),
        scratch_shapes=[pltpu.VMEM((groups * take, C), jnp.float32)],
        compiler_params=pltpu.CompilerParams(vmem_limit_bytes=VMEM_LIMIT),
        name="merge",
    )(keep, came)


def sum_kernel(take, blocks, out):
    groups, held, _ = blocks.shape
    total = jnp.zeros((take, C), jnp.float32)
    for p in range(groups):
        total += blocks[p, pl.ds(0, take)] * jnp.exp2(blocks[p, pl.ds(take, 1)] - 14.0)
    power = power_of(total)
    total = total * jnp.exp2(14.0 - power)
    for p in range(groups):
        out[p, pl.ds(0, take)] = total
        out[p, pl.ds(take, held - take)] = jnp.broadcast_to(power, (held - take, C))


def sum_blocks(take, blocks):
    return pl.pallas_call(
        lambda *refs: sum_kernel(take, *refs),
        out_shape=jax.ShapeDtypeStruct(blocks.shape, jnp.float32),
        in_specs=[vmem()],
        out_specs=vmem(),
        compiler_params=pltpu.CompilerParams(vmem_limit_bytes=VMEM_LIMIT),
        name="sum_blocks",
    )(blocks)


def decode_kernel(take, scale, mine, other, out):
    core = parity("gy")
    groups = mine.shape[0]
    for half, blocks in ((core, mine), (1 - core, other)):
        for p in range(groups):
            rows = min(take, HALF - p * take)
            if rows > 0:
                factor = jnp.exp2(blocks[p, pl.ds(take, 1)] - 14.0) * scale
                out[half, pl.ds(p * take, rows)] = blocks[p, pl.ds(0, rows)] * factor


def decode(take, scale, mine, other):
    return pl.pallas_call(
        lambda *refs: decode_kernel(take, scale, *refs),
        out_shape=jax.ShapeDtypeStruct((2, HALF, C), jnp.float32),
        in_specs=[vmem()] * 2,
        out_specs=vmem(),
        compiler_params=pltpu.CompilerParams(vmem_limit_bytes=VMEM_LIMIT),
        name="decode",
    )(mine, other)


def product_kernel(f, near, mask_ref, kernel_ref, bricks, x0, x1, y0, y1, out, lx, ly, corners, wide, v, *flipped):
    weights = kernel_ref
    if f == 1:
        weights = flipped[0]
        for o in range(27):
            weights[pl.ds((26 - o) * C, C)] = kernel_ref[pl.ds(o * C, C)].T
    fill_layers(f, bricks, (x0, x1), (y0, y1), lx, ly, corners)

    def per_slot(s, carry):
        build_columns(s, bricks, near, lx, ly, corners, wide, v)
        total = jnp.zeros((512, C), jnp.float32)
        for x in range(3):
            cells = v[s, pl.ds(x, 8)].reshape(512, 9 * C)
            total += jnp.dot(cells, weights[pl.ds(x * 9 * C, 9 * C)], preferred_element_type=jnp.float32)
        out[s] = (total * mask_columns(mask_ref, s)).astype(jnp.bfloat16)
        return carry

    lax.fori_loop(0, SLOTS, per_slot, 0)


def product(f, near, mask, kernel, bricks, x_came, y_came):
    return pl.pallas_call(
        lambda *refs: product_kernel(f, *refs),
        out_shape=jax.ShapeDtypeStruct((SLOTS, 512, C), jnp.bfloat16),
        in_specs=[smem()] + [vmem()] * 7,
        out_specs=vmem(),
        scratch_shapes=columns_scratch() + ([pltpu.VMEM((ROWS, C), jnp.bfloat16)] if f else []),
        compiler_params=pltpu.CompilerParams(vmem_limit_bytes=VMEM_LIMIT),
        cost_estimate=pl.CostEstimate(flops=2 * 2048 * ROWS * C, bytes_accessed=4 << 20, transcendentals=0),
        name=("output_product", "input_grad_product")[f],
    )(near, mask, kernel, bricks, *x_came, *y_came)


def swapped(value, axis, k):
    pairs = []
    for low in range(k, lax.axis_size(axis) - 1, 2):
        pairs += [(low, low + 1), (low + 1, low)]
    return lax.ppermute(value, axis, pairs)


def local(features, out_grad, kernel, voxel_mask, neighbours, face_sends, edge_sends):
    size_x, size_y = lax.axis_size("gx"), lax.axis_size("gy")
    parts = size_x * size_y
    groups = parts // 2
    take = -(-HALF // groups)
    held = -(-(take + 1) // 16) * 16
    same_core = [[i for i in range(parts) if i % size_y % 2 == core] for core in range(2)]

    def spread(blocks):
        return lax.all_to_all(
            blocks.astype(jnp.float16), ("gx", "gy"), 0, 0, axis_index_groups=same_core, tiled=True
        )

    act, grd, y0, y1, x0, x1 = pack(
        features.reshape(SLOTS, 512, C), out_grad.reshape(SLOTS, 512, C), voxel_mask, face_sends, edge_sends
    )
    y_came = [swapped(y0, "gy", 0), swapped(y1, "gy", 1)]
    x0, x1 = forward_corners((x0, x1), y_came)
    x_came = [swapped(x0, "gx", 0), swapped(x1, "gx", 1)]
    keep, send = weight_terms(neighbours, act, grd, x_came, y_came)
    blocks = merge(groups, take, held, keep, swapped(send, "gy", 0))
    mine = spread(sum_blocks(take, spread(blocks).astype(jnp.float32)))
    other = swapped(mine, "gy", 0)
    scale = 1.0 / math.sqrt(parts * SLOTS * 512)
    weight = decode(take, scale, mine.astype(jnp.float32), other.astype(jnp.float32))
    rows = kernel.reshape(ROWS, C)
    output = product(0, neighbours, voxel_mask, rows, act, x_came, y_came)
    input_grad = product(1, neighbours, voxel_mask, rows, grd, x_came, y_came)
    shape = (SLOTS, 8, 8, 8, C)
    return output.reshape(shape), input_grad.reshape(shape), weight.reshape(27, C, C)


def solution(mesh):
    spec = P(("gx", "gy"))
    return jax.shard_map(
        local,
        mesh=mesh,
        in_specs=(spec, spec, P(), spec, spec, spec, spec),
        out_specs=(spec, spec, P()),
        check_vma=False,
    )
```

time: 110 us -> 82.9 us (0.75)
  waiting for transfers between devices: 29 us -> 3.98 us
  starting transfers between devices: 22 us -> 8.83 us
  blocking collectives: 30.3 us -> 42.2 us
  Pallas kernels: 17.9 us -> 21.5 us
  local copies, waits for them, and re-layouts: 7.36 us -> 4.8 us
    ppermute x8 -> x6, waiting for transfers between devices: 16.5 us -> 3.98 us  [swapped(): return lax.ppermute(value, axis, pairs)]
    all_to_all x1 -> x0, waiting for transfers between devices: 12.5 us -> none  [total_weights(): gathered = lax.all_to_all(copies, ('gx', 'gy'), 0, 0, tiled=True)]
    all_to_all x1 -> x2, blocking collectives: 30.3 us -> 42.2 us  [spread(): lax.all_to_all(blocks.astype(jnp.float16), ('gx', 'gy'), 0, 0, axis_index...]
    ppermute x8 -> x6, starting transfers between devices: 18.4 us -> 8.83 us  [swapped(): return lax.ppermute(value, axis, pairs)]
    all_to_all x1 -> x0, starting transfers between devices: 3.62 us -> none  [total_weights(): gathered = lax.all_to_all(copies, ('gx', 'gy'), 0, 0, tiled=True)]
    pallas_call x3 -> x8, Pallas kernels: 17.9 us -> 21.5 us  [the longest x2 12.4 us: product(): pl.pallas_call(lambda *refs: product_kernel(f, *refs), out_shape=jax.Shap...]
    mul x1 -> x0, local copies, waits for them, and re-layouts: 1.33 us -> none  [local(): weight * scale]
  transfers between devices with their start and end apart: 9 -> 6, of which waited for: 3 -> 3; matrix products, arithmetic and copies ran while one was open for 0% -> 0% of each run, Pallas kernels for 10% -> 15%
where the time goes in v1:
time: 82.9 us; the launch traced here: 82.4 us
  blocking collectives  42.2 us (51%)
  Pallas kernels  21.5 us (26%)
  starting transfers between devices  8.83 us (11%)
  local copies, waits for them, and re-layouts  4.8 us (6%)
  waiting for transfers between devices  3.98 us (5%)
    all_to_all x2, blocking collectives, spread(): lax.all_to_all(blocks.astype(jnp.float16), ('gx', 'gy'), 0, 0, axis_index...  42.2 us
    pallas_call x2, Pallas kernels, product(): pl.pallas_call(lambda *refs: product_kernel(f, *refs), out_shape=jax.Shap...  12.4 us
    ppermute x6, starting transfers between devices, swapped(): return lax.ppermute(value, axis, pairs)  8.83 us
    pallas_call x1, Pallas kernels, weight_terms(): pl.pallas_call(weight_kernel, out_shape=[half, half], in_specs=[smem()] +...  6.05 us
    unnamed x16, local copies, waits for them, and re-layouts  4.8 us
    ppermute x6, waiting for transfers between devices, swapped(): return lax.ppermute(value, axis, pairs)  3.98 us
  transfers between devices with their start and end apart: 6, of which 3 were waited for; matrix products, arithmetic and copies ran while one was open for 0% of the time, Pallas kernels for 15%

profile of v1, /device:TPU:0, one launch (start us, length us, event | category | flops | bytes accessed | tf_op | source)
XLA Modules:
  0.0 82.4 jit_solution(10802231384520600365)
XLA Ops:
  0.6 0.0 copy-start
  0.6 1.0 %copy-done = bf16[4,8,8,8,128]{4,3,2,1,0:T(8,128)(2,1)S(1)} copy-done((bf16[4,8,8,8,128]{4,3,2,1,0:T(8,128)(2,1)S(1)}, bf16[4,8,8,8,128]{4,3,2,1,0:T(8,128)(2,1)}, u32[]{:S(2)}) %copy-start) | copy-done | bytes 524312
  1.7 0.0 copy-start.1
  1.7 1.0 %copy-done.1 = bf16[4,8,8,8,128]{4,3,2,1,0:T(8,128)(2,1)S(1)} copy-done((bf16[4,8,8,8,128]{4,3,2,1,0:T(8,128)(2,1)S(1)}, bf16[4,8,8,8,128]{4,3,2,1,0:T(8,128)(2,1)}, u32[]{:S(2)}) %copy-start.1) | copy-done | bytes 524312
  2.7 0.0 copy-start.2
  2.7 0.7 copy-done.2
  3.4 0.0 copy-start.4
  3.4 0.7 copy-done.4
  4.1 0.0 copy-start.5
  4.1 0.7 copy-done.5
  4.7 1.2 %pack.1 = (bf16[4,512,128]{2,1,0:T(8,128)(2,1)S(1)}, bf16[4,512,128]{2,1,0:T(8,128)(2,1)S(1)}, bf16[288,128]{1,0:T(8,128)(2,1)S(1)}, bf16[288,128]{1,0:T(8,128)(...) custom-call(s32[2,4]{1,0:T(2,128)S(1)} %bitcast.10, s32[1,4]{1,0:T(1,128)S(1)} %bitcast.11, ...), custom_call_target="tpu_custom_call" | custom-call | tf_op jit(solution)/shard_map/pack/pallas_call | solution.py:88
  6.0 0.5 collective-permute-start
  6.5 0.7 collective-permute-start.1
  7.1 0.3 collective-permute-done.y0.refs_6_
  7.4 0.0 collective-permute-done.1.y1.refs_7_
  7.4 2.9 %collective-permute-start.2 = (bf16[288,128]{1,0:T(8,128)(2,1)S(1)}, bf16[288,128]{1,0:T(8,128)(2,1)S(1)}, u32[]{:S(2)}, u32[]{:S(2)}) collective-permute-start(bf16[288,128]{1,0:T(8,128)(2,1)S(1)} %get-tuple-element.18), channel_id=1, source_target_pairs={{0,4},{4,0},{8,12},{12,8},{16,20},{20,16},{24,28},{28,24},{1,5},{5... | collective-permute-start | bytes 221192 | tf_op jit(solution)/shard_map/ppermute | solution.py:371
  10.3 0.7 collective-permute-start.3
  11.0 1.7 %collective-permute-done.2.refs_4_.x0 = bf16[288,128]{1,0:T(8,128)(2,1)S(1)} collective-permute-done((bf16[288,128]{1,0:T(8,128)(2,1)S(1)}, bf16[288,128]{1,0:T(8,128)(2,1)S(1)}, u32[]{:S(2)}, u32[]{:S(2)}) %collective-permute-start.2) | collective-permute-done | bytes 73760 | tf_op jit(solution)/shard_map/ppermute | solution.py:371
  12.7 0.0 collective-permute-done.3.refs_5_.x1
  12.7 0.0 copy-start.7
  12.7 0.7 copy-done.7
  13.3 6.1 %weight_terms.1 = (f32[1728,128]{1,0:T(8,128)S(1)}, f32[1728,128]{1,0:T(8,128)S(1)}) custom-call(s32[4,27]{1,0:T(4,128)S(1)} %copy-done.7, bf16[4,512,128]{2,1,0:T(8,128)(2,1)S(1)} %get-tuple-element.13.refs_3_.act, bf16[4,512,128]{2,1,0:T(8,128)(2,1)S(1)} %get-tuple-element.20.refs_3_.grd, bf16[288,128]{1,0:T(8,128)(2,1)S(1)} %collective-permute-done.2.refs_4_.x0, ...), custom_call_target="tpu_custom_call" | custom-call | flops 1811939328 | bytes 6291456 | tf_op jit(solution)/shard_map/weight_terms/pallas_call | solution.py:248
  19.4 4.1 %collective-permute-start.4 = (f32[1728,128]{1,0:T(8,128)S(1)}, f32[1728,128]{1,0:T(8,128)S(1)}, u32[]{:S(2)}, u32[]{:S(2)}) collective-permute-start(f32[1728,128]{1,0:T(8,128)S(1)} %get-tuple-element.22), channel_id=1, source_target_pairs={{0,1},{1,0},{2,3},{3,2},{4,5},{5,4},{6,7},{7,6},{8,9},{9,8},{10,11... | collective-permute-start | bytes 2654216 | tf_op jit(solution)/shard_map/ppermute | solution.py:371
  23.5 2.1 %collective-permute-done.4.refs_1_ = f32[1728,128]{1,0:T(8,128)S(1)} collective-permute-done((f32[1728,128]{1,0:T(8,128)S(1)}, f32[1728,128]{1,0:T(8,128)S(1)}, u32[]{:S(2)}, u32[]{:S(2)}) %collective-permute-start.4) | collective-permute-done | bytes 884768 | tf_op jit(solution)/shard_map/ppermute | solution.py:371
  25.5 0.3 merge.1
  25.8 0.1 convert_element_type.15
  25.9 25.4 %all_to_all.10 = f16[16,112,128]{2,1,0:T(8,128)(2,1)S(1)} all-to-all(f16[16,112,128]{2,1,0:T(8,128)(2,1)S(1)} %convert_element_type.15), channel_id=1, replica_groups={{0,2,4,6,8,10,12,14,16,18,20,22,24,26,28,30},{1,3,5,7,9,11,13,15,17,19,..., dimensions={0} | all-to-all | bytes 917504 | tf_op jit(solution)/shard_map/all_to_all | solution.py:383
  51.3 0.1 convert_element_type.16.refs_0_
  51.4 0.0 copy-start.3
  51.4 0.0 copy-start.6
  51.4 0.3 sum_blocks.1
  51.7 0.1 convert_element_type.17
  51.8 16.8 %all_to_all.11 = f16[16,112,128]{2,1,0:T(8,128)(2,1)S(1)} all-to-all(f16[16,112,128]{2,1,0:T(8,128)(2,1)S(1)} %convert_element_type.17), channel_id=1, replica_groups={{0,2,4,6,8,10,12,14,16,18,20,22,24,26,28,30},{1,3,5,7,9,11,13,15,17,19,..., dimensions={0} | all-to-all | bytes 917504 | tf_op jit(solution)/shard_map/all_to_all | solution.py:383
  68.6 0.0 collective-permute-start.5
  68.6 0.0 copy-done.3
  68.6 0.0 copy-done.6
  68.6 6.3 %input_grad_product.1 = bf16[4,512,128]{2,1,0:T(8,128)(2,1)} custom-call(s32[4,27]{1,0:T(4,128)S(1)} %copy-done.7, s32[4,512]{1,0:T(4,128)S(1)} %copy-done.3, bf16[3456,128]{1,0:T(8,128)(2,1)S(1)} %bitcast.12, bf16[4,512,128]{2,1,0:T(8,128)(2,1)S(1)} %get-tuple-element.20.refs_3_.grd, bf16[288,128]{1,0:T(8,128)(2,1)S(1)} %collective-permute-done.2.refs_4_.x0, ...), custom_call_target="tpu_custom_call" | custom-call | flops 1811939328 | bytes 4194304 | tf_op jit(solution)/shard_map/input_grad_product/pallas_call | solution.py:355
  74.9 6.1 %output_product.1 = bf16[4,512,128]{2,1,0:T(8,128)(2,1)} custom-call(s32[4,27]{1,0:T(4,128)S(1)} %copy-done.7, s32[4,512]{1,0:T(4,128)S(1)} %copy-done.3, bf16[3456,128]{1,0:T(8,128)(2,1)S(1)} %bitcast.13, bf16[4,512,128]{2,1,0:T(8,128)(2,1)S(1)} %get-tuple-element.13.refs_3_.act, bf16[288,128]{1,0:T(8,128)(2,1)S(1)} %collective-permute-done.2.refs_4_.x0, ...), custom_call_target="tpu_custom_call" | custom-call | flops 1811939328 | bytes 4194304 | tf_op jit(solution)/shard_map/output_product/pallas_call | solution.py:355
  81.0 0.1 convert_element_type.18.refs_0_
  81.0 0.0 collective-permute-done.5
  81.0 0.1 convert_element_type.19.refs_1_
  81.1 1.3 %decode.1 = f32[2,1728,128]{2,1,0:T(8,128)} custom-call(f32[16,112,128]{2,1,0:T(8,128)S(1)} %convert_element_type.18.refs_0_, f32[16,112,128]{2,1,0:T(8,128)S(1)} %convert_element_type.19.refs_1_), custom_call_target="tpu_custom_call" | custom-call | tf_op jit(solution)/shard_map/decode/pallas_call | solution.py:324
  (1 shorter events, 0.0 us)
Async XLA Ops:
  0.6 1.0 %copy-start = (bf16[4,8,8,8,128]{4,3,2,1,0:T(8,128)(2,1)S(1)}, bf16[4,8,8,8,128]{4,3,2,1,0:T(8,128)(2,1)}, u32[]{:S(2)}) copy-start(bf16[4,8,8,8,128]{4,3,2,1,0:T(8,128)(2,1)} %param.7) | copy-start | bytes 1572868
  1.7 1.0 %copy-start.1 = (bf16[4,8,8,8,128]{4,3,2,1,0:T(8,128)(2,1)S(1)}, bf16[4,8,8,8,128]{4,3,2,1,0:T(8,128)(2,1)}, u32[]{:S(2)}) copy-start(bf16[4,8,8,8,128]{4,3,2,1,0:T(8,128)(2,1)} %param.8) | copy-start | bytes 1572868
  2.7 0.7 copy-start.2
  3.4 0.7 copy-start.4
  4.1 0.7 copy-start.5
  6.0 1.4 %collective-permute-start = (bf16[288,128]{1,0:T(8,128)(2,1)S(1)}, bf16[288,128]{1,0:T(8,128)(2,1)S(1)}, u32[]{:S(2)}, u32[]{:S(2)}) collective-permute-start(bf16[288,128]{1,0:T(8,128)(2,1)S(1)} %get-tuple-element.16), channel_id=1, source_target_pairs={{0,1},{1,0},{2,3},{3,2},{4,5},{5,4},{6,7},{7,6},{8,9},{9,8},{10,11... | collective-permute-start | bytes 221192 | tf_op jit(solution)/shard_map/ppermute | solution.py:371
  6.5 0.9 %collective-permute-start.1 = (bf16[288,128]{1,0:T(8,128)(2,1)S(1)}, bf16[288,128]{1,0:T(8,128)(2,1)S(1)}, u32[]{:S(2)}, u32[]{:S(2)}) collective-permute-start(bf16[288,128]{1,0:T(8,128)(2,1)S(1)} %get-tuple-element.17), channel_id=1, source_target_pairs={{1,2},{2,1},{5,6},{6,5},{9,10},{10,9},{13,14},{14,13},{17,18},{18,... | collective-permute-start | bytes 221192 | tf_op jit(solution)/shard_map/ppermute | solution.py:371
  7.4 5.2 %collective-permute-start.2 = (bf16[288,128]{1,0:T(8,128)(2,1)S(1)}, bf16[288,128]{1,0:T(8,128)(2,1)S(1)}, u32[]{:S(2)}, u32[]{:S(2)}) collective-permute-start(bf16[288,128]{1,0:T(8,128)(2,1)S(1)} %get-tuple-element.18), channel_id=1, source_target_pairs={{0,4},{4,0},{8,12},{12,8},{16,20},{20,16},{24,28},{28,24},{1,5},{5... | collective-permute-start | bytes 221192 | tf_op jit(solution)/shard_map/ppermute | solution.py:371
  10.3 2.3 %collective-permute-start.3 = (bf16[288,128]{1,0:T(8,128)(2,1)S(1)}, bf16[288,128]{1,0:T(8,128)(2,1)S(1)}, u32[]{:S(2)}, u32[]{:S(2)}) collective-permute-start(bf16[288,128]{1,0:T(8,128)(2,1)S(1)} %get-tuple-element.19), channel_id=1, source_target_pairs={{4,8},{8,4},{12,16},{16,12},{20,24},{24,20},{5,9},{9,5},{13,17},{1... | collective-permute-start | bytes 221192 | tf_op jit(solution)/shard_map/ppermute | solution.py:371
  12.7 0.7 copy-start.7
  19.4 6.1 %collective-permute-start.4 = (f32[1728,128]{1,0:T(8,128)S(1)}, f32[1728,128]{1,0:T(8,128)S(1)}, u32[]{:S(2)}, u32[]{:S(2)}) collective-permute-start(f32[1728,128]{1,0:T(8,128)S(1)} %get-tuple-element.22), channel_id=1, source_target_pairs={{0,1},{1,0},{2,3},{3,2},{4,5},{5,4},{6,7},{7,6},{8,9},{9,8},{10,11... | collective-permute-start | bytes 2654216 | tf_op jit(solution)/shard_map/ppermute | solution.py:371
  51.4 17.2 %copy-start.3 = (s32[4,512]{1,0:T(4,128)S(1)}, s32[4,512]{1,0:T(4,128)}, u32[]{:S(2)}) copy-start(s32[4,512]{1,0:T(4,128)} %refs_1_.3) | copy-start | bytes 24580
  51.4 17.2 %copy-start.6 = (bf16[27,128,128]{2,1,0:T(8,128)(2,1)S(1)}, bf16[27,128,128]{2,1,0:T(8,128)(2,1)}, u32[]{:S(2)}) copy-start(bf16[27,128,128]{2,1,0:T(8,128)(2,1)} %param.9) | copy-start | bytes 2654212
  68.6 12.5 %collective-permute-start.5 = (f16[16,112,128]{2,1,0:T(8,128)(2,1)S(1)}, f16[16,112,128]{2,1,0:T(8,128)(2,1)S(1)}, u32[]{:S(2)}, u32[]{:S(2)}) collective-permute-start(f16[16,112,128]{2,1,0:T(8,128)(2,1)S(1)} %all_to_all.11), channel_id=1, source_target_pairs={{0,1},{1,0},{2,3},{3,2},{4,5},{5,4},{6,7},{7,6},{8,9},{9,8},{10,11... | collective-permute-start | bytes 1376264 | tf_op jit(solution)/shard_map/ppermute | solution.py:371

commit v2 on v1

--- a/solution.py
+++ b/solution.py
@@ -24,8 +24,16 @@
     return pl.BlockSpec(memory_space=pltpu.VMEM)
 
 
-def smem():
-    return pl.BlockSpec(memory_space=pltpu.SMEM)
+def hbm():
+    return pl.BlockSpec(memory_space=pltpu.HBM)
+
+
+def fetched(*pairs):
+    copies = [pltpu.make_async_copy(src, dst, sem) for src, dst, sem in pairs]
+    for copy in copies:
+        copy.start()
+    for copy in copies:
+        copy.wait()
 
 
 def mask_columns(mask_ref, s):
@@ -42,18 +50,16 @@
     return 1 - odd if k == 0 else odd
 
 
-def pack_kernel(face_ref, edge_ref, feat_hbm, grad_hbm, mask_hbm, act_ref, grd_ref, *refs):
+def pack_kernel(face_hbm, edge_hbm, feat_hbm, grad_hbm, mask_hbm, act_ref, grd_ref, *refs):
     y_out, x_out = refs[0:2], refs[2:4]
-    raw, mask_ref, full, sems = refs[4:]
-    copies = [
-        pltpu.make_async_copy(mask_hbm, mask_ref, sems.at[0]),
-        pltpu.make_async_copy(feat_hbm, raw.at[0], sems.at[1]),
-        pltpu.make_async_copy(grad_hbm, raw.at[1], sems.at[2]),
-    ]
-    for copy in copies:
-        copy.start()
-    for copy in copies:
-        copy.wait()
+    face_ref, edge_ref, raw, mask_ref, full, sems = refs[4:]
+    fetched(
+        (mask_hbm, mask_ref, sems.at[0]),
+        (feat_hbm, raw.at[0], sems.at[1]),
+        (grad_hbm, raw.at[1], sems.at[2]),
+        (face_hbm, face_ref, sems.at[3]),
+        (edge_hbm, edge_ref, sems.at[4]),
+    )
     for s in range(SLOTS):
         rows = mask_columns(mask_ref, s)
         for f, dst in enumerate((act_ref, grd_ref)):
@@ -88,13 +94,15 @@
     return pl.pallas_call(
         pack_kernel,
         out_shape=[brick, brick] + [send] * 4,
-        in_specs=[smem(), smem()] + [pl.BlockSpec(memory_space=pl.ANY)] * 3,
+        in_specs=[hbm()] * 5,
         out_specs=[vmem()] * 6,
         scratch_shapes=[
+            pltpu.SMEM((FACE, 4), jnp.int32),
+            pltpu.SMEM((1, 4), jnp.int32),
             pltpu.VMEM((2, SLOTS, 512, C), jnp.bfloat16),
             pltpu.VMEM((SLOTS, 512), jnp.int32),
             pltpu.VMEM((2, SLOTS, 8, 8, 8, C), jnp.float32),
-            pltpu.SemaphoreType.DMA((3,)),
+            pltpu.SemaphoreType.DMA((5,)),
         ],
         compiler_params=pltpu.CompilerParams(vmem_limit_bytes=VMEM_LIMIT),
         name="pack",
@@ -124,21 +132,31 @@
     )(*x_send, *y_came)
 
 
-def fill_layers(f, bricks, x_came, y_came, lx, ly, corners):
-    odd_x, odd_y = parity("gx"), parity("gy")
-    zero_layer = jnp.zeros((8, 8, C), jnp.float32)
+def fill_own(bricks, lx, ly, corners):
     for s in range(SLOTS):
         whole = bricks[s].astype(jnp.float32).reshape(8, 8, 8, C)
         for side, at in ((0, 7), (1, 0)):
             lx[side, s] = whole[at]
             ly[side, s] = whole[:, at]
+            for other, far in ((0, 7), (1, 0)):
+                corners[2 * side + other, s] = whole[at, far]
+
+
+def fill_zero(lx, ly, corners, first):
+    for ref in (lx, ly, corners):
+        count = ref.shape[1] - first
+        ref[:, pl.ds(first, count)] = jnp.zeros((ref.shape[0], count) + ref.shape[2:], jnp.float32)
+
+
+def fill_came(f, x_came, y_came, lx, ly, corners):
+    odd_x, odd_y = parity("gx"), parity("gy")
     for came, odd, dst in ((x_came, odd_x, lx), (y_came, odd_y, ly)):
         for k in range(2):
             side = side_of(k, odd)
             for r in range(FACE):
                 rows = came[k][pl.ds((f * FACE + r) * 64, 64)]
                 dst[side, SLOTS + r] = rows.astype(jnp.float32).reshape(8, 8, C)
-            dst[k, SLOTS + FACE] = zero_layer
+            dst[k, SLOTS + FACE] = jnp.zeros((8, 8, C), jnp.float32)
     for k in range(2):
         side = side_of(k, odd_x)
         for j in range(2):
@@ -146,18 +164,14 @@
             corners[2 * side + j, SLOTS + 2 * FACE] = rows[8 * f : 8 * f + 8]
     for sx in range(2):
         for sy in range(2):
-            ax = 0 if sx else 7
-            ay = 0 if sy else 7
             c = 2 * sx + sy
-            for s in range(SLOTS):
-                corners[c, s] = lx[sx, s, ay]
             for r in range(FACE):
-                corners[c, SLOTS + r] = lx[sx, SLOTS + r, ay]
-                corners[c, SLOTS + FACE + r] = ly[sy, SLOTS + r, ax]
+                corners[c, SLOTS + r] = lx[sx, SLOTS + r, 0 if sy else 7]
+                corners[c, SLOTS + FACE + r] = ly[sy, SLOTS + r, 0 if sx else 7]
             corners[c, SLOTS + 2 * FACE + 1] = jnp.zeros((8, C), jnp.float32)
 
 
-def build_columns(s, bricks, near, lx, ly, corners, wide, v):
+def build_columns(s, bricks, near, lx, ly, corners, wide, which):
     line = lax.broadcasted_iota(jnp.int32, (8, C), 0)
 
     def spread(cells, at_x, at_y, depth):
@@ -182,10 +196,15 @@
         low, mid, high = near[s, base], near[s, base + 1], near[s, base + 2]
         entry = jnp.minimum(jnp.minimum(low, mid), high)
         depth = jnp.where(low < ZERO, -1, jnp.where(high < ZERO, 1, 0))
+        if which == "own":
+            depth = jnp.where(entry < SLOTS, depth, 2)
+        if which == "rim":
+            depth = jnp.where(entry < SLOTS, 2, depth)
         return entry, depth
 
     middle = pl.ds(1, 8)
-    spread(bricks[s].astype(jnp.float32).reshape(8, 8, 8, C), middle, middle, None)
+    if which != "rim":
+        spread(bricks[s].astype(jnp.float32).reshape(8, 8, 8, C), middle, middle, None)
     for side, n in ((0, -1), (1, 1)):
         edge_at = pl.ds(0 if n < 0 else 9, 1)
         entry, depth = column(n, 0)
@@ -207,6 +226,9 @@
             place = jnp.where(in_x, SLOTS + entry - first_x, place)
             place = jnp.where(entry < SLOTS, entry, place)
             spread(corners[2 * sx + sy, place].reshape(1, 1, 8, C), pl.ds(9 * sx, 1), pl.ds(9 * sy, 1), depth)
+
+
+def stack_columns(s, wide, v):
     for y in range(3):
         for z in range(3):
             cells = wide[z, :, pl.ds(y, 8)].reshape(10, 64, C).astype(jnp.bfloat16)
@@ -219,15 +241,19 @@
         pltpu.VMEM((2, SLOTS + FACE + 1, 8, 8, C), jnp.float32),
         pltpu.VMEM((4, SLOTS + 2 * FACE + 2, 8, C), jnp.float32),
         pltpu.VMEM((3, 10, 10, 8, C), jnp.float32),
-        pltpu.VMEM((SLOTS, 10, 64, 9 * C), jnp.bfloat16),
+        pltpu.SMEM((SLOTS, 27), jnp.int32),
+        pltpu.SemaphoreType.DMA(()),
     ]
 
 
-def weight_kernel(near, act, grd, x0, x1, y0, y1, keep, send, lx, ly, corners, wide, v, total):
-    fill_layers(0, act, (x0, x1), (y0, y1), lx, ly, corners)
+def inner_kernel(near_hbm, act, grd, out, lx, ly, corners, wide, near, sem, v):
+    fetched((near_hbm, near, sem))
+    fill_own(act, lx, ly, corners)
+    fill_zero(lx, ly, corners, SLOTS)
 
     def per_slot(s, carry):
-        build_columns(s, act, near, lx, ly, corners, wide, v)
+        build_columns(s, act, near, lx, ly, corners, wide, "own")
+        stack_columns(s, wide, v)
         return carry
 
     lax.fori_loop(0, SLOTS, per_slot, 0)
@@ -235,26 +261,80 @@
     for x in range(3):
         for j in range(9):
             cells = v[:, pl.ds(x, 8), :, pl.ds(j * C, C)].reshape(SLOTS * 512, C)
-            total[pl.ds((9 * x + j) * C, C)] = lax.dot_general(
+            out[pl.ds((9 * x + j) * C, C)] = lax.dot_general(
                 cells, rows, (((0,), (0,)), ((), ())), preferred_element_type=jnp.float32
             )
+
+
+def inner_terms(near, act, grd):
+    return pl.pallas_call(
+        inner_kernel,
+        out_shape=jax.ShapeDtypeStruct((ROWS, C), jnp.float32),
+        in_specs=[hbm()] + [vmem()] * 2,
+        out_specs=vmem(),
+        scratch_shapes=columns_scratch() + [pltpu.VMEM((SLOTS, 10, 64, 9 * C), jnp.bfloat16)],
+        compiler_params=pltpu.CompilerParams(vmem_limit_bytes=VMEM_LIMIT),
+        cost_estimate=pl.CostEstimate(flops=2 * 2048 * ROWS * C, bytes_accessed=6 << 20, transcendentals=0),
+        name="inner_terms",
+    )(near, act, grd)
+
+
+def rim_kernel(near_hbm, inner, grd, x0, x1, y0, y1, keep, send, lx, ly, corners, wide, near, sem, vx, vy, total):
+    fetched((near_hbm, near, sem))
+    fill_came(0, (x0, x1), (y0, y1), lx, ly, corners)
+    for s in range(SLOTS):
+        build_columns(s, None, near, lx, ly, corners, wide, "rim")
+        rows = pl.ds(64 * s, 64)
+        for side in range(2):
+            for j in range(9):
+                cells = wide[j % 3, 9 * side, pl.ds(j // 3, 8)]
+                vx[side, rows, pl.ds(j * C, C)] = cells.reshape(64, C).astype(jnp.bfloat16)
+        for z in range(3):
+            for sx in range(2):
+                for sy in range(2):
+                    wide[z, 9 * sx, 9 * sy] = jnp.zeros((8, C), jnp.float32)
+        for side in range(2):
+            for j in range(9):
+                cells = wide[j % 3, pl.ds(j // 3, 8), 9 * side]
+                vy[side, rows, pl.ds(j * C, C)] = cells.reshape(64, C).astype(jnp.bfloat16)
+    grads = grd[...]
+    lines = grads.astype(jnp.float32).reshape(SLOTS, 8, 8, 8, C)
+
+    def term(v, side, j, rows):
+        return lax.dot_general(
+            v[side, :, pl.ds(j * C, C)], rows, (((0,), (0,)), ((), ())), preferred_element_type=jnp.float32
+        )
+
+    rows_x = [grads[:, 448 * side : 448 * side + 64].reshape(SLOTS * 64, C) for side in range(2)]
+    rows_y = [lines[:, :, 7 * side].reshape(SLOTS * 64, C).astype(jnp.bfloat16) for side in range(2)]
+    for x in range(3):
+        for y in range(3):
+            for z in range(3):
+                at = pl.ds((9 * x + 3 * y + z) * C, C)
+                value = inner[at]
+                if x != 1:
+                    value += term(vx, x // 2, 3 * y + z, rows_x[x // 2])
+                if y != 1:
+                    value += term(vy, y // 2, 3 * x + z, rows_y[y // 2])
+                total[at] = value
     core = parity("gy")
     keep[...] = total[pl.ds(pl.multiple_of(core * HALF, 8), HALF)]
     send[...] = total[pl.ds(pl.multiple_of((1 - core) * HALF, 8), HALF)]
 
 
-def weight_terms(near, act, grd, x_came, y_came):
+def rim_terms(near, inner, grd, x_came, y_came):
     half = jax.ShapeDtypeStruct((HALF, C), jnp.float32)
-    return pl.pallas_call(
-        weight_kernel,
+    side = pltpu.VMEM((2, SLOTS * 64, 9 * C), jnp.bfloat16)
+    return pl.pallas_call(
+        rim_kernel,
         out_shape=[half, half],
-        in_specs=[smem()] + [vmem()] * 6,
+        in_specs=[hbm()] + [vmem()] * 6,
         out_specs=[vmem()] * 2,
-        scratch_shapes=columns_scratch() + [pltpu.VMEM((ROWS, C), jnp.float32)],
-        compiler_params=pltpu.CompilerParams(vmem_limit_bytes=VMEM_LIMIT),
-        cost_estimate=pl.CostEstimate(flops=2 * 2048 * ROWS * C, bytes_accessed=6 << 20, transcendentals=0),
-        name="weight_terms",
-    )(near, act, grd, *x_came, *y_came)
+        scratch_shapes=columns_scratch() + [side, side, pltpu.VMEM((ROWS, C), jnp.float32)],
+        compiler_params=pltpu.CompilerParams(vmem_limit_bytes=VMEM_LIMIT),
+        cost_estimate=pl.CostEstimate(flops=2 * 256 * 36 * C * C, bytes_accessed=6 << 20, transcendentals=0),
+        name="rim_terms",
+    )(near, inner, grd, *x_came, *y_came)
 
 
 def power_of(values):
@@ -331,16 +411,20 @@
     )(mine, other)
 
 
-def product_kernel(f, near, mask_ref, kernel_ref, bricks, x0, x1, y0, y1, out, lx, ly, corners, wide, v, *flipped):
+def product_kernel(f, near_hbm, mask_ref, kernel_ref, bricks, x0, x1, y0, y1, out, *refs):
+    lx, ly, corners, wide, near, sem, v, *flipped = refs
+    fetched((near_hbm, near, sem))
     weights = kernel_ref
     if f == 1:
         weights = flipped[0]
         for o in range(27):
             weights[pl.ds((26 - o) * C, C)] = kernel_ref[pl.ds(o * C, C)].T
-    fill_layers(f, bricks, (x0, x1), (y0, y1), lx, ly, corners)
+    fill_own(bricks, lx, ly, corners)
+    fill_came(f, (x0, x1), (y0, y1), lx, ly, corners)
 
     def per_slot(s, carry):
-        build_columns(s, bricks, near, lx, ly, corners, wide, v)
+        build_columns(s, bricks, near, lx, ly, corners, wide, "all")
+        stack_columns(s, wide, v)
         total = jnp.zeros((512, C), jnp.float32)
         for x in range(3):
             cells = v[s, pl.ds(x, 8)].reshape(512, 9 * C)
@@ -355,9 +439,11 @@
     return pl.pallas_call(
         lambda *refs: product_kernel(f, *refs),
         out_shape=jax.ShapeDtypeStruct((SLOTS, 512, C), jnp.bfloat16),
-        in_specs=[smem()] + [vmem()] * 7,
+        in_specs=[hbm()] + [vmem()] * 7,
         out_specs=vmem(),
-        scratch_shapes=columns_scratch() + ([pltpu.VMEM((ROWS, C), jnp.bfloat16)] if f else []),
+        scratch_shapes=columns_scratch()
+        + [pltpu.VMEM((SLOTS, 10, 64, 9 * C), jnp.bfloat16)]
+        + ([pltpu.VMEM((ROWS, C), jnp.bfloat16)] if f else []),
         compiler_params=pltpu.CompilerParams(vmem_limit_bytes=VMEM_LIMIT),
         cost_estimate=pl.CostEstimate(flops=2 * 2048 * ROWS * C, bytes_accessed=4 << 20, transcendentals=0),
         name=("output_product", "input_grad_product")[f],
@@ -380,9 +466,7 @@
     same_core = [[i for i in range(parts) if i % size_y % 2 == core] for core in range(2)]
 
     def spread(blocks):
-        return lax.all_to_all(
-            blocks.astype(jnp.float16), ("gx", "gy"), 0, 0, axis_index_groups=same_core, tiled=True
-        )
+        return lax.all_to_all(blocks, ("gx", "gy"), 0, 0, axis_index_groups=same_core, tiled=True)
 
     act, grd, y0, y1, x0, x1 = pack(
         features.reshape(SLOTS, 512, C), out_grad.reshape(SLOTS, 512, C), voxel_mask, face_sends, edge_sends
@@ -390,15 +474,20 @@
     y_came = [swapped(y0, "gy", 0), swapped(y1, "gy", 1)]
     x0, x1 = forward_corners((x0, x1), y_came)
     x_came = [swapped(x0, "gx", 0), swapped(x1, "gx", 1)]
-    keep, send = weight_terms(neighbours, act, grd, x_came, y_came)
-    blocks = merge(groups, take, held, keep, swapped(send, "gy", 0))
-    mine = spread(sum_blocks(take, spread(blocks).astype(jnp.float32)))
+    inner = inner_terms(neighbours, act, grd)
+    keep, send = rim_terms(neighbours, inner, grd, x_came, y_came)
+    blocks = merge(groups, take, held, keep, swapped(send, "gy", 0)).astype(jnp.float16)
+    rows = kernel.reshape(ROWS, C)
+    blocks, act = lax.optimization_barrier((blocks, act))
+    output = product(0, neighbours, voxel_mask, rows, act, x_came, y_came)
+    arrived, output = lax.optimization_barrier((spread(blocks), output))
+    copies = sum_blocks(take, arrived.astype(jnp.float32)).astype(jnp.float16)
+    copies, grd = lax.optimization_barrier((copies, grd))
+    input_grad = product(1, neighbours, voxel_mask, rows, grd, x_came, y_came)
+    mine, input_grad = lax.optimization_barrier((spread(copies), input_grad))
     other = swapped(mine, "gy", 0)
     scale = 1.0 / math.sqrt(parts * SLOTS * 512)
     weight = decode(take, scale, mine.astype(jnp.float32), other.astype(jnp.float32))
-    rows = kernel.reshape(ROWS, C)
-    output = product(0, neighbours, voxel_mask, rows, act, x_came, y_came)
-    input_grad = product(1, neighbours, voxel_mask, rows, grd, x_came, y_came)
     shape = (SLOTS, 8, 8, 8, C)
     return output.reshape(shape), input_grad.reshape(shape), weight.reshape(27, C, C)
 

time: 82.9 us -> 74.6 us (0.90)
  blocking collectives: 42.2 us -> 0 us
  waiting for transfers between devices: 3.98 us -> 19 us
  starting transfers between devices: 8.83 us -> 22 us
  Pallas kernels: 21.5 us -> 24.4 us
  other arithmetic: 0.31 us -> 1.84 us
  local copies, waits for them, and re-layouts: 4.8 us -> 6 us
    all_to_all x2 -> x0, blocking collectives: 42.2 us -> none  [spread(): lax.all_to_all(blocks.astype(jnp.float16), ('gx', 'gy'), 0, 0, axis_index...]
    all_to_all x0 -> x2, waiting for transfers between devices: none -> 15 us  [spread(): lax.all_to_all(blocks, ('gx', 'gy'), 0, 0, axis_index_groups=same_core, t...]
    all_to_all x0 -> x2, starting transfers between devices: none -> 12.6 us  [spread(): lax.all_to_all(blocks, ('gx', 'gy'), 0, 0, axis_index_groups=same_core, t...]
    pallas_call x1 -> x2, Pallas kernels: 6.05 us -> 8.88 us  [the longest x1 5.42 us: inner_terms(): pl.pallas_call(inner_kernel, out_shape=jax.ShapeDtypeStruct((ROWS, C), jn...]
    convert_element_type x3, other arithmetic: 0.19 us -> 1.72 us  [the longest x2 0.89 us: local(): copies = sum_blocks(take, arrived.astype(jnp.float32)).astype(jnp.float16)]
    unnamed x16 -> x20, local copies, waits for them, and re-layouts: 4.8 us -> 6 us
  transfers between devices with their start and end apart: 6 -> 8, of which waited for: 3 -> 5; matrix products, arithmetic and copies ran while one was open for 0% -> 0% of each run, Pallas kernels for 15% -> 24%
where the time goes in v2:
time: 74.6 us; the launch traced here: 74.1 us
  Pallas kernels  24.4 us (33%)
  starting transfers between devices  22 us (29%)
  waiting for transfers between devices  19 us (25%)
  local copies, waits for them, and re-layouts  6 us (8%)
  other arithmetic  1.84 us (2%)
  between operations  0.82 us (1%)
    all_to_all x2, waiting for transfers between devices, spread(): lax.all_to_all(blocks, ('gx', 'gy'), 0, 0, axis_index_groups=same_core, t...  15 us
    all_to_all x2, starting transfers between devices, spread(): lax.all_to_all(blocks, ('gx', 'gy'), 0, 0, axis_index_groups=same_core, t...  12.6 us
    pallas_call x2, Pallas kernels, product(): pl.pallas_call(lambda *refs: product_kernel(f, *refs), out_shape=jax.Shap...  12.4 us
    ppermute x6, starting transfers between devices, swapped(): return lax.ppermute(value, axis, pairs)  9.42 us
    unnamed x20, local copies, waits for them, and re-layouts  6 us
    pallas_call x1, Pallas kernels, inner_terms(): pl.pallas_call(inner_kernel, out_shape=jax.ShapeDtypeStruct((ROWS, C), jn...  5.42 us
    ppermute x6, waiting for transfers between devices, swapped(): return lax.ppermute(value, axis, pairs)  4.06 us
    pallas_call x1, Pallas kernels, rim_terms(): pl.pallas_call(rim_kernel, out_shape=[half, half], in_specs=[hbm()] + [vm...  3.47 us
  transfers between devices with their start and end apart: 8, of which 5 were waited for; matrix products, arithmetic and copies ran while one was open for 0% of the time, Pallas kernels for 24%

profile of v2, /device:TPU:0, one launch (start us, length us, event | category | flops | bytes accessed | tf_op | source)
XLA Modules:
  0.0 74.1 jit_solution(3480319304206917017)
XLA Ops:
  0.6 0.0 copy-start.1
  0.6 1.0 %copy-done.1 = bf16[4,8,8,8,128]{4,3,2,1,0:T(8,128)(2,1)S(1)} copy-done((bf16[4,8,8,8,128]{4,3,2,1,0:T(8,128)(2,1)S(1)}, bf16[4,8,8,8,128]{4,3,2,1,0:T(8,128)(2,1)}, u32[]{:S(2)}) %copy-start.1) | copy-done | bytes 524312
  1.7 0.0 copy-start.2
  1.7 1.0 %copy-done.2 = bf16[4,8,8,8,128]{4,3,2,1,0:T(8,128)(2,1)S(1)} copy-done((bf16[4,8,8,8,128]{4,3,2,1,0:T(8,128)(2,1)S(1)}, bf16[4,8,8,8,128]{4,3,2,1,0:T(8,128)(2,1)}, u32[]{:S(2)}) %copy-start.2) | copy-done | bytes 524312
  2.7 0.0 copy-start.3
  2.7 0.7 copy-done.3
  3.4 0.0 copy-start.7
  3.4 0.7 copy-done.7
  4.1 0.0 copy-start.8
  4.1 0.7 copy-done.8
  4.7 1.2 %pack.1 = (bf16[4,512,128]{2,1,0:T(8,128)(2,1)S(1)}, bf16[4,512,128]{2,1,0:T(8,128)(2,1)S(1)}, bf16[288,128]{1,0:T(8,128)(2,1)S(1)}, bf16[288,128]{1,0:T(8,128)(...) custom-call(s32[2,4]{1,0:T(2,128)S(1)} %bitcast.10, s32[1,4]{1,0:T(1,128)S(1)} %bitcast.11, ...), custom_call_target="tpu_custom_call" | custom-call | tf_op jit(solution)/shard_map/pack/pallas_call | solution.py:94
  6.0 0.5 collective-permute-start
  6.5 0.7 collective-permute-start.1
  7.1 0.3 collective-permute-done.y0.refs_6_
  7.4 0.0 collective-permute-done.1.y1.refs_7_
  7.4 2.9 %collective-permute-start.2 = (bf16[288,128]{1,0:T(8,128)(2,1)S(1)}, bf16[288,128]{1,0:T(8,128)(2,1)S(1)}, u32[]{:S(2)}, u32[]{:S(2)}) collective-permute-start(bf16[288,128]{1,0:T(8,128)(2,1)S(1)} %get-tuple-element.27), channel_id=1, source_target_pairs={{0,4},{4,0},{8,12},{12,8},{16,20},{20,16},{24,28},{28,24},{1,5},{5... | collective-permute-start | bytes 221192 | tf_op jit(solution)/shard_map/ppermute | solution.py:457
  10.3 0.7 collective-permute-start.3
  11.0 0.0 copy-start.5
  11.0 0.7 copy-done.5
  11.7 5.4 %inner_terms.1.inner = f32[3456,128]{1,0:T(8,128)S(1)} custom-call(s32[4,27]{1,0:T(4,128)S(1)} %copy-done.5, bf16[4,512,128]{2,1,0:T(8,128)(2,1)S(1)} %get-tuple-element.32.act.refs_3_, bf16[4,512,128]{2,1,0:T(8,128)(2,1)S(1)} %get-tuple-element.36.grd.refs_3_), custom_call_target="tpu_custom_call" | custom-call | flops 1811939328 | bytes 6291456 | tf_op jit(solution)/shard_map/inner_terms/pallas_call | solution.py:270
  17.1 0.0 copy-start
  17.1 1.2 %copy-done = f32[3456,128]{1,0:T(8,128)} copy-done((f32[3456,128]{1,0:T(8,128)}, f32[3456,128]{1,0:T(8,128)S(1)}, u32[]{:S(2)}) %copy-start) | copy-done | bytes 1769496
  18.3 0.0 collective-permute-done.2.x0.refs_4_
  18.3 0.0 collective-permute-done.3.x1.refs_5_
  18.3 3.5 %rim_terms.1 = (f32[1728,128]{1,0:T(8,128)S(1)}, f32[1728,128]{1,0:T(8,128)S(1)}) custom-call(s32[4,27]{1,0:T(4,128)S(1)} %copy-done.5, f32[3456,128]{1,0:T(8,128)} %copy-done, bf16[4,512,128]{2,1,0:T(8,128)(2,1)S(1)} %get-tuple-element.36.grd.refs_3_, bf16[288,128]{1,0:T(8,128)(2,1)S(1)} %collective-permute-done.2.x0.refs_4_, ...), custom_call_target="tpu_custom_call" | custom-call | flops 301989888 | bytes 6291456 | tf_op jit(solution)/shard_map/rim_terms/pallas_call | solution.py:328
  21.8 4.7 %collective-permute-start.4 = (f32[1728,128]{1,0:T(8,128)S(1)}, f32[1728,128]{1,0:T(8,128)S(1)}, u32[]{:S(2)}, u32[]{:S(2)}) collective-permute-start(f32[1728,128]{1,0:T(8,128)S(1)} %get-tuple-element.30), channel_id=1, source_target_pairs={{0,1},{1,0},{2,3},{3,2},{4,5},{5,4},{6,7},{7,6},{8,9},{9,8},{10,11... | collective-permute-start | bytes 2654216 | tf_op jit(solution)/shard_map/ppermute | solution.py:457
  26.5 2.1 %collective-permute-done.4.refs_1_ = f32[1728,128]{1,0:T(8,128)S(1)} collective-permute-done((f32[1728,128]{1,0:T(8,128)S(1)}, f32[1728,128]{1,0:T(8,128)S(1)}, u32[]{:S(2)}, u32[]{:S(2)}) %collective-permute-start.4) | collective-permute-done | bytes 884768 | tf_op jit(solution)/shard_map/ppermute | solution.py:457
  28.5 0.3 merge.1
  28.8 0.0 copy-start.4
  28.8 0.0 copy-start.6
  28.8 0.0 copy-start.9
  28.9 0.8 %convert_element_type.15 = f16[16,112,128]{2,1,0:T(8,128)(2,1)} convert(f32[16,112,128]{2,1,0:T(8,128)S(1)} %merge.1) | non-fusion elementwise | flops 229376 | bytes 1376256 | tf_op jit(solution)/shard_map/convert_element_type | solution.py:479
  29.7 8.8 %all-to-all-start = ((f16[16,112,128]{2,1,0:T(8,128)(2,1)}), f16[16,112,128]{2,1,0:T(8,128)(2,1)S(1)}, u32[]{:S(2)}, u32[]{:S(2)}) async-start(f16[16,112,128]{2,1,0:T(8,128)(2,1)} %convert_element_type.15), calls=%async_computation | async-start | bytes 917504 | tf_op jit(solution)/shard_map/all_to_all | solution.py:469
  38.5 0.0 copy-done.4
  38.5 0.0 copy-done.6
  38.5 0.0 copy-done.9
  38.5 6.1 %output_product.1 = bf16[4,512,128]{2,1,0:T(8,128)(2,1)} custom-call(s32[4,27]{1,0:T(4,128)S(1)} %copy-done.6, s32[4,512]{1,0:T(4,128)S(1)} %copy-done.4, bf16[3456,128]{1,0:T(8,128)(2,1)S(1)} %bitcast.12, bf16[4,512,128]{2,1,0:T(8,128)(2,1)S(1)} %get-tuple-element.32.act.refs_3_, bf16[288,128]{1,0:T(8,128)(2,1)S(1)} %collective-permute-done.2.x0.refs_4_, ...), custom_call_target="tpu_custom_call" | custom-call | flops 1811939328 | bytes 4194304 | tf_op jit(solution)/shard_map/output_product/pallas_call | solution.py:439
  44.6 8.0 %all-to-all-done = f16[16,112,128]{2,1,0:T(8,128)(2,1)S(1)} async-done(((f16[16,112,128]{2,1,0:T(8,128)(2,1)}), f16[16,112,128]{2,1,0:T(8,128)(2,1)S(1)}, u32[]{:S(2)}, u32[]{:S(2)}) %all-to-all-start) | async-done | bytes 458784 | tf_op jit(solution)/shard_map/all_to_all | solution.py:469
  52.7 0.1 convert_element_type.16.refs_0_
  52.7 0.3 sum_blocks.1
  53.0 0.8 %convert_element_type.17 = f16[16,112,128]{2,1,0:T(8,128)(2,1)} convert(f32[16,112,128]{2,1,0:T(8,128)S(1)} %sum_blocks.1) | non-fusion elementwise | flops 229376 | bytes 1376256 | tf_op jit(solution)/shard_map/convert_element_type | solution.py:484
  53.8 3.8 %all-to-all-start.1 = ((f16[16,112,128]{2,1,0:T(8,128)(2,1)}), f16[16,112,128]{2,1,0:T(8,128)(2,1)S(1)}, u32[]{:S(2)}, u32[]{:S(2)}) async-start(f16[16,112,128]{2,1,0:T(8,128)(2,1)} %convert_element_type.17), calls=%async_computation.1 | async-start | bytes 917504 | tf_op jit(solution)/shard_map/all_to_all | solution.py:469
  57.6 6.3 %input_grad_product.1 = bf16[4,512,128]{2,1,0:T(8,128)(2,1)} custom-call(s32[4,27]{1,0:T(4,128)S(1)} %copy-done.6, s32[4,512]{1,0:T(4,128)S(1)} %copy-done.4, bf16[3456,128]{1,0:T(8,128)(2,1)S(1)} %bitcast.13, bf16[4,512,128]{2,1,0:T(8,128)(2,1)S(1)} %get-tuple-element.36.grd.refs_3_, bf16[288,128]{1,0:T(8,128)(2,1)S(1)} %collective-permute-done.2.x0.refs_4_, ...), custom_call_target="tpu_custom_call" | custom-call | flops 1811939328 | bytes 4194304 | tf_op jit(solution)/shard_map/input_grad_product/pallas_call | solution.py:439
  63.9 6.9 %all-to-all-done.1 = f16[16,112,128]{2,1,0:T(8,128)(2,1)S(1)} async-done(((f16[16,112,128]{2,1,0:T(8,128)(2,1)}), f16[16,112,128]{2,1,0:T(8,128)(2,1)S(1)}, u32[]{:S(2)}, u32[]{:S(2)}) %all-to-all-start.1) | async-done | bytes 458784 | tf_op jit(solution)/shard_map/all_to_all | solution.py:469
  70.8 0.0 collective-permute-start.5
  70.8 0.1 convert_element_type.18.refs_0_
  70.9 1.7 %collective-permute-done.5 = f16[16,112,128]{2,1,0:T(8,128)(2,1)S(1)} collective-permute-done((f16[16,112,128]{2,1,0:T(8,128)(2,1)S(1)}, f16[16,112,128]{2,1,0:T(8,128)(2,1)S(1)}, u32[]{:S(2)}, u32[]{:S(2)}) %collective-permute-start.5) | collective-permute-done | bytes 458784 | tf_op jit(solution)/shard_map/ppermute | solution.py:457
  72.7 0.1 convert_element_type.19.refs_1_
  72.7 1.3 %decode.1 = f32[2,1728,128]{2,1,0:T(8,128)} custom-call(f32[16,112,128]{2,1,0:T(8,128)S(1)} %convert_element_type.18.refs_0_, f32[16,112,128]{2,1,0:T(8,128)S(1)} %convert_element_type.19.refs_1_), custom_call_target="tpu_custom_call" | custom-call | tf_op jit(solution)/shard_map/decode/pallas_call | solution.py:404
  (1 shorter events, 0.0 us)
Async XLA Ops:
  0.6 1.0 %copy-start.1 = (bf16[4,8,8,8,128]{4,3,2,1,0:T(8,128)(2,1)S(1)}, bf16[4,8,8,8,128]{4,3,2,1,0:T(8,128)(2,1)}, u32[]{:S(2)}) copy-start(bf16[4,8,8,8,128]{4,3,2,1,0:T(8,128)(2,1)} %param.7) | copy-start | bytes 1572868
  1.7 1.0 %copy-start.2 = (bf16[4,8,8,8,128]{4,3,2,1,0:T(8,128)(2,1)S(1)}, bf16[4,8,8,8,128]{4,3,2,1,0:T(8,128)(2,1)}, u32[]{:S(2)}) copy-start(bf16[4,8,8,8,128]{4,3,2,1,0:T(8,128)(2,1)} %param.8) | copy-start | bytes 1572868
  2.7 0.7 copy-start.3
  3.4 0.7 copy-start.7
  4.1 0.7 copy-start.8
  6.0 1.4 %collective-permute-start = (bf16[288,128]{1,0:T(8,128)(2,1)S(1)}, bf16[288,128]{1,0:T(8,128)(2,1)S(1)}, u32[]{:S(2)}, u32[]{:S(2)}) collective-permute-start(bf16[288,128]{1,0:T(8,128)(2,1)S(1)} %get-tuple-element.25), channel_id=1, source_target_pairs={{0,1},{1,0},{2,3},{3,2},{4,5},{5,4},{6,7},{7,6},{8,9},{9,8},{10,11... | collective-permute-start | bytes 221192 | tf_op jit(solution)/shard_map/ppermute | solution.py:457
  6.5 0.9 %collective-permute-start.1 = (bf16[288,128]{1,0:T(8,128)(2,1)S(1)}, bf16[288,128]{1,0:T(8,128)(2,1)S(1)}, u32[]{:S(2)}, u32[]{:S(2)}) collective-permute-start(bf16[288,128]{1,0:T(8,128)(2,1)S(1)} %get-tuple-element.26), channel_id=1, source_target_pairs={{1,2},{2,1},{5,6},{6,5},{9,10},{10,9},{13,14},{14,13},{17,18},{18,... | collective-permute-start | bytes 221192 | tf_op jit(solution)/shard_map/ppermute | solution.py:457
  7.4 10.9 %collective-permute-start.2 = (bf16[288,128]{1,0:T(8,128)(2,1)S(1)}, bf16[288,128]{1,0:T(8,128)(2,1)S(1)}, u32[]{:S(2)}, u32[]{:S(2)}) collective-permute-start(bf16[288,128]{1,0:T(8,128)(2,1)S(1)} %get-tuple-element.27), channel_id=1, source_target_pairs={{0,4},{4,0},{8,12},{12,8},{16,20},{20,16},{24,28},{28,24},{1,5},{5... | collective-permute-start | bytes 221192 | tf_op jit(solution)/shard_map/ppermute | solution.py:457
  10.3 8.0 %collective-permute-start.3 = (bf16[288,128]{1,0:T(8,128)(2,1)S(1)}, bf16[288,128]{1,0:T(8,128)(2,1)S(1)}, u32[]{:S(2)}, u32[]{:S(2)}) collective-permute-start(bf16[288,128]{1,0:T(8,128)(2,1)S(1)} %get-tuple-element.28), channel_id=1, source_target_pairs={{4,8},{8,4},{12,16},{16,12},{20,24},{24,20},{5,9},{9,5},{13,17},{1... | collective-permute-start | bytes 221192 | tf_op jit(solution)/shard_map/ppermute | solution.py:457
  11.0 0.7 copy-start.5
  17.1 1.2 %copy-start = (f32[3456,128]{1,0:T(8,128)}, f32[3456,128]{1,0:T(8,128)S(1)}, u32[]{:S(2)}) copy-start(f32[3456,128]{1,0:T(8,128)S(1)} %inner_terms.1.inner) | copy-start | bytes 5308420
  21.8 6.7 %collective-permute-start.4 = (f32[1728,128]{1,0:T(8,128)S(1)}, f32[1728,128]{1,0:T(8,128)S(1)}, u32[]{:S(2)}, u32[]{:S(2)}) collective-permute-start(f32[1728,128]{1,0:T(8,128)S(1)} %get-tuple-element.30), channel_id=1, source_target_pairs={{0,1},{1,0},{2,3},{3,2},{4,5},{5,4},{6,7},{7,6},{8,9},{9,8},{10,11... | collective-permute-start | bytes 2654216 | tf_op jit(solution)/shard_map/ppermute | solution.py:457
  28.8 9.7 %copy-start.4 = (s32[4,512]{1,0:T(4,128)S(1)}, s32[4,512]{1,0:T(4,128)}, u32[]{:S(2)}) copy-start(s32[4,512]{1,0:T(4,128)} %refs_1_.3) | copy-start | bytes 24580
  28.8 9.7 %copy-start.6 = (s32[4,27]{1,0:T(4,128)S(1)}, s32[4,27]{1,0:T(4,128)}, u32[]{:S(2)}) copy-start(s32[4,27]{1,0:T(4,128)} %refs_0_.3) | copy-start | bytes 1300
  28.8 9.7 %copy-start.9 = (bf16[27,128,128]{2,1,0:T(8,128)(2,1)S(1)}, bf16[27,128,128]{2,1,0:T(8,128)(2,1)}, u32[]{:S(2)}) copy-start(bf16[27,128,128]{2,1,0:T(8,128)(2,1)} %param.9) | copy-start | bytes 2654212
  29.7 23.0 %all-to-all-start = ((f16[16,112,128]{2,1,0:T(8,128)(2,1)}), f16[16,112,128]{2,1,0:T(8,128)(2,1)S(1)}, u32[]{:S(2)}, u32[]{:S(2)}) async-start(f16[16,112,128]{2,1,0:T(8,128)(2,1)} %convert_element_type.15), calls=%async_computation | async-start | bytes 917504 | tf_op jit(solution)/shard_map/all_to_all | solution.py:469
  53.8 17.0 %all-to-all-start.1 = ((f16[16,112,128]{2,1,0:T(8,128)(2,1)}), f16[16,112,128]{2,1,0:T(8,128)(2,1)S(1)}, u32[]{:S(2)}, u32[]{:S(2)}) async-start(f16[16,112,128]{2,1,0:T(8,128)(2,1)} %convert_element_type.17), calls=%async_computation.1 | async-start | bytes 917504 | tf_op jit(solution)/shard_map/all_to_all | solution.py:469
  70.8 1.8 %collective-permute-start.5 = (f16[16,112,128]{2,1,0:T(8,128)(2,1)S(1)}, f16[16,112,128]{2,1,0:T(8,128)(2,1)S(1)}, u32[]{:S(2)}, u32[]{:S(2)}) collective-permute-start(f16[16,112,128]{2,1,0:T(8,128)(2,1)S(1)} %all-to-all-done.1), channel_id=1, source_target_pairs={{0,1},{1,0},{2,3},{3,2},{4,5},{5,4},{6,7},{7,6},{8,9},{9,8},{10,11... | collective-permute-start | bytes 1376264 | tf_op jit(solution)/shard_map/ppermute | solution.py:457

commit v3 on v2

--- a/solution.py
+++ b/solution.py
@@ -15,9 +15,11 @@
 ZERO = SLOTS + 4 * FACE + 4
 ROWS = 27 * C
 FACE_ROWS = 2 * FACE * 64
-SEND_ROWS = FACE_ROWS + 32
+X_ROWS = FACE_ROWS + 32
+Y_ROWS = FACE_ROWS + 48
 HALF = ROWS // 2
-VMEM_LIMIT = 50 * 1024 * 1024
+VMEM_LIMIT = 32 * 1024 * 1024
+PACK_LIMIT = 60 * 1024 * 1024
 
 
 def vmem():
@@ -50,15 +52,24 @@
     return 1 - odd if k == 0 else odd
 
 
-def pack_kernel(face_hbm, edge_hbm, feat_hbm, grad_hbm, mask_hbm, act_ref, grd_ref, *refs):
+def shifts(cells, same, below, above):
+    line = lax.broadcasted_iota(jnp.int32, cells.shape, cells.ndim - 2)
+    axis = cells.ndim - 2
+    up = jnp.where((same & (line >= 1)) | (below & (line == 0)), pltpu.roll(cells, 1, axis), 0.0)
+    down = jnp.where((same & (line <= 6)) | (above & (line == 7)), pltpu.roll(cells, 7, axis), 0.0)
+    return up, jnp.where(same, cells, 0.0), down
+
+
+def pack_kernel(face_hbm, edge_hbm, near_hbm, feat_hbm, grad_hbm, mask_hbm, act_ref, grd_ref, *refs):
     y_out, x_out = refs[0:2], refs[2:4]
-    face_ref, edge_ref, raw, mask_ref, full, sems = refs[4:]
+    face_ref, edge_ref, near, raw, mask_ref, full, sems = refs[4:]
     fetched(
         (mask_hbm, mask_ref, sems.at[0]),
         (feat_hbm, raw.at[0], sems.at[1]),
         (grad_hbm, raw.at[1], sems.at[2]),
         (face_hbm, face_ref, sems.at[3]),
         (edge_hbm, edge_ref, sems.at[4]),
+        (near_hbm, near, sems.at[5]),
     )
     for s in range(SLOTS):
         rows = mask_columns(mask_ref, s)
@@ -77,59 +88,72 @@
                     layer = full[f, slot, :, 7 * side] if axis else full[f, slot, 7 * side]
                     layer = jnp.where(entry < SLOTS, layer, 0.0)
                     outs[k][pl.ds((f * FACE + r) * 64, 64)] = layer.reshape(64, C).astype(jnp.bfloat16)
+            lines = []
             for far in range(2):
+                corner = 2 * far + side if axis else 2 * side + far
+                entry = edge_ref[0, corner]
+                slot = jnp.clip(entry, 0, SLOTS - 1)
+                live = entry < SLOTS
+                at_x, at_y = (7 * far, 7 * side) if axis else (7 * side, 7 * far)
                 if axis == 0:
-                    outs[k][pl.ds(FACE_ROWS + 16 * far, 16)] = jnp.zeros((16, C), jnp.bfloat16)
+                    for f in range(2):
+                        lines.append(jnp.where(live, full[f, slot, at_x, at_y], 0.0))
                     continue
-                entry = edge_ref[0, 2 * far + side]
-                slot = jnp.clip(entry, 0, SLOTS - 1)
-                lines = [full[f, slot, 7 * far, 7 * side] for f in range(2)]
-                lines = jnp.where(entry < SLOTS, jnp.concatenate(lines, axis=0), 0.0)
-                outs[k][pl.ds(FACE_ROWS + 16 * far, 16)] = lines.astype(jnp.bfloat16)
-
-
-def pack(features, out_grad, mask, face_sends, edge_sends):
-    send = jax.ShapeDtypeStruct((SEND_ROWS, C), jnp.bfloat16)
+                base = 18 * far + 6 * side
+                low, mid, high = near[slot, base], near[slot, base + 1], near[slot, base + 2]
+                up, same, down = shifts(
+                    full[1, slot, at_x, at_y],
+                    live & (mid < ZERO),
+                    live & (high < ZERO),
+                    live & (low < ZERO),
+                )
+                lines += [down, same, up]
+            lines = jnp.concatenate(lines, axis=0).astype(jnp.bfloat16)
+            outs[k][pl.ds(FACE_ROWS, lines.shape[0])] = lines
+
+
+def pack(features, out_grad, mask, near, face_sends, edge_sends):
+    sends = [jax.ShapeDtypeStruct((rows, C), jnp.bfloat16) for rows in (Y_ROWS, Y_ROWS, X_ROWS, X_ROWS)]
     brick = jax.ShapeDtypeStruct((SLOTS, 512, C), jnp.bfloat16)
     return pl.pallas_call(
         pack_kernel,
-        out_shape=[brick, brick] + [send] * 4,
-        in_specs=[hbm()] * 5,
+        out_shape=[brick, brick] + sends,
+        in_specs=[hbm()] * 6,
         out_specs=[vmem()] * 6,
         scratch_shapes=[
             pltpu.SMEM((FACE, 4), jnp.int32),
             pltpu.SMEM((1, 4), jnp.int32),
+            pltpu.SMEM((SLOTS, 27), jnp.int32),
             pltpu.VMEM((2, SLOTS, 512, C), jnp.bfloat16),
             pltpu.VMEM((SLOTS, 512), jnp.int32),
             pltpu.VMEM((2, SLOTS, 8, 8, 8, C), jnp.float32),
-            pltpu.SemaphoreType.DMA((5,)),
+            pltpu.SemaphoreType.DMA((6,)),
         ],
-        compiler_params=pltpu.CompilerParams(vmem_limit_bytes=VMEM_LIMIT),
+        compiler_params=pltpu.CompilerParams(vmem_limit_bytes=PACK_LIMIT),
         name="pack",
-    )(face_sends.T, edge_sends.T, features, out_grad, mask)
-
-
-def forward_kernel(x0, x1, y0, y1, out0, out1):
+    )(face_sends.T, edge_sends.T, near, features, out_grad, mask)
+
+
+def forward_kernel(x0, x1, out0, out1):
     odd_x, odd_y = parity("gx"), parity("gy")
     for k, out in enumerate((out0, out1)):
-        far = side_of(k, odd_x)
-        for j, came in enumerate((y0, y1)):
-            source = side_of(j, odd_y)
+        far = side_of(k, odd_y)
+        for j, came in enumerate((x0, x1)):
+            source = side_of(j, odd_x)
             rows = came[pl.ds(pl.multiple_of(FACE_ROWS + 16 * far, 16), 16)]
-            out[pl.ds(pl.multiple_of(FACE_ROWS + 16 * source, 16), 16)] = rows
-        out[pl.ds(0, FACE_ROWS)] = (x0, x1)[k][pl.ds(0, FACE_ROWS)]
-
-
-def forward_corners(x_send, y_came):
-    send = jax.ShapeDtypeStruct((SEND_ROWS, C), jnp.bfloat16)
+            out[pl.ds(pl.multiple_of(16 * source, 16), 16)] = rows
+
+
+def forward_corners(x_came):
+    send = jax.ShapeDtypeStruct((32, C), jnp.bfloat16)
     return pl.pallas_call(
         forward_kernel,
         out_shape=[send] * 2,
-        in_specs=[vmem()] * 4,
+        in_specs=[vmem()] * 2,
         out_specs=[vmem()] * 2,
         compiler_params=pltpu.CompilerParams(vmem_limit_bytes=VMEM_LIMIT),
         name="forward_corners",
-    )(*x_send, *y_came)
+    )(*x_came)
 
 
 def fill_own(bricks, lx, ly, corners):
@@ -148,7 +172,7 @@
         ref[:, pl.ds(first, count)] = jnp.zeros((ref.shape[0], count) + ref.shape[2:], jnp.float32)
 
 
-def fill_came(f, x_came, y_came, lx, ly, corners):
+def fill_came(f, x_came, y_came, edges, lx, ly, corners):
     odd_x, odd_y = parity("gx"), parity("gy")
     for came, odd, dst in ((x_came, odd_x, lx), (y_came, odd_y, ly)):
         for k in range(2):
@@ -157,11 +181,11 @@
                 rows = came[k][pl.ds((f * FACE + r) * 64, 64)]
                 dst[side, SLOTS + r] = rows.astype(jnp.float32).reshape(8, 8, C)
             dst[k, SLOTS + FACE] = jnp.zeros((8, 8, C), jnp.float32)
-    for k in range(2):
-        side = side_of(k, odd_x)
+    for k, came in enumerate(edges):
+        side = side_of(k, odd_y)
         for j in range(2):
-            rows = x_came[k][pl.ds(FACE_ROWS + 16 * j, 16)].astype(jnp.float32)
-            corners[2 * side + j, SLOTS + 2 * FACE] = rows[8 * f : 8 * f + 8]
+            rows = came[pl.ds(16 * j, 16)].astype(jnp.float32)
+            corners[2 * j + side, SLOTS + 2 * FACE] = rows[8 * f : 8 * f + 8]
     for sx in range(2):
         for sy in range(2):
             c = 2 * sx + sy
@@ -172,23 +196,9 @@
 
 
 def build_columns(s, bricks, near, lx, ly, corners, wide, which):
-    line = lax.broadcasted_iota(jnp.int32, (8, C), 0)
-
     def spread(cells, at_x, at_y, depth):
-        if depth is None:
-            keep = ((line >= 1), None, (line <= 6))
-        else:
-            same = depth == 0
-            keep = (
-                (same & (line >= 1)) | ((depth == -1) & (line == 0)),
-                same & (line >= 0),
-                (same & (line <= 6)) | ((depth == 1) & (line == 7)),
-            )
         flat = cells.reshape(-1, 8, C)
-        for k in range(3):
-            moved = flat if k == 1 else pltpu.roll(flat, 1 if k == 0 else 7, 1)
-            if keep[k] is not None:
-                moved = jnp.where(keep[k][None], moved, 0.0)
+        for k, moved in enumerate(shifts(flat, depth == 0, depth == -1, depth == 1)):
             wide[k, at_x, at_y] = moved.reshape(cells.shape)
 
     def column(nx, ny):
@@ -199,12 +209,12 @@
         if which == "own":
             depth = jnp.where(entry < SLOTS, depth, 2)
         if which == "rim":
-            depth = jnp.where(entry < SLOTS, 2, depth)
+            depth = jnp.where((entry >= SLOTS) & (entry < SLOTS + 4 * FACE), depth, 2)
         return entry, depth
 
     middle = pl.ds(1, 8)
     if which != "rim":
-        spread(bricks[s].astype(jnp.float32).reshape(8, 8, 8, C), middle, middle, None)
+        spread(bricks[s].astype(jnp.float32).reshape(8, 8, 8, C), middle, middle, 0)
     for side, n in ((0, -1), (1, 1)):
         edge_at = pl.ds(0 if n < 0 else 9, 1)
         entry, depth = column(n, 0)
@@ -259,11 +269,10 @@
     lax.fori_loop(0, SLOTS, per_slot, 0)
     rows = grd[...].reshape(SLOTS * 512, C)
     for x in range(3):
-        for j in range(9):
-            cells = v[:, pl.ds(x, 8), :, pl.ds(j * C, C)].reshape(SLOTS * 512, C)
-            out[pl.ds((9 * x + j) * C, C)] = lax.dot_general(
-                cells, rows, (((0,), (0,)), ((), ())), preferred_element_type=jnp.float32
-            )
+        cells = v[:, pl.ds(x, 8)].reshape(SLOTS * 512, 9 * C)
+        out[pl.ds(9 * x * C, 9 * C)] = lax.dot_general(
+            cells, rows, (((0,), (0,)), ((), ())), preferred_element_type=jnp.float32
+        )
 
 
 def inner_terms(near, act, grd):
@@ -279,9 +288,17 @@
     )(near, act, grd)
 
 
-def rim_kernel(near_hbm, inner, grd, x0, x1, y0, y1, keep, send, lx, ly, corners, wide, near, sem, vx, vy, total):
+def rim_kernel(near_hbm, inner, grd, x0, x1, y0, y1, keep, send, lx, ly, corners, wide, near, sem, *refs):
+    vx, vy, ends_a, ends_g, total = refs
     fetched((near_hbm, near, sem))
-    fill_came(0, (x0, x1), (y0, y1), lx, ly, corners)
+    fill_came(0, (x0, x1), (y0, y1), (), lx, ly, corners)
+    for k, came in enumerate((x0, x1)):
+        side = side_of(k, parity("gx"))
+        for j in range(2):
+            ends_a[side, j] = came[pl.ds(FACE_ROWS + 16 * j, 16)].astype(jnp.float32)[0:8]
+    for k, came in enumerate((y0, y1)):
+        side = side_of(k, parity("gy"))
+        ends_g[side] = came[pl.ds(FACE_ROWS, 48)].astype(jnp.float32).reshape(2, 3, 8, C)
     for s in range(SLOTS):
         build_columns(s, None, near, lx, ly, corners, wide, "rim")
         rows = pl.ds(64 * s, 64)
@@ -300,22 +317,30 @@
     grads = grd[...]
     lines = grads.astype(jnp.float32).reshape(SLOTS, 8, 8, 8, C)
 
-    def term(v, side, j, rows):
-        return lax.dot_general(
-            v[side, :, pl.ds(j * C, C)], rows, (((0,), (0,)), ((), ())), preferred_element_type=jnp.float32
-        )
-
-    rows_x = [grads[:, 448 * side : 448 * side + 64].reshape(SLOTS * 64, C) for side in range(2)]
-    rows_y = [lines[:, :, 7 * side].reshape(SLOTS * 64, C).astype(jnp.bfloat16) for side in range(2)]
+    def term(cells, rows):
+        return lax.dot_general(cells, rows, (((0,), (0,)), ((), ())), preferred_element_type=jnp.float32)
+
+    def end(line):
+        return jnp.concatenate([line, jnp.zeros((8, C), jnp.float32)], axis=0).astype(jnp.bfloat16)
+
+    side_x, side_y = [], []
+    for side in range(2):
+        rows = grads[:, 448 * side : 448 * side + 64].reshape(SLOTS * 64, C)
+        side_x.append(term(vx[side], rows))
+        rows = lines[:, :, 7 * side].reshape(SLOTS * 64, C).astype(jnp.bfloat16)
+        side_y.append(term(vy[side], rows))
     for x in range(3):
         for y in range(3):
             for z in range(3):
                 at = pl.ds((9 * x + 3 * y + z) * C, C)
                 value = inner[at]
                 if x != 1:
-                    value += term(vx, x // 2, 3 * y + z, rows_x[x // 2])
+                    value += side_x[x // 2][(3 * y + z) * C : (3 * y + z + 1) * C]
                 if y != 1:
-                    value += term(vy, y // 2, 3 * x + z, rows_y[y // 2])
+                    value += side_y[y // 2][(3 * x + z) * C : (3 * x + z + 1) * C]
+                if x != 1 and y != 1:
+                    sx, sy = x // 2, 1 - y // 2
+                    value += term(end(ends_a[sx, sy]), end(ends_g[sy, sx, z]))
                 total[at] = value
     core = parity("gy")
     keep[...] = total[pl.ds(pl.multiple_of(core * HALF, 8), HALF)]
@@ -330,7 +355,14 @@
         out_shape=[half, half],
         in_specs=[hbm()] + [vmem()] * 6,
         out_specs=[vmem()] * 2,
-        scratch_shapes=columns_scratch() + [side, side, pltpu.VMEM((ROWS, C), jnp.float32)],
+        scratch_shapes=columns_scratch()
+        + [
+            side,
+            side,
+            pltpu.VMEM((2, 2, 8, C), jnp.float32),
+            pltpu.VMEM((2, 2, 3, 8, C), jnp.float32),
+            pltpu.VMEM((ROWS, C), jnp.float32),
+        ],
         compiler_params=pltpu.CompilerParams(vmem_limit_bytes=VMEM_LIMIT),
         cost_estimate=pl.CostEstimate(flops=2 * 256 * 36 * C * C, bytes_accessed=6 << 20, transcendentals=0),
         name="rim_terms",
@@ -389,29 +421,33 @@
     )(blocks)
 
 
-def decode_kernel(take, scale, mine, other, out):
+def decode_kernel(take, scale, own, blocks, *refs):
+    out, half, sem = refs[-3:]
+    groups = blocks.shape[0]
+    for p in range(groups):
+        rows = min(take, HALF - p * take)
+        if rows > 0:
+            factor = jnp.exp2(blocks[p, pl.ds(take, 1)] - 14.0) * scale
+            half[pl.ds(p * take, rows)] = blocks[p, pl.ds(0, rows)] * factor
     core = parity("gy")
-    groups = mine.shape[0]
-    for half, blocks in ((core, mine), (1 - core, other)):
-        for p in range(groups):
-            rows = min(take, HALF - p * take)
-            if rows > 0:
-                factor = jnp.exp2(blocks[p, pl.ds(take, 1)] - 14.0) * scale
-                out[half, pl.ds(p * take, rows)] = blocks[p, pl.ds(0, rows)] * factor
-
-
-def decode(take, scale, mine, other):
-    return pl.pallas_call(
-        lambda *refs: decode_kernel(take, scale, *refs),
+    fetched((half, out.at[core if own else 1 - core], sem))
+
+
+def decode(take, scale, blocks, begun=None):
+    rest = () if begun is None else (begun,)
+    return pl.pallas_call(
+        lambda *refs: decode_kernel(take, scale, not rest, *refs),
         out_shape=jax.ShapeDtypeStruct((2, HALF, C), jnp.float32),
-        in_specs=[vmem()] * 2,
-        out_specs=vmem(),
-        compiler_params=pltpu.CompilerParams(vmem_limit_bytes=VMEM_LIMIT),
-        name="decode",
-    )(mine, other)
-
-
-def product_kernel(f, near_hbm, mask_ref, kernel_ref, bricks, x0, x1, y0, y1, out, *refs):
+        in_specs=[vmem()] + [hbm()] * len(rest),
+        out_specs=hbm(),
+        scratch_shapes=[pltpu.VMEM((HALF, C), jnp.float32), pltpu.SemaphoreType.DMA(())],
+        input_output_aliases={1: 0} if rest else {},
+        compiler_params=pltpu.CompilerParams(vmem_limit_bytes=VMEM_LIMIT),
+        name="decode_other" if rest else "decode_own",
+    )(blocks, *rest)
+
+
+def product_kernel(f, near_hbm, mask_ref, kernel_ref, bricks, x0, x1, y0, y1, e0, e1, out, *refs):
     lx, ly, corners, wide, near, sem, v, *flipped = refs
     fetched((near_hbm, near, sem))
     weights = kernel_ref
@@ -420,7 +456,7 @@
         for o in range(27):
             weights[pl.ds((26 - o) * C, C)] = kernel_ref[pl.ds(o * C, C)].T
     fill_own(bricks, lx, ly, corners)
-    fill_came(f, (x0, x1), (y0, y1), lx, ly, corners)
+    fill_came(f, (x0, x1), (y0, y1), (e0, e1), lx, ly, corners)
 
     def per_slot(s, carry):
         build_columns(s, bricks, near, lx, ly, corners, wide, "all")
@@ -435,11 +471,11 @@
     lax.fori_loop(0, SLOTS, per_slot, 0)
 
 
-def product(f, near, mask, kernel, bricks, x_came, y_came):
+def product(f, near, mask, kernel, bricks, x_came, y_came, edges):
     return pl.pallas_call(
         lambda *refs: product_kernel(f, *refs),
         out_shape=jax.ShapeDtypeStruct((SLOTS, 512, C), jnp.bfloat16),
-        in_specs=[hbm()] + [vmem()] * 7,
+        in_specs=[hbm()] + [vmem()] * 9,
         out_specs=vmem(),
         scratch_shapes=columns_scratch()
         + [pltpu.VMEM((SLOTS, 10, 64, 9 * C), jnp.bfloat16)]
@@ -447,7 +483,7 @@
         compiler_params=pltpu.CompilerParams(vmem_limit_bytes=VMEM_LIMIT),
         cost_estimate=pl.CostEstimate(flops=2 * 2048 * ROWS * C, bytes_accessed=4 << 20, transcendentals=0),
         name=("output_product", "input_grad_product")[f],
-    )(near, mask, kernel, bricks, *x_came, *y_came)
+    )(near, mask, kernel, bricks, *x_came, *y_came, *edges)
 
 
 def swapped(value, axis, k):
@@ -469,25 +505,33 @@
         return lax.all_to_all(blocks, ("gx", "gy"), 0, 0, axis_index_groups=same_core, tiled=True)
 
     act, grd, y0, y1, x0, x1 = pack(
-        features.reshape(SLOTS, 512, C), out_grad.reshape(SLOTS, 512, C), voxel_mask, face_sends, edge_sends
+        features.reshape(SLOTS, 512, C),
+        out_grad.reshape(SLOTS, 512, C),
+        voxel_mask,
+        neighbours,
+        face_sends,
+        edge_sends,
     )
-    y_came = [swapped(y0, "gy", 0), swapped(y1, "gy", 1)]
-    x0, x1 = forward_corners((x0, x1), y_came)
-    x_came = [swapped(x0, "gx", 0), swapped(x1, "gx", 1)]
+    y1, x1 = swapped(y1, "gy", 1), swapped(x1, "gx", 1)
+    x0, y0 = swapped(x0, "gx", 0), swapped(y0, "gy", 0)
+    x_came, y_came = [x0, x1], [y0, y1]
     inner = inner_terms(neighbours, act, grd)
     keep, send = rim_terms(neighbours, inner, grd, x_came, y_came)
     blocks = merge(groups, take, held, keep, swapped(send, "gy", 0)).astype(jnp.float16)
     rows = kernel.reshape(ROWS, C)
-    blocks, act = lax.optimization_barrier((blocks, act))
-    output = product(0, neighbours, voxel_mask, rows, act, x_came, y_came)
+    blocks, act, x_came = lax.optimization_barrier((blocks, act, x_came))
+    e0, e1 = forward_corners(x_came)
+    edges = [swapped(e0, "gy", 0), swapped(e1, "gy", 1)]
+    output = product(0, neighbours, voxel_mask, rows, act, x_came, y_came, edges)
     arrived, output = lax.optimization_barrier((spread(blocks), output))
     copies = sum_blocks(take, arrived.astype(jnp.float32)).astype(jnp.float16)
     copies, grd = lax.optimization_barrier((copies, grd))
-    input_grad = product(1, neighbours, voxel_mask, rows, grd, x_came, y_came)
+    input_grad = product(1, neighbours, voxel_mask, rows, grd, x_came, y_came, edges)
     mine, input_grad = lax.optimization_barrier((spread(copies), input_grad))
     other = swapped(mine, "gy", 0)
     scale = 1.0 / math.sqrt(parts * SLOTS * 512)
-    weight = decode(take, scale, mine.astype(jnp.float32), other.astype(jnp.float32))
+    weight = decode(take, scale, mine.astype(jnp.float32))
+    weight = decode(take, scale, other.astype(jnp.float32), weight)
     shape = (SLOTS, 8, 8, 8, C)
     return output.reshape(shape), input_grad.reshape(shape), weight.reshape(27, C, C)
 

time: 74.6 us -> 69.2 us (0.928)
  local copies, waits for them, and re-layouts: 6 us -> 2.79 us
  starting transfers between devices: 22 us -> 20 us
  waiting for transfers between devices: 19 us -> 17.8 us
  Pallas kernels: 24.4 us -> 25.4 us
    unnamed x20 -> x16, local copies, waits for them, and re-layouts: 6 us -> 2.79 us
    pallas_call x2 -> x3, Pallas kernels: 2.54 us -> 4.81 us  [the longest x1 2.83 us: pack(): pl.pallas_call(pack_kernel, out_shape=[brick, brick] + sends, in_specs=[h...]
    ppermute x6 -> x8, starting transfers between devices: 9.42 us -> 8.08 us  [swapped(): return lax.ppermute(value, axis, pairs)]
    pallas_call x1, Pallas kernels: 3.47 us -> 2.14 us  [rim_terms(): pl.pallas_call(rim_kernel, out_shape=[half, half], in_specs=[hbm()] + [vm...]
    ppermute x6 -> x8, waiting for transfers between devices: 4.06 us -> 3.31 us  [swapped(): return lax.ppermute(value, axis, pairs)]
  transfers between devices with their start and end apart: 8 -> 10, of which waited for: 5 -> 5; matrix products, arithmetic and copies ran while one was open for 0% -> 0% of each run, Pallas kernels for 24% -> 27%
where the time goes in v3:
time: 69.2 us; the launch traced here: 68.7 us
  Pallas kernels  25.4 us (37%)
  starting transfers between devices  20 us (29%)
  waiting for transfers between devices  17.8 us (26%)
  local copies, waits for them, and re-layouts  2.79 us (4%)
  other arithmetic  1.84 us (3%)
  between operations  0.88 us (1%)
    all_to_all x2, waiting for transfers between devices, spread(): lax.all_to_all(blocks, ('gx', 'gy'), 0, 0, axis_index_groups=same_core, t...  14.5 us
    pallas_call x2, Pallas kernels, product(): pl.pallas_call(lambda *refs: product_kernel(f, *refs), out_shape=jax.Shap...  12.4 us
    all_to_all x2, starting transfers between devices, spread(): lax.all_to_all(blocks, ('gx', 'gy'), 0, 0, axis_index_groups=same_core, t...  12 us
    ppermute x8, starting transfers between devices, swapped(): return lax.ppermute(value, axis, pairs)  8.08 us
    pallas_call x1, Pallas kernels, inner_terms(): pl.pallas_call(inner_kernel, out_shape=jax.ShapeDtypeStruct((ROWS, C), jn...  5.42 us
    ppermute x8, waiting for transfers between devices, swapped(): return lax.ppermute(value, axis, pairs)  3.31 us
    pallas_call x1, Pallas kernels, pack(): pl.pallas_call(pack_kernel, out_shape=[brick, brick] + sends, in_specs=[h...  2.83 us
    unnamed x16, local copies, waits for them, and re-layouts  2.79 us
  transfers between devices with their start and end apart: 10, of which 5 were waited for; matrix products, arithmetic and copies ran while one was open for 0% of the time, Pallas kernels for 27%

profile of v3, /device:TPU:0, one launch (start us, length us, event | category | flops | bytes accessed | tf_op | source)
XLA Modules:
  0.0 68.7 jit_solution(4899081379572566286)
XLA Ops:
  0.6 2.8 %pack.1 = (bf16[4,512,128]{2,1,0:T(8,128)(2,1)}, bf16[4,512,128]{2,1,0:T(8,128)(2,1)}, bf16[304,128]{1,0:T(8,128)(2,1)}, bf16[304,128]{1,0:T(8,128)(2,1)}, bf16[...) custom-call(s32[2,4]{1,0:T(2,128)} %bitcast.13, s32[1,4]{1,0:T(1,128)} %bitcast.14, s32[4,27]{1,0:T(4,128)} %refs_0_.3, ...), custom_call_target="tpu_custom_call" | custom-call | tf_op jit(solution)/shard_map/pack/pallas_call | solution.py:118
  3.5 3.0 %collective-permute-start = (bf16[288,128]{1,0:T(8,128)(2,1)}, bf16[288,128]{1,0:T(8,128)(2,1)S(1)}, u32[]{:S(2)}, u32[]{:S(2)}) collective-permute-start(bf16[288,128]{1,0:T(8,128)(2,1)} %get-tuple-element.25), channel_id=1, source_target_pairs={{0,4},{4,0},{8,12},{12,8},{16,20},{20,16},{24,28},{28,24},{1,5},{5... | collective-permute-start | bytes 221192 | tf_op jit(solution)/shard_map/ppermute | solution.py:493
  6.5 0.7 collective-permute-start.1
  7.1 0.1 collective-permute-start.2
  7.2 0.7 collective-permute-start.3
  7.9 0.0 copy-start
  7.9 1.0 %copy-done = bf16[4,512,128]{2,1,0:T(8,128)(2,1)S(1)} copy-done((bf16[4,512,128]{2,1,0:T(8,128)(2,1)S(1)}, bf16[4,512,128]{2,1,0:T(8,128)(2,1)}, u32[]{:S(2)}) %copy-start) | copy-done | bytes 524312
  8.9 0.0 copy-start.3
  8.9 0.7 copy-done.3
  9.6 0.0 copy-start.6
  9.6 1.0 %copy-done.6 = bf16[4,512,128]{2,1,0:T(8,128)(2,1)S(1)} copy-done((bf16[4,512,128]{2,1,0:T(8,128)(2,1)S(1)}, bf16[4,512,128]{2,1,0:T(8,128)(2,1)}, u32[]{:S(2)}) %copy-start.6) | copy-done | bytes 524312
  10.7 0.0 copy-start.1
  10.7 5.4 %inner_terms.1.inner = f32[3456,128]{1,0:T(8,128)S(1)} custom-call(s32[4,27]{1,0:T(4,128)S(1)} %copy-done.3, bf16[4,512,128]{2,1,0:T(8,128)(2,1)S(1)} %copy-done.6, bf16[4,512,128]{2,1,0:T(8,128)(2,1)S(1)} %copy-done), custom_call_target="tpu_custom_call" | custom-call | flops 1811939328 | bytes 6291456 | tf_op jit(solution)/shard_map/inner_terms/pallas_call | solution.py:279
  16.1 0.0 collective-permute-done.x0.refs_4_
  16.1 0.0 collective-permute-done.1.x1.refs_5_
  16.1 0.0 collective-permute-done.2.y0.refs_6_
  16.1 0.0 collective-permute-done.3.y1.refs_7_
  16.1 0.0 copy-done.1
  16.1 2.1 %rim_terms.1 = (f32[1728,128]{1,0:T(8,128)S(1)}, f32[1728,128]{1,0:T(8,128)S(1)}) custom-call(s32[4,27]{1,0:T(4,128)S(1)} %copy-done.3, f32[3456,128]{1,0:T(8,128)S(1)} %inner_terms.1.inner, bf16[4,512,128]{2,1,0:T(8,128)(2,1)S(1)} %copy-done.1, bf16[288,128]{1,0:T(8,128)(2,1)S(1)} %collective-permute-done.x0.refs_4_, ...), custom_call_target="tpu_custom_call" | custom-call | flops 301989888 | bytes 6291456 | tf_op jit(solution)/shard_map/rim_terms/pallas_call | solution.py:353
  18.3 3.0 %collective-permute-start.4 = (f32[1728,128]{1,0:T(8,128)S(1)}, f32[1728,128]{1,0:T(8,128)S(1)}, u32[]{:S(2)}, u32[]{:S(2)}) collective-permute-start(f32[1728,128]{1,0:T(8,128)S(1)} %get-tuple-element.30), channel_id=1, source_target_pairs={{0,1},{1,0},{2,3},{3,2},{4,5},{5,4},{6,7},{7,6},{8,9},{9,8},{10,11... | collective-permute-start | bytes 2654216 | tf_op jit(solution)/shard_map/ppermute | solution.py:493
  21.2 2.1 %collective-permute-done.4.refs_1_ = f32[1728,128]{1,0:T(8,128)S(1)} collective-permute-done((f32[1728,128]{1,0:T(8,128)S(1)}, f32[1728,128]{1,0:T(8,128)S(1)}, u32[]{:S(2)}, u32[]{:S(2)}) %collective-permute-start.4) | collective-permute-done | bytes 884768 | tf_op jit(solution)/shard_map/ppermute | solution.py:493
  23.3 0.3 merge.1
  23.6 0.0 copy-start.2
  23.6 0.0 copy-start.4
  23.7 0.0 copy-start.5
  23.7 0.0 copy-start.7
  23.7 0.8 %convert_element_type.15 = f16[16,112,128]{2,1,0:T(8,128)(2,1)} convert(f32[16,112,128]{2,1,0:T(8,128)S(1)} %merge.1) | non-fusion elementwise | flops 229376 | bytes 1376256 | tf_op jit(solution)/shard_map/convert_element_type | solution.py:520
  24.5 8.0 %all-to-all-start = ((f16[16,112,128]{2,1,0:T(8,128)(2,1)}), f16[16,112,128]{2,1,0:T(8,128)(2,1)S(1)}, u32[]{:S(2)}, u32[]{:S(2)}) async-start(f16[16,112,128]{2,1,0:T(8,128)(2,1)} %convert_element_type.15), calls=%async_computation | async-start | bytes 917504 | tf_op jit(solution)/shard_map/all_to_all | solution.py:505
  32.5 0.1 collective-permute-start.5
  32.6 0.7 collective-permute-start.6
  33.3 0.5 collective-permute-done.5.refs_8_
  33.8 0.0 collective-permute-done.6.refs_9_
  33.8 0.0 copy-done.2
  33.8 0.0 copy-done.4
  33.8 0.0 copy-done.5
  33.8 0.0 copy-done.7
  33.8 6.1 %output_product.1 = bf16[4,512,128]{2,1,0:T(8,128)(2,1)} custom-call(s32[4,27]{1,0:T(4,128)S(1)} %copy-done.4, s32[4,512]{1,0:T(4,128)S(1)} %copy-done.2, bf16[3456,128]{1,0:T(8,128)(2,1)S(1)} %bitcast.8, bf16[4,512,128]{2,1,0:T(8,128)(2,1)S(1)} %copy-done.7, bf16[288,128]{1,0:T(8,128)(2,1)S(1)} %collective-permute-done.x0.refs_4_, ...), custom_call_target="tpu_custom_call" | custom-call | flops 1811939328 | bytes 4194304 | tf_op jit(solution)/shard_map/output_product/pallas_call | solution.py:475
  39.9 6.8 %all-to-all-done = f16[16,112,128]{2,1,0:T(8,128)(2,1)S(1)} async-done(((f16[16,112,128]{2,1,0:T(8,128)(2,1)}), f16[16,112,128]{2,1,0:T(8,128)(2,1)S(1)}, u32[]{:S(2)}, u32[]{:S(2)}) %all-to-all-start) | async-done | bytes 458784 | tf_op jit(solution)/shard_map/all_to_all | solution.py:505
  46.6 0.1 convert_element_type.16.refs_0_
  46.7 0.3 sum_blocks.1
  47.0 0.8 %convert_element_type.17 = f16[16,112,128]{2,1,0:T(8,128)(2,1)} convert(f32[16,112,128]{2,1,0:T(8,128)S(1)} %sum_blocks.1) | non-fusion elementwise | flops 229376 | bytes 1376256 | tf_op jit(solution)/shard_map/convert_element_type | solution.py:527
  47.8 4.0 %all-to-all-start.1 = ((f16[16,112,128]{2,1,0:T(8,128)(2,1)}), f16[16,112,128]{2,1,0:T(8,128)(2,1)S(1)}, u32[]{:S(2)}, u32[]{:S(2)}) async-start(f16[16,112,128]{2,1,0:T(8,128)(2,1)} %convert_element_type.17), calls=%async_computation.1 | async-start | bytes 917504 | tf_op jit(solution)/shard_map/all_to_all | solution.py:505
  51.8 6.3 %input_grad_product.1 = bf16[4,512,128]{2,1,0:T(8,128)(2,1)} custom-call(s32[4,27]{1,0:T(4,128)S(1)} %copy-done.4, s32[4,512]{1,0:T(4,128)S(1)} %copy-done.2, bf16[3456,128]{1,0:T(8,128)(2,1)S(1)} %bitcast.9, bf16[4,512,128]{2,1,0:T(8,128)(2,1)S(1)} %copy-done.1, bf16[288,128]{1,0:T(8,128)(2,1)S(1)} %collective-permute-done.x0.refs_4_, ...), custom_call_target="tpu_custom_call" | custom-call | flops 1811939328 | bytes 4194304 | tf_op jit(solution)/shard_map/input_grad_product/pallas_call | solution.py:475
  58.1 7.7 %all-to-all-done.1 = f16[16,112,128]{2,1,0:T(8,128)(2,1)S(1)} async-done(((f16[16,112,128]{2,1,0:T(8,128)(2,1)}), f16[16,112,128]{2,1,0:T(8,128)(2,1)S(1)}, u32[]{:S(2)}, u32[]{:S(2)}) %all-to-all-start.1) | async-done | bytes 458784 | tf_op jit(solution)/shard_map/all_to_all | solution.py:505
  65.8 0.0 collective-permute-start.7
  65.8 0.1 convert_element_type.19.refs_0_
  65.9 1.0 %decode_own.1.refs_1_ = f32[2,1728,128]{2,1,0:T(8,128)} custom-call(f32[16,112,128]{2,1,0:T(8,128)S(1)} %convert_element_type.19.refs_0_), custom_call_target="tpu_custom_call" | custom-call | tf_op jit(solution)/shard_map/decode_own/pallas_call | solution.py:438
  66.9 0.8 %collective-permute-done.7 = f16[16,112,128]{2,1,0:T(8,128)(2,1)S(1)} collective-permute-done((f16[16,112,128]{2,1,0:T(8,128)(2,1)S(1)}, f16[16,112,128]{2,1,0:T(8,128)(2,1)S(1)}, u32[]{:S(2)}, u32[]{:S(2)}) %collective-permute-start.7) | collective-permute-done | bytes 458784 | tf_op jit(solution)/shard_map/ppermute | solution.py:493
  67.6 0.1 convert_element_type.18.refs_0_
  67.7 1.0 %decode_other.1 = f32[2,1728,128]{2,1,0:T(8,128)} custom-call(f32[16,112,128]{2,1,0:T(8,128)S(1)} %convert_element_type.18.refs_0_, f32[2,1728,128]{2,1,0:T(8,128)} %decode_own.1.refs_1_), custom_call_target="tpu_custom_call", output_to_operand_aliasing={{}: (1, {})} | custom-call | tf_op jit(solution)/shard_map/decode_other/pallas_call | solution.py:438
  (1 shorter events, 0.0 us)
Async XLA Ops:
  3.5 12.6 %collective-permute-start = (bf16[288,128]{1,0:T(8,128)(2,1)}, bf16[288,128]{1,0:T(8,128)(2,1)S(1)}, u32[]{:S(2)}, u32[]{:S(2)}) collective-permute-start(bf16[288,128]{1,0:T(8,128)(2,1)} %get-tuple-element.25), channel_id=1, source_target_pairs={{0,4},{4,0},{8,12},{12,8},{16,20},{20,16},{24,28},{28,24},{1,5},{5... | collective-permute-start | bytes 221192 | tf_op jit(solution)/shard_map/ppermute | solution.py:493
  6.5 9.6 %collective-permute-start.1 = (bf16[288,128]{1,0:T(8,128)(2,1)}, bf16[288,128]{1,0:T(8,128)(2,1)S(1)}, u32[]{:S(2)}, u32[]{:S(2)}) collective-permute-start(bf16[288,128]{1,0:T(8,128)(2,1)} %get-tuple-element.26), channel_id=1, source_target_pairs={{4,8},{8,4},{12,16},{16,12},{20,24},{24,20},{5,9},{9,5},{13,17},{1... | collective-permute-start | bytes 221192 | tf_op jit(solution)/shard_map/ppermute | solution.py:493
  7.1 9.0 %collective-permute-start.2 = (bf16[304,128]{1,0:T(8,128)(2,1)}, bf16[304,128]{1,0:T(8,128)(2,1)S(1)}, u32[]{:S(2)}, u32[]{:S(2)}) collective-permute-start(bf16[304,128]{1,0:T(8,128)(2,1)} %get-tuple-element.27), channel_id=1, source_target_pairs={{0,1},{1,0},{2,3},{3,2},{4,5},{5,4},{6,7},{7,6},{8,9},{9,8},{10,11... | collective-permute-start | bytes 233480 | tf_op jit(solution)/shard_map/ppermute | solution.py:493
  7.2 8.9 %collective-permute-start.3 = (bf16[304,128]{1,0:T(8,128)(2,1)}, bf16[304,128]{1,0:T(8,128)(2,1)S(1)}, u32[]{:S(2)}, u32[]{:S(2)}) collective-permute-start(bf16[304,128]{1,0:T(8,128)(2,1)} %get-tuple-element.28), channel_id=1, source_target_pairs={{1,2},{2,1},{5,6},{6,5},{9,10},{10,9},{13,14},{14,13},{17,18},{18,... | collective-permute-start | bytes 233480 | tf_op jit(solution)/shard_map/ppermute | solution.py:493
  7.9 1.0 %copy-start = (bf16[4,512,128]{2,1,0:T(8,128)(2,1)S(1)}, bf16[4,512,128]{2,1,0:T(8,128)(2,1)}, u32[]{:S(2)}) copy-start(bf16[4,512,128]{2,1,0:T(8,128)(2,1)} %get-tuple-element.40.grd.refs_3_) | copy-start | bytes 1572868
  8.9 0.7 copy-start.3
  9.6 1.0 %copy-start.6 = (bf16[4,512,128]{2,1,0:T(8,128)(2,1)S(1)}, bf16[4,512,128]{2,1,0:T(8,128)(2,1)}, u32[]{:S(2)}) copy-start(bf16[4,512,128]{2,1,0:T(8,128)(2,1)} %get-tuple-element.32.act.refs_3_) | copy-start | bytes 1572868
  10.7 5.5 %copy-start.1 = (bf16[4,512,128]{2,1,0:T(8,128)(2,1)S(1)}, bf16[4,512,128]{2,1,0:T(8,128)(2,1)}, u32[]{:S(2)}) copy-start(bf16[4,512,128]{2,1,0:T(8,128)(2,1)} %get-tuple-element.40.grd.refs_3_) | copy-start | bytes 1572868
  18.3 5.0 %collective-permute-start.4 = (f32[1728,128]{1,0:T(8,128)S(1)}, f32[1728,128]{1,0:T(8,128)S(1)}, u32[]{:S(2)}, u32[]{:S(2)}) collective-permute-start(f32[1728,128]{1,0:T(8,128)S(1)} %get-tuple-element.30), channel_id=1, source_target_pairs={{0,1},{1,0},{2,3},{3,2},{4,5},{5,4},{6,7},{7,6},{8,9},{9,8},{10,11... | collective-permute-start | bytes 2654216 | tf_op jit(solution)/shard_map/ppermute | solution.py:493
  23.6 10.1 %copy-start.2 = (s32[4,512]{1,0:T(4,128)S(1)}, s32[4,512]{1,0:T(4,128)}, u32[]{:S(2)}) copy-start(s32[4,512]{1,0:T(4,128)} %refs_1_.3) | copy-start | bytes 24580
  23.6 10.1 %copy-start.4 = (s32[4,27]{1,0:T(4,128)S(1)}, s32[4,27]{1,0:T(4,128)}, u32[]{:S(2)}) copy-start(s32[4,27]{1,0:T(4,128)} %refs_0_.3) | copy-start | bytes 1300
  23.7 10.1 %copy-start.5 = (bf16[27,128,128]{2,1,0:T(8,128)(2,1)S(1)}, bf16[27,128,128]{2,1,0:T(8,128)(2,1)}, u32[]{:S(2)}) copy-start(bf16[27,128,128]{2,1,0:T(8,128)(2,1)} %param.9) | copy-start | bytes 2654212
  23.7 10.1 %copy-start.7 = (bf16[4,512,128]{2,1,0:T(8,128)(2,1)S(1)}, bf16[4,512,128]{2,1,0:T(8,128)(2,1)}, u32[]{:S(2)}) copy-start(bf16[4,512,128]{2,1,0:T(8,128)(2,1)} %get-tuple-element.32.act.refs_3_) | copy-start | bytes 1572868
  24.5 22.1 %all-to-all-start = ((f16[16,112,128]{2,1,0:T(8,128)(2,1)}), f16[16,112,128]{2,1,0:T(8,128)(2,1)S(1)}, u32[]{:S(2)}, u32[]{:S(2)}) async-start(f16[16,112,128]{2,1,0:T(8,128)(2,1)} %convert_element_type.15), calls=%async_computation | async-start | bytes 917504 | tf_op jit(solution)/shard_map/all_to_all | solution.py:505
  32.5 1.2 %collective-permute-start.5 = (bf16[32,128]{1,0:T(8,128)(2,1)S(1)}, bf16[32,128]{1,0:T(8,128)(2,1)S(1)}, u32[]{:S(2)}, u32[]{:S(2)}) collective-permute-start(bf16[32,128]{1,0:T(8,128)(2,1)S(1)} %get-tuple-element.35), channel_id=1, source_target_pairs={{0,1},{1,0},{2,3},{3,2},{4,5},{5,4},{6,7},{7,6},{8,9},{9,8},{10,11... | collective-permute-start | bytes 24584 | tf_op jit(solution)/shard_map/ppermute | solution.py:493
  32.6 1.2 %collective-permute-start.6 = (bf16[32,128]{1,0:T(8,128)(2,1)S(1)}, bf16[32,128]{1,0:T(8,128)(2,1)S(1)}, u32[]{:S(2)}, u32[]{:S(2)}) collective-permute-start(bf16[32,128]{1,0:T(8,128)(2,1)S(1)} %get-tuple-element.36), channel_id=1, source_target_pairs={{1,2},{2,1},{5,6},{6,5},{9,10},{10,9},{13,14},{14,13},{17,18},{18,... | collective-permute-start | bytes 24584 | tf_op jit(solution)/shard_map/ppermute | solution.py:493
  47.8 18.0 %all-to-all-start.1 = ((f16[16,112,128]{2,1,0:T(8,128)(2,1)}), f16[16,112,128]{2,1,0:T(8,128)(2,1)S(1)}, u32[]{:S(2)}, u32[]{:S(2)}) async-start(f16[16,112,128]{2,1,0:T(8,128)(2,1)} %convert_element_type.17), calls=%async_computation.1 | async-start | bytes 917504 | tf_op jit(solution)/shard_map/all_to_all | solution.py:505
  65.8 1.8 %collective-permute-start.7 = (f16[16,112,128]{2,1,0:T(8,128)(2,1)S(1)}, f16[16,112,128]{2,1,0:T(8,128)(2,1)S(1)}, u32[]{:S(2)}, u32[]{:S(2)}) collective-permute-start(f16[16,112,128]{2,1,0:T(8,128)(2,1)S(1)} %all-to-all-done.1), channel_id=1, source_target_pairs={{0,1},{1,0},{2,3},{3,2},{4,5},{5,4},{6,7},{7,6},{8,9},{9,8},{10,11... | collective-permute-start | bytes 1376264 | tf_op jit(solution)/shard_map/ppermute | solution.py:493

commit v4 on v3

--- a/solution.py
+++ b/solution.py
@@ -134,11 +134,34 @@
     )(face_sends.T, edge_sends.T, near, features, out_grad, mask)
 
 
-def forward_kernel(x0, x1, out0, out1):
+def parts_of(ref):
+    rows = ref.shape[0] // 2
+    return ref.at[pl.ds(0, rows)], ref.at[pl.ds(rows, rows)]
+
+
+def join_kernel(x0, x1, y0, y1, x_out, y_out):
+    for out, pair in ((x_out, (x0, x1)), (y_out, (y0, y1))):
+        for k, dst in enumerate(parts_of(out)):
+            dst[...] = pair[k][...]
+
+
+def join(x0, x1, y0, y1):
+    outs = [jax.ShapeDtypeStruct((2 * rows, C), jnp.bfloat16) for rows in (X_ROWS, Y_ROWS)]
+    return pl.pallas_call(
+        join_kernel,
+        out_shape=outs,
+        in_specs=[vmem()] * 4,
+        out_specs=[vmem()] * 2,
+        compiler_params=pltpu.CompilerParams(vmem_limit_bytes=VMEM_LIMIT),
+        name="join_sides",
+    )(x0, x1, y0, y1)
+
+
+def forward_kernel(x_came, out0, out1):
     odd_x, odd_y = parity("gx"), parity("gy")
     for k, out in enumerate((out0, out1)):
         far = side_of(k, odd_y)
-        for j, came in enumerate((x0, x1)):
+        for j, came in enumerate(parts_of(x_came)):
             source = side_of(j, odd_x)
             rows = came[pl.ds(pl.multiple_of(FACE_ROWS + 16 * far, 16), 16)]
             out[pl.ds(pl.multiple_of(16 * source, 16), 16)] = rows
@@ -149,11 +172,11 @@
     return pl.pallas_call(
         forward_kernel,
         out_shape=[send] * 2,
-        in_specs=[vmem()] * 2,
+        in_specs=[vmem()],
         out_specs=[vmem()] * 2,
         compiler_params=pltpu.CompilerParams(vmem_limit_bytes=VMEM_LIMIT),
         name="forward_corners",
-    )(*x_came)
+    )(x_came)
 
 
 def fill_own(bricks, lx, ly, corners):
@@ -175,10 +198,10 @@
 def fill_came(f, x_came, y_came, edges, lx, ly, corners):
     odd_x, odd_y = parity("gx"), parity("gy")
     for came, odd, dst in ((x_came, odd_x, lx), (y_came, odd_y, ly)):
-        for k in range(2):
+        for k, part in enumerate(parts_of(came)):
             side = side_of(k, odd)
             for r in range(FACE):
-                rows = came[k][pl.ds((f * FACE + r) * 64, 64)]
+                rows = part[pl.ds((f * FACE + r) * 64, 64)]
                 dst[side, SLOTS + r] = rows.astype(jnp.float32).reshape(8, 8, C)
             dst[k, SLOTS + FACE] = jnp.zeros((8, 8, C), jnp.float32)
     for k, came in enumerate(edges):
@@ -256,7 +279,7 @@
     ]
 
 
-def inner_kernel(near_hbm, act, grd, out, lx, ly, corners, wide, near, sem, v):
+def columns_kernel(near_hbm, act, v, lx, ly, corners, wide, near, sem):
     fetched((near_hbm, near, sem))
     fill_own(act, lx, ly, corners)
     fill_zero(lx, ly, corners, SLOTS)
@@ -267,36 +290,54 @@
         return carry
 
     lax.fori_loop(0, SLOTS, per_slot, 0)
-    rows = grd[...].reshape(SLOTS * 512, C)
+
+
+def own_columns(near, act):
+    return pl.pallas_call(
+        columns_kernel,
+        out_shape=jax.ShapeDtypeStruct((SLOTS, 10, 64, 9 * C), jnp.bfloat16),
+        in_specs=[hbm(), vmem()],
+        out_specs=vmem(),
+        scratch_shapes=columns_scratch(),
+        compiler_params=pltpu.CompilerParams(vmem_limit_bytes=VMEM_LIMIT),
+        cost_estimate=pl.CostEstimate(flops=1 << 24, bytes_accessed=6 << 20, transcendentals=0),
+        name="own_columns",
+    )(near, act)
+
+
+def inner_kernel(v, grd, out, turned):
+    for s in range(SLOTS):
+        for q in range(4):
+            turned[:, pl.ds((4 * s + q) * C, C)] = grd[s, pl.ds(q * C, C)].T
     for x in range(3):
         cells = v[:, pl.ds(x, 8)].reshape(SLOTS * 512, 9 * C)
-        out[pl.ds(9 * x * C, 9 * C)] = lax.dot_general(
-            cells, rows, (((0,), (0,)), ((), ())), preferred_element_type=jnp.float32
-        )
-
-
-def inner_terms(near, act, grd):
+        terms = jnp.dot(turned[...], cells, preferred_element_type=jnp.float32)
+        for j in range(9):
+            out[pl.ds((9 * x + j) * C, C)] = terms[:, j * C : (j + 1) * C].T
+
+
+def inner_terms(v, grd):
     return pl.pallas_call(
         inner_kernel,
         out_shape=jax.ShapeDtypeStruct((ROWS, C), jnp.float32),
-        in_specs=[hbm()] + [vmem()] * 2,
+        in_specs=[vmem()] * 2,
         out_specs=vmem(),
-        scratch_shapes=columns_scratch() + [pltpu.VMEM((SLOTS, 10, 64, 9 * C), jnp.bfloat16)],
+        scratch_shapes=[pltpu.VMEM((C, SLOTS * 512), jnp.bfloat16)],
         compiler_params=pltpu.CompilerParams(vmem_limit_bytes=VMEM_LIMIT),
         cost_estimate=pl.CostEstimate(flops=2 * 2048 * ROWS * C, bytes_accessed=6 << 20, transcendentals=0),
         name="inner_terms",
-    )(near, act, grd)
-
-
-def rim_kernel(near_hbm, inner, grd, x0, x1, y0, y1, keep, send, lx, ly, corners, wide, near, sem, *refs):
+    )(v, grd)
+
+
+def rim_kernel(near_hbm, inner, grd, x_ref, y_ref, keep, send, lx, ly, corners, wide, near, sem, *refs):
     vx, vy, ends_a, ends_g, total = refs
     fetched((near_hbm, near, sem))
-    fill_came(0, (x0, x1), (y0, y1), (), lx, ly, corners)
-    for k, came in enumerate((x0, x1)):
+    fill_came(0, x_ref, y_ref, (), lx, ly, corners)
+    for k, came in enumerate(parts_of(x_ref)):
         side = side_of(k, parity("gx"))
         for j in range(2):
             ends_a[side, j] = came[pl.ds(FACE_ROWS + 16 * j, 16)].astype(jnp.float32)[0:8]
-    for k, came in enumerate((y0, y1)):
+    for k, came in enumerate(parts_of(y_ref)):
         side = side_of(k, parity("gy"))
         ends_g[side] = came[pl.ds(FACE_ROWS, 48)].astype(jnp.float32).reshape(2, 3, 8, C)
     for s in range(SLOTS):
@@ -353,7 +394,7 @@
     return pl.pallas_call(
         rim_kernel,
         out_shape=[half, half],
-        in_specs=[hbm()] + [vmem()] * 6,
+        in_specs=[hbm()] + [vmem()] * 4,
         out_specs=[vmem()] * 2,
         scratch_shapes=columns_scratch()
         + [
@@ -366,7 +407,7 @@
         compiler_params=pltpu.CompilerParams(vmem_limit_bytes=VMEM_LIMIT),
         cost_estimate=pl.CostEstimate(flops=2 * 256 * 36 * C * C, bytes_accessed=6 << 20, transcendentals=0),
         name="rim_terms",
-    )(near, inner, grd, *x_came, *y_came)
+    )(near, inner, grd, x_came, y_came)
 
 
 def power_of(values):
@@ -447,7 +488,7 @@
     )(blocks, *rest)
 
 
-def product_kernel(f, near_hbm, mask_ref, kernel_ref, bricks, x0, x1, y0, y1, e0, e1, out, *refs):
+def product_kernel(f, near_hbm, mask_ref, kernel_ref, bricks, x_ref, y_ref, e0, e1, out, *refs):
     lx, ly, corners, wide, near, sem, v, *flipped = refs
     fetched((near_hbm, near, sem))
     weights = kernel_ref
@@ -456,7 +497,7 @@
         for o in range(27):
             weights[pl.ds((26 - o) * C, C)] = kernel_ref[pl.ds(o * C, C)].T
     fill_own(bricks, lx, ly, corners)
-    fill_came(f, (x0, x1), (y0, y1), (e0, e1), lx, ly, corners)
+    fill_came(f, x_ref, y_ref, (e0, e1), lx, ly, corners)
 
     def per_slot(s, carry):
         build_columns(s, bricks, near, lx, ly, corners, wide, "all")
@@ -475,7 +516,7 @@
     return pl.pallas_call(
         lambda *refs: product_kernel(f, *refs),
         out_shape=jax.ShapeDtypeStruct((SLOTS, 512, C), jnp.bfloat16),
-        in_specs=[hbm()] + [vmem()] * 9,
+        in_specs=[hbm()] + [vmem()] * 7,
         out_specs=vmem(),
         scratch_shapes=columns_scratch()
         + [pltpu.VMEM((SLOTS, 10, 64, 9 * C), jnp.bfloat16)]
@@ -483,13 +524,19 @@
         compiler_params=pltpu.CompilerParams(vmem_limit_bytes=VMEM_LIMIT),
         cost_estimate=pl.CostEstimate(flops=2 * 2048 * ROWS * C, bytes_accessed=4 << 20, transcendentals=0),
         name=("output_product", "input_grad_product")[f],
-    )(near, mask, kernel, bricks, *x_came, *y_came, *edges)
+    )(near, mask, kernel, bricks, x_came, y_came, *edges)
 
 
 def swapped(value, axis, k):
     pairs = []
     for low in range(k, lax.axis_size(axis) - 1, 2):
         pairs += [(low, low + 1), (low + 1, low)]
+    return lax.ppermute(value, axis, pairs)
+
+
+def hopped(value, axis):
+    size = lax.axis_size(axis)
+    pairs = [(i, i + 2) for i in range(1, size - 2, 2)] + [(i, i - 2) for i in range(2, size, 2)]
     return lax.ppermute(value, axis, pairs)
 
 
@@ -512,10 +559,12 @@
         face_sends,
         edge_sends,
     )
-    y1, x1 = swapped(y1, "gy", 1), swapped(x1, "gx", 1)
-    x0, y0 = swapped(x0, "gx", 0), swapped(y0, "gy", 0)
-    x_came, y_came = [x0, x1], [y0, y1]
-    inner = inner_terms(neighbours, act, grd)
+    x1, y1 = hopped(x1, "gx"), hopped(y1, "gy")
+    v = own_columns(neighbours, act)
+    x1, y1, v = lax.optimization_barrier((x1, y1, v))
+    x_came, y_came = join(x0, x1, y0, y1)
+    x_came, y_came = swapped(x_came, "gx", 0), swapped(y_came, "gy", 0)
+    inner = inner_terms(v, grd)
     keep, send = rim_terms(neighbours, inner, grd, x_came, y_came)
     blocks = merge(groups, take, held, keep, swapped(send, "gy", 0)).astype(jnp.float16)
     rows = kernel.reshape(ROWS, C)

time: 69.2 us -> 68.4 us (0.988)
  waiting for transfers between devices: 17.8 us -> 21.3 us
  Pallas kernels: 25.4 us -> 23.8 us
  starting transfers between devices: 20 us -> 18.5 us
  local copies, waits for them, and re-layouts: 2.79 us -> 1.75 us
    ppermute x8 -> x6, starting transfers between devices: 8.08 us -> 4.75 us  [swapped(): return lax.ppermute(value, axis, pairs)]
    pallas_call x1, Pallas kernels: 5.42 us -> 2.34 us  [inner_terms(): pl.pallas_call(inner_kernel, out_shape=jax.ShapeDtypeStruct((ROWS, C), jn...]
    ppermute x0 -> x2, waiting for transfers between devices: none -> 2.92 us  [hopped(): return lax.ppermute(value, axis, pairs)]
    ppermute x0 -> x2, starting transfers between devices: none -> 2.58 us  [hopped(): return lax.ppermute(value, axis, pairs)]
    pallas_call x1 -> x3, Pallas kernels: 0.02 us -> 1.55 us  [the longest x1 1.51 us: own_columns(): pl.pallas_call(columns_kernel, out_shape=jax.ShapeDtypeStruct((SLOTS, 10,...]
    unnamed x16 -> x18, local copies, waits for them, and re-layouts: 2.79 us -> 1.75 us
    all_to_all x2, starting transfers between devices: 12 us -> 11.1 us  [spread(): lax.all_to_all(blocks, ('gx', 'gy'), 0, 0, axis_index_groups=same_core, t...]
    ppermute x8 -> x6, waiting for transfers between devices: 3.31 us -> 3.85 us  [swapped(): return lax.ppermute(value, axis, pairs)]
  transfers between devices with their start and end apart: 10 -> 10, of which waited for: 5 -> 7; matrix products, arithmetic and copies ran while one was open for 0% -> 0% of each run, Pallas kernels for 27% -> 25%
where the time goes in v4:
time: 68.4 us; the launch traced here: 68 us
  Pallas kernels  23.8 us (35%)
  waiting for transfers between devices  21.3 us (31%)
  starting transfers between devices  18.5 us (27%)
  other arithmetic  1.84 us (3%)
  local copies, waits for them, and re-layouts  1.75 us (3%)
  between operations  0.84 us (1%)
    all_to_all x2, waiting for transfers between devices, spread(): lax.all_to_all(blocks, ('gx', 'gy'), 0, 0, axis_index_groups=same_core, t...  14.5 us
    pallas_call x2, Pallas kernels, product(): pl.pallas_call(lambda *refs: product_kernel(f, *refs), out_shape=jax.Shap...  12.4 us
    all_to_all x2, starting transfers between devices, spread(): lax.all_to_all(blocks, ('gx', 'gy'), 0, 0, axis_index_groups=same_core, t...  11.1 us
    ppermute x6, starting transfers between devices, swapped(): return lax.ppermute(value, axis, pairs)  4.75 us
    ppermute x6, waiting for transfers between devices, swapped(): return lax.ppermute(value, axis, pairs)  3.85 us
    ppermute x2, waiting for transfers between devices, hopped(): return lax.ppermute(value, axis, pairs)  2.92 us
    pallas_call x1, Pallas kernels, pack(): pl.pallas_call(pack_kernel, out_shape=[brick, brick] + sends, in_specs=[h...  2.81 us
    ppermute x2, starting transfers between devices, hopped(): return lax.ppermute(value, axis, pairs)  2.58 us
  transfers between devices with their start and end apart: 10, of which 7 were waited for; matrix products, arithmetic and copies ran while one was open for 0% of the time, Pallas kernels for 25%

profile of v4, /device:TPU:0, one launch (start us, length us, event | category | flops | bytes accessed | tf_op | source)
XLA Modules:
  0.0 68.0 jit_solution(5316393090016950477)
XLA Ops:
  0.6 2.8 %pack.1 = (bf16[4,512,128]{2,1,0:T(8,128)(2,1)}, bf16[4,512,128]{2,1,0:T(8,128)(2,1)}, bf16[304,128]{1,0:T(8,128)(2,1)}, bf16[304,128]{1,0:T(8,128)(2,1)}, bf16[...) custom-call(s32[2,4]{1,0:T(2,128)} %bitcast.13, s32[1,4]{1,0:T(1,128)} %bitcast.14, s32[4,27]{1,0:T(4,128)} %refs_0_.3, ...), custom_call_target="tpu_custom_call" | custom-call | tf_op jit(solution)/shard_map/pack/pallas_call | solution.py:118
  3.4 1.3 %collective-permute-start.1 = (bf16[304,128]{1,0:T(8,128)(2,1)}, bf16[304,128]{1,0:T(8,128)(2,1)S(1)}, u32[]{:S(2)}, u32[]{:S(2)}) collective-permute-start(bf16[304,128]{1,0:T(8,128)(2,1)} %get-tuple-element.28), channel_id=1, source_target_pairs={{1,3},{2,0},{5,7},{6,4},{9,11},{10,8},{13,15},{14,12},{17,19},{18,... | collective-permute-start | bytes 233480 | tf_op jit(solution)/shard_map/ppermute | solution.py:540
  4.7 1.3 %collective-permute-start = (bf16[288,128]{1,0:T(8,128)(2,1)}, bf16[288,128]{1,0:T(8,128)(2,1)S(1)}, u32[]{:S(2)}, u32[]{:S(2)}) collective-permute-start(bf16[288,128]{1,0:T(8,128)(2,1)} %get-tuple-element.27), channel_id=1, source_target_pairs={{4,12},{12,20},{20,28},{8,0},{16,8},{24,16},{5,13},{13,21},{21,29}... | collective-permute-start | bytes 221192 | tf_op jit(solution)/shard_map/ppermute | solution.py:540
  6.0 0.0 copy-start.1
  6.1 1.0 %copy-done.1 = bf16[4,512,128]{2,1,0:T(8,128)(2,1)S(1)} copy-done((bf16[4,512,128]{2,1,0:T(8,128)(2,1)S(1)}, bf16[4,512,128]{2,1,0:T(8,128)(2,1)}, u32[]{:S(2)}) %copy-start.1) | copy-done | bytes 524312
  7.1 0.0 copy-start.5
  7.1 0.7 copy-done.5
  7.8 0.0 copy-start.3
  7.8 0.0 copy-start.4
  7.8 0.0 copy-start
  7.8 1.5 %own_columns.1.v = bf16[4,10,64,1152]{3,2,1,0:T(8,128)(2,1)S(1)} custom-call(s32[4,27]{1,0:T(4,128)S(1)} %copy-done.5, bf16[4,512,128]{2,1,0:T(8,128)(2,1)S(1)} %copy-done.1), custom_call_target="tpu_custom_call" | custom-call | flops 16777216 | bytes 6291456 | tf_op jit(solution)/shard_map/own_columns/pallas_call | solution.py:296
  9.3 2.9 %collective-permute-done.x1 = bf16[288,128]{1,0:T(8,128)(2,1)S(1)} collective-permute-done((bf16[288,128]{1,0:T(8,128)(2,1)}, bf16[288,128]{1,0:T(8,128)(2,1)S(1)}, u32[]{:S(2)}, u32[]{:S(2)}) %collective-permute-start) | collective-permute-done | bytes 73760 | tf_op jit(solution)/shard_map/ppermute | solution.py:540
  12.2 0.0 collective-permute-done.1.y1
  12.2 0.0 copy-done.3
  12.2 0.0 copy-done.4
  12.3 2.3 %collective-permute-start.2 = (bf16[576,128]{1,0:T(8,128)(2,1)S(1)}, bf16[576,128]{1,0:T(8,128)(2,1)S(1)}, u32[]{:S(2)}, u32[]{:S(2)}) collective-permute-start(bf16[576,128]{1,0:T(8,128)(2,1)S(1)} %get-tuple-element.36), channel_id=1, source_target_pairs={{0,4},{4,0},{8,12},{12,8},{16,20},{20,16},{24,28},{28,24},{1,5},{5... | collective-permute-start | bytes 442376 | tf_op jit(solution)/shard_map/ppermute | solution.py:534
  14.6 1.1 %collective-permute-start.3 = (bf16[608,128]{1,0:T(8,128)(2,1)S(1)}, bf16[608,128]{1,0:T(8,128)(2,1)S(1)}, u32[]{:S(2)}, u32[]{:S(2)}) collective-permute-start(bf16[608,128]{1,0:T(8,128)(2,1)S(1)} %get-tuple-element.37), channel_id=1, source_target_pairs={{0,1},{1,0},{2,3},{3,2},{4,5},{5,4},{6,7},{7,6},{8,9},{9,8},{10,11... | collective-permute-start | bytes 466952 | tf_op jit(solution)/shard_map/ppermute | solution.py:534
  15.7 0.0 copy-done
  15.7 2.3 %inner_terms.1.inner = f32[3456,128]{1,0:T(8,128)S(1)} custom-call(bf16[4,10,64,1152]{3,2,1,0:T(8,128)(2,1)S(1)} %own_columns.1.v, bf16[4,512,128]{2,1,0:T(8,128)(2,1)S(1)} %copy-done), custom_call_target="tpu_custom_call" | custom-call | flops 1811939328 | bytes 6291456 | tf_op jit(solution)/shard_map/inner_terms/pallas_call | solution.py:320
  18.0 0.6 collective-permute-done.2.x_ref.x_came.refs_4_
  18.6 0.0 collective-permute-done.3.y_ref.refs_5_
  18.6 2.1 %rim_terms.1 = (f32[1728,128]{1,0:T(8,128)S(1)}, f32[1728,128]{1,0:T(8,128)S(1)}) custom-call(s32[4,27]{1,0:T(4,128)S(1)} %copy-done.5, f32[3456,128]{1,0:T(8,128)S(1)} %inner_terms.1.inner, bf16[4,512,128]{2,1,0:T(8,128)(2,1)S(1)} %copy-done, bf16[576,128]{1,0:T(8,128)(2,1)S(1)} %collective-permute-done.2.x_ref.x_came.refs_4_, ...), custom_call_target="tpu_custom_call" | custom-call | flops 301989888 | bytes 6291456 | tf_op jit(solution)/shard_map/rim_terms/pallas_call | solution.py:394
  20.7 0.6 collective-permute-start.4
  21.3 2.1 %collective-permute-done.4.refs_1_ = f32[1728,128]{1,0:T(8,128)S(1)} collective-permute-done((f32[1728,128]{1,0:T(8,128)S(1)}, f32[1728,128]{1,0:T(8,128)S(1)}, u32[]{:S(2)}, u32[]{:S(2)}) %collective-permute-start.4) | collective-permute-done | bytes 884768 | tf_op jit(solution)/shard_map/ppermute | solution.py:534
  23.4 0.3 merge.1
  23.7 0.0 copy-start.2
  23.7 0.0 copy-start.6
  23.7 0.0 copy-start.7
  23.8 0.0 copy-start.8
  23.8 0.8 %convert_element_type.15 = f16[16,112,128]{2,1,0:T(8,128)(2,1)} convert(f32[16,112,128]{2,1,0:T(8,128)S(1)} %merge.1) | non-fusion elementwise | flops 229376 | bytes 1376256 | tf_op jit(solution)/shard_map/convert_element_type | solution.py:569
  24.6 7.2 %all-to-all-start = ((f16[16,112,128]{2,1,0:T(8,128)(2,1)}), f16[16,112,128]{2,1,0:T(8,128)(2,1)S(1)}, u32[]{:S(2)}, u32[]{:S(2)}) async-start(f16[16,112,128]{2,1,0:T(8,128)(2,1)} %convert_element_type.15), calls=%async_computation | async-start | bytes 917504 | tf_op jit(solution)/shard_map/all_to_all | solution.py:552
  31.8 0.1 collective-permute-start.5
  31.9 0.7 collective-permute-start.6
  32.5 0.5 collective-permute-done.5.refs_6_
  33.0 0.0 collective-permute-done.6.refs_7_
  33.0 0.0 copy-done.2
  33.0 0.0 copy-done.6
  33.0 0.0 copy-done.7
  33.1 0.0 copy-done.8
  33.1 6.1 %output_product.1 = bf16[4,512,128]{2,1,0:T(8,128)(2,1)} custom-call(s32[4,27]{1,0:T(4,128)S(1)} %copy-done.6, s32[4,512]{1,0:T(4,128)S(1)} %copy-done.7, bf16[3456,128]{1,0:T(8,128)(2,1)S(1)} %bitcast.8, bf16[4,512,128]{2,1,0:T(8,128)(2,1)S(1)} %copy-done.2, bf16[576,128]{1,0:T(8,128)(2,1)S(1)} %collective-permute-done.2.x_ref.x_came.refs_4_, ...), custom_call_target="tpu_custom_call" | custom-call | flops 1811939328 | bytes 4194304 | tf_op jit(solution)/shard_map/output_product/pallas_call | solution.py:516
  39.2 6.8 %all-to-all-done = f16[16,112,128]{2,1,0:T(8,128)(2,1)S(1)} async-done(((f16[16,112,128]{2,1,0:T(8,128)(2,1)}), f16[16,112,128]{2,1,0:T(8,128)(2,1)S(1)}, u32[]{:S(2)}, u32[]{:S(2)}) %all-to-all-start) | async-done | bytes 458784 | tf_op jit(solution)/shard_map/all_to_all | solution.py:552
  45.9 0.1 convert_element_type.16.refs_0_
  46.0 0.3 sum_blocks.1
  46.3 0.8 %convert_element_type.17 = f16[16,112,128]{2,1,0:T(8,128)(2,1)} convert(f32[16,112,128]{2,1,0:T(8,128)S(1)} %sum_blocks.1) | non-fusion elementwise | flops 229376 | bytes 1376256 | tf_op jit(solution)/shard_map/convert_element_type | solution.py:576
  47.1 4.0 %all-to-all-start.1 = ((f16[16,112,128]{2,1,0:T(8,128)(2,1)}), f16[16,112,128]{2,1,0:T(8,128)(2,1)S(1)}, u32[]{:S(2)}, u32[]{:S(2)}) async-start(f16[16,112,128]{2,1,0:T(8,128)(2,1)} %convert_element_type.17), calls=%async_computation.1 | async-start | bytes 917504 | tf_op jit(solution)/shard_map/all_to_all | solution.py:552
  51.1 6.3 %input_grad_product.1 = bf16[4,512,128]{2,1,0:T(8,128)(2,1)} custom-call(s32[4,27]{1,0:T(4,128)S(1)} %copy-done.6, s32[4,512]{1,0:T(4,128)S(1)} %copy-done.7, bf16[3456,128]{1,0:T(8,128)(2,1)S(1)} %bitcast.9, bf16[4,512,128]{2,1,0:T(8,128)(2,1)S(1)} %copy-done, bf16[576,128]{1,0:T(8,128)(2,1)S(1)} %collective-permute-done.2.x_ref.x_came.refs_4_, ...), custom_call_target="tpu_custom_call" | custom-call | flops 1811939328 | bytes 4194304 | tf_op jit(solution)/shard_map/input_grad_product/pallas_call | solution.py:516
  57.4 7.7 %all-to-all-done.1 = f16[16,112,128]{2,1,0:T(8,128)(2,1)S(1)} async-done(((f16[16,112,128]{2,1,0:T(8,128)(2,1)}), f16[16,112,128]{2,1,0:T(8,128)(2,1)S(1)}, u32[]{:S(2)}, u32[]{:S(2)}) %all-to-all-start.1) | async-done | bytes 458784 | tf_op jit(solution)/shard_map/all_to_all | solution.py:552
  65.1 0.0 collective-permute-start.7
  65.1 0.1 convert_element_type.19.refs_0_
  65.2 1.0 %decode_own.1.refs_1_ = f32[2,1728,128]{2,1,0:T(8,128)} custom-call(f32[16,112,128]{2,1,0:T(8,128)S(1)} %convert_element_type.19.refs_0_), custom_call_target="tpu_custom_call" | custom-call | tf_op jit(solution)/shard_map/decode_own/pallas_call | solution.py:479
  66.2 0.8 %collective-permute-done.7 = f16[16,112,128]{2,1,0:T(8,128)(2,1)S(1)} collective-permute-done((f16[16,112,128]{2,1,0:T(8,128)(2,1)S(1)}, f16[16,112,128]{2,1,0:T(8,128)(2,1)S(1)}, u32[]{:S(2)}, u32[]{:S(2)}) %collective-permute-start.7) | collective-permute-done | bytes 458784 | tf_op jit(solution)/shard_map/ppermute | solution.py:534
  66.9 0.1 convert_element_type.18.refs_0_
  67.0 1.0 %decode_other.1 = f32[2,1728,128]{2,1,0:T(8,128)} custom-call(f32[16,112,128]{2,1,0:T(8,128)S(1)} %convert_element_type.18.refs_0_, f32[2,1728,128]{2,1,0:T(8,128)} %decode_own.1.refs_1_), custom_call_target="tpu_custom_call", output_to_operand_aliasing={{}: (1, {})} | custom-call | tf_op jit(solution)/shard_map/decode_other/pallas_call | solution.py:479
  (2 shorter events, 0.0 us)
Async XLA Ops:
  3.4 8.8 %collective-permute-start.1 = (bf16[304,128]{1,0:T(8,128)(2,1)}, bf16[304,128]{1,0:T(8,128)(2,1)S(1)}, u32[]{:S(2)}, u32[]{:S(2)}) collective-permute-start(bf16[304,128]{1,0:T(8,128)(2,1)} %get-tuple-element.28), channel_id=1, source_target_pairs={{1,3},{2,0},{5,7},{6,4},{9,11},{10,8},{13,15},{14,12},{17,19},{18,... | collective-permute-start | bytes 233480 | tf_op jit(solution)/shard_map/ppermute | solution.py:540
  4.7 7.5 %collective-permute-start = (bf16[288,128]{1,0:T(8,128)(2,1)}, bf16[288,128]{1,0:T(8,128)(2,1)S(1)}, u32[]{:S(2)}, u32[]{:S(2)}) collective-permute-start(bf16[288,128]{1,0:T(8,128)(2,1)} %get-tuple-element.27), channel_id=1, source_target_pairs={{4,12},{12,20},{20,28},{8,0},{16,8},{24,16},{5,13},{13,21},{21,29}... | collective-permute-start | bytes 221192 | tf_op jit(solution)/shard_map/ppermute | solution.py:540
  6.0 1.0 %copy-start.1 = (bf16[4,512,128]{2,1,0:T(8,128)(2,1)S(1)}, bf16[4,512,128]{2,1,0:T(8,128)(2,1)}, u32[]{:S(2)}) copy-start(bf16[4,512,128]{2,1,0:T(8,128)(2,1)} %get-tuple-element.41.act.refs_3_) | copy-start | bytes 1572868
  7.1 0.7 %copy-start.5 = (s32[4,27]{1,0:T(4,128)S(1)}, s32[4,27]{1,0:T(4,128)}, u32[]{:S(2)}) copy-start(s32[4,27]{1,0:T(4,128)} %refs_0_.3) | copy-start | bytes 1300
  7.8 4.4 %copy-start.3 = (bf16[304,128]{1,0:T(8,128)(2,1)S(1)}, bf16[304,128]{1,0:T(8,128)(2,1)}, u32[]{:S(2)}) copy-start(bf16[304,128]{1,0:T(8,128)(2,1)} %get-tuple-element.34.y0) | copy-start | bytes 233476
  7.8 4.4 %copy-start.4 = (bf16[288,128]{1,0:T(8,128)(2,1)S(1)}, bf16[288,128]{1,0:T(8,128)(2,1)}, u32[]{:S(2)}) copy-start(bf16[288,128]{1,0:T(8,128)(2,1)} %get-tuple-element.32.x0) | copy-start | bytes 221188
  7.8 7.9 %copy-start = (bf16[4,512,128]{2,1,0:T(8,128)(2,1)S(1)}, bf16[4,512,128]{2,1,0:T(8,128)(2,1)}, u32[]{:S(2)}) copy-start(bf16[4,512,128]{2,1,0:T(8,128)(2,1)} %get-tuple-element.48.grd.refs_3_) | copy-start | bytes 1572868
  12.3 6.3 %collective-permute-start.2 = (bf16[576,128]{1,0:T(8,128)(2,1)S(1)}, bf16[576,128]{1,0:T(8,128)(2,1)S(1)}, u32[]{:S(2)}, u32[]{:S(2)}) collective-permute-start(bf16[576,128]{1,0:T(8,128)(2,1)S(1)} %get-tuple-element.36), channel_id=1, source_target_pairs={{0,4},{4,0},{8,12},{12,8},{16,20},{20,16},{24,28},{28,24},{1,5},{5... | collective-permute-start | bytes 442376 | tf_op jit(solution)/shard_map/ppermute | solution.py:534
  14.6 4.0 %collective-permute-start.3 = (bf16[608,128]{1,0:T(8,128)(2,1)S(1)}, bf16[608,128]{1,0:T(8,128)(2,1)S(1)}, u32[]{:S(2)}, u32[]{:S(2)}) collective-permute-start(bf16[608,128]{1,0:T(8,128)(2,1)S(1)} %get-tuple-element.37), channel_id=1, source_target_pairs={{0,1},{1,0},{2,3},{3,2},{4,5},{5,4},{6,7},{7,6},{8,9},{9,8},{10,11... | collective-permute-start | bytes 466952 | tf_op jit(solution)/shard_map/ppermute | solution.py:534
  20.7 2.6 %collective-permute-start.4 = (f32[1728,128]{1,0:T(8,128)S(1)}, f32[1728,128]{1,0:T(8,128)S(1)}, u32[]{:S(2)}, u32[]{:S(2)}) collective-permute-start(f32[1728,128]{1,0:T(8,128)S(1)} %get-tuple-element.39), channel_id=1, source_target_pairs={{0,1},{1,0},{2,3},{3,2},{4,5},{5,4},{6,7},{7,6},{8,9},{9,8},{10,11... | collective-permute-start | bytes 2654216 | tf_op jit(solution)/shard_map/ppermute | solution.py:534
  23.7 9.3 %copy-start.2 = (bf16[4,512,128]{2,1,0:T(8,128)(2,1)S(1)}, bf16[4,512,128]{2,1,0:T(8,128)(2,1)}, u32[]{:S(2)}) copy-start(bf16[4,512,128]{2,1,0:T(8,128)(2,1)} %get-tuple-element.41.act.refs_3_) | copy-start | bytes 1572868
  23.7 9.3 %copy-start.6 = (s32[4,27]{1,0:T(4,128)S(1)}, s32[4,27]{1,0:T(4,128)}, u32[]{:S(2)}) copy-start(s32[4,27]{1,0:T(4,128)} %refs_0_.3) | copy-start | bytes 1300
  23.7 9.3 %copy-start.7 = (s32[4,512]{1,0:T(4,128)S(1)}, s32[4,512]{1,0:T(4,128)}, u32[]{:S(2)}) copy-start(s32[4,512]{1,0:T(4,128)} %refs_1_.3) | copy-start | bytes 24580
  23.8 9.3 %copy-start.8 = (bf16[27,128,128]{2,1,0:T(8,128)(2,1)S(1)}, bf16[27,128,128]{2,1,0:T(8,128)(2,1)}, u32[]{:S(2)}) copy-start(bf16[27,128,128]{2,1,0:T(8,128)(2,1)} %param.9) | copy-start | bytes 2654212
  24.6 21.3 %all-to-all-start = ((f16[16,112,128]{2,1,0:T(8,128)(2,1)}), f16[16,112,128]{2,1,0:T(8,128)(2,1)S(1)}, u32[]{:S(2)}, u32[]{:S(2)}) async-start(f16[16,112,128]{2,1,0:T(8,128)(2,1)} %convert_element_type.15), calls=%async_computation | async-start | bytes 917504 | tf_op jit(solution)/shard_map/all_to_all | solution.py:552
  31.8 1.2 %collective-permute-start.5 = (bf16[32,128]{1,0:T(8,128)(2,1)S(1)}, bf16[32,128]{1,0:T(8,128)(2,1)S(1)}, u32[]{:S(2)}, u32[]{:S(2)}) collective-permute-start(bf16[32,128]{1,0:T(8,128)(2,1)S(1)} %get-tuple-element.43), channel_id=1, source_target_pairs={{0,1},{1,0},{2,3},{3,2},{4,5},{5,4},{6,7},{7,6},{8,9},{9,8},{10,11... | collective-permute-start | bytes 24584 | tf_op jit(solution)/shard_map/ppermute | solution.py:534
  31.9 1.2 %collective-permute-start.6 = (bf16[32,128]{1,0:T(8,128)(2,1)S(1)}, bf16[32,128]{1,0:T(8,128)(2,1)S(1)}, u32[]{:S(2)}, u32[]{:S(2)}) collective-permute-start(bf16[32,128]{1,0:T(8,128)(2,1)S(1)} %get-tuple-element.44), channel_id=1, source_target_pairs={{1,2},{2,1},{5,6},{6,5},{9,10},{10,9},{13,14},{14,13},{17,18},{18,... | collective-permute-start | bytes 24584 | tf_op jit(solution)/shard_map/ppermute | solution.py:534
  47.1 18.0 %all-to-all-start.1 = ((f16[16,112,128]{2,1,0:T(8,128)(2,1)}), f16[16,112,128]{2,1,0:T(8,128)(2,1)S(1)}, u32[]{:S(2)}, u32[]{:S(2)}) async-start(f16[16,112,128]{2,1,0:T(8,128)(2,1)} %convert_element_type.17), calls=%async_computation.1 | async-start | bytes 917504 | tf_op jit(solution)/shard_map/all_to_all | solution.py:552
  65.1 1.8 %collective-permute-start.7 = (f16[16,112,128]{2,1,0:T(8,128)(2,1)S(1)}, f16[16,112,128]{2,1,0:T(8,128)(2,1)S(1)}, u32[]{:S(2)}, u32[]{:S(2)}) collective-permute-start(f16[16,112,128]{2,1,0:T(8,128)(2,1)S(1)} %all-to-all-done.1), channel_id=1, source_target_pairs={{0,1},{1,0},{2,3},{3,2},{4,5},{5,4},{6,7},{7,6},{8,9},{9,8},{10,11... | collective-permute-start | bytes 1376264 | tf_op jit(solution)/shard_map/ppermute | solution.py:534

commit v5 on v4

--- a/solution.py
+++ b/solution.py
@@ -14,7 +14,7 @@
 FACE = 2
 ZERO = SLOTS + 4 * FACE + 4
 ROWS = 27 * C
-FACE_ROWS = 2 * FACE * 64
+FACE_ROWS = FACE * 64
 X_ROWS = FACE_ROWS + 32
 Y_ROWS = FACE_ROWS + 48
 HALF = ROWS // 2
@@ -30,11 +30,15 @@
     return pl.BlockSpec(memory_space=pltpu.HBM)
 
 
-def fetched(*pairs):
+def fetching(*pairs):
     copies = [pltpu.make_async_copy(src, dst, sem) for src, dst, sem in pairs]
     for copy in copies:
         copy.start()
-    for copy in copies:
+    return copies
+
+
+def fetched(*pairs):
+    for copy in fetching(*pairs):
         copy.wait()
 
 
@@ -87,7 +91,8 @@
                     slot = jnp.clip(entry, 0, SLOTS - 1)
                     layer = full[f, slot, :, 7 * side] if axis else full[f, slot, 7 * side]
                     layer = jnp.where(entry < SLOTS, layer, 0.0)
-                    outs[k][pl.ds((f * FACE + r) * 64, 64)] = layer.reshape(64, C).astype(jnp.bfloat16)
+                    first = f * (Y_ROWS if axis else X_ROWS) + r * 64
+                    outs[k][pl.ds(first, 64)] = layer.reshape(64, C).astype(jnp.bfloat16)
             lines = []
             for far in range(2):
                 corner = 2 * far + side if axis else 2 * side + far
@@ -113,7 +118,7 @@
 
 
 def pack(features, out_grad, mask, near, face_sends, edge_sends):
-    sends = [jax.ShapeDtypeStruct((rows, C), jnp.bfloat16) for rows in (Y_ROWS, Y_ROWS, X_ROWS, X_ROWS)]
+    sends = [jax.ShapeDtypeStruct((rows, C), jnp.bfloat16) for rows in 2 * (Y_ROWS + FACE_ROWS,) + 2 * (X_ROWS + FACE_ROWS,)]
     brick = jax.ShapeDtypeStruct((SLOTS, 512, C), jnp.bfloat16)
     return pl.pallas_call(
         pack_kernel,
@@ -139,19 +144,23 @@
     return ref.at[pl.ds(0, rows)], ref.at[pl.ds(rows, rows)]
 
 
-def join_kernel(x0, x1, y0, y1, x_out, y_out):
-    for out, pair in ((x_out, (x0, x1)), (y_out, (y0, y1))):
-        for k, dst in enumerate(parts_of(out)):
-            dst[...] = pair[k][...]
+def join_kernel(x0, x1, y0, y1, *outs):
+    for axis, pair in enumerate(((x0, x1), (y0, y1))):
+        rows = (X_ROWS, Y_ROWS)[axis]
+        for k, src in enumerate(pair):
+            outs[axis][pl.ds(k * rows, rows)] = src[pl.ds(0, rows)]
+            outs[2 + axis][pl.ds(k * FACE_ROWS, FACE_ROWS)] = src[pl.ds(rows, FACE_ROWS)]
 
 
 def join(x0, x1, y0, y1):
-    outs = [jax.ShapeDtypeStruct((2 * rows, C), jnp.bfloat16) for rows in (X_ROWS, Y_ROWS)]
+    outs = [
+        jax.ShapeDtypeStruct((2 * rows, C), jnp.bfloat16) for rows in (X_ROWS, Y_ROWS, FACE_ROWS, FACE_ROWS)
+    ]
     return pl.pallas_call(
         join_kernel,
         out_shape=outs,
         in_specs=[vmem()] * 4,
-        out_specs=[vmem()] * 2,
+        out_specs=[vmem()] * 4,
         compiler_params=pltpu.CompilerParams(vmem_limit_bytes=VMEM_LIMIT),
         name="join_sides",
     )(x0, x1, y0, y1)
@@ -201,7 +210,7 @@
         for k, part in enumerate(parts_of(came)):
             side = side_of(k, odd)
             for r in range(FACE):
-                rows = part[pl.ds((f * FACE + r) * 64, 64)]
+                rows = part[pl.ds(r * 64, 64)]
                 dst[side, SLOTS + r] = rows.astype(jnp.float32).reshape(8, 8, C)
             dst[k, SLOTS + FACE] = jnp.zeros((8, 8, C), jnp.float32)
     for k, came in enumerate(edges):
@@ -280,9 +289,10 @@
 
 
 def columns_kernel(near_hbm, act, v, lx, ly, corners, wide, near, sem):
-    fetched((near_hbm, near, sem))
+    (table,) = fetching((near_hbm, near, sem))
     fill_own(act, lx, ly, corners)
     fill_zero(lx, ly, corners, SLOTS)
+    table.wait()
 
     def per_slot(s, carry):
         build_columns(s, act, near, lx, ly, corners, wide, "own")
@@ -330,8 +340,8 @@
 
 
 def rim_kernel(near_hbm, inner, grd, x_ref, y_ref, keep, send, lx, ly, corners, wide, near, sem, *refs):
-    vx, vy, ends_a, ends_g, total = refs
-    fetched((near_hbm, near, sem))
+    vx, vy, ends_a, ends_g, side_x, side_y = refs
+    (table,) = fetching((near_hbm, near, sem))
     fill_came(0, x_ref, y_ref, (), lx, ly, corners)
     for k, came in enumerate(parts_of(x_ref)):
         side = side_of(k, parity("gx"))
@@ -340,6 +350,7 @@
     for k, came in enumerate(parts_of(y_ref)):
         side = side_of(k, parity("gy"))
         ends_g[side] = came[pl.ds(FACE_ROWS, 48)].astype(jnp.float32).reshape(2, 3, 8, C)
+    table.wait()
     for s in range(SLOTS):
         build_columns(s, None, near, lx, ly, corners, wide, "rim")
         rows = pl.ds(64 * s, 64)
@@ -364,28 +375,39 @@
     def end(line):
         return jnp.concatenate([line, jnp.zeros((8, C), jnp.float32)], axis=0).astype(jnp.bfloat16)
 
-    side_x, side_y = [], []
     for side in range(2):
         rows = grads[:, 448 * side : 448 * side + 64].reshape(SLOTS * 64, C)
-        side_x.append(term(vx[side], rows))
+        side_x[side] = term(vx[side], rows)
         rows = lines[:, :, 7 * side].reshape(SLOTS * 64, C).astype(jnp.bfloat16)
-        side_y.append(term(vy[side], rows))
-    for x in range(3):
-        for y in range(3):
-            for z in range(3):
-                at = pl.ds((9 * x + 3 * y + z) * C, C)
-                value = inner[at]
-                if x != 1:
-                    value += side_x[x // 2][(3 * y + z) * C : (3 * y + z + 1) * C]
-                if y != 1:
-                    value += side_y[y // 2][(3 * x + z) * C : (3 * x + z + 1) * C]
-                if x != 1 and y != 1:
-                    sx, sy = x // 2, 1 - y // 2
-                    value += term(end(ends_a[sx, sy]), end(ends_g[sy, sx, z]))
-                total[at] = value
+        side_y[side] = term(vy[side], rows)
+    def write(halves):
+        for x in range(3):
+            for y in range(3):
+                for z in range(3):
+                    first = (9 * x + 3 * y + z) * C
+                    value = inner[pl.ds(first, C)]
+                    if x != 1:
+                        value += side_x[x // 2, pl.ds((3 * y + z) * C, C)]
+                    if y != 1:
+                        value += side_y[y // 2, pl.ds((3 * x + z) * C, C)]
+                    if x != 1 and y != 1:
+                        sx, sy = x // 2, 1 - y // 2
+                        value += term(end(ends_a[sx, sy]), end(ends_g[sy, sx, z]))
+                    for half in range(2):
+                        low = max(first, half * HALF)
+                        rows = min(first + C, (half + 1) * HALF) - low
+                        if rows > 0:
+                            halves[half][pl.ds(low - half * HALF, rows)] = value[low - first : low - first + rows]
+
     core = parity("gy")
-    keep[...] = total[pl.ds(pl.multiple_of(core * HALF, 8), HALF)]
-    send[...] = total[pl.ds(pl.multiple_of((1 - core) * HALF, 8), HALF)]
+
+    @pl.when(core == 0)
+    def _():
+        write((keep, send))
+
+    @pl.when(core == 1)
+    def _():
+        write((send, keep))
 
 
 def rim_terms(near, inner, grd, x_came, y_came):
@@ -402,7 +424,8 @@
             side,
             pltpu.VMEM((2, 2, 8, C), jnp.float32),
             pltpu.VMEM((2, 2, 3, 8, C), jnp.float32),
-            pltpu.VMEM((ROWS, C), jnp.float32),
+            pltpu.VMEM((2, 9 * C, C), jnp.float32),
+            pltpu.VMEM((2, 9 * C, C), jnp.float32),
         ],
         compiler_params=pltpu.CompilerParams(vmem_limit_bytes=VMEM_LIMIT),
         cost_estimate=pl.CostEstimate(flops=2 * 256 * 36 * C * C, bytes_accessed=6 << 20, transcendentals=0),
@@ -463,15 +486,24 @@
 
 
 def decode_kernel(take, scale, own, blocks, *refs):
-    out, half, sem = refs[-3:]
+    out, half, sems = refs[-3:]
     groups = blocks.shape[0]
+    core = parity("gy")
+    target = out.at[core if own else 1 - core]
+    copies = []
+    done = 0
     for p in range(groups):
         rows = min(take, HALF - p * take)
         if rows > 0:
             factor = jnp.exp2(blocks[p, pl.ds(take, 1)] - 14.0) * scale
             half[pl.ds(p * take, rows)] = blocks[p, pl.ds(0, rows)] * factor
-    core = parity("gy")
-    fetched((half, out.at[core if own else 1 - core], sem))
+        ready = min((p + 1) * take, HALF)
+        if ready - done >= HALF // 4 and ready % 8 == 0 or p == groups - 1:
+            piece = pl.ds(done, ready - done)
+            copies += fetching((half.at[piece], target.at[piece], sems.at[len(copies)]))
+            done = ready
+    for copy in copies:
+        copy.wait()
 
 
 def decode(take, scale, blocks, begun=None):
@@ -481,7 +513,7 @@
         out_shape=jax.ShapeDtypeStruct((2, HALF, C), jnp.float32),
         in_specs=[vmem()] + [hbm()] * len(rest),
         out_specs=hbm(),
-        scratch_shapes=[pltpu.VMEM((HALF, C), jnp.float32), pltpu.SemaphoreType.DMA(())],
+        scratch_shapes=[pltpu.VMEM((HALF, C), jnp.float32), pltpu.SemaphoreType.DMA((5,))],
         input_output_aliases={1: 0} if rest else {},
         compiler_params=pltpu.CompilerParams(vmem_limit_bytes=VMEM_LIMIT),
         name="decode_other" if rest else "decode_own",
@@ -490,7 +522,7 @@
 
 def product_kernel(f, near_hbm, mask_ref, kernel_ref, bricks, x_ref, y_ref, e0, e1, out, *refs):
     lx, ly, corners, wide, near, sem, v, *flipped = refs
-    fetched((near_hbm, near, sem))
+    (table,) = fetching((near_hbm, near, sem))
     weights = kernel_ref
     if f == 1:
         weights = flipped[0]
@@ -498,6 +530,7 @@
             weights[pl.ds((26 - o) * C, C)] = kernel_ref[pl.ds(o * C, C)].T
     fill_own(bricks, lx, ly, corners)
     fill_came(f, x_ref, y_ref, (e0, e1), lx, ly, corners)
+    table.wait()
 
     def per_slot(s, carry):
         build_columns(s, bricks, near, lx, ly, corners, wide, "all")
@@ -562,20 +595,21 @@
     x1, y1 = hopped(x1, "gx"), hopped(y1, "gy")
     v = own_columns(neighbours, act)
     x1, y1, v = lax.optimization_barrier((x1, y1, v))
-    x_came, y_came = join(x0, x1, y0, y1)
+    x_came, y_came, x_more, y_more = join(x0, x1, y0, y1)
     x_came, y_came = swapped(x_came, "gx", 0), swapped(y_came, "gy", 0)
     inner = inner_terms(v, grd)
     keep, send = rim_terms(neighbours, inner, grd, x_came, y_came)
     blocks = merge(groups, take, held, keep, swapped(send, "gy", 0)).astype(jnp.float16)
     rows = kernel.reshape(ROWS, C)
-    blocks, act, x_came = lax.optimization_barrier((blocks, act, x_came))
+    blocks, act, x_came, x_more, y_more = lax.optimization_barrier((blocks, act, x_came, x_more, y_more))
+    x_more, y_more = swapped(x_more, "gx", 0), swapped(y_more, "gy", 0)
     e0, e1 = forward_corners(x_came)
     edges = [swapped(e0, "gy", 0), swapped(e1, "gy", 1)]
     output = product(0, neighbours, voxel_mask, rows, act, x_came, y_came, edges)
     arrived, output = lax.optimization_barrier((spread(blocks), output))
     copies = sum_blocks(take, arrived.astype(jnp.float32)).astype(jnp.float16)
     copies, grd = lax.optimization_barrier((copies, grd))
-    input_grad = product(1, neighbours, voxel_mask, rows, grd, x_came, y_came, edges)
+    input_grad = product(1, neighbours, voxel_mask, rows, grd, x_more, y_more, edges)
     mine, input_grad = lax.optimization_barrier((spread(copies), input_grad))
     other = swapped(mine, "gy", 0)
     scale = 1.0 / math.sqrt(parts * SLOTS * 512)

time: 68.4 us -> 67.5 us (0.987)
  waiting for transfers between devices: 21.3 us -> 19.5 us
  starting transfers between devices: 18.5 us -> 19.8 us
    all_to_all x2, waiting for transfers between devices: 14.5 us -> 7.96 us  [spread(): lax.all_to_all(blocks, ('gx', 'gy'), 0, 0, axis_index_groups=same_core, t...]
    ppermute x6 -> x8, waiting for transfers between devices: 3.85 us -> 8.53 us  [swapped(): return lax.ppermute(value, axis, pairs)]
    ppermute x6 -> x8, starting transfers between devices: 4.75 us -> 6.13 us  [swapped(): return lax.ppermute(value, axis, pairs)]
  transfers between devices with their start and end apart: 10 -> 12, of which waited for: 7 -> 7; matrix products, arithmetic and copies ran while one was open for 0% -> 0% of each run, Pallas kernels for 25% -> 25%
where the time goes in v5:
time: 67.5 us; the launch traced here: 67 us
  Pallas kernels  23.3 us (35%)
  starting transfers between devices  19.8 us (29%)
  waiting for transfers between devices  19.5 us (29%)
  other arithmetic  1.84 us (3%)
  local copies, waits for them, and re-layouts  1.75 us (3%)
  between operations  0.86 us (1%)
    pallas_call x2, Pallas kernels, product(): pl.pallas_call(lambda *refs: product_kernel(f, *refs), out_shape=jax.Shap...  12.1 us
    all_to_all x2, starting transfers between devices, spread(): lax.all_to_all(blocks, ('gx', 'gy'), 0, 0, axis_index_groups=same_core, t...  11.1 us
    ppermute x8, waiting for transfers between devices, swapped(): return lax.ppermute(value, axis, pairs)  8.53 us
    all_to_all x2, waiting for transfers between devices, spread(): lax.all_to_all(blocks, ('gx', 'gy'), 0, 0, axis_index_groups=same_core, t...  7.96 us
    ppermute x8, starting transfers between devices, swapped(): return lax.ppermute(value, axis, pairs)  6.13 us
    ppermute x2, waiting for transfers between devices, hopped(): return lax.ppermute(value, axis, pairs)  2.99 us
    pallas_call x1, Pallas kernels, pack(): pl.pallas_call(pack_kernel, out_shape=[brick, brick] + sends, in_specs=[h...  2.82 us
    ppermute x2, starting transfers between devices, hopped(): return lax.ppermute(value, axis, pairs)  2.58 us
  transfers between devices with their start and end apart: 12, of which 7 were waited for; matrix products, arithmetic and copies ran while one was open for 0% of the time, Pallas kernels for 25%

profile of v5, /device:TPU:0, one launch (start us, length us, event | category | flops | bytes accessed | tf_op | source)
XLA Modules:
  0.0 67.0 jit_solution(9979117877989271545)
XLA Ops:
  0.6 2.8 %pack.1 = (bf16[4,512,128]{2,1,0:T(8,128)(2,1)}, bf16[4,512,128]{2,1,0:T(8,128)(2,1)}, bf16[304,128]{1,0:T(8,128)(2,1)}, bf16[304,128]{1,0:T(8,128)(2,1)}, bf16[...) custom-call(s32[2,4]{1,0:T(2,128)} %bitcast.13, s32[1,4]{1,0:T(1,128)} %bitcast.14, s32[4,27]{1,0:T(4,128)} %refs_0_.3, ...), custom_call_target="tpu_custom_call" | custom-call | tf_op jit(solution)/shard_map/pack/pallas_call | solution.py:123
  3.5 1.3 %collective-permute-start.1 = (bf16[304,128]{1,0:T(8,128)(2,1)}, bf16[304,128]{1,0:T(8,128)(2,1)S(1)}, u32[]{:S(2)}, u32[]{:S(2)}) collective-permute-start(bf16[304,128]{1,0:T(8,128)(2,1)} %get-tuple-element.32), channel_id=1, source_target_pairs={{1,3},{2,0},{5,7},{6,4},{9,11},{10,8},{13,15},{14,12},{17,19},{18,... | collective-permute-start | bytes 233480 | tf_op jit(solution)/shard_map/ppermute | solution.py:573
  4.8 1.3 %collective-permute-start = (bf16[288,128]{1,0:T(8,128)(2,1)}, bf16[288,128]{1,0:T(8,128)(2,1)S(1)}, u32[]{:S(2)}, u32[]{:S(2)}) collective-permute-start(bf16[288,128]{1,0:T(8,128)(2,1)} %get-tuple-element.31), channel_id=1, source_target_pairs={{4,12},{12,20},{20,28},{8,0},{16,8},{24,16},{5,13},{13,21},{21,29}... | collective-permute-start | bytes 221192 | tf_op jit(solution)/shard_map/ppermute | solution.py:573
  6.1 0.0 copy-start.1
  6.1 1.0 %copy-done.1 = bf16[4,512,128]{2,1,0:T(8,128)(2,1)S(1)} copy-done((bf16[4,512,128]{2,1,0:T(8,128)(2,1)S(1)}, bf16[4,512,128]{2,1,0:T(8,128)(2,1)}, u32[]{:S(2)}) %copy-start.1) | copy-done | bytes 524312
  7.1 0.0 copy-start.5
  7.1 0.7 %copy-done.5 = s32[4,27]{1,0:T(4,128)S(1)} copy-done((s32[4,27]{1,0:T(4,128)S(1)}, s32[4,27]{1,0:T(4,128)}, u32[]{:S(2)}) %copy-start.5) | copy-done | bytes 456
  7.8 0.0 copy-start.3
  7.8 0.0 copy-start.4
  7.8 0.0 copy-start
  7.8 1.4 %own_columns.1.v = bf16[4,10,64,1152]{3,2,1,0:T(8,128)(2,1)S(1)} custom-call(s32[4,27]{1,0:T(4,128)S(1)} %copy-done.5, bf16[4,512,128]{2,1,0:T(8,128)(2,1)S(1)} %copy-done.1), custom_call_target="tpu_custom_call" | custom-call | flops 16777216 | bytes 6291456 | tf_op jit(solution)/shard_map/own_columns/pallas_call | solution.py:306
  9.2 3.0 %collective-permute-done.x1 = bf16[288,128]{1,0:T(8,128)(2,1)S(1)} collective-permute-done((bf16[288,128]{1,0:T(8,128)(2,1)}, bf16[288,128]{1,0:T(8,128)(2,1)S(1)}, u32[]{:S(2)}, u32[]{:S(2)}) %collective-permute-start) | collective-permute-done | bytes 73760 | tf_op jit(solution)/shard_map/ppermute | solution.py:573
  12.2 0.0 collective-permute-done.1.y1
  12.2 0.0 copy-done.3
  12.2 0.0 copy-done.4
  12.3 2.2 %collective-permute-start.2 = (bf16[320,128]{1,0:T(8,128)(2,1)S(1)}, bf16[320,128]{1,0:T(8,128)(2,1)S(1)}, u32[]{:S(2)}, u32[]{:S(2)}) collective-permute-start(bf16[320,128]{1,0:T(8,128)(2,1)S(1)} %get-tuple-element.40), channel_id=1, source_target_pairs={{0,4},{4,0},{8,12},{12,8},{16,20},{20,16},{24,28},{28,24},{1,5},{5... | collective-permute-start | bytes 245768 | tf_op jit(solution)/shard_map/ppermute | solution.py:567
  14.5 1.1 %collective-permute-start.3 = (bf16[352,128]{1,0:T(8,128)(2,1)S(1)}, bf16[352,128]{1,0:T(8,128)(2,1)S(1)}, u32[]{:S(2)}, u32[]{:S(2)}) collective-permute-start(bf16[352,128]{1,0:T(8,128)(2,1)S(1)} %get-tuple-element.41), channel_id=1, source_target_pairs={{0,1},{1,0},{2,3},{3,2},{4,5},{5,4},{6,7},{7,6},{8,9},{9,8},{10,11... | collective-permute-start | bytes 270344 | tf_op jit(solution)/shard_map/ppermute | solution.py:567
  15.6 0.0 copy-done
  15.6 2.3 %inner_terms.1.inner = f32[3456,128]{1,0:T(8,128)S(1)} custom-call(bf16[4,10,64,1152]{3,2,1,0:T(8,128)(2,1)S(1)} %own_columns.1.v, bf16[4,512,128]{2,1,0:T(8,128)(2,1)S(1)} %copy-done), custom_call_target="tpu_custom_call" | custom-call | flops 1811939328 | bytes 6291456 | tf_op jit(solution)/shard_map/inner_terms/pallas_call | solution.py:330
  18.0 0.0 collective-permute-done.2.x_ref.x_came.refs_4_
  18.0 0.0 collective-permute-done.3.y_ref.refs_5_
  18.0 2.0 %rim_terms.1 = (f32[1728,128]{1,0:T(8,128)S(1)}, f32[1728,128]{1,0:T(8,128)S(1)}) custom-call(s32[4,27]{1,0:T(4,128)S(1)} %copy-done.5, f32[3456,128]{1,0:T(8,128)S(1)} %inner_terms.1.inner, bf16[4,512,128]{2,1,0:T(8,128)(2,1)S(1)} %copy-done, bf16[320,128]{1,0:T(8,128)(2,1)S(1)} %collective-permute-done.2.x_ref.x_came.refs_4_, ...), custom_call_target="tpu_custom_call" | custom-call | flops 301989888 | bytes 6291456 | tf_op jit(solution)/shard_map/rim_terms/pallas_call | solution.py:416
  20.0 0.1 collective-permute-start.4
  20.1 2.4 %collective-permute-done.4.refs_1_ = f32[1728,128]{1,0:T(8,128)S(1)} collective-permute-done((f32[1728,128]{1,0:T(8,128)S(1)}, f32[1728,128]{1,0:T(8,128)S(1)}, u32[]{:S(2)}, u32[]{:S(2)}) %collective-permute-start.4) | collective-permute-done | bytes 884768 | tf_op jit(solution)/shard_map/ppermute | solution.py:567
  22.5 0.3 merge.1
  22.8 0.0 copy-start.2
  22.9 0.0 copy-start.6
  22.9 0.0 copy-start.7
  22.9 0.0 copy-start.8
  22.9 0.8 %convert_element_type.15 = f16[16,112,128]{2,1,0:T(8,128)(2,1)} convert(f32[16,112,128]{2,1,0:T(8,128)S(1)} %merge.1) | non-fusion elementwise | flops 229376 | bytes 1376256 | tf_op jit(solution)/shard_map/convert_element_type | solution.py:602
  23.7 7.2 %all-to-all-start = ((f16[16,112,128]{2,1,0:T(8,128)(2,1)}), f16[16,112,128]{2,1,0:T(8,128)(2,1)S(1)}, u32[]{:S(2)}, u32[]{:S(2)}) async-start(f16[16,112,128]{2,1,0:T(8,128)(2,1)} %convert_element_type.15), calls=%async_computation | async-start | bytes 917504 | tf_op jit(solution)/shard_map/all_to_all | solution.py:585
  31.0 0.1 collective-permute-start.5
  31.0 0.7 collective-permute-start.6
  31.7 0.5 collective-permute-done.5.refs_6_
  32.2 0.0 collective-permute-done.6.refs_7_
  32.2 0.0 copy-done.2
  32.2 0.0 copy-done.6
  32.2 0.0 copy-done.7
  32.2 0.0 copy-done.8
  32.2 6.0 %output_product.1 = bf16[4,512,128]{2,1,0:T(8,128)(2,1)} custom-call(s32[4,27]{1,0:T(4,128)S(1)} %copy-done.6, s32[4,512]{1,0:T(4,128)S(1)} %copy-done.7, bf16[3456,128]{1,0:T(8,128)(2,1)S(1)} %bitcast.8, bf16[4,512,128]{2,1,0:T(8,128)(2,1)S(1)} %copy-done.2, bf16[320,128]{1,0:T(8,128)(2,1)S(1)} %collective-permute-done.2.x_ref.x_came.refs_4_, ...), custom_call_target="tpu_custom_call" | custom-call | flops 1811939328 | bytes 4194304 | tf_op jit(solution)/shard_map/output_product/pallas_call | solution.py:549
  38.2 6.9 %all-to-all-done = f16[16,112,128]{2,1,0:T(8,128)(2,1)S(1)} async-done(((f16[16,112,128]{2,1,0:T(8,128)(2,1)}), f16[16,112,128]{2,1,0:T(8,128)(2,1)S(1)}, u32[]{:S(2)}, u32[]{:S(2)}) %all-to-all-start) | async-done | bytes 458784 | tf_op jit(solution)/shard_map/all_to_all | solution.py:585
  45.1 0.1 convert_element_type.16.refs_0_
  45.2 0.3 sum_blocks.1
  45.4 0.8 %convert_element_type.17 = f16[16,112,128]{2,1,0:T(8,128)(2,1)} convert(f32[16,112,128]{2,1,0:T(8,128)S(1)} %sum_blocks.1) | non-fusion elementwise | flops 229376 | bytes 1376256 | tf_op jit(solution)/shard_map/convert_element_type | solution.py:610
  46.3 3.9 %all-to-all-start.1 = ((f16[16,112,128]{2,1,0:T(8,128)(2,1)}), f16[16,112,128]{2,1,0:T(8,128)(2,1)S(1)}, u32[]{:S(2)}, u32[]{:S(2)}) async-start(f16[16,112,128]{2,1,0:T(8,128)(2,1)} %convert_element_type.17), calls=%async_computation.1 | async-start | bytes 917504 | tf_op jit(solution)/shard_map/all_to_all | solution.py:585
  50.2 1.9 %collective-permute-start.7 = (bf16[256,128]{1,0:T(8,128)(2,1)S(1)}, bf16[256,128]{1,0:T(8,128)(2,1)S(1)}, u32[]{:S(2)}, u32[]{:S(2)}) collective-permute-start(bf16[256,128]{1,0:T(8,128)(2,1)S(1)} %get-tuple-element.55), channel_id=1, source_target_pairs={{0,4},{4,0},{8,12},{12,8},{16,20},{20,16},{24,28},{28,24},{1,5},{5... | collective-permute-start | bytes 196616 | tf_op jit(solution)/shard_map/ppermute | solution.py:567
  52.1 0.0 collective-permute-start.8
  52.1 4.9 %collective-permute-done.7.refs_4_ = bf16[256,128]{1,0:T(8,128)(2,1)S(1)} collective-permute-done((bf16[256,128]{1,0:T(8,128)(2,1)S(1)}, bf16[256,128]{1,0:T(8,128)(2,1)S(1)}, u32[]{:S(2)}, u32[]{:S(2)}) %collective-permute-start.7) | collective-permute-done | bytes 65568 | tf_op jit(solution)/shard_map/ppermute | solution.py:567
  57.0 0.0 collective-permute-done.8.refs_5_
  57.0 6.1 %input_grad_product.1 = bf16[4,512,128]{2,1,0:T(8,128)(2,1)} custom-call(s32[4,27]{1,0:T(4,128)S(1)} %copy-done.6, s32[4,512]{1,0:T(4,128)S(1)} %copy-done.7, bf16[3456,128]{1,0:T(8,128)(2,1)S(1)} %bitcast.9, bf16[4,512,128]{2,1,0:T(8,128)(2,1)S(1)} %copy-done, bf16[256,128]{1,0:T(8,128)(2,1)S(1)} %collective-permute-done.7.refs_4_, ...), custom_call_target="tpu_custom_call" | custom-call | flops 1811939328 | bytes 4194304 | tf_op jit(solution)/shard_map/input_grad_product/pallas_call | solution.py:549
  63.1 1.1 %all-to-all-done.1 = f16[16,112,128]{2,1,0:T(8,128)(2,1)S(1)} async-done(((f16[16,112,128]{2,1,0:T(8,128)(2,1)}), f16[16,112,128]{2,1,0:T(8,128)(2,1)S(1)}, u32[]{:S(2)}, u32[]{:S(2)}) %all-to-all-start.1) | async-done | bytes 458784 | tf_op jit(solution)/shard_map/all_to_all | solution.py:585
  64.2 0.0 collective-permute-start.9
  64.2 0.1 convert_element_type.19.refs_0_
  64.2 1.0 %decode_own.1.refs_1_ = f32[2,1728,128]{2,1,0:T(8,128)} custom-call(f32[16,112,128]{2,1,0:T(8,128)S(1)} %convert_element_type.19.refs_0_), custom_call_target="tpu_custom_call" | custom-call | tf_op jit(solution)/shard_map/decode_own/pallas_call | solution.py:511
  65.2 0.8 %collective-permute-done.9 = f16[16,112,128]{2,1,0:T(8,128)(2,1)S(1)} collective-permute-done((f16[16,112,128]{2,1,0:T(8,128)(2,1)S(1)}, f16[16,112,128]{2,1,0:T(8,128)(2,1)S(1)}, u32[]{:S(2)}, u32[]{:S(2)}) %collective-permute-start.9) | collective-permute-done | bytes 458784 | tf_op jit(solution)/shard_map/ppermute | solution.py:567
  66.0 0.1 convert_element_type.18.refs_0_
  66.1 1.0 %decode_other.1 = f32[2,1728,128]{2,1,0:T(8,128)} custom-call(f32[16,112,128]{2,1,0:T(8,128)S(1)} %convert_element_type.18.refs_0_, f32[2,1728,128]{2,1,0:T(8,128)} %decode_own.1.refs_1_), custom_call_target="tpu_custom_call", output_to_operand_aliasing={{}: (1, {})} | custom-call | tf_op jit(solution)/shard_map/decode_other/pallas_call | solution.py:511
  (2 shorter events, 0.0 us)
Async XLA Ops:
  3.5 8.8 %collective-permute-start.1 = (bf16[304,128]{1,0:T(8,128)(2,1)}, bf16[304,128]{1,0:T(8,128)(2,1)S(1)}, u32[]{:S(2)}, u32[]{:S(2)}) collective-permute-start(bf16[304,128]{1,0:T(8,128)(2,1)} %get-tuple-element.32), channel_id=1, source_target_pairs={{1,3},{2,0},{5,7},{6,4},{9,11},{10,8},{13,15},{14,12},{17,19},{18,... | collective-permute-start | bytes 233480 | tf_op jit(solution)/shard_map/ppermute | solution.py:573
  4.8 7.5 %collective-permute-start = (bf16[288,128]{1,0:T(8,128)(2,1)}, bf16[288,128]{1,0:T(8,128)(2,1)S(1)}, u32[]{:S(2)}, u32[]{:S(2)}) collective-permute-start(bf16[288,128]{1,0:T(8,128)(2,1)} %get-tuple-element.31), channel_id=1, source_target_pairs={{4,12},{12,20},{20,28},{8,0},{16,8},{24,16},{5,13},{13,21},{21,29}... | collective-permute-start | bytes 221192 | tf_op jit(solution)/shard_map/ppermute | solution.py:573
  6.1 1.0 %copy-start.1 = (bf16[4,512,128]{2,1,0:T(8,128)(2,1)S(1)}, bf16[4,512,128]{2,1,0:T(8,128)(2,1)}, u32[]{:S(2)}) copy-start(bf16[4,512,128]{2,1,0:T(8,128)(2,1)} %get-tuple-element.47.act.refs_3_) | copy-start | bytes 1572868
  7.1 0.7 %copy-start.5 = (s32[4,27]{1,0:T(4,128)S(1)}, s32[4,27]{1,0:T(4,128)}, u32[]{:S(2)}) copy-start(s32[4,27]{1,0:T(4,128)} %refs_0_.3) | copy-start | bytes 1300
  7.8 4.4 %copy-start.3 = (bf16[304,128]{1,0:T(8,128)(2,1)S(1)}, bf16[304,128]{1,0:T(8,128)(2,1)}, u32[]{:S(2)}) copy-start(bf16[304,128]{1,0:T(8,128)(2,1)} %get-tuple-element.38.y0) | copy-start | bytes 233476
  7.8 4.4 %copy-start.4 = (bf16[288,128]{1,0:T(8,128)(2,1)S(1)}, bf16[288,128]{1,0:T(8,128)(2,1)}, u32[]{:S(2)}) copy-start(bf16[288,128]{1,0:T(8,128)(2,1)} %get-tuple-element.36.x0) | copy-start | bytes 221188
  7.8 7.8 %copy-start = (bf16[4,512,128]{2,1,0:T(8,128)(2,1)S(1)}, bf16[4,512,128]{2,1,0:T(8,128)(2,1)}, u32[]{:S(2)}) copy-start(bf16[4,512,128]{2,1,0:T(8,128)(2,1)} %get-tuple-element.54.grd.refs_3_) | copy-start | bytes 1572868
  12.3 5.7 %collective-permute-start.2 = (bf16[320,128]{1,0:T(8,128)(2,1)S(1)}, bf16[320,128]{1,0:T(8,128)(2,1)S(1)}, u32[]{:S(2)}, u32[]{:S(2)}) collective-permute-start(bf16[320,128]{1,0:T(8,128)(2,1)S(1)} %get-tuple-element.40), channel_id=1, source_target_pairs={{0,4},{4,0},{8,12},{12,8},{16,20},{20,16},{24,28},{28,24},{1,5},{5... | collective-permute-start | bytes 245768 | tf_op jit(solution)/shard_map/ppermute | solution.py:567
  14.5 3.5 %collective-permute-start.3 = (bf16[352,128]{1,0:T(8,128)(2,1)S(1)}, bf16[352,128]{1,0:T(8,128)(2,1)S(1)}, u32[]{:S(2)}, u32[]{:S(2)}) collective-permute-start(bf16[352,128]{1,0:T(8,128)(2,1)S(1)} %get-tuple-element.41), channel_id=1, source_target_pairs={{0,1},{1,0},{2,3},{3,2},{4,5},{5,4},{6,7},{7,6},{8,9},{9,8},{10,11... | collective-permute-start | bytes 270344 | tf_op jit(solution)/shard_map/ppermute | solution.py:567
  20.0 2.5 %collective-permute-start.4 = (f32[1728,128]{1,0:T(8,128)S(1)}, f32[1728,128]{1,0:T(8,128)S(1)}, u32[]{:S(2)}, u32[]{:S(2)}) collective-permute-start(f32[1728,128]{1,0:T(8,128)S(1)} %get-tuple-element.43), channel_id=1, source_target_pairs={{0,1},{1,0},{2,3},{3,2},{4,5},{5,4},{6,7},{7,6},{8,9},{9,8},{10,11... | collective-permute-start | bytes 2654216 | tf_op jit(solution)/shard_map/ppermute | solution.py:567
  22.8 9.4 %copy-start.2 = (bf16[4,512,128]{2,1,0:T(8,128)(2,1)S(1)}, bf16[4,512,128]{2,1,0:T(8,128)(2,1)}, u32[]{:S(2)}) copy-start(bf16[4,512,128]{2,1,0:T(8,128)(2,1)} %get-tuple-element.47.act.refs_3_) | copy-start | bytes 1572868
  22.9 9.4 %copy-start.6 = (s32[4,27]{1,0:T(4,128)S(1)}, s32[4,27]{1,0:T(4,128)}, u32[]{:S(2)}) copy-start(s32[4,27]{1,0:T(4,128)} %refs_0_.3) | copy-start | bytes 1300
  22.9 9.3 %copy-start.7 = (s32[4,512]{1,0:T(4,128)S(1)}, s32[4,512]{1,0:T(4,128)}, u32[]{:S(2)}) copy-start(s32[4,512]{1,0:T(4,128)} %refs_1_.3) | copy-start | bytes 24580
  22.9 9.3 %copy-start.8 = (bf16[27,128,128]{2,1,0:T(8,128)(2,1)S(1)}, bf16[27,128,128]{2,1,0:T(8,128)(2,1)}, u32[]{:S(2)}) copy-start(bf16[27,128,128]{2,1,0:T(8,128)(2,1)} %param.9) | copy-start | bytes 2654212
  23.7 21.4 %all-to-all-start = ((f16[16,112,128]{2,1,0:T(8,128)(2,1)}), f16[16,112,128]{2,1,0:T(8,128)(2,1)S(1)}, u32[]{:S(2)}, u32[]{:S(2)}) async-start(f16[16,112,128]{2,1,0:T(8,128)(2,1)} %convert_element_type.15), calls=%async_computation | async-start | bytes 917504 | tf_op jit(solution)/shard_map/all_to_all | solution.py:585
  31.0 1.2 %collective-permute-start.5 = (bf16[32,128]{1,0:T(8,128)(2,1)S(1)}, bf16[32,128]{1,0:T(8,128)(2,1)S(1)}, u32[]{:S(2)}, u32[]{:S(2)}) collective-permute-start(bf16[32,128]{1,0:T(8,128)(2,1)S(1)} %get-tuple-element.49), channel_id=1, source_target_pairs={{0,1},{1,0},{2,3},{3,2},{4,5},{5,4},{6,7},{7,6},{8,9},{9,8},{10,11... | collective-permute-start | bytes 24584 | tf_op jit(solution)/shard_map/ppermute | solution.py:567
  31.0 1.2 %collective-permute-start.6 = (bf16[32,128]{1,0:T(8,128)(2,1)S(1)}, bf16[32,128]{1,0:T(8,128)(2,1)S(1)}, u32[]{:S(2)}, u32[]{:S(2)}) collective-permute-start(bf16[32,128]{1,0:T(8,128)(2,1)S(1)} %get-tuple-element.50), channel_id=1, source_target_pairs={{1,2},{2,1},{5,6},{6,5},{9,10},{10,9},{13,14},{14,13},{17,18},{18,... | collective-permute-start | bytes 24584 | tf_op jit(solution)/shard_map/ppermute | solution.py:567
  46.3 17.9 %all-to-all-start.1 = ((f16[16,112,128]{2,1,0:T(8,128)(2,1)}), f16[16,112,128]{2,1,0:T(8,128)(2,1)S(1)}, u32[]{:S(2)}, u32[]{:S(2)}) async-start(f16[16,112,128]{2,1,0:T(8,128)(2,1)} %convert_element_type.17), calls=%async_computation.1 | async-start | bytes 917504 | tf_op jit(solution)/shard_map/all_to_all | solution.py:585
  50.2 6.8 %collective-permute-start.7 = (bf16[256,128]{1,0:T(8,128)(2,1)S(1)}, bf16[256,128]{1,0:T(8,128)(2,1)S(1)}, u32[]{:S(2)}, u32[]{:S(2)}) collective-permute-start(bf16[256,128]{1,0:T(8,128)(2,1)S(1)} %get-tuple-element.55), channel_id=1, source_target_pairs={{0,4},{4,0},{8,12},{12,8},{16,20},{20,16},{24,28},{28,24},{1,5},{5... | collective-permute-start | bytes 196616 | tf_op jit(solution)/shard_map/ppermute | solution.py:567
  52.1 4.9 %collective-permute-start.8 = (bf16[256,128]{1,0:T(8,128)(2,1)S(1)}, bf16[256,128]{1,0:T(8,128)(2,1)S(1)}, u32[]{:S(2)}, u32[]{:S(2)}) collective-permute-start(bf16[256,128]{1,0:T(8,128)(2,1)S(1)} %get-tuple-element.56), channel_id=1, source_target_pairs={{0,1},{1,0},{2,3},{3,2},{4,5},{5,4},{6,7},{7,6},{8,9},{9,8},{10,11... | collective-permute-start | bytes 196616 | tf_op jit(solution)/shard_map/ppermute | solution.py:567
  64.2 1.8 %collective-permute-start.9 = (f16[16,112,128]{2,1,0:T(8,128)(2,1)S(1)}, f16[16,112,128]{2,1,0:T(8,128)(2,1)S(1)}, u32[]{:S(2)}, u32[]{:S(2)}) collective-permute-start(f16[16,112,128]{2,1,0:T(8,128)(2,1)S(1)} %all-to-all-done.1), channel_id=1, source_target_pairs={{0,1},{1,0},{2,3},{3,2},{4,5},{5,4},{6,7},{7,6},{8,9},{9,8},{10,11... | collective-permute-start | bytes 1376264 | tf_op jit(solution)/shard_map/ppermute | solution.py:567

commit v6 on v5

--- a/solution.py
+++ b/solution.py
@@ -579,7 +579,8 @@
     groups = parts // 2
     take = -(-HALF // groups)
     held = -(-(take + 1) // 16) * 16
-    same_core = [[i for i in range(parts) if i % size_y % 2 == core] for core in range(2)]
+    order = [(i + parts // 2) % parts for i in range(parts)]
+    same_core = [[i for i in order if i % size_y % 2 == core] for core in range(2)]
 
     def spread(blocks):
         return lax.all_to_all(blocks, ("gx", "gy"), 0, 0, axis_index_groups=same_core, tiled=True)
@@ -606,7 +607,7 @@
     e0, e1 = forward_corners(x_came)
     edges = [swapped(e0, "gy", 0), swapped(e1, "gy", 1)]
     output = product(0, neighbours, voxel_mask, rows, act, x_came, y_came, edges)
-    arrived, output = lax.optimization_barrier((spread(blocks), output))
+    arrived, output, x_more, y_more = lax.optimization_barrier((spread(blocks), output, x_more, y_more))
     copies = sum_blocks(take, arrived.astype(jnp.float32)).astype(jnp.float16)
     copies, grd = lax.optimization_barrier((copies, grd))
     input_grad = product(1, neighbours, voxel_mask, rows, grd, x_more, y_more, edges)

time: 67.5 us -> 65.1 us (0.964)
  waiting for transfers between devices: 19.5 us -> 12.9 us
  starting transfers between devices: 19.8 us -> 24.1 us
    ppermute x8, waiting for transfers between devices: 8.53 us -> 3.18 us  [swapped(): return lax.ppermute(value, axis, pairs)]
    ppermute x8, starting transfers between devices: 6.13 us -> 8.28 us  [swapped(): return lax.ppermute(value, axis, pairs)]
    all_to_all x2, starting transfers between devices: 11.1 us -> 13.2 us  [spread(): lax.all_to_all(blocks, ('gx', 'gy'), 0, 0, axis_index_groups=same_core, t...]
    all_to_all x2, waiting for transfers between devices: 7.96 us -> 6.69 us  [spread(): lax.all_to_all(blocks, ('gx', 'gy'), 0, 0, axis_index_groups=same_core, t...]
  transfers between devices with their start and end apart: 12 -> 12, of which waited for: 7 -> 5; matrix products, arithmetic and copies ran while one was open for 0% -> 0% of each run, Pallas kernels for 25% -> 26%
where the time goes in v6:
time: 65.1 us; the launch traced here: 64.6 us
  starting transfers between devices  24.1 us (37%)
  Pallas kernels  23.3 us (36%)
  waiting for transfers between devices  12.9 us (20%)
  other arithmetic  1.84 us (3%)
  local copies, waits for them, and re-layouts  1.75 us (3%)
  between operations  0.86 us (1%)
    all_to_all x2, starting transfers between devices, spread(): lax.all_to_all(blocks, ('gx', 'gy'), 0, 0, axis_index_groups=same_core, t...  13.2 us
    pallas_call x2, Pallas kernels, product(): pl.pallas_call(lambda *refs: product_kernel(f, *refs), out_shape=jax.Shap...  12.1 us
    ppermute x8, starting transfers between devices, swapped(): return lax.ppermute(value, axis, pairs)  8.28 us
    all_to_all x2, waiting for transfers between devices, spread(): lax.all_to_all(blocks, ('gx', 'gy'), 0, 0, axis_index_groups=same_core, t...  6.69 us
    ppermute x8, waiting for transfers between devices, swapped(): return lax.ppermute(value, axis, pairs)  3.18 us
    ppermute x2, waiting for transfers between devices, hopped(): return lax.ppermute(value, axis, pairs)  2.99 us
    pallas_call x1, Pallas kernels, pack(): pl.pallas_call(pack_kernel, out_shape=[brick, brick] + sends, in_specs=[h...  2.82 us
    ppermute x2, starting transfers between devices, hopped(): return lax.ppermute(value, axis, pairs)  2.58 us
  transfers between devices with their start and end apart: 12, of which 5 were waited for; matrix products, arithmetic and copies ran while one was open for 0% of the time, Pallas kernels for 26%

profile of v6, /device:TPU:0, one launch (start us, length us, event | category | flops | bytes accessed | tf_op | source)
XLA Modules:
  0.0 64.6 jit_solution(1497351532133690670)
XLA Ops:
  0.6 2.8 %pack.1 = (bf16[4,512,128]{2,1,0:T(8,128)(2,1)}, bf16[4,512,128]{2,1,0:T(8,128)(2,1)}, bf16[304,128]{1,0:T(8,128)(2,1)}, bf16[304,128]{1,0:T(8,128)(2,1)}, bf16[...) custom-call(s32[2,4]{1,0:T(2,128)} %bitcast.13, s32[1,4]{1,0:T(1,128)} %bitcast.14, s32[4,27]{1,0:T(4,128)} %refs_0_.3, ...), custom_call_target="tpu_custom_call" | custom-call | tf_op jit(solution)/shard_map/pack/pallas_call | solution.py:123
  3.5 1.3 %collective-permute-start.1 = (bf16[304,128]{1,0:T(8,128)(2,1)}, bf16[304,128]{1,0:T(8,128)(2,1)S(1)}, u32[]{:S(2)}, u32[]{:S(2)}) collective-permute-start(bf16[304,128]{1,0:T(8,128)(2,1)} %get-tuple-element.34), channel_id=1, source_target_pairs={{1,3},{2,0},{5,7},{6,4},{9,11},{10,8},{13,15},{14,12},{17,19},{18,... | collective-permute-start | bytes 233480 | tf_op jit(solution)/shard_map/ppermute | solution.py:573
  4.8 1.3 %collective-permute-start = (bf16[288,128]{1,0:T(8,128)(2,1)}, bf16[288,128]{1,0:T(8,128)(2,1)S(1)}, u32[]{:S(2)}, u32[]{:S(2)}) collective-permute-start(bf16[288,128]{1,0:T(8,128)(2,1)} %get-tuple-element.33), channel_id=1, source_target_pairs={{4,12},{12,20},{20,28},{8,0},{16,8},{24,16},{5,13},{13,21},{21,29}... | collective-permute-start | bytes 221192 | tf_op jit(solution)/shard_map/ppermute | solution.py:573
  6.1 0.0 copy-start.1
  6.1 1.0 %copy-done.1 = bf16[4,512,128]{2,1,0:T(8,128)(2,1)S(1)} copy-done((bf16[4,512,128]{2,1,0:T(8,128)(2,1)S(1)}, bf16[4,512,128]{2,1,0:T(8,128)(2,1)}, u32[]{:S(2)}) %copy-start.1) | copy-done | bytes 524312
  7.1 0.0 copy-start.5
  7.1 0.7 %copy-done.5 = s32[4,27]{1,0:T(4,128)S(1)} copy-done((s32[4,27]{1,0:T(4,128)S(1)}, s32[4,27]{1,0:T(4,128)}, u32[]{:S(2)}) %copy-start.5) | copy-done | bytes 456
  7.8 0.0 copy-start.3
  7.8 0.0 copy-start.4
  7.8 0.0 copy-start
  7.8 1.4 %own_columns.1.v = bf16[4,10,64,1152]{3,2,1,0:T(8,128)(2,1)S(1)} custom-call(s32[4,27]{1,0:T(4,128)S(1)} %copy-done.5, bf16[4,512,128]{2,1,0:T(8,128)(2,1)S(1)} %copy-done.1), custom_call_target="tpu_custom_call" | custom-call | flops 16777216 | bytes 6291456 | tf_op jit(solution)/shard_map/own_columns/pallas_call | solution.py:306
  9.2 3.0 %collective-permute-done.x1 = bf16[288,128]{1,0:T(8,128)(2,1)S(1)} collective-permute-done((bf16[288,128]{1,0:T(8,128)(2,1)}, bf16[288,128]{1,0:T(8,128)(2,1)S(1)}, u32[]{:S(2)}, u32[]{:S(2)}) %collective-permute-start) | collective-permute-done | bytes 73760 | tf_op jit(solution)/shard_map/ppermute | solution.py:573
  12.2 0.0 collective-permute-done.1.y1
  12.2 0.0 copy-done.3
  12.2 0.0 copy-done.4
  12.3 2.2 %collective-permute-start.2 = (bf16[320,128]{1,0:T(8,128)(2,1)S(1)}, bf16[320,128]{1,0:T(8,128)(2,1)S(1)}, u32[]{:S(2)}, u32[]{:S(2)}) collective-permute-start(bf16[320,128]{1,0:T(8,128)(2,1)S(1)} %get-tuple-element.42), channel_id=1, source_target_pairs={{0,4},{4,0},{8,12},{12,8},{16,20},{20,16},{24,28},{28,24},{1,5},{5... | collective-permute-start | bytes 245768 | tf_op jit(solution)/shard_map/ppermute | solution.py:567
  14.5 1.1 %collective-permute-start.3 = (bf16[352,128]{1,0:T(8,128)(2,1)S(1)}, bf16[352,128]{1,0:T(8,128)(2,1)S(1)}, u32[]{:S(2)}, u32[]{:S(2)}) collective-permute-start(bf16[352,128]{1,0:T(8,128)(2,1)S(1)} %get-tuple-element.43), channel_id=1, source_target_pairs={{0,1},{1,0},{2,3},{3,2},{4,5},{5,4},{6,7},{7,6},{8,9},{9,8},{10,11... | collective-permute-start | bytes 270344 | tf_op jit(solution)/shard_map/ppermute | solution.py:567
  15.6 0.0 copy-done
  15.6 2.3 %inner_terms.1.inner = f32[3456,128]{1,0:T(8,128)S(1)} custom-call(bf16[4,10,64,1152]{3,2,1,0:T(8,128)(2,1)S(1)} %own_columns.1.v, bf16[4,512,128]{2,1,0:T(8,128)(2,1)S(1)} %copy-done), custom_call_target="tpu_custom_call" | custom-call | flops 1811939328 | bytes 6291456 | tf_op jit(solution)/shard_map/inner_terms/pallas_call | solution.py:330
  18.0 0.0 collective-permute-done.2.x_ref.x_came.refs_4_
  18.0 0.0 collective-permute-done.3.y_ref.refs_5_
  18.0 2.0 %rim_terms.1 = (f32[1728,128]{1,0:T(8,128)S(1)}, f32[1728,128]{1,0:T(8,128)S(1)}) custom-call(s32[4,27]{1,0:T(4,128)S(1)} %copy-done.5, f32[3456,128]{1,0:T(8,128)S(1)} %inner_terms.1.inner, bf16[4,512,128]{2,1,0:T(8,128)(2,1)S(1)} %copy-done, bf16[320,128]{1,0:T(8,128)(2,1)S(1)} %collective-permute-done.2.x_ref.x_came.refs_4_, ...), custom_call_target="tpu_custom_call" | custom-call | flops 301989888 | bytes 6291456 | tf_op jit(solution)/shard_map/rim_terms/pallas_call | solution.py:416
  20.0 0.1 collective-permute-start.4
  20.1 2.4 %collective-permute-done.4.refs_1_ = f32[1728,128]{1,0:T(8,128)S(1)} collective-permute-done((f32[1728,128]{1,0:T(8,128)S(1)}, f32[1728,128]{1,0:T(8,128)S(1)}, u32[]{:S(2)}, u32[]{:S(2)}) %collective-permute-start.4) | collective-permute-done | bytes 884768 | tf_op jit(solution)/shard_map/ppermute | solution.py:567
  22.5 0.3 merge.1
  22.8 0.0 copy-start.2
  22.9 0.0 copy-start.6
  22.9 0.0 copy-start.7
  22.9 0.0 copy-start.8
  22.9 0.8 %convert_element_type.15 = f16[16,112,128]{2,1,0:T(8,128)(2,1)} convert(f32[16,112,128]{2,1,0:T(8,128)S(1)} %merge.1) | non-fusion elementwise | flops 229376 | bytes 1376256 | tf_op jit(solution)/shard_map/convert_element_type | solution.py:603
  23.7 7.7 %all-to-all-start = ((f16[16,112,128]{2,1,0:T(8,128)(2,1)}), f16[16,112,128]{2,1,0:T(8,128)(2,1)S(1)}, u32[]{:S(2)}, u32[]{:S(2)}) async-start(f16[16,112,128]{2,1,0:T(8,128)(2,1)} %convert_element_type.15), calls=%async_computation | async-start | bytes 917504 | tf_op jit(solution)/shard_map/all_to_all | solution.py:586
  31.4 0.1 collective-permute-start.5
  31.5 0.7 %collective-permute-start.6 = (bf16[32,128]{1,0:T(8,128)(2,1)S(1)}, bf16[32,128]{1,0:T(8,128)(2,1)S(1)}, u32[]{:S(2)}, u32[]{:S(2)}) collective-permute-start(bf16[32,128]{1,0:T(8,128)(2,1)S(1)} %get-tuple-element.52), channel_id=1, source_target_pairs={{1,2},{2,1},{5,6},{6,5},{9,10},{10,9},{13,14},{14,13},{17,18},{18,... | collective-permute-start | bytes 24584 | tf_op jit(solution)/shard_map/ppermute | solution.py:567
  32.2 1.5 %collective-permute-start.7 = (bf16[256,128]{1,0:T(8,128)(2,1)S(1)}, bf16[256,128]{1,0:T(8,128)(2,1)S(1)}, u32[]{:S(2)}, u32[]{:S(2)}) collective-permute-start(bf16[256,128]{1,0:T(8,128)(2,1)S(1)} %get-tuple-element.53), channel_id=1, source_target_pairs={{0,4},{4,0},{8,12},{12,8},{16,20},{20,16},{24,28},{28,24},{1,5},{5... | collective-permute-start | bytes 196616 | tf_op jit(solution)/shard_map/ppermute | solution.py:567
  33.7 2.5 %collective-permute-start.8 = (bf16[256,128]{1,0:T(8,128)(2,1)S(1)}, bf16[256,128]{1,0:T(8,128)(2,1)S(1)}, u32[]{:S(2)}, u32[]{:S(2)}) collective-permute-start(bf16[256,128]{1,0:T(8,128)(2,1)S(1)} %get-tuple-element.54), channel_id=1, source_target_pairs={{0,1},{1,0},{2,3},{3,2},{4,5},{5,4},{6,7},{7,6},{8,9},{9,8},{10,11... | collective-permute-start | bytes 196616 | tf_op jit(solution)/shard_map/ppermute | solution.py:567
  36.2 0.0 collective-permute-done.5.refs_6_
  36.2 0.0 collective-permute-done.6.refs_7_
  36.2 0.0 copy-done.2
  36.2 0.0 copy-done.6
  36.2 0.0 copy-done.7
  36.3 0.0 copy-done.8
  36.3 6.0 %output_product.1 = bf16[4,512,128]{2,1,0:T(8,128)(2,1)} custom-call(s32[4,27]{1,0:T(4,128)S(1)} %copy-done.6, s32[4,512]{1,0:T(4,128)S(1)} %copy-done.7, bf16[3456,128]{1,0:T(8,128)(2,1)S(1)} %bitcast.8, bf16[4,512,128]{2,1,0:T(8,128)(2,1)S(1)} %copy-done.2, bf16[320,128]{1,0:T(8,128)(2,1)S(1)} %collective-permute-done.2.x_ref.x_came.refs_4_, ...), custom_call_target="tpu_custom_call" | custom-call | flops 1811939328 | bytes 4194304 | tf_op jit(solution)/shard_map/output_product/pallas_call | solution.py:549
  42.3 0.0 collective-permute-done.7.refs_4_
  42.3 0.0 collective-permute-done.8.refs_5_
  42.3 1.0 %all-to-all-done = f16[16,112,128]{2,1,0:T(8,128)(2,1)S(1)} async-done(((f16[16,112,128]{2,1,0:T(8,128)(2,1)}), f16[16,112,128]{2,1,0:T(8,128)(2,1)S(1)}, u32[]{:S(2)}, u32[]{:S(2)}) %all-to-all-start) | async-done | bytes 458784 | tf_op jit(solution)/shard_map/all_to_all | solution.py:586
  43.3 0.1 convert_element_type.16.refs_0_
  43.4 0.3 sum_blocks.1
  43.6 0.8 %convert_element_type.17 = f16[16,112,128]{2,1,0:T(8,128)(2,1)} convert(f32[16,112,128]{2,1,0:T(8,128)S(1)} %sum_blocks.1) | non-fusion elementwise | flops 229376 | bytes 1376256 | tf_op jit(solution)/shard_map/convert_element_type | solution.py:611
  44.5 5.5 %all-to-all-start.1 = ((f16[16,112,128]{2,1,0:T(8,128)(2,1)}), f16[16,112,128]{2,1,0:T(8,128)(2,1)S(1)}, u32[]{:S(2)}, u32[]{:S(2)}) async-start(f16[16,112,128]{2,1,0:T(8,128)(2,1)} %convert_element_type.17), calls=%async_computation.1 | async-start | bytes 917504 | tf_op jit(solution)/shard_map/all_to_all | solution.py:586
  50.0 6.1 %input_grad_product.1 = bf16[4,512,128]{2,1,0:T(8,128)(2,1)} custom-call(s32[4,27]{1,0:T(4,128)S(1)} %copy-done.6, s32[4,512]{1,0:T(4,128)S(1)} %copy-done.7, bf16[3456,128]{1,0:T(8,128)(2,1)S(1)} %bitcast.9, bf16[4,512,128]{2,1,0:T(8,128)(2,1)S(1)} %copy-done, bf16[256,128]{1,0:T(8,128)(2,1)S(1)} %collective-permute-done.7.refs_4_, ...), custom_call_target="tpu_custom_call" | custom-call | flops 1811939328 | bytes 4194304 | tf_op jit(solution)/shard_map/input_grad_product/pallas_call | solution.py:549
  56.1 5.7 %all-to-all-done.1 = f16[16,112,128]{2,1,0:T(8,128)(2,1)S(1)} async-done(((f16[16,112,128]{2,1,0:T(8,128)(2,1)}), f16[16,112,128]{2,1,0:T(8,128)(2,1)S(1)}, u32[]{:S(2)}, u32[]{:S(2)}) %all-to-all-start.1) | async-done | bytes 458784 | tf_op jit(solution)/shard_map/all_to_all | solution.py:586
  61.8 0.0 collective-permute-start.9
  61.8 0.1 convert_element_type.19.refs_0_
  61.8 1.0 %decode_own.1.refs_1_ = f32[2,1728,128]{2,1,0:T(8,128)} custom-call(f32[16,112,128]{2,1,0:T(8,128)S(1)} %convert_element_type.19.refs_0_), custom_call_target="tpu_custom_call" | custom-call | tf_op jit(solution)/shard_map/decode_own/pallas_call | solution.py:511
  62.8 0.8 %collective-permute-done.9 = f16[16,112,128]{2,1,0:T(8,128)(2,1)S(1)} collective-permute-done((f16[16,112,128]{2,1,0:T(8,128)(2,1)S(1)}, f16[16,112,128]{2,1,0:T(8,128)(2,1)S(1)}, u32[]{:S(2)}, u32[]{:S(2)}) %collective-permute-start.9) | collective-permute-done | bytes 458784 | tf_op jit(solution)/shard_map/ppermute | solution.py:567
  63.6 0.1 convert_element_type.18.refs_0_
  63.7 1.0 %decode_other.1 = f32[2,1728,128]{2,1,0:T(8,128)} custom-call(f32[16,112,128]{2,1,0:T(8,128)S(1)} %convert_element_type.18.refs_0_, f32[2,1728,128]{2,1,0:T(8,128)} %decode_own.1.refs_1_), custom_call_target="tpu_custom_call", output_to_operand_aliasing={{}: (1, {})} | custom-call | tf_op jit(solution)/shard_map/decode_other/pallas_call | solution.py:511
  (2 shorter events, 0.0 us)
Async XLA Ops:
  3.5 8.8 %collective-permute-start.1 = (bf16[304,128]{1,0:T(8,128)(2,1)}, bf16[304,128]{1,0:T(8,128)(2,1)S(1)}, u32[]{:S(2)}, u32[]{:S(2)}) collective-permute-start(bf16[304,128]{1,0:T(8,128)(2,1)} %get-tuple-element.34), channel_id=1, source_target_pairs={{1,3},{2,0},{5,7},{6,4},{9,11},{10,8},{13,15},{14,12},{17,19},{18,... | collective-permute-start | bytes 233480 | tf_op jit(solution)/shard_map/ppermute | solution.py:573
  4.8 7.5 %collective-permute-start = (bf16[288,128]{1,0:T(8,128)(2,1)}, bf16[288,128]{1,0:T(8,128)(2,1)S(1)}, u32[]{:S(2)}, u32[]{:S(2)}) collective-permute-start(bf16[288,128]{1,0:T(8,128)(2,1)} %get-tuple-element.33), channel_id=1, source_target_pairs={{4,12},{12,20},{20,28},{8,0},{16,8},{24,16},{5,13},{13,21},{21,29}... | collective-permute-start | bytes 221192 | tf_op jit(solution)/shard_map/ppermute | solution.py:573
  6.1 1.0 %copy-start.1 = (bf16[4,512,128]{2,1,0:T(8,128)(2,1)S(1)}, bf16[4,512,128]{2,1,0:T(8,128)(2,1)}, u32[]{:S(2)}) copy-start(bf16[4,512,128]{2,1,0:T(8,128)(2,1)} %get-tuple-element.49.act.refs_3_) | copy-start | bytes 1572868
  7.1 0.7 %copy-start.5 = (s32[4,27]{1,0:T(4,128)S(1)}, s32[4,27]{1,0:T(4,128)}, u32[]{:S(2)}) copy-start(s32[4,27]{1,0:T(4,128)} %refs_0_.3) | copy-start | bytes 1300
  7.8 4.4 %copy-start.3 = (bf16[304,128]{1,0:T(8,128)(2,1)S(1)}, bf16[304,128]{1,0:T(8,128)(2,1)}, u32[]{:S(2)}) copy-start(bf16[304,128]{1,0:T(8,128)(2,1)} %get-tuple-element.40.y0) | copy-start | bytes 233476
  7.8 4.4 %copy-start.4 = (bf16[288,128]{1,0:T(8,128)(2,1)S(1)}, bf16[288,128]{1,0:T(8,128)(2,1)}, u32[]{:S(2)}) copy-start(bf16[288,128]{1,0:T(8,128)(2,1)} %get-tuple-element.38.x0) | copy-start | bytes 221188
  7.8 7.8 %copy-start = (bf16[4,512,128]{2,1,0:T(8,128)(2,1)S(1)}, bf16[4,512,128]{2,1,0:T(8,128)(2,1)}, u32[]{:S(2)}) copy-start(bf16[4,512,128]{2,1,0:T(8,128)(2,1)} %get-tuple-element.58.grd.refs_3_) | copy-start | bytes 1572868
  12.3 5.7 %collective-permute-start.2 = (bf16[320,128]{1,0:T(8,128)(2,1)S(1)}, bf16[320,128]{1,0:T(8,128)(2,1)S(1)}, u32[]{:S(2)}, u32[]{:S(2)}) collective-permute-start(bf16[320,128]{1,0:T(8,128)(2,1)S(1)} %get-tuple-element.42), channel_id=1, source_target_pairs={{0,4},{4,0},{8,12},{12,8},{16,20},{20,16},{24,28},{28,24},{1,5},{5... | collective-permute-start | bytes 245768 | tf_op jit(solution)/shard_map/ppermute | solution.py:567
  14.5 3.5 %collective-permute-start.3 = (bf16[352,128]{1,0:T(8,128)(2,1)S(1)}, bf16[352,128]{1,0:T(8,128)(2,1)S(1)}, u32[]{:S(2)}, u32[]{:S(2)}) collective-permute-start(bf16[352,128]{1,0:T(8,128)(2,1)S(1)} %get-tuple-element.43), channel_id=1, source_target_pairs={{0,1},{1,0},{2,3},{3,2},{4,5},{5,4},{6,7},{7,6},{8,9},{9,8},{10,11... | collective-permute-start | bytes 270344 | tf_op jit(solution)/shard_map/ppermute | solution.py:567
  20.0 2.5 %collective-permute-start.4 = (f32[1728,128]{1,0:T(8,128)S(1)}, f32[1728,128]{1,0:T(8,128)S(1)}, u32[]{:S(2)}, u32[]{:S(2)}) collective-permute-start(f32[1728,128]{1,0:T(8,128)S(1)} %get-tuple-element.45), channel_id=1, source_target_pairs={{0,1},{1,0},{2,3},{3,2},{4,5},{5,4},{6,7},{7,6},{8,9},{9,8},{10,11... | collective-permute-start | bytes 2654216 | tf_op jit(solution)/shard_map/ppermute | solution.py:567
  22.8 13.4 %copy-start.2 = (bf16[4,512,128]{2,1,0:T(8,128)(2,1)S(1)}, bf16[4,512,128]{2,1,0:T(8,128)(2,1)}, u32[]{:S(2)}) copy-start(bf16[4,512,128]{2,1,0:T(8,128)(2,1)} %get-tuple-element.49.act.refs_3_) | copy-start | bytes 1572868
  22.9 13.4 %copy-start.6 = (s32[4,27]{1,0:T(4,128)S(1)}, s32[4,27]{1,0:T(4,128)}, u32[]{:S(2)}) copy-start(s32[4,27]{1,0:T(4,128)} %refs_0_.3) | copy-start | bytes 1300
  22.9 13.4 %copy-start.7 = (s32[4,512]{1,0:T(4,128)S(1)}, s32[4,512]{1,0:T(4,128)}, u32[]{:S(2)}) copy-start(s32[4,512]{1,0:T(4,128)} %refs_1_.3) | copy-start | bytes 24580
  22.9 13.4 %copy-start.8 = (bf16[27,128,128]{2,1,0:T(8,128)(2,1)S(1)}, bf16[27,128,128]{2,1,0:T(8,128)(2,1)}, u32[]{:S(2)}) copy-start(bf16[27,128,128]{2,1,0:T(8,128)(2,1)} %param.9) | copy-start | bytes 2654212
  23.7 19.6 %all-to-all-start = ((f16[16,112,128]{2,1,0:T(8,128)(2,1)}), f16[16,112,128]{2,1,0:T(8,128)(2,1)S(1)}, u32[]{:S(2)}, u32[]{:S(2)}) async-start(f16[16,112,128]{2,1,0:T(8,128)(2,1)} %convert_element_type.15), calls=%async_computation | async-start | bytes 917504 | tf_op jit(solution)/shard_map/all_to_all | solution.py:586
  31.4 4.8 %collective-permute-start.5 = (bf16[32,128]{1,0:T(8,128)(2,1)S(1)}, bf16[32,128]{1,0:T(8,128)(2,1)S(1)}, u32[]{:S(2)}, u32[]{:S(2)}) collective-permute-start(bf16[32,128]{1,0:T(8,128)(2,1)S(1)} %get-tuple-element.51), channel_id=1, source_target_pairs={{0,1},{1,0},{2,3},{3,2},{4,5},{5,4},{6,7},{7,6},{8,9},{9,8},{10,11... | collective-permute-start | bytes 24584 | tf_op jit(solution)/shard_map/ppermute | solution.py:567
  31.5 4.8 %collective-permute-start.6 = (bf16[32,128]{1,0:T(8,128)(2,1)S(1)}, bf16[32,128]{1,0:T(8,128)(2,1)S(1)}, u32[]{:S(2)}, u32[]{:S(2)}) collective-permute-start(bf16[32,128]{1,0:T(8,128)(2,1)S(1)} %get-tuple-element.52), channel_id=1, source_target_pairs={{1,2},{2,1},{5,6},{6,5},{9,10},{10,9},{13,14},{14,13},{17,18},{18,... | collective-permute-start | bytes 24584 | tf_op jit(solution)/shard_map/ppermute | solution.py:567
  32.2 10.1 %collective-permute-start.7 = (bf16[256,128]{1,0:T(8,128)(2,1)S(1)}, bf16[256,128]{1,0:T(8,128)(2,1)S(1)}, u32[]{:S(2)}, u32[]{:S(2)}) collective-permute-start(bf16[256,128]{1,0:T(8,128)(2,1)S(1)} %get-tuple-element.53), channel_id=1, source_target_pairs={{0,4},{4,0},{8,12},{12,8},{16,20},{20,16},{24,28},{28,24},{1,5},{5... | collective-permute-start | bytes 196616 | tf_op jit(solution)/shard_map/ppermute | solution.py:567
  33.7 8.6 %collective-permute-start.8 = (bf16[256,128]{1,0:T(8,128)(2,1)S(1)}, bf16[256,128]{1,0:T(8,128)(2,1)S(1)}, u32[]{:S(2)}, u32[]{:S(2)}) collective-permute-start(bf16[256,128]{1,0:T(8,128)(2,1)S(1)} %get-tuple-element.54), channel_id=1, source_target_pairs={{0,1},{1,0},{2,3},{3,2},{4,5},{5,4},{6,7},{7,6},{8,9},{9,8},{10,11... | collective-permute-start | bytes 196616 | tf_op jit(solution)/shard_map/ppermute | solution.py:567
  44.5 17.3 %all-to-all-start.1 = ((f16[16,112,128]{2,1,0:T(8,128)(2,1)}), f16[16,112,128]{2,1,0:T(8,128)(2,1)S(1)}, u32[]{:S(2)}, u32[]{:S(2)}) async-start(f16[16,112,128]{2,1,0:T(8,128)(2,1)} %convert_element_type.17), calls=%async_computation.1 | async-start | bytes 917504 | tf_op jit(solution)/shard_map/all_to_all | solution.py:586
  61.8 1.8 %collective-permute-start.9 = (f16[16,112,128]{2,1,0:T(8,128)(2,1)S(1)}, f16[16,112,128]{2,1,0:T(8,128)(2,1)S(1)}, u32[]{:S(2)}, u32[]{:S(2)}) collective-permute-start(f16[16,112,128]{2,1,0:T(8,128)(2,1)S(1)} %all-to-all-done.1), channel_id=1, source_target_pairs={{0,1},{1,0},{2,3},{3,2},{4,5},{5,4},{6,7},{7,6},{8,9},{9,8},{10,11... | collective-permute-start | bytes 1376264 | tf_op jit(solution)/shard_map/ppermute | solution.py:567

commit v7 on v6

--- a/solution.py
+++ b/solution.py
@@ -20,6 +20,8 @@
 HALF = ROWS // 2
 VMEM_LIMIT = 32 * 1024 * 1024
 PACK_LIMIT = 60 * 1024 * 1024
+ROOM_BRICKS = 48
+ROOM_TABLES = 12 * 1024
 
 
 def vmem():
@@ -64,23 +66,29 @@
     return up, jnp.where(same, cells, 0.0), down
 
 
-def pack_kernel(face_hbm, edge_hbm, near_hbm, feat_hbm, grad_hbm, mask_hbm, act_ref, grd_ref, *refs):
+def pack_kernel(face_hbm, edge_hbm, near_hbm, feat_hbm, grad_hbm, mask_hbm, act_out, grd_out, near_out, *refs):
     y_out, x_out = refs[0:2], refs[2:4]
     face_ref, edge_ref, near, raw, mask_ref, full, sems = refs[4:]
-    fetched(
+    got_mask, got_feat, got_grad, *tables = fetching(
         (mask_hbm, mask_ref, sems.at[0]),
         (feat_hbm, raw.at[0], sems.at[1]),
         (grad_hbm, raw.at[1], sems.at[2]),
         (face_hbm, face_ref, sems.at[3]),
         (edge_hbm, edge_ref, sems.at[4]),
         (near_hbm, near, sems.at[5]),
+        (near_hbm, near_out.at[0], sems.at[6]),
     )
-    for s in range(SLOTS):
-        rows = mask_columns(mask_ref, s)
-        for f, dst in enumerate((act_ref, grd_ref)):
-            masked = raw[f, s].astype(jnp.float32) * rows
+    got_mask.wait()
+    results = []
+    for f, got in enumerate((got_feat, got_grad)):
+        got.wait()
+        for s in range(SLOTS):
+            masked = raw[f, s].astype(jnp.float32) * mask_columns(mask_ref, s)
             full[f, s] = masked.reshape(8, 8, 8, C)
-            dst[s] = masked.astype(jnp.bfloat16)
+            raw[f, s] = masked.astype(jnp.bfloat16)
+        results += fetching((raw.at[f], (act_out.at[0], grd_out)[f], sems.at[7 + f]))
+    for table in tables:
+        table.wait()
     for axis, outs in enumerate((x_out, y_out)):
         odd = parity("gy" if axis else "gx")
         for k in range(2):
@@ -115,16 +123,24 @@
                 lines += [down, same, up]
             lines = jnp.concatenate(lines, axis=0).astype(jnp.bfloat16)
             outs[k][pl.ds(FACE_ROWS, lines.shape[0])] = lines
+    for result in results:
+        result.wait()
 
 
 def pack(features, out_grad, mask, near, face_sends, edge_sends):
-    sends = [jax.ShapeDtypeStruct((rows, C), jnp.bfloat16) for rows in 2 * (Y_ROWS + FACE_ROWS,) + 2 * (X_ROWS + FACE_ROWS,)]
-    brick = jax.ShapeDtypeStruct((SLOTS, 512, C), jnp.bfloat16)
+    sends = [
+        jax.ShapeDtypeStruct((rows + FACE_ROWS, C), jnp.bfloat16) for rows in (Y_ROWS, Y_ROWS, X_ROWS, X_ROWS)
+    ]
     return pl.pallas_call(
         pack_kernel,
-        out_shape=[brick, brick] + sends,
+        out_shape=[
+            jax.ShapeDtypeStruct((ROOM_BRICKS, SLOTS, 512, C), jnp.bfloat16),
+            jax.ShapeDtypeStruct((SLOTS, 512, C), jnp.bfloat16),
+            jax.ShapeDtypeStruct((ROOM_TABLES, SLOTS, 27), jnp.int32),
+        ]
+        + sends,
         in_specs=[hbm()] * 6,
-        out_specs=[vmem()] * 6,
+        out_specs=[hbm()] * 3 + [vmem()] * 4,
         scratch_shapes=[
             pltpu.SMEM((FACE, 4), jnp.int32),
             pltpu.SMEM((1, 4), jnp.int32),
@@ -132,7 +148,7 @@
             pltpu.VMEM((2, SLOTS, 512, C), jnp.bfloat16),
             pltpu.VMEM((SLOTS, 512), jnp.int32),
             pltpu.VMEM((2, SLOTS, 8, 8, 8, C), jnp.float32),
-            pltpu.SemaphoreType.DMA((6,)),
+            pltpu.SemaphoreType.DMA((9,)),
         ],
         compiler_params=pltpu.CompilerParams(vmem_limit_bytes=PACK_LIMIT),
         name="pack",
@@ -288,10 +304,11 @@
     ]
 
 
-def columns_kernel(near_hbm, act, v, lx, ly, corners, wide, near, sem):
-    (table,) = fetching((near_hbm, near, sem))
+def columns_kernel(near_hbm, act_hbm, v, lx, ly, corners, wide, near, sem, act, act_sem):
+    table, bricks = fetching((near_hbm.at[0], near, sem), (act_hbm.at[0], act, act_sem))
+    fill_zero(lx, ly, corners, SLOTS)
+    bricks.wait()
     fill_own(act, lx, ly, corners)
-    fill_zero(lx, ly, corners, SLOTS)
     table.wait()
 
     def per_slot(s, carry):
@@ -306,9 +323,10 @@
     return pl.pallas_call(
         columns_kernel,
         out_shape=jax.ShapeDtypeStruct((SLOTS, 10, 64, 9 * C), jnp.bfloat16),
-        in_specs=[hbm(), vmem()],
+        in_specs=[hbm()] * 2,
         out_specs=vmem(),
-        scratch_shapes=columns_scratch(),
+        scratch_shapes=columns_scratch()
+        + [pltpu.VMEM((SLOTS, 512, C), jnp.bfloat16), pltpu.SemaphoreType.DMA(())],
         compiler_params=pltpu.CompilerParams(vmem_limit_bytes=VMEM_LIMIT),
         cost_estimate=pl.CostEstimate(flops=1 << 24, bytes_accessed=6 << 20, transcendentals=0),
         name="own_columns",
@@ -321,15 +339,13 @@
             turned[:, pl.ds((4 * s + q) * C, C)] = grd[s, pl.ds(q * C, C)].T
     for x in range(3):
         cells = v[:, pl.ds(x, 8)].reshape(SLOTS * 512, 9 * C)
-        terms = jnp.dot(turned[...], cells, preferred_element_type=jnp.float32)
-        for j in range(9):
-            out[pl.ds((9 * x + j) * C, C)] = terms[:, j * C : (j + 1) * C].T
+        out[x] = jnp.dot(turned[...], cells, preferred_element_type=jnp.float32)
 
 
 def inner_terms(v, grd):
     return pl.pallas_call(
         inner_kernel,
-        out_shape=jax.ShapeDtypeStruct((ROWS, C), jnp.float32),
+        out_shape=jax.ShapeDtypeStruct((3, C, 9 * C), jnp.float32),
         in_specs=[vmem()] * 2,
         out_specs=vmem(),
         scratch_shapes=[pltpu.VMEM((C, SLOTS * 512), jnp.bfloat16)],
@@ -369,30 +385,31 @@
     grads = grd[...]
     lines = grads.astype(jnp.float32).reshape(SLOTS, 8, 8, 8, C)
 
-    def term(cells, rows):
-        return lax.dot_general(cells, rows, (((0,), (0,)), ((), ())), preferred_element_type=jnp.float32)
+    def term(rows, cells):
+        return lax.dot_general(rows, cells, (((0,), (0,)), ((), ())), preferred_element_type=jnp.float32)
 
     def end(line):
         return jnp.concatenate([line, jnp.zeros((8, C), jnp.float32)], axis=0).astype(jnp.bfloat16)
 
     for side in range(2):
         rows = grads[:, 448 * side : 448 * side + 64].reshape(SLOTS * 64, C)
-        side_x[side] = term(vx[side], rows)
+        side_x[side] = term(rows, vx[side])
         rows = lines[:, :, 7 * side].reshape(SLOTS * 64, C).astype(jnp.bfloat16)
-        side_y[side] = term(vy[side], rows)
+        side_y[side] = term(rows, vy[side])
     def write(halves):
         for x in range(3):
             for y in range(3):
                 for z in range(3):
                     first = (9 * x + 3 * y + z) * C
-                    value = inner[pl.ds(first, C)]
+                    value = inner[x, :, pl.ds((3 * y + z) * C, C)]
                     if x != 1:
-                        value += side_x[x // 2, pl.ds((3 * y + z) * C, C)]
+                        value += side_x[x // 2, :, pl.ds((3 * y + z) * C, C)]
                     if y != 1:
-                        value += side_y[y // 2, pl.ds((3 * x + z) * C, C)]
+                        value += side_y[y // 2, :, pl.ds((3 * x + z) * C, C)]
                     if x != 1 and y != 1:
                         sx, sy = x // 2, 1 - y // 2
-                        value += term(end(ends_a[sx, sy]), end(ends_g[sy, sx, z]))
+                        value += term(end(ends_g[sy, sx, z]), end(ends_a[sx, sy]))
+                    value = value.T
                     for half in range(2):
                         low = max(first, half * HALF)
                         rows = min(first + C, (half + 1) * HALF) - low
@@ -424,8 +441,8 @@
             side,
             pltpu.VMEM((2, 2, 8, C), jnp.float32),
             pltpu.VMEM((2, 2, 3, 8, C), jnp.float32),
-            pltpu.VMEM((2, 9 * C, C), jnp.float32),
-            pltpu.VMEM((2, 9 * C, C), jnp.float32),
+            pltpu.VMEM((2, C, 9 * C), jnp.float32),
+            pltpu.VMEM((2, C, 9 * C), jnp.float32),
         ],
         compiler_params=pltpu.CompilerParams(vmem_limit_bytes=VMEM_LIMIT),
         cost_estimate=pl.CostEstimate(flops=2 * 256 * 36 * C * C, bytes_accessed=6 << 20, transcendentals=0),
@@ -521,11 +538,14 @@
 
 
 def product_kernel(f, near_hbm, mask_ref, kernel_ref, bricks, x_ref, y_ref, e0, e1, out, *refs):
-    lx, ly, corners, wide, near, sem, v, *flipped = refs
+    lx, ly, corners, wide, near, sem, v, *more = refs
     (table,) = fetching((near_hbm, near, sem))
     weights = kernel_ref
-    if f == 1:
-        weights = flipped[0]
+    if f == 0:
+        fetched((bricks.at[0], more[0], more[1]))
+        bricks = more[0]
+    else:
+        weights = more[0]
         for o in range(27):
             weights[pl.ds((26 - o) * C, C)] = kernel_ref[pl.ds(o * C, C)].T
     fill_own(bricks, lx, ly, corners)
@@ -549,11 +569,15 @@
     return pl.pallas_call(
         lambda *refs: product_kernel(f, *refs),
         out_shape=jax.ShapeDtypeStruct((SLOTS, 512, C), jnp.bfloat16),
-        in_specs=[hbm()] + [vmem()] * 7,
+        in_specs=[hbm()] + [vmem()] * 2 + [vmem() if f else hbm()] + [vmem()] * 4,
         out_specs=vmem(),
         scratch_shapes=columns_scratch()
         + [pltpu.VMEM((SLOTS, 10, 64, 9 * C), jnp.bfloat16)]
-        + ([pltpu.VMEM((ROWS, C), jnp.bfloat16)] if f else []),
+        + (
+            [pltpu.VMEM((ROWS, C), jnp.bfloat16)]
+            if f
+            else [pltpu.VMEM((SLOTS, 512, C), jnp.bfloat16), pltpu.SemaphoreType.DMA(())]
+        ),
         compiler_params=pltpu.CompilerParams(vmem_limit_bytes=VMEM_LIMIT),
         cost_estimate=pl.CostEstimate(flops=2 * 2048 * ROWS * C, bytes_accessed=4 << 20, transcendentals=0),
         name=("output_product", "input_grad_product")[f],
@@ -585,7 +609,7 @@
     def spread(blocks):
         return lax.all_to_all(blocks, ("gx", "gy"), 0, 0, axis_index_groups=same_core, tiled=True)
 
-    act, grd, y0, y1, x0, x1 = pack(
+    act, grd, table, y0, y1, x0, x1 = pack(
         features.reshape(SLOTS, 512, C),
         out_grad.reshape(SLOTS, 512, C),
         voxel_mask,
@@ -594,7 +618,7 @@
         edge_sends,
     )
     x1, y1 = hopped(x1, "gx"), hopped(y1, "gy")
-    v = own_columns(neighbours, act)
+    v = own_columns(table, act)
     x1, y1, v = lax.optimization_barrier((x1, y1, v))
     x_came, y_came, x_more, y_more = join(x0, x1, y0, y1)
     x_came, y_came = swapped(x_came, "gx", 0), swapped(y_came, "gy", 0)

time: 65.1 us -> 66.9 us (1.028)
  Pallas kernels: 23.3 us -> 25.6 us
  local copies, waits for them, and re-layouts: 1.75 us -> 0.03 us
  waiting for transfers between devices: 12.9 us -> 14.1 us
    unnamed x18 -> x12, local copies, waits for them, and re-layouts: 1.75 us -> 0.03 us
    ppermute x2, waiting for transfers between devices: 2.99 us -> 4.08 us  [hopped(): return lax.ppermute(value, axis, pairs)]
    ppermute x8, starting transfers between devices: 8.28 us -> 7.3 us  [swapped(): return lax.ppermute(value, axis, pairs)]
    all_to_all x2, starting transfers between devices: 13.2 us -> 14.1 us  [spread(): lax.all_to_all(blocks, ('gx', 'gy'), 0, 0, axis_index_groups=same_core, t...]
    ppermute x8, waiting for transfers between devices: 3.18 us -> 3.88 us  [swapped(): return lax.ppermute(value, axis, pairs)]
  transfers between devices with their start and end apart: 12 -> 12, of which waited for: 5 -> 6; matrix products, arithmetic and copies ran while one was open for 0% -> 0% of each run, Pallas kernels for 26% -> 27%
where the time goes in v7:
time: 66.9 us; the launch traced here: 66.4 us
  Pallas kernels  25.6 us (38%)
  starting transfers between devices  24 us (36%)
  waiting for transfers between devices  14.1 us (21%)
  other arithmetic  1.84 us (3%)
  between operations  0.83 us (1%)
    all_to_all x2, starting transfers between devices, spread(): lax.all_to_all(blocks, ('gx', 'gy'), 0, 0, axis_index_groups=same_core, t...  14.1 us
    pallas_call x2, Pallas kernels, product(): pl.pallas_call(lambda *refs: product_kernel(f, *refs), out_shape=jax.Shap...  12.6 us
    ppermute x8, starting transfers between devices, swapped(): return lax.ppermute(value, axis, pairs)  7.3 us
    all_to_all x2, waiting for transfers between devices, spread(): lax.all_to_all(blocks, ('gx', 'gy'), 0, 0, axis_index_groups=same_core, t...  6.18 us
    ppermute x2, waiting for transfers between devices, hopped(): return lax.ppermute(value, axis, pairs)  4.08 us
    ppermute x8, waiting for transfers between devices, swapped(): return lax.ppermute(value, axis, pairs)  3.88 us
    pallas_call x1, Pallas kernels, pack(): pl.pallas_call(pack_kernel, out_shape=[jax.ShapeDtypeStruct((ROOM_BRICKS,...  3.56 us
    ppermute x2, starting transfers between devices, hopped(): return lax.ppermute(value, axis, pairs)  2.58 us
  transfers between devices with their start and end apart: 12, of which 6 were waited for; matrix products, arithmetic and copies ran while one was open for 0% of the time, Pallas kernels for 27%

profile of v7, /device:TPU:0, one launch (start us, length us, event | category | flops | bytes accessed | tf_op | source)
XLA Modules:
  0.0 66.4 jit_solution(11085689265455418570)
XLA Ops:
  0.6 3.6 %pack.1 = (bf16[48,4,512,128]{3,2,1,0:T(8,128)(2,1)}, bf16[4,512,128]{2,1,0:T(8,128)(2,1)}, s32[12288,4,27]{2,1,0:T(4,128)}, bf16[304,128]{1,0:T(8,128)(2,1)}, b...) custom-call(s32[2,4]{1,0:T(2,128)} %bitcast.14, s32[1,4]{1,0:T(1,128)} %bitcast.15, ...), custom_call_target="tpu_custom_call" | custom-call | tf_op jit(solution)/shard_map/pack/pallas_call | solution.py:134
  4.2 1.3 %collective-permute-start.1 = (bf16[304,128]{1,0:T(8,128)(2,1)}, bf16[304,128]{1,0:T(8,128)(2,1)S(1)}, u32[]{:S(2)}, u32[]{:S(2)}) collective-permute-start(bf16[304,128]{1,0:T(8,128)(2,1)} %get-tuple-element.35), channel_id=1, source_target_pairs={{1,3},{2,0},{5,7},{6,4},{9,11},{10,8},{13,15},{14,12},{17,19},{18,... | collective-permute-start | bytes 233480 | tf_op jit(solution)/shard_map/ppermute | solution.py:597
  5.5 1.3 %collective-permute-start = (bf16[288,128]{1,0:T(8,128)(2,1)}, bf16[288,128]{1,0:T(8,128)(2,1)S(1)}, u32[]{:S(2)}, u32[]{:S(2)}) collective-permute-start(bf16[288,128]{1,0:T(8,128)(2,1)} %get-tuple-element.34), channel_id=1, source_target_pairs={{4,12},{12,20},{20,28},{8,0},{16,8},{24,16},{5,13},{13,21},{21,29}... | collective-permute-start | bytes 221192 | tf_op jit(solution)/shard_map/ppermute | solution.py:597
  6.8 0.0 copy-start.2
  6.8 0.0 copy-start.3
  6.8 0.0 copy-start
  6.8 2.0 %own_columns.1.v = bf16[4,10,64,1152]{3,2,1,0:T(8,128)(2,1)S(1)} custom-call(s32[12288,4,27]{2,1,0:T(4,128)} %get-tuple-element.36.near_hbm, bf16[48,4,512,128]{3,2,1,0:T(8,128)(2,1)} %get-tuple-element.51.act_hbm.refs_3_), custom_call_target="tpu_custom_call" | custom-call | flops 16777216 | bytes 6291456 | tf_op jit(solution)/shard_map/own_columns/pallas_call | solution.py:323
  8.9 0.0 copy-start.5
  8.9 4.1 %collective-permute-done.x1 = bf16[288,128]{1,0:T(8,128)(2,1)S(1)} collective-permute-done((bf16[288,128]{1,0:T(8,128)(2,1)}, bf16[288,128]{1,0:T(8,128)(2,1)S(1)}, u32[]{:S(2)}, u32[]{:S(2)}) %collective-permute-start) | collective-permute-done | bytes 73760 | tf_op jit(solution)/shard_map/ppermute | solution.py:597
  13.0 0.0 collective-permute-done.1.y1
  13.0 0.0 copy-done.2
  13.0 0.0 copy-done.3
  13.0 1.3 %collective-permute-start.2 = (bf16[320,128]{1,0:T(8,128)(2,1)S(1)}, bf16[320,128]{1,0:T(8,128)(2,1)S(1)}, u32[]{:S(2)}, u32[]{:S(2)}) collective-permute-start(bf16[320,128]{1,0:T(8,128)(2,1)S(1)} %get-tuple-element.44), channel_id=1, source_target_pairs={{0,4},{4,0},{8,12},{12,8},{16,20},{20,16},{24,28},{28,24},{1,5},{5... | collective-permute-start | bytes 245768 | tf_op jit(solution)/shard_map/ppermute | solution.py:591
  14.3 1.0 %collective-permute-start.3 = (bf16[352,128]{1,0:T(8,128)(2,1)S(1)}, bf16[352,128]{1,0:T(8,128)(2,1)S(1)}, u32[]{:S(2)}, u32[]{:S(2)}) collective-permute-start(bf16[352,128]{1,0:T(8,128)(2,1)S(1)} %get-tuple-element.45), channel_id=1, source_target_pairs={{0,1},{1,0},{2,3},{3,2},{4,5},{5,4},{6,7},{7,6},{8,9},{9,8},{10,11... | collective-permute-start | bytes 270344 | tf_op jit(solution)/shard_map/ppermute | solution.py:591
  15.3 0.0 copy-done
  15.3 0.0 copy-start.1
  15.3 0.0 copy-start.4
  15.3 2.3 %inner_terms.1.inner = f32[3,128,1152]{2,1,0:T(8,128)S(1)} custom-call(bf16[4,10,64,1152]{3,2,1,0:T(8,128)(2,1)S(1)} %own_columns.1.v, bf16[4,512,128]{2,1,0:T(8,128)(2,1)S(1)} %copy-done), custom_call_target="tpu_custom_call" | custom-call | flops 1811939328 | bytes 6291456 | tf_op jit(solution)/shard_map/inner_terms/pallas_call | solution.py:346
  17.6 0.8 %collective-permute-done.2.x_ref.x_came.refs_4_ = bf16[320,128]{1,0:T(8,128)(2,1)S(1)} collective-permute-done((bf16[320,128]{1,0:T(8,128)(2,1)S(1)}, bf16[320,128]{1,0:T(8,128)(2,1)S(1)}, u32[]{:S(2)}, u32[]{:S(2)}) %collective-permute-start.2) | collective-permute-done | bytes 81952 | tf_op jit(solution)/shard_map/ppermute | solution.py:591
  18.4 0.0 collective-permute-done.3.y_ref.refs_5_
  18.4 0.0 copy-done.5
  18.4 2.5 %rim_terms.1 = (f32[1728,128]{1,0:T(8,128)S(1)}, f32[1728,128]{1,0:T(8,128)S(1)}) custom-call(s32[4,27]{1,0:T(4,128)S(1)} %copy-done.5, f32[3,128,1152]{2,1,0:T(8,128)S(1)} %inner_terms.1.inner, bf16[4,512,128]{2,1,0:T(8,128)(2,1)S(1)} %copy-done, bf16[320,128]{1,0:T(8,128)(2,1)S(1)} %collective-permute-done.2.x_ref.x_came.refs_4_, ...), custom_call_target="tpu_custom_call" | custom-call | flops 301989888 | bytes 6291456 | tf_op jit(solution)/shard_map/rim_terms/pallas_call | solution.py:433
  20.9 0.2 collective-permute-start.4
  21.2 2.3 %collective-permute-done.4.refs_1_ = f32[1728,128]{1,0:T(8,128)S(1)} collective-permute-done((f32[1728,128]{1,0:T(8,128)S(1)}, f32[1728,128]{1,0:T(8,128)S(1)}, u32[]{:S(2)}, u32[]{:S(2)}) %collective-permute-start.4) | collective-permute-done | bytes 884768 | tf_op jit(solution)/shard_map/ppermute | solution.py:591
  23.4 0.3 merge.1
  23.8 0.8 %convert_element_type.15 = f16[16,112,128]{2,1,0:T(8,128)(2,1)} convert(f32[16,112,128]{2,1,0:T(8,128)S(1)} %merge.1) | non-fusion elementwise | flops 229376 | bytes 1376256 | tf_op jit(solution)/shard_map/convert_element_type | solution.py:627
  24.6 8.0 %all-to-all-start = ((f16[16,112,128]{2,1,0:T(8,128)(2,1)}), f16[16,112,128]{2,1,0:T(8,128)(2,1)S(1)}, u32[]{:S(2)}, u32[]{:S(2)}) async-start(f16[16,112,128]{2,1,0:T(8,128)(2,1)} %convert_element_type.15), calls=%async_computation | async-start | bytes 917504 | tf_op jit(solution)/shard_map/all_to_all | solution.py:610
  32.7 0.1 collective-permute-start.5
  32.7 0.7 collective-permute-start.6
  33.4 1.5 %collective-permute-start.7 = (bf16[256,128]{1,0:T(8,128)(2,1)S(1)}, bf16[256,128]{1,0:T(8,128)(2,1)S(1)}, u32[]{:S(2)}, u32[]{:S(2)}) collective-permute-start(bf16[256,128]{1,0:T(8,128)(2,1)S(1)} %get-tuple-element.55), channel_id=1, source_target_pairs={{0,4},{4,0},{8,12},{12,8},{16,20},{20,16},{24,28},{28,24},{1,5},{5... | collective-permute-start | bytes 196616 | tf_op jit(solution)/shard_map/ppermute | solution.py:591
  34.9 2.5 %collective-permute-start.8 = (bf16[256,128]{1,0:T(8,128)(2,1)S(1)}, bf16[256,128]{1,0:T(8,128)(2,1)S(1)}, u32[]{:S(2)}, u32[]{:S(2)}) collective-permute-start(bf16[256,128]{1,0:T(8,128)(2,1)S(1)} %get-tuple-element.56), channel_id=1, source_target_pairs={{0,1},{1,0},{2,3},{3,2},{4,5},{5,4},{6,7},{7,6},{8,9},{9,8},{10,11... | collective-permute-start | bytes 196616 | tf_op jit(solution)/shard_map/ppermute | solution.py:591
  37.5 0.0 collective-permute-done.5.refs_6_
  37.5 0.0 collective-permute-done.6.refs_7_
  37.5 0.0 copy-done.1
  37.5 0.0 copy-done.4
  37.5 6.5 %output_product.1 = bf16[4,512,128]{2,1,0:T(8,128)(2,1)} custom-call(s32[4,27]{1,0:T(4,128)S(1)} %copy-done.5, s32[4,512]{1,0:T(4,128)S(1)} %copy-done.4, bf16[3456,128]{1,0:T(8,128)(2,1)S(1)} %bitcast.8, bf16[48,4,512,128]{3,2,1,0:T(8,128)(2,1)} %get-tuple-element.51.act_hbm.refs_3_, bf16[320,128]{1,0:T(8,128)(2,1)S(1)} %collective-permute-done.2.x_ref.x_came.refs_4_, ...), custom_call_target="tpu_custom_call" | custom-call | flops 1811939328 | bytes 4194304 | tf_op jit(solution)/shard_map/output_product/pallas_call | solution.py:569
  44.0 0.0 collective-permute-done.7.refs_4_
  44.1 0.0 collective-permute-done.8.refs_5_
  44.1 0.5 all-to-all-done
  44.5 0.1 convert_element_type.16.refs_0_
  44.6 0.3 sum_blocks.1
  44.9 0.8 %convert_element_type.17 = f16[16,112,128]{2,1,0:T(8,128)(2,1)} convert(f32[16,112,128]{2,1,0:T(8,128)S(1)} %sum_blocks.1) | non-fusion elementwise | flops 229376 | bytes 1376256 | tf_op jit(solution)/shard_map/convert_element_type | solution.py:635
  45.7 6.0 %all-to-all-start.1 = ((f16[16,112,128]{2,1,0:T(8,128)(2,1)}), f16[16,112,128]{2,1,0:T(8,128)(2,1)S(1)}, u32[]{:S(2)}, u32[]{:S(2)}) async-start(f16[16,112,128]{2,1,0:T(8,128)(2,1)} %convert_element_type.17), calls=%async_computation.1 | async-start | bytes 917504 | tf_op jit(solution)/shard_map/all_to_all | solution.py:610
  51.8 6.1 %input_grad_product.1 = bf16[4,512,128]{2,1,0:T(8,128)(2,1)} custom-call(s32[4,27]{1,0:T(4,128)S(1)} %copy-done.5, s32[4,512]{1,0:T(4,128)S(1)} %copy-done.4, bf16[3456,128]{1,0:T(8,128)(2,1)S(1)} %bitcast.9, bf16[4,512,128]{2,1,0:T(8,128)(2,1)S(1)} %copy-done, bf16[256,128]{1,0:T(8,128)(2,1)S(1)} %collective-permute-done.7.refs_4_, ...), custom_call_target="tpu_custom_call" | custom-call | flops 1811939328 | bytes 4194304 | tf_op jit(solution)/shard_map/input_grad_product/pallas_call | solution.py:569
  57.8 5.7 %all-to-all-done.1 = f16[16,112,128]{2,1,0:T(8,128)(2,1)S(1)} async-done(((f16[16,112,128]{2,1,0:T(8,128)(2,1)}), f16[16,112,128]{2,1,0:T(8,128)(2,1)S(1)}, u32[]{:S(2)}, u32[]{:S(2)}) %all-to-all-start.1) | async-done | bytes 458784 | tf_op jit(solution)/shard_map/all_to_all | solution.py:610
  63.5 0.0 collective-permute-start.9
  63.5 0.1 convert_element_type.19.refs_0_
  63.6 1.0 %decode_own.1.refs_1_ = f32[2,1728,128]{2,1,0:T(8,128)} custom-call(f32[16,112,128]{2,1,0:T(8,128)S(1)} %convert_element_type.19.refs_0_), custom_call_target="tpu_custom_call" | custom-call | tf_op jit(solution)/shard_map/decode_own/pallas_call | solution.py:528
  64.6 0.8 %collective-permute-done.9 = f16[16,112,128]{2,1,0:T(8,128)(2,1)S(1)} collective-permute-done((f16[16,112,128]{2,1,0:T(8,128)(2,1)S(1)}, f16[16,112,128]{2,1,0:T(8,128)(2,1)S(1)}, u32[]{:S(2)}, u32[]{:S(2)}) %collective-permute-start.9) | collective-permute-done | bytes 458784 | tf_op jit(solution)/shard_map/ppermute | solution.py:591
  65.4 0.1 convert_element_type.18.refs_0_
  65.4 1.0 %decode_other.1 = f32[2,1728,128]{2,1,0:T(8,128)} custom-call(f32[16,112,128]{2,1,0:T(8,128)S(1)} %convert_element_type.18.refs_0_, f32[2,1728,128]{2,1,0:T(8,128)} %decode_own.1.refs_1_), custom_call_target="tpu_custom_call", output_to_operand_aliasing={{}: (1, {})} | custom-call | tf_op jit(solution)/shard_map/decode_other/pallas_call | solution.py:528
  (2 shorter events, 0.0 us)
Async XLA Ops:
  4.2 8.8 %collective-permute-start.1 = (bf16[304,128]{1,0:T(8,128)(2,1)}, bf16[304,128]{1,0:T(8,128)(2,1)S(1)}, u32[]{:S(2)}, u32[]{:S(2)}) collective-permute-start(bf16[304,128]{1,0:T(8,128)(2,1)} %get-tuple-element.35), channel_id=1, source_target_pairs={{1,3},{2,0},{5,7},{6,4},{9,11},{10,8},{13,15},{14,12},{17,19},{18,... | collective-permute-start | bytes 233480 | tf_op jit(solution)/shard_map/ppermute | solution.py:597
  5.5 7.5 %collective-permute-start = (bf16[288,128]{1,0:T(8,128)(2,1)}, bf16[288,128]{1,0:T(8,128)(2,1)S(1)}, u32[]{:S(2)}, u32[]{:S(2)}) collective-permute-start(bf16[288,128]{1,0:T(8,128)(2,1)} %get-tuple-element.34), channel_id=1, source_target_pairs={{4,12},{12,20},{20,28},{8,0},{16,8},{24,16},{5,13},{13,21},{21,29}... | collective-permute-start | bytes 221192 | tf_op jit(solution)/shard_map/ppermute | solution.py:597
  6.8 6.2 %copy-start.2 = (bf16[304,128]{1,0:T(8,128)(2,1)S(1)}, bf16[304,128]{1,0:T(8,128)(2,1)}, u32[]{:S(2)}) copy-start(bf16[304,128]{1,0:T(8,128)(2,1)} %get-tuple-element.42.y0) | copy-start | bytes 233476
  6.8 6.2 %copy-start.3 = (bf16[288,128]{1,0:T(8,128)(2,1)S(1)}, bf16[288,128]{1,0:T(8,128)(2,1)}, u32[]{:S(2)}) copy-start(bf16[288,128]{1,0:T(8,128)(2,1)} %get-tuple-element.40.x0) | copy-start | bytes 221188
  6.8 8.5 %copy-start = (bf16[4,512,128]{2,1,0:T(8,128)(2,1)S(1)}, bf16[4,512,128]{2,1,0:T(8,128)(2,1)}, u32[]{:S(2)}) copy-start(bf16[4,512,128]{2,1,0:T(8,128)(2,1)} %get-tuple-element.60.grd.refs_3_) | copy-start | bytes 1572868
  8.9 9.5 %copy-start.5 = (s32[4,27]{1,0:T(4,128)S(1)}, s32[4,27]{1,0:T(4,128)}, u32[]{:S(2)}) copy-start(s32[4,27]{1,0:T(4,128)} %refs_0_.3) | copy-start | bytes 1300
  13.0 5.4 %collective-permute-start.2 = (bf16[320,128]{1,0:T(8,128)(2,1)S(1)}, bf16[320,128]{1,0:T(8,128)(2,1)S(1)}, u32[]{:S(2)}, u32[]{:S(2)}) collective-permute-start(bf16[320,128]{1,0:T(8,128)(2,1)S(1)} %get-tuple-element.44), channel_id=1, source_target_pairs={{0,4},{4,0},{8,12},{12,8},{16,20},{20,16},{24,28},{28,24},{1,5},{5... | collective-permute-start | bytes 245768 | tf_op jit(solution)/shard_map/ppermute | solution.py:591
  14.3 4.1 %collective-permute-start.3 = (bf16[352,128]{1,0:T(8,128)(2,1)S(1)}, bf16[352,128]{1,0:T(8,128)(2,1)S(1)}, u32[]{:S(2)}, u32[]{:S(2)}) collective-permute-start(bf16[352,128]{1,0:T(8,128)(2,1)S(1)} %get-tuple-element.45), channel_id=1, source_target_pairs={{0,1},{1,0},{2,3},{3,2},{4,5},{5,4},{6,7},{7,6},{8,9},{9,8},{10,11... | collective-permute-start | bytes 270344 | tf_op jit(solution)/shard_map/ppermute | solution.py:591
  15.3 22.2 %copy-start.1 = (bf16[27,128,128]{2,1,0:T(8,128)(2,1)S(1)}, bf16[27,128,128]{2,1,0:T(8,128)(2,1)}, u32[]{:S(2)}) copy-start(bf16[27,128,128]{2,1,0:T(8,128)(2,1)} %param.9) | copy-start | bytes 2654212
  15.3 22.2 %copy-start.4 = (s32[4,512]{1,0:T(4,128)S(1)}, s32[4,512]{1,0:T(4,128)}, u32[]{:S(2)}) copy-start(s32[4,512]{1,0:T(4,128)} %refs_1_.3) | copy-start | bytes 24580
  20.9 2.5 %collective-permute-start.4 = (f32[1728,128]{1,0:T(8,128)S(1)}, f32[1728,128]{1,0:T(8,128)S(1)}, u32[]{:S(2)}, u32[]{:S(2)}) collective-permute-start(f32[1728,128]{1,0:T(8,128)S(1)} %get-tuple-element.47), channel_id=1, source_target_pairs={{0,1},{1,0},{2,3},{3,2},{4,5},{5,4},{6,7},{7,6},{8,9},{9,8},{10,11... | collective-permute-start | bytes 2654216 | tf_op jit(solution)/shard_map/ppermute | solution.py:591
  24.6 19.9 %all-to-all-start = ((f16[16,112,128]{2,1,0:T(8,128)(2,1)}), f16[16,112,128]{2,1,0:T(8,128)(2,1)S(1)}, u32[]{:S(2)}, u32[]{:S(2)}) async-start(f16[16,112,128]{2,1,0:T(8,128)(2,1)} %convert_element_type.15), calls=%async_computation | async-start | bytes 917504 | tf_op jit(solution)/shard_map/all_to_all | solution.py:610
  32.7 4.8 %collective-permute-start.5 = (bf16[32,128]{1,0:T(8,128)(2,1)S(1)}, bf16[32,128]{1,0:T(8,128)(2,1)S(1)}, u32[]{:S(2)}, u32[]{:S(2)}) collective-permute-start(bf16[32,128]{1,0:T(8,128)(2,1)S(1)} %get-tuple-element.53), channel_id=1, source_target_pairs={{0,1},{1,0},{2,3},{3,2},{4,5},{5,4},{6,7},{7,6},{8,9},{9,8},{10,11... | collective-permute-start | bytes 24584 | tf_op jit(solution)/shard_map/ppermute | solution.py:591
  32.7 4.8 %collective-permute-start.6 = (bf16[32,128]{1,0:T(8,128)(2,1)S(1)}, bf16[32,128]{1,0:T(8,128)(2,1)S(1)}, u32[]{:S(2)}, u32[]{:S(2)}) collective-permute-start(bf16[32,128]{1,0:T(8,128)(2,1)S(1)} %get-tuple-element.54), channel_id=1, source_target_pairs={{1,2},{2,1},{5,6},{6,5},{9,10},{10,9},{13,14},{14,13},{17,18},{18,... | collective-permute-start | bytes 24584 | tf_op jit(solution)/shard_map/ppermute | solution.py:591
  33.4 10.6 %collective-permute-start.7 = (bf16[256,128]{1,0:T(8,128)(2,1)S(1)}, bf16[256,128]{1,0:T(8,128)(2,1)S(1)}, u32[]{:S(2)}, u32[]{:S(2)}) collective-permute-start(bf16[256,128]{1,0:T(8,128)(2,1)S(1)} %get-tuple-element.55), channel_id=1, source_target_pairs={{0,4},{4,0},{8,12},{12,8},{16,20},{20,16},{24,28},{28,24},{1,5},{5... | collective-permute-start | bytes 196616 | tf_op jit(solution)/shard_map/ppermute | solution.py:591
  34.9 9.1 %collective-permute-start.8 = (bf16[256,128]{1,0:T(8,128)(2,1)S(1)}, bf16[256,128]{1,0:T(8,128)(2,1)S(1)}, u32[]{:S(2)}, u32[]{:S(2)}) collective-permute-start(bf16[256,128]{1,0:T(8,128)(2,1)S(1)} %get-tuple-element.56), channel_id=1, source_target_pairs={{0,1},{1,0},{2,3},{3,2},{4,5},{5,4},{6,7},{7,6},{8,9},{9,8},{10,11... | collective-permute-start | bytes 196616 | tf_op jit(solution)/shard_map/ppermute | solution.py:591
  45.7 17.8 %all-to-all-start.1 = ((f16[16,112,128]{2,1,0:T(8,128)(2,1)}), f16[16,112,128]{2,1,0:T(8,128)(2,1)S(1)}, u32[]{:S(2)}, u32[]{:S(2)}) async-start(f16[16,112,128]{2,1,0:T(8,128)(2,1)} %convert_element_type.17), calls=%async_computation.1 | async-start | bytes 917504 | tf_op jit(solution)/shard_map/all_to_all | solution.py:610
  63.5 1.8 %collective-permute-start.9 = (f16[16,112,128]{2,1,0:T(8,128)(2,1)S(1)}, f16[16,112,128]{2,1,0:T(8,128)(2,1)S(1)}, u32[]{:S(2)}, u32[]{:S(2)}) collective-permute-start(f16[16,112,128]{2,1,0:T(8,128)(2,1)S(1)} %all-to-all-done.1), channel_id=1, source_target_pairs={{0,1},{1,0},{2,3},{3,2},{4,5},{5,4},{6,7},{7,6},{8,9},{9,8},{10,11... | collective-permute-start | bytes 1376264 | tf_op jit(solution)/shard_map/ppermute | solution.py:591

commit v8 on v6

--- a/solution.py
+++ b/solution.py
@@ -18,8 +18,11 @@
 X_ROWS = FACE_ROWS + 32
 Y_ROWS = FACE_ROWS + 48
 HALF = ROWS // 2
+SPARE_ROWS = 32
 VMEM_LIMIT = 32 * 1024 * 1024
 PACK_LIMIT = 60 * 1024 * 1024
+ROOM_BRICKS = 48
+ROOM_TABLES = 12 * 1024
 
 
 def vmem():
@@ -43,8 +46,8 @@
 
 
 def mask_columns(mask_ref, s):
-    m = mask_ref[...].astype(jnp.float32)
-    pick = (lax.broadcasted_iota(jnp.int32, (SLOTS, C), 0) == s).astype(jnp.float32)
+    m = mask_ref[...].astype(jnp.float32).astype(jnp.bfloat16)
+    pick = (lax.broadcasted_iota(jnp.int32, (SLOTS, C), 0) == s).astype(jnp.float32).astype(jnp.bfloat16)
     return lax.dot_general(m, pick, (((0,), (0,)), ((), ())), preferred_element_type=jnp.float32)
 
 
@@ -64,23 +67,34 @@
     return up, jnp.where(same, cells, 0.0), down
 
 
-def pack_kernel(face_hbm, edge_hbm, near_hbm, feat_hbm, grad_hbm, mask_hbm, act_ref, grd_ref, *refs):
+def pack_kernel(face_hbm, edge_hbm, near_hbm, feat_hbm, grad_hbm, mask_hbm, held_out, act_out, grd_out, near_out, *refs):
     y_out, x_out = refs[0:2], refs[2:4]
     face_ref, edge_ref, near, raw, mask_ref, full, sems = refs[4:]
-    fetched(
+    got_mask, got_feat, got_grad, *tables = fetching(
         (mask_hbm, mask_ref, sems.at[0]),
         (feat_hbm, raw.at[0], sems.at[1]),
         (grad_hbm, raw.at[1], sems.at[2]),
         (face_hbm, face_ref, sems.at[3]),
         (edge_hbm, edge_ref, sems.at[4]),
         (near_hbm, near, sems.at[5]),
+        (near_hbm, near_out.at[0], sems.at[6]),
     )
+    got_mask.wait()
+    got_feat.wait()
+    got_grad.wait()
     for s in range(SLOTS):
         rows = mask_columns(mask_ref, s)
-        for f, dst in enumerate((act_ref, grd_ref)):
+        for f in range(2):
             masked = raw[f, s].astype(jnp.float32) * rows
             full[f, s] = masked.reshape(8, 8, 8, C)
-            dst[s] = masked.astype(jnp.bfloat16)
+            raw[f, s] = masked.astype(jnp.bfloat16)
+    results = fetching(
+        (raw.at[0], held_out.at[0], sems.at[7]),
+        (raw.at[0], act_out, sems.at[8]),
+        (raw.at[1], grd_out, sems.at[9]),
+    )
+    for table in tables:
+        table.wait()
     for axis, outs in enumerate((x_out, y_out)):
         odd = parity("gy" if axis else "gx")
         for k in range(2):
@@ -115,16 +129,27 @@
                 lines += [down, same, up]
             lines = jnp.concatenate(lines, axis=0).astype(jnp.bfloat16)
             outs[k][pl.ds(FACE_ROWS, lines.shape[0])] = lines
+    x_out[1][pl.ds(X_ROWS + FACE_ROWS, SPARE_ROWS)] = jnp.zeros((SPARE_ROWS, C), jnp.bfloat16)
+    for result in results:
+        result.wait()
 
 
 def pack(features, out_grad, mask, near, face_sends, edge_sends):
-    sends = [jax.ShapeDtypeStruct((rows, C), jnp.bfloat16) for rows in 2 * (Y_ROWS + FACE_ROWS,) + 2 * (X_ROWS + FACE_ROWS,)]
-    brick = jax.ShapeDtypeStruct((SLOTS, 512, C), jnp.bfloat16)
+    sends = [
+        jax.ShapeDtypeStruct((rows + FACE_ROWS, C), jnp.bfloat16)
+        for rows in (Y_ROWS, Y_ROWS, X_ROWS, X_ROWS + SPARE_ROWS)
+    ]
     return pl.pallas_call(
         pack_kernel,
-        out_shape=[brick, brick] + sends,
+        out_shape=[
+            jax.ShapeDtypeStruct((ROOM_BRICKS, SLOTS, 512, C), jnp.bfloat16),
+            jax.ShapeDtypeStruct((SLOTS, 512, C), jnp.bfloat16),
+            jax.ShapeDtypeStruct((SLOTS, 512, C), jnp.bfloat16),
+            jax.ShapeDtypeStruct((ROOM_TABLES, SLOTS, 27), jnp.int32),
+        ]
+        + sends,
         in_specs=[hbm()] * 6,
-        out_specs=[vmem()] * 6,
+        out_specs=[hbm()] * 4 + [vmem()] * 4,
         scratch_shapes=[
             pltpu.SMEM((FACE, 4), jnp.int32),
             pltpu.SMEM((1, 4), jnp.int32),
@@ -132,7 +157,7 @@
             pltpu.VMEM((2, SLOTS, 512, C), jnp.bfloat16),
             pltpu.VMEM((SLOTS, 512), jnp.int32),
             pltpu.VMEM((2, SLOTS, 8, 8, 8, C), jnp.float32),
-            pltpu.SemaphoreType.DMA((6,)),
+            pltpu.SemaphoreType.DMA((10,)),
         ],
         compiler_params=pltpu.CompilerParams(vmem_limit_bytes=PACK_LIMIT),
         name="pack",
@@ -144,26 +169,25 @@
     return ref.at[pl.ds(0, rows)], ref.at[pl.ds(rows, rows)]
 
 
-def join_kernel(x0, x1, y0, y1, *outs):
-    for axis, pair in enumerate(((x0, x1), (y0, y1))):
-        rows = (X_ROWS, Y_ROWS)[axis]
-        for k, src in enumerate(pair):
-            outs[axis][pl.ds(k * rows, rows)] = src[pl.ds(0, rows)]
-            outs[2 + axis][pl.ds(k * FACE_ROWS, FACE_ROWS)] = src[pl.ds(rows, FACE_ROWS)]
-
-
-def join(x0, x1, y0, y1):
+def join_kernel(first, second, out, more):
+    rows = first.shape[0] - FACE_ROWS
+    for k, src in enumerate((first, second)):
+        out[pl.ds(k * rows, rows)] = src[pl.ds(0, rows)]
+        more[pl.ds(k * FACE_ROWS, FACE_ROWS)] = src[pl.ds(rows, FACE_ROWS)]
+
+
+def join(first, second):
     outs = [
-        jax.ShapeDtypeStruct((2 * rows, C), jnp.bfloat16) for rows in (X_ROWS, Y_ROWS, FACE_ROWS, FACE_ROWS)
+        jax.ShapeDtypeStruct((2 * rows, C), jnp.bfloat16) for rows in (first.shape[0] - FACE_ROWS, FACE_ROWS)
     ]
     return pl.pallas_call(
         join_kernel,
         out_shape=outs,
-        in_specs=[vmem()] * 4,
-        out_specs=[vmem()] * 4,
+        in_specs=[vmem()] * 2,
+        out_specs=[vmem()] * 2,
         compiler_params=pltpu.CompilerParams(vmem_limit_bytes=VMEM_LIMIT),
         name="join_sides",
-    )(x0, x1, y0, y1)
+    )(first, second)
 
 
 def forward_kernel(x_came, out0, out1):
@@ -288,10 +312,11 @@
     ]
 
 
-def columns_kernel(near_hbm, act, v, lx, ly, corners, wide, near, sem):
-    (table,) = fetching((near_hbm, near, sem))
+def columns_kernel(near_hbm, act_hbm, v, lx, ly, corners, wide, near, sem, act, act_sem):
+    table, bricks = fetching((near_hbm.at[0], near, sem), (act_hbm.at[0], act, act_sem))
+    fill_zero(lx, ly, corners, SLOTS)
+    bricks.wait()
     fill_own(act, lx, ly, corners)
-    fill_zero(lx, ly, corners, SLOTS)
     table.wait()
 
     def per_slot(s, carry):
@@ -306,9 +331,10 @@
     return pl.pallas_call(
         columns_kernel,
         out_shape=jax.ShapeDtypeStruct((SLOTS, 10, 64, 9 * C), jnp.bfloat16),
-        in_specs=[hbm(), vmem()],
+        in_specs=[hbm()] * 2,
         out_specs=vmem(),
-        scratch_shapes=columns_scratch(),
+        scratch_shapes=columns_scratch()
+        + [pltpu.VMEM((SLOTS, 512, C), jnp.bfloat16), pltpu.SemaphoreType.DMA(())],
         compiler_params=pltpu.CompilerParams(vmem_limit_bytes=VMEM_LIMIT),
         cost_estimate=pl.CostEstimate(flops=1 << 24, bytes_accessed=6 << 20, transcendentals=0),
         name="own_columns",
@@ -585,7 +611,7 @@
     def spread(blocks):
         return lax.all_to_all(blocks, ("gx", "gy"), 0, 0, axis_index_groups=same_core, tiled=True)
 
-    act, grd, y0, y1, x0, x1 = pack(
+    held_act, act, grd, table, y0, y1, x0, x1 = pack(
         features.reshape(SLOTS, 512, C),
         out_grad.reshape(SLOTS, 512, C),
         voxel_mask,
@@ -593,11 +619,15 @@
         face_sends,
         edge_sends,
     )
-    x1, y1 = hopped(x1, "gx"), hopped(y1, "gy")
-    v = own_columns(neighbours, act)
-    x1, y1, v = lax.optimization_barrier((x1, y1, v))
-    x_came, y_came, x_more, y_more = join(x0, x1, y0, y1)
-    x_came, y_came = swapped(x_came, "gx", 0), swapped(y_came, "gy", 0)
+    y1 = hopped(y1, "gy")
+    x1 = hopped(x1, "gx")
+    v = own_columns(table, held_act)
+    x1, v = lax.optimization_barrier((x1, v))
+    x_came, x_more = join(x0, x1)
+    x_more, y1 = lax.optimization_barrier((x_more, y1))
+    x_came = swapped(x_came, "gx", 0)
+    y_came, y_more = join(y0, y1)
+    y_came = swapped(y_came, "gy", 0)
     inner = inner_terms(v, grd)
     keep, send = rim_terms(neighbours, inner, grd, x_came, y_came)
     blocks = merge(groups, take, held, keep, swapped(send, "gy", 0)).astype(jnp.float16)

time: 65.1 us -> 64.7 us (level)
  local copies, waits for them, and re-layouts: 1.75 us -> 0.04 us
  Pallas kernels: 23.3 us -> 24.6 us
    ppermute x8, starting transfers between devices: 8.28 us -> 10.3 us  [swapped(): return lax.ppermute(value, axis, pairs)]
    unnamed x18 -> x14, local copies, waits for them, and re-layouts: 1.75 us -> 0.04 us
    all_to_all x2, starting transfers between devices: 13.2 us -> 11.6 us  [spread(): lax.all_to_all(blocks, ('gx', 'gy'), 0, 0, axis_index_groups=same_core, t...]
    pallas_call x2 -> x3, Pallas kernels: 2.85 us -> 3.61 us  [the longest x1 3.59 us: pack(): pl.pallas_call(pack_kernel, out_shape=[jax.ShapeDtypeStruct((ROOM_BRICKS,...]
  transfers between devices with their start and end apart: 12 -> 12, of which waited for: 5 -> 6; matrix products, arithmetic and copies ran while one was open for 0% -> 0% of each run, Pallas kernels for 26% -> 27%
where the time goes in v8:
time: 64.7 us; the launch traced here: 64.3 us
  Pallas kernels  24.6 us (38%)
  starting transfers between devices  24.5 us (38%)
  waiting for transfers between devices  12.4 us (19%)
  other arithmetic  1.84 us (3%)
  between operations  0.88 us (1%)
    pallas_call x2, Pallas kernels, product(): pl.pallas_call(lambda *refs: product_kernel(f, *refs), out_shape=jax.Shap...  12.1 us
    all_to_all x2, starting transfers between devices, spread(): lax.all_to_all(blocks, ('gx', 'gy'), 0, 0, axis_index_groups=same_core, t...  11.6 us
    ppermute x8, starting transfers between devices, swapped(): return lax.ppermute(value, axis, pairs)  10.3 us
    all_to_all x2, waiting for transfers between devices, spread(): lax.all_to_all(blocks, ('gx', 'gy'), 0, 0, axis_index_groups=same_core, t...  6.18 us
    pallas_call x1, Pallas kernels, pack(): pl.pallas_call(pack_kernel, out_shape=[jax.ShapeDtypeStruct((ROOM_BRICKS,...  3.59 us
    ppermute x2, waiting for transfers between devices, hopped(): return lax.ppermute(value, axis, pairs)  3.42 us
    ppermute x8, waiting for transfers between devices, swapped(): return lax.ppermute(value, axis, pairs)  2.84 us
    ppermute x2, starting transfers between devices, hopped(): return lax.ppermute(value, axis, pairs)  2.58 us
  transfers between devices with their start and end apart: 12, of which 6 were waited for; matrix products, arithmetic and copies ran while one was open for 0% of the time, Pallas kernels for 27%

profile of v8, /device:TPU:0, one launch (start us, length us, event | category | flops | bytes accessed | tf_op | source)
XLA Modules:
  0.0 64.3 jit_solution(2393208659316317056)
XLA Ops:
  0.6 3.6 %pack.1 = (bf16[48,4,512,128]{3,2,1,0:T(8,128)(2,1)}, bf16[4,512,128]{2,1,0:T(8,128)(2,1)}, bf16[4,512,128]{2,1,0:T(8,128)(2,1)}, s32[12288,4,27]{2,1,0:T(4,128)...) custom-call(s32[2,4]{1,0:T(2,128)} %bitcast.13, ...), custom_call_target="tpu_custom_call" | custom-call | tf_op jit(solution)/shard_map/pack/pallas_call | solution.py:142
  4.2 1.3 %collective-permute-start = (bf16[320,128]{1,0:T(8,128)(2,1)}, bf16[320,128]{1,0:T(8,128)(2,1)S(1)}, u32[]{:S(2)}, u32[]{:S(2)}) collective-permute-start(bf16[320,128]{1,0:T(8,128)(2,1)} %get-tuple-element.36), channel_id=1, source_target_pairs={{4,12},{12,20},{20,28},{8,0},{16,8},{24,16},{5,13},{13,21},{21,29}... | collective-permute-start | bytes 245768 | tf_op jit(solution)/shard_map/ppermute | solution.py:599
  5.5 1.3 %collective-permute-start.2 = (bf16[304,128]{1,0:T(8,128)(2,1)}, bf16[304,128]{1,0:T(8,128)(2,1)S(1)}, u32[]{:S(2)}, u32[]{:S(2)}) collective-permute-start(bf16[304,128]{1,0:T(8,128)(2,1)} %get-tuple-element.46), channel_id=1, source_target_pairs={{1,3},{2,0},{5,7},{6,4},{9,11},{10,8},{13,15},{14,12},{17,19},{18,... | collective-permute-start | bytes 233480 | tf_op jit(solution)/shard_map/ppermute | solution.py:599
  6.8 0.0 copy-start.2
  6.8 0.0 copy-start.1
  6.8 0.0 copy-start
  6.9 2.0 %own_columns.1.v = bf16[4,10,64,1152]{3,2,1,0:T(8,128)(2,1)S(1)} custom-call(s32[12288,4,27]{2,1,0:T(4,128)} %get-tuple-element.37.near_hbm, bf16[48,4,512,128]{3,2,1,0:T(8,128)(2,1)} %get-tuple-element.38.act_hbm), custom_call_target="tpu_custom_call" | custom-call | flops 16777216 | bytes 6291456 | tf_op jit(solution)/shard_map/own_columns/pallas_call | solution.py:331
  8.9 0.0 copy-start.4
  8.9 2.9 %collective-permute-done.second = bf16[320,128]{1,0:T(8,128)(2,1)S(1)} collective-permute-done((bf16[320,128]{1,0:T(8,128)(2,1)}, bf16[320,128]{1,0:T(8,128)(2,1)S(1)}, u32[]{:S(2)}, u32[]{:S(2)}) %collective-permute-start) | collective-permute-done | bytes 81952 | tf_op jit(solution)/shard_map/ppermute | solution.py:599
  11.8 0.0 copy-done.2
  11.8 0.5 collective-permute-done.2.second
  12.4 4.8 %collective-permute-start.1 = (bf16[320,128]{1,0:T(8,128)(2,1)S(1)}, bf16[320,128]{1,0:T(8,128)(2,1)S(1)}, u32[]{:S(2)}, u32[]{:S(2)}) collective-permute-start(bf16[320,128]{1,0:T(8,128)(2,1)S(1)} %get-tuple-element.43), channel_id=1, source_target_pairs={{0,4},{4,0},{8,12},{12,8},{16,20},{20,16},{24,28},{28,24},{1,5},{5... | collective-permute-start | bytes 245768 | tf_op jit(solution)/shard_map/ppermute | solution.py:593
  17.2 0.0 copy-done.1
  17.2 0.1 collective-permute-start.3
  17.3 0.0 copy-done
  17.3 0.0 copy-start.3
  17.3 0.0 copy-start.5
  17.3 0.0 copy-start.6
  17.3 2.3 %inner_terms.1.inner = f32[3456,128]{1,0:T(8,128)S(1)} custom-call(bf16[4,10,64,1152]{3,2,1,0:T(8,128)(2,1)S(1)} %own_columns.1.v, bf16[4,512,128]{2,1,0:T(8,128)(2,1)S(1)} %copy-done), custom_call_target="tpu_custom_call" | custom-call | flops 1811939328 | bytes 6291456 | tf_op jit(solution)/shard_map/inner_terms/pallas_call | solution.py:356
  19.6 0.0 collective-permute-done.1.x_ref.x_came.refs_4_
  19.7 0.0 collective-permute-done.3.y_ref.refs_5_
  19.7 0.0 copy-done.4
  19.7 2.0 %rim_terms.1 = (f32[1728,128]{1,0:T(8,128)S(1)}, f32[1728,128]{1,0:T(8,128)S(1)}) custom-call(s32[4,27]{1,0:T(4,128)S(1)} %copy-done.4, f32[3456,128]{1,0:T(8,128)S(1)} %inner_terms.1.inner, bf16[4,512,128]{2,1,0:T(8,128)(2,1)S(1)} %copy-done, bf16[320,128]{1,0:T(8,128)(2,1)S(1)} %collective-permute-done.1.x_ref.x_came.refs_4_, ...), custom_call_target="tpu_custom_call" | custom-call | flops 301989888 | bytes 6291456 | tf_op jit(solution)/shard_map/rim_terms/pallas_call | solution.py:442
  21.6 0.5 collective-permute-start.4
  22.2 2.1 %collective-permute-done.4.refs_1_ = f32[1728,128]{1,0:T(8,128)S(1)} collective-permute-done((f32[1728,128]{1,0:T(8,128)S(1)}, f32[1728,128]{1,0:T(8,128)S(1)}, u32[]{:S(2)}, u32[]{:S(2)}) %collective-permute-start.4) | collective-permute-done | bytes 884768 | tf_op jit(solution)/shard_map/ppermute | solution.py:593
  24.2 0.3 merge.1
  24.6 0.8 %convert_element_type.15 = f16[16,112,128]{2,1,0:T(8,128)(2,1)} convert(f32[16,112,128]{2,1,0:T(8,128)S(1)} %merge.1) | non-fusion elementwise | flops 229376 | bytes 1376256 | tf_op jit(solution)/shard_map/convert_element_type | solution.py:633
  25.4 6.0 %all-to-all-start = ((f16[16,112,128]{2,1,0:T(8,128)(2,1)}), f16[16,112,128]{2,1,0:T(8,128)(2,1)S(1)}, u32[]{:S(2)}, u32[]{:S(2)}) async-start(f16[16,112,128]{2,1,0:T(8,128)(2,1)} %convert_element_type.15), calls=%async_computation | async-start | bytes 917504 | tf_op jit(solution)/shard_map/all_to_all | solution.py:612
  31.4 0.1 collective-permute-start.5
  31.6 0.6 %collective-permute-start.6 = (bf16[32,128]{1,0:T(8,128)(2,1)S(1)}, bf16[32,128]{1,0:T(8,128)(2,1)S(1)}, u32[]{:S(2)}, u32[]{:S(2)}) collective-permute-start(bf16[32,128]{1,0:T(8,128)(2,1)S(1)} %get-tuple-element.58), channel_id=1, source_target_pairs={{1,2},{2,1},{5,6},{6,5},{9,10},{10,9},{13,14},{14,13},{17,18},{18,... | collective-permute-start | bytes 24584 | tf_op jit(solution)/shard_map/ppermute | solution.py:593
  32.2 1.5 %collective-permute-start.7 = (bf16[256,128]{1,0:T(8,128)(2,1)S(1)}, bf16[256,128]{1,0:T(8,128)(2,1)S(1)}, u32[]{:S(2)}, u32[]{:S(2)}) collective-permute-start(bf16[256,128]{1,0:T(8,128)(2,1)S(1)} %get-tuple-element.59), channel_id=1, source_target_pairs={{0,4},{4,0},{8,12},{12,8},{16,20},{20,16},{24,28},{28,24},{1,5},{5... | collective-permute-start | bytes 196616 | tf_op jit(solution)/shard_map/ppermute | solution.py:593
  33.8 2.6 %collective-permute-start.8 = (bf16[256,128]{1,0:T(8,128)(2,1)S(1)}, bf16[256,128]{1,0:T(8,128)(2,1)S(1)}, u32[]{:S(2)}, u32[]{:S(2)}) collective-permute-start(bf16[256,128]{1,0:T(8,128)(2,1)S(1)} %get-tuple-element.60), channel_id=1, source_target_pairs={{0,1},{1,0},{2,3},{3,2},{4,5},{5,4},{6,7},{7,6},{8,9},{9,8},{10,11... | collective-permute-start | bytes 196616 | tf_op jit(solution)/shard_map/ppermute | solution.py:593
  36.3 0.0 collective-permute-done.5.refs_6_
  36.3 0.0 collective-permute-done.6.refs_7_
  36.3 0.0 copy-done.3
  36.3 0.0 copy-done.5
  36.3 0.0 copy-done.6
  36.3 6.0 %output_product.1 = bf16[4,512,128]{2,1,0:T(8,128)(2,1)} custom-call(s32[4,27]{1,0:T(4,128)S(1)} %copy-done.4, s32[4,512]{1,0:T(4,128)S(1)} %copy-done.3, bf16[3456,128]{1,0:T(8,128)(2,1)S(1)} %bitcast.8, bf16[4,512,128]{2,1,0:T(8,128)(2,1)S(1)} %copy-done.6, bf16[320,128]{1,0:T(8,128)(2,1)S(1)} %collective-permute-done.1.x_ref.x_came.refs_4_, ...), custom_call_target="tpu_custom_call" | custom-call | flops 1811939328 | bytes 4194304 | tf_op jit(solution)/shard_map/output_product/pallas_call | solution.py:575
  42.4 0.0 collective-permute-done.7.refs_4_
  42.4 0.0 collective-permute-done.8.refs_5_
  42.4 1.0 %all-to-all-done = f16[16,112,128]{2,1,0:T(8,128)(2,1)S(1)} async-done(((f16[16,112,128]{2,1,0:T(8,128)(2,1)}), f16[16,112,128]{2,1,0:T(8,128)(2,1)S(1)}, u32[]{:S(2)}, u32[]{:S(2)}) %all-to-all-start) | async-done | bytes 458784 | tf_op jit(solution)/shard_map/all_to_all | solution.py:612
  43.4 0.1 convert_element_type.16.refs_0_
  43.5 0.3 sum_blocks.1
  43.7 0.8 %convert_element_type.17 = f16[16,112,128]{2,1,0:T(8,128)(2,1)} convert(f32[16,112,128]{2,1,0:T(8,128)S(1)} %sum_blocks.1) | non-fusion elementwise | flops 229376 | bytes 1376256 | tf_op jit(solution)/shard_map/convert_element_type | solution.py:641
  44.6 5.6 %all-to-all-start.1 = ((f16[16,112,128]{2,1,0:T(8,128)(2,1)}), f16[16,112,128]{2,1,0:T(8,128)(2,1)S(1)}, u32[]{:S(2)}, u32[]{:S(2)}) async-start(f16[16,112,128]{2,1,0:T(8,128)(2,1)} %convert_element_type.17), calls=%async_computation.1 | async-start | bytes 917504 | tf_op jit(solution)/shard_map/all_to_all | solution.py:612
  50.2 6.1 %input_grad_product.1 = bf16[4,512,128]{2,1,0:T(8,128)(2,1)} custom-call(s32[4,27]{1,0:T(4,128)S(1)} %copy-done.4, s32[4,512]{1,0:T(4,128)S(1)} %copy-done.3, bf16[3456,128]{1,0:T(8,128)(2,1)S(1)} %bitcast.9, bf16[4,512,128]{2,1,0:T(8,128)(2,1)S(1)} %copy-done, bf16[256,128]{1,0:T(8,128)(2,1)S(1)} %collective-permute-done.7.refs_4_, ...), custom_call_target="tpu_custom_call" | custom-call | flops 1811939328 | bytes 4194304 | tf_op jit(solution)/shard_map/input_grad_product/pallas_call | solution.py:575
  56.2 5.2 %all-to-all-done.1 = f16[16,112,128]{2,1,0:T(8,128)(2,1)S(1)} async-done(((f16[16,112,128]{2,1,0:T(8,128)(2,1)}), f16[16,112,128]{2,1,0:T(8,128)(2,1)S(1)}, u32[]{:S(2)}, u32[]{:S(2)}) %all-to-all-start.1) | async-done | bytes 458784 | tf_op jit(solution)/shard_map/all_to_all | solution.py:612
  61.4 0.0 collective-permute-start.9
  61.4 0.1 convert_element_type.19.refs_0_
  61.5 1.0 %decode_own.1.refs_1_ = f32[2,1728,128]{2,1,0:T(8,128)} custom-call(f32[16,112,128]{2,1,0:T(8,128)S(1)} %convert_element_type.19.refs_0_), custom_call_target="tpu_custom_call" | custom-call | tf_op jit(solution)/shard_map/decode_own/pallas_call | solution.py:537
  62.4 0.8 %collective-permute-done.9 = f16[16,112,128]{2,1,0:T(8,128)(2,1)S(1)} collective-permute-done((f16[16,112,128]{2,1,0:T(8,128)(2,1)S(1)}, f16[16,112,128]{2,1,0:T(8,128)(2,1)S(1)}, u32[]{:S(2)}, u32[]{:S(2)}) %collective-permute-start.9) | collective-permute-done | bytes 458784 | tf_op jit(solution)/shard_map/ppermute | solution.py:593
  63.2 0.1 convert_element_type.18.refs_0_
  63.3 1.0 %decode_other.1 = f32[2,1728,128]{2,1,0:T(8,128)} custom-call(f32[16,112,128]{2,1,0:T(8,128)S(1)} %convert_element_type.18.refs_0_, f32[2,1728,128]{2,1,0:T(8,128)} %decode_own.1.refs_1_), custom_call_target="tpu_custom_call", output_to_operand_aliasing={{}: (1, {})} | custom-call | tf_op jit(solution)/shard_map/decode_other/pallas_call | solution.py:537
  (3 shorter events, 0.0 us)
Async XLA Ops:
  4.2 7.6 %collective-permute-start = (bf16[320,128]{1,0:T(8,128)(2,1)}, bf16[320,128]{1,0:T(8,128)(2,1)S(1)}, u32[]{:S(2)}, u32[]{:S(2)}) collective-permute-start(bf16[320,128]{1,0:T(8,128)(2,1)} %get-tuple-element.36), channel_id=1, source_target_pairs={{4,12},{12,20},{20,28},{8,0},{16,8},{24,16},{5,13},{13,21},{21,29}... | collective-permute-start | bytes 245768 | tf_op jit(solution)/shard_map/ppermute | solution.py:599
  5.5 6.8 %collective-permute-start.2 = (bf16[304,128]{1,0:T(8,128)(2,1)}, bf16[304,128]{1,0:T(8,128)(2,1)S(1)}, u32[]{:S(2)}, u32[]{:S(2)}) collective-permute-start(bf16[304,128]{1,0:T(8,128)(2,1)} %get-tuple-element.46), channel_id=1, source_target_pairs={{1,3},{2,0},{5,7},{6,4},{9,11},{10,8},{13,15},{14,12},{17,19},{18,... | collective-permute-start | bytes 233480 | tf_op jit(solution)/shard_map/ppermute | solution.py:599
  6.8 5.0 %copy-start.2 = (bf16[288,128]{1,0:T(8,128)(2,1)S(1)}, bf16[288,128]{1,0:T(8,128)(2,1)}, u32[]{:S(2)}) copy-start(bf16[288,128]{1,0:T(8,128)(2,1)} %get-tuple-element.41.first) | copy-start | bytes 221188
  6.8 10.3 %copy-start.1 = (bf16[304,128]{1,0:T(8,128)(2,1)S(1)}, bf16[304,128]{1,0:T(8,128)(2,1)}, u32[]{:S(2)}) copy-start(bf16[304,128]{1,0:T(8,128)(2,1)} %get-tuple-element.44.first) | copy-start | bytes 233476
  6.8 10.4 %copy-start = (bf16[4,512,128]{2,1,0:T(8,128)(2,1)S(1)}, bf16[4,512,128]{2,1,0:T(8,128)(2,1)}, u32[]{:S(2)}) copy-start(bf16[4,512,128]{2,1,0:T(8,128)(2,1)} %get-tuple-element.64.grd.refs_3_) | copy-start | bytes 1572868
  8.9 10.8 %copy-start.4 = (s32[4,27]{1,0:T(4,128)S(1)}, s32[4,27]{1,0:T(4,128)}, u32[]{:S(2)}) copy-start(s32[4,27]{1,0:T(4,128)} %refs_0_.3) | copy-start | bytes 1300
  12.4 7.3 %collective-permute-start.1 = (bf16[320,128]{1,0:T(8,128)(2,1)S(1)}, bf16[320,128]{1,0:T(8,128)(2,1)S(1)}, u32[]{:S(2)}, u32[]{:S(2)}) collective-permute-start(bf16[320,128]{1,0:T(8,128)(2,1)S(1)} %get-tuple-element.43), channel_id=1, source_target_pairs={{0,4},{4,0},{8,12},{12,8},{16,20},{20,16},{24,28},{28,24},{1,5},{5... | collective-permute-start | bytes 245768 | tf_op jit(solution)/shard_map/ppermute | solution.py:593
  17.2 2.5 %collective-permute-start.3 = (bf16[352,128]{1,0:T(8,128)(2,1)S(1)}, bf16[352,128]{1,0:T(8,128)(2,1)S(1)}, u32[]{:S(2)}, u32[]{:S(2)}) collective-permute-start(bf16[352,128]{1,0:T(8,128)(2,1)S(1)} %get-tuple-element.48), channel_id=1, source_target_pairs={{0,1},{1,0},{2,3},{3,2},{4,5},{5,4},{6,7},{7,6},{8,9},{9,8},{10,11... | collective-permute-start | bytes 270344 | tf_op jit(solution)/shard_map/ppermute | solution.py:593
  17.3 19.1 %copy-start.3 = (s32[4,512]{1,0:T(4,128)S(1)}, s32[4,512]{1,0:T(4,128)}, u32[]{:S(2)}) copy-start(s32[4,512]{1,0:T(4,128)} %refs_1_.3) | copy-start | bytes 24580
  17.3 19.0 %copy-start.5 = (bf16[27,128,128]{2,1,0:T(8,128)(2,1)S(1)}, bf16[27,128,128]{2,1,0:T(8,128)(2,1)}, u32[]{:S(2)}) copy-start(bf16[27,128,128]{2,1,0:T(8,128)(2,1)} %param.9) | copy-start | bytes 2654212
  17.3 19.0 %copy-start.6 = (bf16[4,512,128]{2,1,0:T(8,128)(2,1)S(1)}, bf16[4,512,128]{2,1,0:T(8,128)(2,1)}, u32[]{:S(2)}) copy-start(bf16[4,512,128]{2,1,0:T(8,128)(2,1)} %get-tuple-element.55.refs_3_) | copy-start | bytes 1572868
  21.6 2.6 %collective-permute-start.4 = (f32[1728,128]{1,0:T(8,128)S(1)}, f32[1728,128]{1,0:T(8,128)S(1)}, u32[]{:S(2)}, u32[]{:S(2)}) collective-permute-start(f32[1728,128]{1,0:T(8,128)S(1)} %get-tuple-element.50), channel_id=1, source_target_pairs={{0,1},{1,0},{2,3},{3,2},{4,5},{5,4},{6,7},{7,6},{8,9},{9,8},{10,11... | collective-permute-start | bytes 2654216 | tf_op jit(solution)/shard_map/ppermute | solution.py:593
  25.4 18.0 %all-to-all-start = ((f16[16,112,128]{2,1,0:T(8,128)(2,1)}), f16[16,112,128]{2,1,0:T(8,128)(2,1)S(1)}, u32[]{:S(2)}, u32[]{:S(2)}) async-start(f16[16,112,128]{2,1,0:T(8,128)(2,1)} %convert_element_type.15), calls=%async_computation | async-start | bytes 917504 | tf_op jit(solution)/shard_map/all_to_all | solution.py:612
  31.4 4.9 %collective-permute-start.5 = (bf16[32,128]{1,0:T(8,128)(2,1)S(1)}, bf16[32,128]{1,0:T(8,128)(2,1)S(1)}, u32[]{:S(2)}, u32[]{:S(2)}) collective-permute-start(bf16[32,128]{1,0:T(8,128)(2,1)S(1)} %get-tuple-element.57), channel_id=1, source_target_pairs={{0,1},{1,0},{2,3},{3,2},{4,5},{5,4},{6,7},{7,6},{8,9},{9,8},{10,11... | collective-permute-start | bytes 24584 | tf_op jit(solution)/shard_map/ppermute | solution.py:593
  31.6 4.8 %collective-permute-start.6 = (bf16[32,128]{1,0:T(8,128)(2,1)S(1)}, bf16[32,128]{1,0:T(8,128)(2,1)S(1)}, u32[]{:S(2)}, u32[]{:S(2)}) collective-permute-start(bf16[32,128]{1,0:T(8,128)(2,1)S(1)} %get-tuple-element.58), channel_id=1, source_target_pairs={{1,2},{2,1},{5,6},{6,5},{9,10},{10,9},{13,14},{14,13},{17,18},{18,... | collective-permute-start | bytes 24584 | tf_op jit(solution)/shard_map/ppermute | solution.py:593
  32.2 10.1 %collective-permute-start.7 = (bf16[256,128]{1,0:T(8,128)(2,1)S(1)}, bf16[256,128]{1,0:T(8,128)(2,1)S(1)}, u32[]{:S(2)}, u32[]{:S(2)}) collective-permute-start(bf16[256,128]{1,0:T(8,128)(2,1)S(1)} %get-tuple-element.59), channel_id=1, source_target_pairs={{0,4},{4,0},{8,12},{12,8},{16,20},{20,16},{24,28},{28,24},{1,5},{5... | collective-permute-start | bytes 196616 | tf_op jit(solution)/shard_map/ppermute | solution.py:593
  33.8 8.6 %collective-permute-start.8 = (bf16[256,128]{1,0:T(8,128)(2,1)S(1)}, bf16[256,128]{1,0:T(8,128)(2,1)S(1)}, u32[]{:S(2)}, u32[]{:S(2)}) collective-permute-start(bf16[256,128]{1,0:T(8,128)(2,1)S(1)} %get-tuple-element.60), channel_id=1, source_target_pairs={{0,1},{1,0},{2,3},{3,2},{4,5},{5,4},{6,7},{7,6},{8,9},{9,8},{10,11... | collective-permute-start | bytes 196616 | tf_op jit(solution)/shard_map/ppermute | solution.py:593
  44.6 16.8 %all-to-all-start.1 = ((f16[16,112,128]{2,1,0:T(8,128)(2,1)}), f16[16,112,128]{2,1,0:T(8,128)(2,1)S(1)}, u32[]{:S(2)}, u32[]{:S(2)}) async-start(f16[16,112,128]{2,1,0:T(8,128)(2,1)} %convert_element_type.17), calls=%async_computation.1 | async-start | bytes 917504 | tf_op jit(solution)/shard_map/all_to_all | solution.py:612
  61.4 1.8 %collective-permute-start.9 = (f16[16,112,128]{2,1,0:T(8,128)(2,1)S(1)}, f16[16,112,128]{2,1,0:T(8,128)(2,1)S(1)}, u32[]{:S(2)}, u32[]{:S(2)}) collective-permute-start(f16[16,112,128]{2,1,0:T(8,128)(2,1)S(1)} %all-to-all-done.1), channel_id=1, source_target_pairs={{0,1},{1,0},{2,3},{3,2},{4,5},{5,4},{6,7},{7,6},{8,9},{9,8},{10,11... | collective-permute-start | bytes 1376264 | tf_op jit(solution)/shard_map/ppermute | solution.py:593

commit v9 on v8

--- a/solution.py
+++ b/solution.py
@@ -15,10 +15,9 @@
 ZERO = SLOTS + 4 * FACE + 4
 ROWS = 27 * C
 FACE_ROWS = FACE * 64
-X_ROWS = FACE_ROWS + 32
+X_ROWS = FACE_ROWS + 64
 Y_ROWS = FACE_ROWS + 48
 HALF = ROWS // 2
-SPARE_ROWS = 32
 VMEM_LIMIT = 32 * 1024 * 1024
 PACK_LIMIT = 60 * 1024 * 1024
 ROOM_BRICKS = 48
@@ -77,7 +76,6 @@
         (face_hbm, face_ref, sems.at[3]),
         (edge_hbm, edge_ref, sems.at[4]),
         (near_hbm, near, sems.at[5]),
-        (near_hbm, near_out.at[0], sems.at[6]),
     )
     got_mask.wait()
     got_feat.wait()
@@ -95,6 +93,7 @@
     )
     for table in tables:
         table.wait()
+    results += fetching((near, near_out.at[0], sems.at[6]))
     for axis, outs in enumerate((x_out, y_out)):
         odd = parity("gy" if axis else "gx")
         for k in range(2):
@@ -127,17 +126,17 @@
                     live & (low < ZERO),
                 )
                 lines += [down, same, up]
+            if axis == 0:
+                lines.append(jnp.zeros((32, C), jnp.float32))
             lines = jnp.concatenate(lines, axis=0).astype(jnp.bfloat16)
             outs[k][pl.ds(FACE_ROWS, lines.shape[0])] = lines
-    x_out[1][pl.ds(X_ROWS + FACE_ROWS, SPARE_ROWS)] = jnp.zeros((SPARE_ROWS, C), jnp.bfloat16)
     for result in results:
         result.wait()
 
 
 def pack(features, out_grad, mask, near, face_sends, edge_sends):
     sends = [
-        jax.ShapeDtypeStruct((rows + FACE_ROWS, C), jnp.bfloat16)
-        for rows in (Y_ROWS, Y_ROWS, X_ROWS, X_ROWS + SPARE_ROWS)
+        jax.ShapeDtypeStruct((rows + FACE_ROWS, C), jnp.bfloat16) for rows in (Y_ROWS, Y_ROWS, X_ROWS, X_ROWS)
     ]
     return pl.pallas_call(
         pack_kernel,
@@ -624,11 +623,12 @@
     v = own_columns(table, held_act)
     x1, v = lax.optimization_barrier((x1, v))
     x_came, x_more = join(x0, x1)
-    x_more, y1 = lax.optimization_barrier((x_more, y1))
+    x_more, v = lax.optimization_barrier((x_more, v))
     x_came = swapped(x_came, "gx", 0)
+    inner = inner_terms(v, grd)
+    inner, y1 = lax.optimization_barrier((inner, y1))
     y_came, y_more = join(y0, y1)
     y_came = swapped(y_came, "gy", 0)
-    inner = inner_terms(v, grd)
     keep, send = rim_terms(neighbours, inner, grd, x_came, y_came)
     blocks = merge(groups, take, held, keep, swapped(send, "gy", 0)).astype(jnp.float16)
     rows = kernel.reshape(ROWS, C)

time: 64.7 us -> 63.6 us (0.983)
  starting transfers between devices: 24.5 us -> 22.9 us
    ppermute x8, starting transfers between devices: 10.3 us -> 8.81 us  [swapped(): return lax.ppermute(value, axis, pairs)]
    ppermute x8, waiting for transfers between devices: 2.84 us -> 3.77 us  [swapped(): return lax.ppermute(value, axis, pairs)]
  transfers between devices with their start and end apart: 12 -> 12, of which waited for: 6 -> 6; matrix products, arithmetic and copies ran while one was open for 0% -> 0% of each run, Pallas kernels for 27% -> 28%
where the time goes in v9:
time: 63.6 us; the launch traced here: 63.2 us
  Pallas kernels  24.6 us (39%)
  starting transfers between devices  22.9 us (36%)
  waiting for transfers between devices  12.9 us (20%)
  other arithmetic  1.84 us (3%)
  between operations  0.86 us (1%)
    pallas_call x2, Pallas kernels, product(): pl.pallas_call(lambda *refs: product_kernel(f, *refs), out_shape=jax.Shap...  12.1 us
    all_to_all x2, starting transfers between devices, spread(): lax.all_to_all(blocks, ('gx', 'gy'), 0, 0, axis_index_groups=same_core, t...  11.5 us
    ppermute x8, starting transfers between devices, swapped(): return lax.ppermute(value, axis, pairs)  8.81 us
    all_to_all x2, waiting for transfers between devices, spread(): lax.all_to_all(blocks, ('gx', 'gy'), 0, 0, axis_index_groups=same_core, t...  6.28 us
    ppermute x8, waiting for transfers between devices, swapped(): return lax.ppermute(value, axis, pairs)  3.77 us
    pallas_call x1, Pallas kernels, pack(): pl.pallas_call(pack_kernel, out_shape=[jax.ShapeDtypeStruct((ROOM_BRICKS,...  3.6 us
    ppermute x2, waiting for transfers between devices, hopped(): return lax.ppermute(value, axis, pairs)  2.89 us
    ppermute x2, starting transfers between devices, hopped(): return lax.ppermute(value, axis, pairs)  2.58 us
  transfers between devices with their start and end apart: 12, of which 6 were waited for; matrix products, arithmetic and copies ran while one was open for 0% of the time, Pallas kernels for 28%

profile of v9, /device:TPU:0, one launch (start us, length us, event | category | flops | bytes accessed | tf_op | source)
XLA Modules:
  0.0 63.2 jit_solution(13038798711916576964)
XLA Ops:
  0.6 3.6 %pack.1 = (bf16[48,4,512,128]{3,2,1,0:T(8,128)(2,1)}, bf16[4,512,128]{2,1,0:T(8,128)(2,1)}, bf16[4,512,128]{2,1,0:T(8,128)(2,1)}, s32[12288,4,27]{2,1,0:T(4,128)...) custom-call(s32[2,4]{1,0:T(2,128)} %bitcast.13, ...), custom_call_target="tpu_custom_call" | custom-call | tf_op jit(solution)/shard_map/pack/pallas_call | solution.py:141
  4.2 1.3 %collective-permute-start = (bf16[320,128]{1,0:T(8,128)(2,1)}, bf16[320,128]{1,0:T(8,128)(2,1)S(1)}, u32[]{:S(2)}, u32[]{:S(2)}) collective-permute-start(bf16[320,128]{1,0:T(8,128)(2,1)} %get-tuple-element.39), channel_id=1, source_target_pairs={{4,12},{12,20},{20,28},{8,0},{16,8},{24,16},{5,13},{13,21},{21,29}... | collective-permute-start | bytes 245768 | tf_op jit(solution)/shard_map/ppermute | solution.py:598
  5.5 1.3 %collective-permute-start.1 = (bf16[304,128]{1,0:T(8,128)(2,1)}, bf16[304,128]{1,0:T(8,128)(2,1)S(1)}, u32[]{:S(2)}, u32[]{:S(2)}) collective-permute-start(bf16[304,128]{1,0:T(8,128)(2,1)} %get-tuple-element.47), channel_id=1, source_target_pairs={{1,3},{2,0},{5,7},{6,4},{9,11},{10,8},{13,15},{14,12},{17,19},{18,... | collective-permute-start | bytes 233480 | tf_op jit(solution)/shard_map/ppermute | solution.py:598
  6.8 0.0 copy-start.1
  6.9 0.0 copy-start
  6.9 2.0 %own_columns.1.v = bf16[4,10,64,1152]{3,2,1,0:T(8,128)(2,1)S(1)} custom-call(s32[12288,4,27]{2,1,0:T(4,128)} %get-tuple-element.40.near_hbm, bf16[48,4,512,128]{3,2,1,0:T(8,128)(2,1)} %get-tuple-element.41.act_hbm), custom_call_target="tpu_custom_call" | custom-call | flops 16777216 | bytes 6291456 | tf_op jit(solution)/shard_map/own_columns/pallas_call | solution.py:330
  8.9 0.0 copy-start.2
  8.9 0.0 copy-start.4
  8.9 2.9 %collective-permute-done.second = bf16[320,128]{1,0:T(8,128)(2,1)S(1)} collective-permute-done((bf16[320,128]{1,0:T(8,128)(2,1)}, bf16[320,128]{1,0:T(8,128)(2,1)S(1)}, u32[]{:S(2)}, u32[]{:S(2)}) %collective-permute-start) | collective-permute-done | bytes 81952 | tf_op jit(solution)/shard_map/ppermute | solution.py:598
  11.8 0.0 copy-done.1
  11.8 2.3 %collective-permute-start.2 = (bf16[384,128]{1,0:T(8,128)(2,1)S(1)}, bf16[384,128]{1,0:T(8,128)(2,1)S(1)}, u32[]{:S(2)}, u32[]{:S(2)}) collective-permute-start(bf16[384,128]{1,0:T(8,128)(2,1)S(1)} %get-tuple-element.49), channel_id=1, source_target_pairs={{0,4},{4,0},{8,12},{12,8},{16,20},{20,16},{24,28},{28,24},{1,5},{5... | collective-permute-start | bytes 294920 | tf_op jit(solution)/shard_map/ppermute | solution.py:592
  14.2 0.0 copy-done
  14.2 2.3 %inner_terms.1.inner = f32[3456,128]{1,0:T(8,128)S(1)} custom-call(bf16[4,10,64,1152]{3,2,1,0:T(8,128)(2,1)S(1)} %own_columns.1.v, bf16[4,512,128]{2,1,0:T(8,128)(2,1)S(1)} %copy-done), custom_call_target="tpu_custom_call" | custom-call | flops 1811939328 | bytes 6291456 | tf_op jit(solution)/shard_map/inner_terms/pallas_call | solution.py:355
  16.5 0.0 copy-start.3
  16.5 0.0 copy-start.5
  16.5 0.0 copy-start.6
  16.5 0.0 collective-permute-done.1.second
  16.6 0.0 copy-done.2
  16.6 1.2 %collective-permute-start.3 = (bf16[352,128]{1,0:T(8,128)(2,1)S(1)}, bf16[352,128]{1,0:T(8,128)(2,1)S(1)}, u32[]{:S(2)}, u32[]{:S(2)}) collective-permute-start(bf16[352,128]{1,0:T(8,128)(2,1)S(1)} %get-tuple-element.52), channel_id=1, source_target_pairs={{0,1},{1,0},{2,3},{3,2},{4,5},{5,4},{6,7},{7,6},{8,9},{9,8},{10,11... | collective-permute-start | bytes 270344 | tf_op jit(solution)/shard_map/ppermute | solution.py:592
  17.8 0.9 %collective-permute-done.3.y_ref.refs_5_ = bf16[352,128]{1,0:T(8,128)(2,1)S(1)} collective-permute-done((bf16[352,128]{1,0:T(8,128)(2,1)S(1)}, bf16[352,128]{1,0:T(8,128)(2,1)S(1)}, u32[]{:S(2)}, u32[]{:S(2)}) %collective-permute-start.3) | collective-permute-done | bytes 90144 | tf_op jit(solution)/shard_map/ppermute | solution.py:592
  18.7 0.0 collective-permute-done.2.x_ref.x_came.refs_4_
  18.7 0.0 copy-done.4
  18.7 1.9 %rim_terms.1 = (f32[1728,128]{1,0:T(8,128)S(1)}, f32[1728,128]{1,0:T(8,128)S(1)}) custom-call(s32[4,27]{1,0:T(4,128)S(1)} %copy-done.4, f32[3456,128]{1,0:T(8,128)S(1)} %inner_terms.1.inner, bf16[4,512,128]{2,1,0:T(8,128)(2,1)S(1)} %copy-done, bf16[384,128]{1,0:T(8,128)(2,1)S(1)} %collective-permute-done.2.x_ref.x_came.refs_4_, ...), custom_call_target="tpu_custom_call" | custom-call | flops 301989888 | bytes 6291456 | tf_op jit(solution)/shard_map/rim_terms/pallas_call | solution.py:441
  20.7 0.4 collective-permute-start.4
  21.1 2.1 %collective-permute-done.4.refs_1_ = f32[1728,128]{1,0:T(8,128)S(1)} collective-permute-done((f32[1728,128]{1,0:T(8,128)S(1)}, f32[1728,128]{1,0:T(8,128)S(1)}, u32[]{:S(2)}, u32[]{:S(2)}) %collective-permute-start.4) | collective-permute-done | bytes 884768 | tf_op jit(solution)/shard_map/ppermute | solution.py:592
  23.2 0.3 merge.1
  23.5 0.8 %convert_element_type.15 = f16[16,112,128]{2,1,0:T(8,128)(2,1)} convert(f32[16,112,128]{2,1,0:T(8,128)S(1)} %merge.1) | non-fusion elementwise | flops 229376 | bytes 1376256 | tf_op jit(solution)/shard_map/convert_element_type | solution.py:633
  24.4 6.0 %all-to-all-start = ((f16[16,112,128]{2,1,0:T(8,128)(2,1)}), f16[16,112,128]{2,1,0:T(8,128)(2,1)S(1)}, u32[]{:S(2)}, u32[]{:S(2)}) async-start(f16[16,112,128]{2,1,0:T(8,128)(2,1)} %convert_element_type.15), calls=%async_computation | async-start | bytes 917504 | tf_op jit(solution)/shard_map/all_to_all | solution.py:611
  30.4 0.1 collective-permute-start.5
  30.5 0.6 %collective-permute-start.6 = (bf16[32,128]{1,0:T(8,128)(2,1)S(1)}, bf16[32,128]{1,0:T(8,128)(2,1)S(1)}, u32[]{:S(2)}, u32[]{:S(2)}) collective-permute-start(bf16[32,128]{1,0:T(8,128)(2,1)S(1)} %get-tuple-element.62), channel_id=1, source_target_pairs={{1,2},{2,1},{5,6},{6,5},{9,10},{10,9},{13,14},{14,13},{17,18},{18,... | collective-permute-start | bytes 24584 | tf_op jit(solution)/shard_map/ppermute | solution.py:592
  31.2 1.5 %collective-permute-start.7 = (bf16[256,128]{1,0:T(8,128)(2,1)S(1)}, bf16[256,128]{1,0:T(8,128)(2,1)S(1)}, u32[]{:S(2)}, u32[]{:S(2)}) collective-permute-start(bf16[256,128]{1,0:T(8,128)(2,1)S(1)} %get-tuple-element.63), channel_id=1, source_target_pairs={{0,4},{4,0},{8,12},{12,8},{16,20},{20,16},{24,28},{28,24},{1,5},{5... | collective-permute-start | bytes 196616 | tf_op jit(solution)/shard_map/ppermute | solution.py:592
  32.7 2.6 %collective-permute-start.8 = (bf16[256,128]{1,0:T(8,128)(2,1)S(1)}, bf16[256,128]{1,0:T(8,128)(2,1)S(1)}, u32[]{:S(2)}, u32[]{:S(2)}) collective-permute-start(bf16[256,128]{1,0:T(8,128)(2,1)S(1)} %get-tuple-element.64), channel_id=1, source_target_pairs={{0,1},{1,0},{2,3},{3,2},{4,5},{5,4},{6,7},{7,6},{8,9},{9,8},{10,11... | collective-permute-start | bytes 196616 | tf_op jit(solution)/shard_map/ppermute | solution.py:592
  35.3 0.0 collective-permute-done.5.refs_6_
  35.3 0.0 collective-permute-done.6.refs_7_
  35.3 0.0 copy-done.3
  35.3 0.0 copy-done.5
  35.3 0.0 copy-done.6
  35.3 6.0 %output_product.1 = bf16[4,512,128]{2,1,0:T(8,128)(2,1)} custom-call(s32[4,27]{1,0:T(4,128)S(1)} %copy-done.4, s32[4,512]{1,0:T(4,128)S(1)} %copy-done.3, bf16[3456,128]{1,0:T(8,128)(2,1)S(1)} %bitcast.8, bf16[4,512,128]{2,1,0:T(8,128)(2,1)S(1)} %copy-done.6, bf16[384,128]{1,0:T(8,128)(2,1)S(1)} %collective-permute-done.2.x_ref.x_came.refs_4_, ...), custom_call_target="tpu_custom_call" | custom-call | flops 1811939328 | bytes 4194304 | tf_op jit(solution)/shard_map/output_product/pallas_call | solution.py:574
  41.3 0.0 collective-permute-done.7.refs_4_
  41.3 0.0 collective-permute-done.8.refs_5_
  41.3 1.1 %all-to-all-done = f16[16,112,128]{2,1,0:T(8,128)(2,1)S(1)} async-done(((f16[16,112,128]{2,1,0:T(8,128)(2,1)}), f16[16,112,128]{2,1,0:T(8,128)(2,1)S(1)}, u32[]{:S(2)}, u32[]{:S(2)}) %all-to-all-start) | async-done | bytes 458784 | tf_op jit(solution)/shard_map/all_to_all | solution.py:611
  42.4 0.1 convert_element_type.16.refs_0_
  42.5 0.3 sum_blocks.1
  42.8 0.8 %convert_element_type.17 = f16[16,112,128]{2,1,0:T(8,128)(2,1)} convert(f32[16,112,128]{2,1,0:T(8,128)S(1)} %sum_blocks.1) | non-fusion elementwise | flops 229376 | bytes 1376256 | tf_op jit(solution)/shard_map/convert_element_type | solution.py:641
  43.6 5.5 %all-to-all-start.1 = ((f16[16,112,128]{2,1,0:T(8,128)(2,1)}), f16[16,112,128]{2,1,0:T(8,128)(2,1)S(1)}, u32[]{:S(2)}, u32[]{:S(2)}) async-start(f16[16,112,128]{2,1,0:T(8,128)(2,1)} %convert_element_type.17), calls=%async_computation.1 | async-start | bytes 917504 | tf_op jit(solution)/shard_map/all_to_all | solution.py:611
  49.1 6.1 %input_grad_product.1 = bf16[4,512,128]{2,1,0:T(8,128)(2,1)} custom-call(s32[4,27]{1,0:T(4,128)S(1)} %copy-done.4, s32[4,512]{1,0:T(4,128)S(1)} %copy-done.3, bf16[3456,128]{1,0:T(8,128)(2,1)S(1)} %bitcast.9, bf16[4,512,128]{2,1,0:T(8,128)(2,1)S(1)} %copy-done, bf16[256,128]{1,0:T(8,128)(2,1)S(1)} %collective-permute-done.7.refs_4_, ...), custom_call_target="tpu_custom_call" | custom-call | flops 1811939328 | bytes 4194304 | tf_op jit(solution)/shard_map/input_grad_product/pallas_call | solution.py:574
  55.2 5.2 %all-to-all-done.1 = f16[16,112,128]{2,1,0:T(8,128)(2,1)S(1)} async-done(((f16[16,112,128]{2,1,0:T(8,128)(2,1)}), f16[16,112,128]{2,1,0:T(8,128)(2,1)S(1)}, u32[]{:S(2)}, u32[]{:S(2)}) %all-to-all-start.1) | async-done | bytes 458784 | tf_op jit(solution)/shard_map/all_to_all | solution.py:611
  60.4 0.0 collective-permute-start.9
  60.4 0.1 convert_element_type.19.refs_0_
  60.4 1.0 %decode_own.1.refs_1_ = f32[2,1728,128]{2,1,0:T(8,128)} custom-call(f32[16,112,128]{2,1,0:T(8,128)S(1)} %convert_element_type.19.refs_0_), custom_call_target="tpu_custom_call" | custom-call | tf_op jit(solution)/shard_map/decode_own/pallas_call | solution.py:536
  61.4 0.8 %collective-permute-done.9 = f16[16,112,128]{2,1,0:T(8,128)(2,1)S(1)} collective-permute-done((f16[16,112,128]{2,1,0:T(8,128)(2,1)S(1)}, f16[16,112,128]{2,1,0:T(8,128)(2,1)S(1)}, u32[]{:S(2)}, u32[]{:S(2)}) %collective-permute-start.9) | collective-permute-done | bytes 458784 | tf_op jit(solution)/shard_map/ppermute | solution.py:592
  62.2 0.1 convert_element_type.18.refs_0_
  62.2 1.0 %decode_other.1 = f32[2,1728,128]{2,1,0:T(8,128)} custom-call(f32[16,112,128]{2,1,0:T(8,128)S(1)} %convert_element_type.18.refs_0_, f32[2,1728,128]{2,1,0:T(8,128)} %decode_own.1.refs_1_), custom_call_target="tpu_custom_call", output_to_operand_aliasing={{}: (1, {})} | custom-call | tf_op jit(solution)/shard_map/decode_other/pallas_call | solution.py:536
  (3 shorter events, 0.0 us)
Async XLA Ops:
  4.2 7.6 %collective-permute-start = (bf16[320,128]{1,0:T(8,128)(2,1)}, bf16[320,128]{1,0:T(8,128)(2,1)S(1)}, u32[]{:S(2)}, u32[]{:S(2)}) collective-permute-start(bf16[320,128]{1,0:T(8,128)(2,1)} %get-tuple-element.39), channel_id=1, source_target_pairs={{4,12},{12,20},{20,28},{8,0},{16,8},{24,16},{5,13},{13,21},{21,29}... | collective-permute-start | bytes 245768 | tf_op jit(solution)/shard_map/ppermute | solution.py:598
  5.5 11.0 %collective-permute-start.1 = (bf16[304,128]{1,0:T(8,128)(2,1)}, bf16[304,128]{1,0:T(8,128)(2,1)S(1)}, u32[]{:S(2)}, u32[]{:S(2)}) collective-permute-start(bf16[304,128]{1,0:T(8,128)(2,1)} %get-tuple-element.47), channel_id=1, source_target_pairs={{1,3},{2,0},{5,7},{6,4},{9,11},{10,8},{13,15},{14,12},{17,19},{18,... | collective-permute-start | bytes 233480 | tf_op jit(solution)/shard_map/ppermute | solution.py:598
  6.8 5.0 %copy-start.1 = (bf16[320,128]{1,0:T(8,128)(2,1)S(1)}, bf16[320,128]{1,0:T(8,128)(2,1)}, u32[]{:S(2)}) copy-start(bf16[320,128]{1,0:T(8,128)(2,1)} %get-tuple-element.38.first) | copy-start | bytes 245764
  6.9 7.3 %copy-start = (bf16[4,512,128]{2,1,0:T(8,128)(2,1)S(1)}, bf16[4,512,128]{2,1,0:T(8,128)(2,1)}, u32[]{:S(2)}) copy-start(bf16[4,512,128]{2,1,0:T(8,128)(2,1)} %get-tuple-element.68.grd.refs_3_) | copy-start | bytes 1572868
  8.9 7.6 %copy-start.2 = (bf16[304,128]{1,0:T(8,128)(2,1)S(1)}, bf16[304,128]{1,0:T(8,128)(2,1)}, u32[]{:S(2)}) copy-start(bf16[304,128]{1,0:T(8,128)(2,1)} %get-tuple-element.50.first) | copy-start | bytes 233476
  8.9 9.8 %copy-start.4 = (s32[4,27]{1,0:T(4,128)S(1)}, s32[4,27]{1,0:T(4,128)}, u32[]{:S(2)}) copy-start(s32[4,27]{1,0:T(4,128)} %refs_0_.3) | copy-start | bytes 1300
  11.8 6.9 %collective-permute-start.2 = (bf16[384,128]{1,0:T(8,128)(2,1)S(1)}, bf16[384,128]{1,0:T(8,128)(2,1)S(1)}, u32[]{:S(2)}, u32[]{:S(2)}) collective-permute-start(bf16[384,128]{1,0:T(8,128)(2,1)S(1)} %get-tuple-element.49), channel_id=1, source_target_pairs={{0,4},{4,0},{8,12},{12,8},{16,20},{20,16},{24,28},{28,24},{1,5},{5... | collective-permute-start | bytes 294920 | tf_op jit(solution)/shard_map/ppermute | solution.py:592
  16.5 18.8 %copy-start.3 = (s32[4,512]{1,0:T(4,128)S(1)}, s32[4,512]{1,0:T(4,128)}, u32[]{:S(2)}) copy-start(s32[4,512]{1,0:T(4,128)} %refs_1_.3) | copy-start | bytes 24580
  16.5 18.7 %copy-start.5 = (bf16[27,128,128]{2,1,0:T(8,128)(2,1)S(1)}, bf16[27,128,128]{2,1,0:T(8,128)(2,1)}, u32[]{:S(2)}) copy-start(bf16[27,128,128]{2,1,0:T(8,128)(2,1)} %param.9) | copy-start | bytes 2654212
  16.5 18.7 %copy-start.6 = (bf16[4,512,128]{2,1,0:T(8,128)(2,1)S(1)}, bf16[4,512,128]{2,1,0:T(8,128)(2,1)}, u32[]{:S(2)}) copy-start(bf16[4,512,128]{2,1,0:T(8,128)(2,1)} %get-tuple-element.59.refs_3_) | copy-start | bytes 1572868
  16.6 2.1 %collective-permute-start.3 = (bf16[352,128]{1,0:T(8,128)(2,1)S(1)}, bf16[352,128]{1,0:T(8,128)(2,1)S(1)}, u32[]{:S(2)}, u32[]{:S(2)}) collective-permute-start(bf16[352,128]{1,0:T(8,128)(2,1)S(1)} %get-tuple-element.52), channel_id=1, source_target_pairs={{0,1},{1,0},{2,3},{3,2},{4,5},{5,4},{6,7},{7,6},{8,9},{9,8},{10,11... | collective-permute-start | bytes 270344 | tf_op jit(solution)/shard_map/ppermute | solution.py:592
  20.7 2.5 %collective-permute-start.4 = (f32[1728,128]{1,0:T(8,128)S(1)}, f32[1728,128]{1,0:T(8,128)S(1)}, u32[]{:S(2)}, u32[]{:S(2)}) collective-permute-start(f32[1728,128]{1,0:T(8,128)S(1)} %get-tuple-element.54), channel_id=1, source_target_pairs={{0,1},{1,0},{2,3},{3,2},{4,5},{5,4},{6,7},{7,6},{8,9},{9,8},{10,11... | collective-permute-start | bytes 2654216 | tf_op jit(solution)/shard_map/ppermute | solution.py:592
  24.4 18.1 %all-to-all-start = ((f16[16,112,128]{2,1,0:T(8,128)(2,1)}), f16[16,112,128]{2,1,0:T(8,128)(2,1)S(1)}, u32[]{:S(2)}, u32[]{:S(2)}) async-start(f16[16,112,128]{2,1,0:T(8,128)(2,1)} %convert_element_type.15), calls=%async_computation | async-start | bytes 917504 | tf_op jit(solution)/shard_map/all_to_all | solution.py:611
  30.4 4.9 %collective-permute-start.5 = (bf16[32,128]{1,0:T(8,128)(2,1)S(1)}, bf16[32,128]{1,0:T(8,128)(2,1)S(1)}, u32[]{:S(2)}, u32[]{:S(2)}) collective-permute-start(bf16[32,128]{1,0:T(8,128)(2,1)S(1)} %get-tuple-element.61), channel_id=1, source_target_pairs={{0,1},{1,0},{2,3},{3,2},{4,5},{5,4},{6,7},{7,6},{8,9},{9,8},{10,11... | collective-permute-start | bytes 24584 | tf_op jit(solution)/shard_map/ppermute | solution.py:592
  30.5 4.8 %collective-permute-start.6 = (bf16[32,128]{1,0:T(8,128)(2,1)S(1)}, bf16[32,128]{1,0:T(8,128)(2,1)S(1)}, u32[]{:S(2)}, u32[]{:S(2)}) collective-permute-start(bf16[32,128]{1,0:T(8,128)(2,1)S(1)} %get-tuple-element.62), channel_id=1, source_target_pairs={{1,2},{2,1},{5,6},{6,5},{9,10},{10,9},{13,14},{14,13},{17,18},{18,... | collective-permute-start | bytes 24584 | tf_op jit(solution)/shard_map/ppermute | solution.py:592
  31.2 10.1 %collective-permute-start.7 = (bf16[256,128]{1,0:T(8,128)(2,1)S(1)}, bf16[256,128]{1,0:T(8,128)(2,1)S(1)}, u32[]{:S(2)}, u32[]{:S(2)}) collective-permute-start(bf16[256,128]{1,0:T(8,128)(2,1)S(1)} %get-tuple-element.63), channel_id=1, source_target_pairs={{0,4},{4,0},{8,12},{12,8},{16,20},{20,16},{24,28},{28,24},{1,5},{5... | collective-permute-start | bytes 196616 | tf_op jit(solution)/shard_map/ppermute | solution.py:592
  32.7 8.6 %collective-permute-start.8 = (bf16[256,128]{1,0:T(8,128)(2,1)S(1)}, bf16[256,128]{1,0:T(8,128)(2,1)S(1)}, u32[]{:S(2)}, u32[]{:S(2)}) collective-permute-start(bf16[256,128]{1,0:T(8,128)(2,1)S(1)} %get-tuple-element.64), channel_id=1, source_target_pairs={{0,1},{1,0},{2,3},{3,2},{4,5},{5,4},{6,7},{7,6},{8,9},{9,8},{10,11... | collective-permute-start | bytes 196616 | tf_op jit(solution)/shard_map/ppermute | solution.py:592
  43.6 16.8 %all-to-all-start.1 = ((f16[16,112,128]{2,1,0:T(8,128)(2,1)}), f16[16,112,128]{2,1,0:T(8,128)(2,1)S(1)}, u32[]{:S(2)}, u32[]{:S(2)}) async-start(f16[16,112,128]{2,1,0:T(8,128)(2,1)} %convert_element_type.17), calls=%async_computation.1 | async-start | bytes 917504 | tf_op jit(solution)/shard_map/all_to_all | solution.py:611
  60.4 1.8 %collective-permute-start.9 = (f16[16,112,128]{2,1,0:T(8,128)(2,1)S(1)}, f16[16,112,128]{2,1,0:T(8,128)(2,1)S(1)}, u32[]{:S(2)}, u32[]{:S(2)}) collective-permute-start(f16[16,112,128]{2,1,0:T(8,128)(2,1)S(1)} %all-to-all-done.1), channel_id=1, source_target_pairs={{0,1},{1,0},{2,3},{3,2},{4,5},{5,4},{6,7},{7,6},{8,9},{9,8},{10,11... | collective-permute-start | bytes 1376264 | tf_op jit(solution)/shard_map/ppermute | solution.py:592

commit v10 on v9

--- a/solution.py
+++ b/solution.py
@@ -67,8 +67,9 @@
 
 
 def pack_kernel(face_hbm, edge_hbm, near_hbm, feat_hbm, grad_hbm, mask_hbm, held_out, act_out, grd_out, near_out, *refs):
-    y_out, x_out = refs[0:2], refs[2:4]
-    face_ref, edge_ref, near, raw, mask_ref, full, sems = refs[4:]
+    sends = refs[0:4]
+    y_out, x_out = refs[4:6], refs[6:8]
+    face_ref, edge_ref, near, raw, mask_ref, full, sems = refs[8:]
     got_mask, got_feat, got_grad, *tables = fetching(
         (mask_hbm, mask_ref, sems.at[0]),
         (feat_hbm, raw.at[0], sems.at[1]),
@@ -130,6 +131,8 @@
                 lines.append(jnp.zeros((32, C), jnp.float32))
             lines = jnp.concatenate(lines, axis=0).astype(jnp.bfloat16)
             outs[k][pl.ds(FACE_ROWS, lines.shape[0])] = lines
+    for i, (built, send) in enumerate(zip(refs[4:8], sends)):
+        results += fetching((built, send, sems.at[10 + i]))
     for result in results:
         result.wait()
 
@@ -148,15 +151,16 @@
         ]
         + sends,
         in_specs=[hbm()] * 6,
-        out_specs=[hbm()] * 4 + [vmem()] * 4,
-        scratch_shapes=[
+        out_specs=[hbm()] * 8,
+        scratch_shapes=[pltpu.VMEM(send.shape, send.dtype) for send in sends]
+        + [
             pltpu.SMEM((FACE, 4), jnp.int32),
             pltpu.SMEM((1, 4), jnp.int32),
             pltpu.SMEM((SLOTS, 27), jnp.int32),
             pltpu.VMEM((2, SLOTS, 512, C), jnp.bfloat16),
             pltpu.VMEM((SLOTS, 512), jnp.int32),
             pltpu.VMEM((2, SLOTS, 8, 8, 8, C), jnp.float32),
-            pltpu.SemaphoreType.DMA((10,)),
+            pltpu.SemaphoreType.DMA((14,)),
         ],
         compiler_params=pltpu.CompilerParams(vmem_limit_bytes=PACK_LIMIT),
         name="pack",

time: 63.6 us -> 63 us (level)
  no operation moved by 1% of the time
where the time goes in v10:
time: 63 us; the launch traced here: 62.6 us
  Pallas kernels  24 us (38%)
  starting transfers between devices  22.9 us (36%)
  waiting for transfers between devices  12.9 us (20%)
  other arithmetic  1.84 us (3%)
  between operations  0.86 us (1%)
    pallas_call x2, Pallas kernels, product(): pl.pallas_call(lambda *refs: product_kernel(f, *refs), out_shape=jax.Shap...  12.1 us
    all_to_all x2, starting transfers between devices, spread(): lax.all_to_all(blocks, ('gx', 'gy'), 0, 0, axis_index_groups=same_core, t...  11.5 us
    ppermute x8, starting transfers between devices, swapped(): return lax.ppermute(value, axis, pairs)  8.81 us
    all_to_all x2, waiting for transfers between devices, spread(): lax.all_to_all(blocks, ('gx', 'gy'), 0, 0, axis_index_groups=same_core, t...  6.29 us
    ppermute x8, waiting for transfers between devices, swapped(): return lax.ppermute(value, axis, pairs)  3.77 us
    pallas_call x1, Pallas kernels, pack(): pl.pallas_call(pack_kernel, out_shape=[jax.ShapeDtypeStruct((ROOM_BRICKS,...  3.01 us
    ppermute x2, waiting for transfers between devices, hopped(): return lax.ppermute(value, axis, pairs)  2.89 us
    ppermute x2, starting transfers between devices, hopped(): return lax.ppermute(value, axis, pairs)  2.58 us
  transfers between devices with their start and end apart: 12, of which 6 were waited for; matrix products, arithmetic and copies ran while one was open for 0% of the time, Pallas kernels for 28%

profile of v10, /device:TPU:0, one launch (start us, length us, event | category | flops | bytes accessed | tf_op | source)
XLA Modules:
  0.0 62.6 jit_solution(14730288124998887057)
XLA Ops:
  0.6 3.0 %pack.1 = (bf16[48,4,512,128]{3,2,1,0:T(8,128)(2,1)}, bf16[4,512,128]{2,1,0:T(8,128)(2,1)}, bf16[4,512,128]{2,1,0:T(8,128)(2,1)}, s32[12288,4,27]{2,1,0:T(4,128)...) custom-call(s32[2,4]{1,0:T(2,128)} %bitcast.13, ...), custom_call_target="tpu_custom_call" | custom-call | tf_op jit(solution)/shard_map/pack/pallas_call | solution.py:144
  3.6 1.3 %collective-permute-start = (bf16[320,128]{1,0:T(8,128)(2,1)}, bf16[320,128]{1,0:T(8,128)(2,1)S(1)}, u32[]{:S(2)}, u32[]{:S(2)}) collective-permute-start(bf16[320,128]{1,0:T(8,128)(2,1)} %get-tuple-element.39), channel_id=1, source_target_pairs={{4,12},{12,20},{20,28},{8,0},{16,8},{24,16},{5,13},{13,21},{21,29}... | collective-permute-start | bytes 245768 | tf_op jit(solution)/shard_map/ppermute | solution.py:602
  4.9 1.3 %collective-permute-start.1 = (bf16[304,128]{1,0:T(8,128)(2,1)}, bf16[304,128]{1,0:T(8,128)(2,1)S(1)}, u32[]{:S(2)}, u32[]{:S(2)}) collective-permute-start(bf16[304,128]{1,0:T(8,128)(2,1)} %get-tuple-element.47), channel_id=1, source_target_pairs={{1,3},{2,0},{5,7},{6,4},{9,11},{10,8},{13,15},{14,12},{17,19},{18,... | collective-permute-start | bytes 233480 | tf_op jit(solution)/shard_map/ppermute | solution.py:602
  6.2 0.0 copy-start.1
  6.3 0.0 copy-start
  6.3 2.0 %own_columns.1.v = bf16[4,10,64,1152]{3,2,1,0:T(8,128)(2,1)S(1)} custom-call(s32[12288,4,27]{2,1,0:T(4,128)} %get-tuple-element.40.near_hbm, bf16[48,4,512,128]{3,2,1,0:T(8,128)(2,1)} %get-tuple-element.41.act_hbm), custom_call_target="tpu_custom_call" | custom-call | flops 16777216 | bytes 6291456 | tf_op jit(solution)/shard_map/own_columns/pallas_call | solution.py:334
  8.3 0.0 copy-start.2
  8.3 0.0 copy-start.4
  8.3 2.9 %collective-permute-done.second = bf16[320,128]{1,0:T(8,128)(2,1)S(1)} collective-permute-done((bf16[320,128]{1,0:T(8,128)(2,1)}, bf16[320,128]{1,0:T(8,128)(2,1)S(1)}, u32[]{:S(2)}, u32[]{:S(2)}) %collective-permute-start) | collective-permute-done | bytes 81952 | tf_op jit(solution)/shard_map/ppermute | solution.py:602
  11.2 0.0 copy-done.1
  11.2 2.3 %collective-permute-start.2 = (bf16[384,128]{1,0:T(8,128)(2,1)S(1)}, bf16[384,128]{1,0:T(8,128)(2,1)S(1)}, u32[]{:S(2)}, u32[]{:S(2)}) collective-permute-start(bf16[384,128]{1,0:T(8,128)(2,1)S(1)} %get-tuple-element.49), channel_id=1, source_target_pairs={{0,4},{4,0},{8,12},{12,8},{16,20},{20,16},{24,28},{28,24},{1,5},{5... | collective-permute-start | bytes 294920 | tf_op jit(solution)/shard_map/ppermute | solution.py:596
  13.6 0.0 copy-done
  13.6 2.3 %inner_terms.1.inner = f32[3456,128]{1,0:T(8,128)S(1)} custom-call(bf16[4,10,64,1152]{3,2,1,0:T(8,128)(2,1)S(1)} %own_columns.1.v, bf16[4,512,128]{2,1,0:T(8,128)(2,1)S(1)} %copy-done), custom_call_target="tpu_custom_call" | custom-call | flops 1811939328 | bytes 6291456 | tf_op jit(solution)/shard_map/inner_terms/pallas_call | solution.py:359
  15.9 0.0 copy-start.3
  15.9 0.0 copy-start.5
  15.9 0.0 copy-start.6
  16.0 0.0 collective-permute-done.1.second
  16.0 0.0 copy-done.2
  16.0 1.2 %collective-permute-start.3 = (bf16[352,128]{1,0:T(8,128)(2,1)S(1)}, bf16[352,128]{1,0:T(8,128)(2,1)S(1)}, u32[]{:S(2)}, u32[]{:S(2)}) collective-permute-start(bf16[352,128]{1,0:T(8,128)(2,1)S(1)} %get-tuple-element.52), channel_id=1, source_target_pairs={{0,1},{1,0},{2,3},{3,2},{4,5},{5,4},{6,7},{7,6},{8,9},{9,8},{10,11... | collective-permute-start | bytes 270344 | tf_op jit(solution)/shard_map/ppermute | solution.py:596
  17.2 0.9 %collective-permute-done.3.y_ref.refs_5_ = bf16[352,128]{1,0:T(8,128)(2,1)S(1)} collective-permute-done((bf16[352,128]{1,0:T(8,128)(2,1)S(1)}, bf16[352,128]{1,0:T(8,128)(2,1)S(1)}, u32[]{:S(2)}, u32[]{:S(2)}) %collective-permute-start.3) | collective-permute-done | bytes 90144 | tf_op jit(solution)/shard_map/ppermute | solution.py:596
  18.1 0.0 collective-permute-done.2.x_ref.x_came.refs_4_
  18.1 0.0 copy-done.4
  18.1 2.0 %rim_terms.1 = (f32[1728,128]{1,0:T(8,128)S(1)}, f32[1728,128]{1,0:T(8,128)S(1)}) custom-call(s32[4,27]{1,0:T(4,128)S(1)} %copy-done.4, f32[3456,128]{1,0:T(8,128)S(1)} %inner_terms.1.inner, bf16[4,512,128]{2,1,0:T(8,128)(2,1)S(1)} %copy-done, bf16[384,128]{1,0:T(8,128)(2,1)S(1)} %collective-permute-done.2.x_ref.x_came.refs_4_, ...), custom_call_target="tpu_custom_call" | custom-call | flops 301989888 | bytes 6291456 | tf_op jit(solution)/shard_map/rim_terms/pallas_call | solution.py:445
  20.1 0.4 collective-permute-start.4
  20.5 2.1 %collective-permute-done.4.refs_1_ = f32[1728,128]{1,0:T(8,128)S(1)} collective-permute-done((f32[1728,128]{1,0:T(8,128)S(1)}, f32[1728,128]{1,0:T(8,128)S(1)}, u32[]{:S(2)}, u32[]{:S(2)}) %collective-permute-start.4) | collective-permute-done | bytes 884768 | tf_op jit(solution)/shard_map/ppermute | solution.py:596
  22.6 0.3 merge.1
  22.9 0.8 %convert_element_type.15 = f16[16,112,128]{2,1,0:T(8,128)(2,1)} convert(f32[16,112,128]{2,1,0:T(8,128)S(1)} %merge.1) | non-fusion elementwise | flops 229376 | bytes 1376256 | tf_op jit(solution)/shard_map/convert_element_type | solution.py:637
  23.8 6.0 %all-to-all-start = ((f16[16,112,128]{2,1,0:T(8,128)(2,1)}), f16[16,112,128]{2,1,0:T(8,128)(2,1)S(1)}, u32[]{:S(2)}, u32[]{:S(2)}) async-start(f16[16,112,128]{2,1,0:T(8,128)(2,1)} %convert_element_type.15), calls=%async_computation | async-start | bytes 917504 | tf_op jit(solution)/shard_map/all_to_all | solution.py:615
  29.8 0.1 collective-permute-start.5
  29.9 0.6 %collective-permute-start.6 = (bf16[32,128]{1,0:T(8,128)(2,1)S(1)}, bf16[32,128]{1,0:T(8,128)(2,1)S(1)}, u32[]{:S(2)}, u32[]{:S(2)}) collective-permute-start(bf16[32,128]{1,0:T(8,128)(2,1)S(1)} %get-tuple-element.62), channel_id=1, source_target_pairs={{1,2},{2,1},{5,6},{6,5},{9,10},{10,9},{13,14},{14,13},{17,18},{18,... | collective-permute-start | bytes 24584 | tf_op jit(solution)/shard_map/ppermute | solution.py:596
  30.6 1.5 %collective-permute-start.7 = (bf16[256,128]{1,0:T(8,128)(2,1)S(1)}, bf16[256,128]{1,0:T(8,128)(2,1)S(1)}, u32[]{:S(2)}, u32[]{:S(2)}) collective-permute-start(bf16[256,128]{1,0:T(8,128)(2,1)S(1)} %get-tuple-element.63), channel_id=1, source_target_pairs={{0,4},{4,0},{8,12},{12,8},{16,20},{20,16},{24,28},{28,24},{1,5},{5... | collective-permute-start | bytes 196616 | tf_op jit(solution)/shard_map/ppermute | solution.py:596
  32.1 2.6 %collective-permute-start.8 = (bf16[256,128]{1,0:T(8,128)(2,1)S(1)}, bf16[256,128]{1,0:T(8,128)(2,1)S(1)}, u32[]{:S(2)}, u32[]{:S(2)}) collective-permute-start(bf16[256,128]{1,0:T(8,128)(2,1)S(1)} %get-tuple-element.64), channel_id=1, source_target_pairs={{0,1},{1,0},{2,3},{3,2},{4,5},{5,4},{6,7},{7,6},{8,9},{9,8},{10,11... | collective-permute-start | bytes 196616 | tf_op jit(solution)/shard_map/ppermute | solution.py:596
  34.7 0.0 collective-permute-done.5.refs_6_
  34.7 0.0 collective-permute-done.6.refs_7_
  34.7 0.0 copy-done.3
  34.7 0.0 copy-done.5
  34.7 0.0 copy-done.6
  34.7 6.0 %output_product.1 = bf16[4,512,128]{2,1,0:T(8,128)(2,1)} custom-call(s32[4,27]{1,0:T(4,128)S(1)} %copy-done.4, s32[4,512]{1,0:T(4,128)S(1)} %copy-done.3, bf16[3456,128]{1,0:T(8,128)(2,1)S(1)} %bitcast.8, bf16[4,512,128]{2,1,0:T(8,128)(2,1)S(1)} %copy-done.6, bf16[384,128]{1,0:T(8,128)(2,1)S(1)} %collective-permute-done.2.x_ref.x_came.refs_4_, ...), custom_call_target="tpu_custom_call" | custom-call | flops 1811939328 | bytes 4194304 | tf_op jit(solution)/shard_map/output_product/pallas_call | solution.py:578
  40.7 0.0 collective-permute-done.7.refs_4_
  40.7 0.0 collective-permute-done.8.refs_5_
  40.7 1.1 %all-to-all-done = f16[16,112,128]{2,1,0:T(8,128)(2,1)S(1)} async-done(((f16[16,112,128]{2,1,0:T(8,128)(2,1)}), f16[16,112,128]{2,1,0:T(8,128)(2,1)S(1)}, u32[]{:S(2)}, u32[]{:S(2)}) %all-to-all-start) | async-done | bytes 458784 | tf_op jit(solution)/shard_map/all_to_all | solution.py:615
  41.8 0.1 convert_element_type.16.refs_0_
  41.9 0.3 sum_blocks.1
  42.2 0.8 %convert_element_type.17 = f16[16,112,128]{2,1,0:T(8,128)(2,1)} convert(f32[16,112,128]{2,1,0:T(8,128)S(1)} %sum_blocks.1) | non-fusion elementwise | flops 229376 | bytes 1376256 | tf_op jit(solution)/shard_map/convert_element_type | solution.py:645
  43.0 5.5 %all-to-all-start.1 = ((f16[16,112,128]{2,1,0:T(8,128)(2,1)}), f16[16,112,128]{2,1,0:T(8,128)(2,1)S(1)}, u32[]{:S(2)}, u32[]{:S(2)}) async-start(f16[16,112,128]{2,1,0:T(8,128)(2,1)} %convert_element_type.17), calls=%async_computation.1 | async-start | bytes 917504 | tf_op jit(solution)/shard_map/all_to_all | solution.py:615
  48.5 6.1 %input_grad_product.1 = bf16[4,512,128]{2,1,0:T(8,128)(2,1)} custom-call(s32[4,27]{1,0:T(4,128)S(1)} %copy-done.4, s32[4,512]{1,0:T(4,128)S(1)} %copy-done.3, bf16[3456,128]{1,0:T(8,128)(2,1)S(1)} %bitcast.9, bf16[4,512,128]{2,1,0:T(8,128)(2,1)S(1)} %copy-done, bf16[256,128]{1,0:T(8,128)(2,1)S(1)} %collective-permute-done.7.refs_4_, ...), custom_call_target="tpu_custom_call" | custom-call | flops 1811939328 | bytes 4194304 | tf_op jit(solution)/shard_map/input_grad_product/pallas_call | solution.py:578
  54.6 5.2 %all-to-all-done.1 = f16[16,112,128]{2,1,0:T(8,128)(2,1)S(1)} async-done(((f16[16,112,128]{2,1,0:T(8,128)(2,1)}), f16[16,112,128]{2,1,0:T(8,128)(2,1)S(1)}, u32[]{:S(2)}, u32[]{:S(2)}) %all-to-all-start.1) | async-done | bytes 458784 | tf_op jit(solution)/shard_map/all_to_all | solution.py:615
  59.8 0.0 collective-permute-start.9
  59.8 0.1 convert_element_type.19.refs_0_
  59.8 1.0 %decode_own.1.refs_1_ = f32[2,1728,128]{2,1,0:T(8,128)} custom-call(f32[16,112,128]{2,1,0:T(8,128)S(1)} %convert_element_type.19.refs_0_), custom_call_target="tpu_custom_call" | custom-call | tf_op jit(solution)/shard_map/decode_own/pallas_call | solution.py:540
  60.8 0.8 %collective-permute-done.9 = f16[16,112,128]{2,1,0:T(8,128)(2,1)S(1)} collective-permute-done((f16[16,112,128]{2,1,0:T(8,128)(2,1)S(1)}, f16[16,112,128]{2,1,0:T(8,128)(2,1)S(1)}, u32[]{:S(2)}, u32[]{:S(2)}) %collective-permute-start.9) | collective-permute-done | bytes 458784 | tf_op jit(solution)/shard_map/ppermute | solution.py:596
  61.6 0.1 convert_element_type.18.refs_0_
  61.7 1.0 %decode_other.1 = f32[2,1728,128]{2,1,0:T(8,128)} custom-call(f32[16,112,128]{2,1,0:T(8,128)S(1)} %convert_element_type.18.refs_0_, f32[2,1728,128]{2,1,0:T(8,128)} %decode_own.1.refs_1_), custom_call_target="tpu_custom_call", output_to_operand_aliasing={{}: (1, {})} | custom-call | tf_op jit(solution)/shard_map/decode_other/pallas_call | solution.py:540
  (3 shorter events, 0.0 us)
Async XLA Ops:
  3.6 7.6 %collective-permute-start = (bf16[320,128]{1,0:T(8,128)(2,1)}, bf16[320,128]{1,0:T(8,128)(2,1)S(1)}, u32[]{:S(2)}, u32[]{:S(2)}) collective-permute-start(bf16[320,128]{1,0:T(8,128)(2,1)} %get-tuple-element.39), channel_id=1, source_target_pairs={{4,12},{12,20},{20,28},{8,0},{16,8},{24,16},{5,13},{13,21},{21,29}... | collective-permute-start | bytes 245768 | tf_op jit(solution)/shard_map/ppermute | solution.py:602
  4.9 11.0 %collective-permute-start.1 = (bf16[304,128]{1,0:T(8,128)(2,1)}, bf16[304,128]{1,0:T(8,128)(2,1)S(1)}, u32[]{:S(2)}, u32[]{:S(2)}) collective-permute-start(bf16[304,128]{1,0:T(8,128)(2,1)} %get-tuple-element.47), channel_id=1, source_target_pairs={{1,3},{2,0},{5,7},{6,4},{9,11},{10,8},{13,15},{14,12},{17,19},{18,... | collective-permute-start | bytes 233480 | tf_op jit(solution)/shard_map/ppermute | solution.py:602
  6.2 5.0 %copy-start.1 = (bf16[320,128]{1,0:T(8,128)(2,1)S(1)}, bf16[320,128]{1,0:T(8,128)(2,1)}, u32[]{:S(2)}) copy-start(bf16[320,128]{1,0:T(8,128)(2,1)} %get-tuple-element.38.first) | copy-start | bytes 245764
  6.3 7.3 %copy-start = (bf16[4,512,128]{2,1,0:T(8,128)(2,1)S(1)}, bf16[4,512,128]{2,1,0:T(8,128)(2,1)}, u32[]{:S(2)}) copy-start(bf16[4,512,128]{2,1,0:T(8,128)(2,1)} %get-tuple-element.68.grd.refs_3_) | copy-start | bytes 1572868
  8.3 7.6 %copy-start.2 = (bf16[304,128]{1,0:T(8,128)(2,1)S(1)}, bf16[304,128]{1,0:T(8,128)(2,1)}, u32[]{:S(2)}) copy-start(bf16[304,128]{1,0:T(8,128)(2,1)} %get-tuple-element.50.first) | copy-start | bytes 233476
  8.3 9.8 %copy-start.4 = (s32[4,27]{1,0:T(4,128)S(1)}, s32[4,27]{1,0:T(4,128)}, u32[]{:S(2)}) copy-start(s32[4,27]{1,0:T(4,128)} %refs_0_.3) | copy-start | bytes 1300
  11.2 6.9 %collective-permute-start.2 = (bf16[384,128]{1,0:T(8,128)(2,1)S(1)}, bf16[384,128]{1,0:T(8,128)(2,1)S(1)}, u32[]{:S(2)}, u32[]{:S(2)}) collective-permute-start(bf16[384,128]{1,0:T(8,128)(2,1)S(1)} %get-tuple-element.49), channel_id=1, source_target_pairs={{0,4},{4,0},{8,12},{12,8},{16,20},{20,16},{24,28},{28,24},{1,5},{5... | collective-permute-start | bytes 294920 | tf_op jit(solution)/shard_map/ppermute | solution.py:596
  15.9 18.7 %copy-start.3 = (s32[4,512]{1,0:T(4,128)S(1)}, s32[4,512]{1,0:T(4,128)}, u32[]{:S(2)}) copy-start(s32[4,512]{1,0:T(4,128)} %refs_1_.3) | copy-start | bytes 24580
  15.9 18.7 %copy-start.5 = (bf16[27,128,128]{2,1,0:T(8,128)(2,1)S(1)}, bf16[27,128,128]{2,1,0:T(8,128)(2,1)}, u32[]{:S(2)}) copy-start(bf16[27,128,128]{2,1,0:T(8,128)(2,1)} %param.9) | copy-start | bytes 2654212
  15.9 18.7 %copy-start.6 = (bf16[4,512,128]{2,1,0:T(8,128)(2,1)S(1)}, bf16[4,512,128]{2,1,0:T(8,128)(2,1)}, u32[]{:S(2)}) copy-start(bf16[4,512,128]{2,1,0:T(8,128)(2,1)} %get-tuple-element.59.refs_3_) | copy-start | bytes 1572868
  16.0 2.1 %collective-permute-start.3 = (bf16[352,128]{1,0:T(8,128)(2,1)S(1)}, bf16[352,128]{1,0:T(8,128)(2,1)S(1)}, u32[]{:S(2)}, u32[]{:S(2)}) collective-permute-start(bf16[352,128]{1,0:T(8,128)(2,1)S(1)} %get-tuple-element.52), channel_id=1, source_target_pairs={{0,1},{1,0},{2,3},{3,2},{4,5},{5,4},{6,7},{7,6},{8,9},{9,8},{10,11... | collective-permute-start | bytes 270344 | tf_op jit(solution)/shard_map/ppermute | solution.py:596
  20.1 2.5 %collective-permute-start.4 = (f32[1728,128]{1,0:T(8,128)S(1)}, f32[1728,128]{1,0:T(8,128)S(1)}, u32[]{:S(2)}, u32[]{:S(2)}) collective-permute-start(f32[1728,128]{1,0:T(8,128)S(1)} %get-tuple-element.54), channel_id=1, source_target_pairs={{0,1},{1,0},{2,3},{3,2},{4,5},{5,4},{6,7},{7,6},{8,9},{9,8},{10,11... | collective-permute-start | bytes 2654216 | tf_op jit(solution)/shard_map/ppermute | solution.py:596
  23.8 18.1 %all-to-all-start = ((f16[16,112,128]{2,1,0:T(8,128)(2,1)}), f16[16,112,128]{2,1,0:T(8,128)(2,1)S(1)}, u32[]{:S(2)}, u32[]{:S(2)}) async-start(f16[16,112,128]{2,1,0:T(8,128)(2,1)} %convert_element_type.15), calls=%async_computation | async-start | bytes 917504 | tf_op jit(solution)/shard_map/all_to_all | solution.py:615
  29.8 4.9 %collective-permute-start.5 = (bf16[32,128]{1,0:T(8,128)(2,1)S(1)}, bf16[32,128]{1,0:T(8,128)(2,1)S(1)}, u32[]{:S(2)}, u32[]{:S(2)}) collective-permute-start(bf16[32,128]{1,0:T(8,128)(2,1)S(1)} %get-tuple-element.61), channel_id=1, source_target_pairs={{0,1},{1,0},{2,3},{3,2},{4,5},{5,4},{6,7},{7,6},{8,9},{9,8},{10,11... | collective-permute-start | bytes 24584 | tf_op jit(solution)/shard_map/ppermute | solution.py:596
  29.9 4.8 %collective-permute-start.6 = (bf16[32,128]{1,0:T(8,128)(2,1)S(1)}, bf16[32,128]{1,0:T(8,128)(2,1)S(1)}, u32[]{:S(2)}, u32[]{:S(2)}) collective-permute-start(bf16[32,128]{1,0:T(8,128)(2,1)S(1)} %get-tuple-element.62), channel_id=1, source_target_pairs={{1,2},{2,1},{5,6},{6,5},{9,10},{10,9},{13,14},{14,13},{17,18},{18,... | collective-permute-start | bytes 24584 | tf_op jit(solution)/shard_map/ppermute | solution.py:596
  30.6 10.1 %collective-permute-start.7 = (bf16[256,128]{1,0:T(8,128)(2,1)S(1)}, bf16[256,128]{1,0:T(8,128)(2,1)S(1)}, u32[]{:S(2)}, u32[]{:S(2)}) collective-permute-start(bf16[256,128]{1,0:T(8,128)(2,1)S(1)} %get-tuple-element.63), channel_id=1, source_target_pairs={{0,4},{4,0},{8,12},{12,8},{16,20},{20,16},{24,28},{28,24},{1,5},{5... | collective-permute-start | bytes 196616 | tf_op jit(solution)/shard_map/ppermute | solution.py:596
  32.1 8.6 %collective-permute-start.8 = (bf16[256,128]{1,0:T(8,128)(2,1)S(1)}, bf16[256,128]{1,0:T(8,128)(2,1)S(1)}, u32[]{:S(2)}, u32[]{:S(2)}) collective-permute-start(bf16[256,128]{1,0:T(8,128)(2,1)S(1)} %get-tuple-element.64), channel_id=1, source_target_pairs={{0,1},{1,0},{2,3},{3,2},{4,5},{5,4},{6,7},{7,6},{8,9},{9,8},{10,11... | collective-permute-start | bytes 196616 | tf_op jit(solution)/shard_map/ppermute | solution.py:596
  43.0 16.8 %all-to-all-start.1 = ((f16[16,112,128]{2,1,0:T(8,128)(2,1)}), f16[16,112,128]{2,1,0:T(8,128)(2,1)S(1)}, u32[]{:S(2)}, u32[]{:S(2)}) async-start(f16[16,112,128]{2,1,0:T(8,128)(2,1)} %convert_element_type.17), calls=%async_computation.1 | async-start | bytes 917504 | tf_op jit(solution)/shard_map/all_to_all | solution.py:615
  59.8 1.8 %collective-permute-start.9 = (f16[16,112,128]{2,1,0:T(8,128)(2,1)S(1)}, f16[16,112,128]{2,1,0:T(8,128)(2,1)S(1)}, u32[]{:S(2)}, u32[]{:S(2)}) collective-permute-start(f16[16,112,128]{2,1,0:T(8,128)(2,1)S(1)} %all-to-all-done.1), channel_id=1, source_target_pairs={{0,1},{1,0},{2,3},{3,2},{4,5},{5,4},{6,7},{7,6},{8,9},{9,8},{10,11... | collective-permute-start | bytes 1376264 | tf_op jit(solution)/shard_map/ppermute | solution.py:596

commit v11 on v10

--- a/solution.py
+++ b/solution.py
@@ -66,7 +66,7 @@
     return up, jnp.where(same, cells, 0.0), down
 
 
-def pack_kernel(face_hbm, edge_hbm, near_hbm, feat_hbm, grad_hbm, mask_hbm, held_out, act_out, grd_out, near_out, *refs):
+def pack_kernel(face_hbm, edge_hbm, near_hbm, feat_hbm, grad_hbm, mask_hbm, act_out, grd_out, near_out, *refs):
     sends = refs[0:4]
     y_out, x_out = refs[4:6], refs[6:8]
     face_ref, edge_ref, near, raw, mask_ref, full, sems = refs[8:]
@@ -88,8 +88,7 @@
             full[f, s] = masked.reshape(8, 8, 8, C)
             raw[f, s] = masked.astype(jnp.bfloat16)
     results = fetching(
-        (raw.at[0], held_out.at[0], sems.at[7]),
-        (raw.at[0], act_out, sems.at[8]),
+        (raw.at[0], act_out.at[0], sems.at[7]),
         (raw.at[1], grd_out, sems.at[9]),
     )
     for table in tables:
@@ -146,12 +145,11 @@
         out_shape=[
             jax.ShapeDtypeStruct((ROOM_BRICKS, SLOTS, 512, C), jnp.bfloat16),
             jax.ShapeDtypeStruct((SLOTS, 512, C), jnp.bfloat16),
-            jax.ShapeDtypeStruct((SLOTS, 512, C), jnp.bfloat16),
             jax.ShapeDtypeStruct((ROOM_TABLES, SLOTS, 27), jnp.int32),
         ]
         + sends,
         in_specs=[hbm()] * 6,
-        out_specs=[hbm()] * 8,
+        out_specs=[hbm()] * 7,
         scratch_shapes=[pltpu.VMEM(send.shape, send.dtype) for send in sends]
         + [
             pltpu.SMEM((FACE, 4), jnp.int32),
@@ -550,11 +548,14 @@
 
 
 def product_kernel(f, near_hbm, mask_ref, kernel_ref, bricks, x_ref, y_ref, e0, e1, out, *refs):
-    lx, ly, corners, wide, near, sem, v, *flipped = refs
+    lx, ly, corners, wide, near, sem, v, *more = refs
     (table,) = fetching((near_hbm, near, sem))
     weights = kernel_ref
-    if f == 1:
-        weights = flipped[0]
+    if f == 0:
+        fetched((bricks.at[0], more[0], more[1]))
+        bricks = more[0]
+    else:
+        weights = more[0]
         for o in range(27):
             weights[pl.ds((26 - o) * C, C)] = kernel_ref[pl.ds(o * C, C)].T
     fill_own(bricks, lx, ly, corners)
@@ -578,11 +579,15 @@
     return pl.pallas_call(
         lambda *refs: product_kernel(f, *refs),
         out_shape=jax.ShapeDtypeStruct((SLOTS, 512, C), jnp.bfloat16),
-        in_specs=[hbm()] + [vmem()] * 7,
+        in_specs=[hbm()] + [vmem()] * 2 + [vmem() if f else hbm()] + [vmem()] * 4,
         out_specs=vmem(),
         scratch_shapes=columns_scratch()
         + [pltpu.VMEM((SLOTS, 10, 64, 9 * C), jnp.bfloat16)]
-        + ([pltpu.VMEM((ROWS, C), jnp.bfloat16)] if f else []),
+        + (
+            [pltpu.VMEM((ROWS, C), jnp.bfloat16)]
+            if f
+            else [pltpu.VMEM((SLOTS, 512, C), jnp.bfloat16), pltpu.SemaphoreType.DMA(())]
+        ),
         compiler_params=pltpu.CompilerParams(vmem_limit_bytes=VMEM_LIMIT),
         cost_estimate=pl.CostEstimate(flops=2 * 2048 * ROWS * C, bytes_accessed=4 << 20, transcendentals=0),
         name=("output_product", "input_grad_product")[f],
@@ -608,13 +613,18 @@
     groups = parts // 2
     take = -(-HALF // groups)
     held = -(-(take + 1) // 16) * 16
-    order = [(i + parts // 2) % parts for i in range(parts)]
-    same_core = [[i for i in order if i % size_y % 2 == core] for core in range(2)]
+    same_core = []
+    for core in range(2):
+        members = [i for i in range(parts) if i % size_y % 2 == core]
+        low, high = members[: groups // 2], members[groups // 2 :]
+        per_chip_row = size_y // 2
+        low = [i for first in range(groups // 2 - per_chip_row, -1, -per_chip_row) for i in low[first : first + per_chip_row]]
+        same_core.append([i for pair in zip(high, low) for i in pair])
 
     def spread(blocks):
         return lax.all_to_all(blocks, ("gx", "gy"), 0, 0, axis_index_groups=same_core, tiled=True)
 
-    held_act, act, grd, table, y0, y1, x0, x1 = pack(
+    act, grd, table, y0, y1, x0, x1 = pack(
         features.reshape(SLOTS, 512, C),
         out_grad.reshape(SLOTS, 512, C),
         voxel_mask,
@@ -624,7 +634,7 @@
     )
     y1 = hopped(y1, "gy")
     x1 = hopped(x1, "gx")
-    v = own_columns(table, held_act)
+    v = own_columns(table, act)
     x1, v = lax.optimization_barrier((x1, v))
     x_came, x_more = join(x0, x1)
     x_more, v = lax.optimization_barrier((x_more, v))

time: 63 us -> 63.4 us (level)
  transfers between devices with their start and end apart: 12 -> 12, of which waited for: 6 -> 6; matrix products, arithmetic and copies ran while one was open for 0% -> 0% of each run, Pallas kernels for 28% -> 29%
where the time goes in v11:
time: 63.4 us; the launch traced here: 62.9 us
  Pallas kernels  24.3 us (38%)
  starting transfers between devices  23.5 us (37%)
  waiting for transfers between devices  12.4 us (20%)
  other arithmetic  1.84 us (3%)
  between operations  0.85 us (1%)
    pallas_call x2, Pallas kernels, product(): pl.pallas_call(lambda *refs: product_kernel(f, *refs), out_shape=jax.Shap...  12.6 us
    all_to_all x2, starting transfers between devices, spread(): lax.all_to_all(blocks, ('gx', 'gy'), 0, 0, axis_index_groups=same_core, t...  12.1 us
    ppermute x8, starting transfers between devices, swapped(): return lax.ppermute(value, axis, pairs)  8.8 us
    all_to_all x2, waiting for transfers between devices, spread(): lax.all_to_all(blocks, ('gx', 'gy'), 0, 0, axis_index_groups=same_core, t...  5.7 us
    ppermute x8, waiting for transfers between devices, swapped(): return lax.ppermute(value, axis, pairs)  3.78 us
    ppermute x2, waiting for transfers between devices, hopped(): return lax.ppermute(value, axis, pairs)  2.89 us
    pallas_call x1, Pallas kernels, pack(): pl.pallas_call(pack_kernel, out_shape=[jax.ShapeDtypeStruct((ROOM_BRICKS,...  2.84 us
    ppermute x2, starting transfers between devices, hopped(): return lax.ppermute(value, axis, pairs)  2.58 us
  transfers between devices with their start and end apart: 12, of which 6 were waited for; matrix products, arithmetic and copies ran while one was open for 0% of the time, Pallas kernels for 29%

profile of v11, /device:TPU:0, one launch (start us, length us, event | category | flops | bytes accessed | tf_op | source)
XLA Modules:
  0.0 62.9 jit_solution(9763788617273708013)
XLA Ops:
  0.6 2.8 %pack.1 = (bf16[48,4,512,128]{3,2,1,0:T(8,128)(2,1)}, bf16[4,512,128]{2,1,0:T(8,128)(2,1)}, s32[12288,4,27]{2,1,0:T(4,128)}, bf16[304,128]{1,0:T(8,128)(2,1)}, b...) custom-call(s32[2,4]{1,0:T(2,128)} %bitcast.14, s32[1,4]{1,0:T(1,128)} %bitcast.15, ...), custom_call_target="tpu_custom_call" | custom-call | tf_op jit(solution)/shard_map/pack/pallas_call | solution.py:143
  3.5 1.3 %collective-permute-start = (bf16[320,128]{1,0:T(8,128)(2,1)}, bf16[320,128]{1,0:T(8,128)(2,1)S(1)}, u32[]{:S(2)}, u32[]{:S(2)}) collective-permute-start(bf16[320,128]{1,0:T(8,128)(2,1)} %get-tuple-element.38), channel_id=1, source_target_pairs={{4,12},{12,20},{20,28},{8,0},{16,8},{24,16},{5,13},{13,21},{21,29}... | collective-permute-start | bytes 245768 | tf_op jit(solution)/shard_map/ppermute | solution.py:607
  4.8 1.3 %collective-permute-start.1 = (bf16[304,128]{1,0:T(8,128)(2,1)}, bf16[304,128]{1,0:T(8,128)(2,1)S(1)}, u32[]{:S(2)}, u32[]{:S(2)}) collective-permute-start(bf16[304,128]{1,0:T(8,128)(2,1)} %get-tuple-element.46), channel_id=1, source_target_pairs={{1,3},{2,0},{5,7},{6,4},{9,11},{10,8},{13,15},{14,12},{17,19},{18,... | collective-permute-start | bytes 233480 | tf_op jit(solution)/shard_map/ppermute | solution.py:607
  6.1 0.0 copy-start.2
  6.1 0.0 copy-start
  6.1 2.0 %own_columns.1.v = bf16[4,10,64,1152]{3,2,1,0:T(8,128)(2,1)S(1)} custom-call(s32[12288,4,27]{2,1,0:T(4,128)} %get-tuple-element.39.near_hbm, bf16[48,4,512,128]{3,2,1,0:T(8,128)(2,1)} %get-tuple-element.57.act_hbm.refs_3_), custom_call_target="tpu_custom_call" | custom-call | flops 16777216 | bytes 6291456 | tf_op jit(solution)/shard_map/own_columns/pallas_call | solution.py:332
  8.1 0.0 copy-start.3
  8.2 0.0 copy-start.5
  8.2 2.9 %collective-permute-done.second = bf16[320,128]{1,0:T(8,128)(2,1)S(1)} collective-permute-done((bf16[320,128]{1,0:T(8,128)(2,1)}, bf16[320,128]{1,0:T(8,128)(2,1)S(1)}, u32[]{:S(2)}, u32[]{:S(2)}) %collective-permute-start) | collective-permute-done | bytes 81952 | tf_op jit(solution)/shard_map/ppermute | solution.py:607
  11.1 0.0 copy-done.2
  11.1 2.3 %collective-permute-start.2 = (bf16[384,128]{1,0:T(8,128)(2,1)S(1)}, bf16[384,128]{1,0:T(8,128)(2,1)S(1)}, u32[]{:S(2)}, u32[]{:S(2)}) collective-permute-start(bf16[384,128]{1,0:T(8,128)(2,1)S(1)} %get-tuple-element.48), channel_id=1, source_target_pairs={{0,4},{4,0},{8,12},{12,8},{16,20},{20,16},{24,28},{28,24},{1,5},{5... | collective-permute-start | bytes 294920 | tf_op jit(solution)/shard_map/ppermute | solution.py:601
  13.4 0.0 copy-done
  13.4 2.3 %inner_terms.1.inner = f32[3456,128]{1,0:T(8,128)S(1)} custom-call(bf16[4,10,64,1152]{3,2,1,0:T(8,128)(2,1)S(1)} %own_columns.1.v, bf16[4,512,128]{2,1,0:T(8,128)(2,1)S(1)} %copy-done), custom_call_target="tpu_custom_call" | custom-call | flops 1811939328 | bytes 6291456 | tf_op jit(solution)/shard_map/inner_terms/pallas_call | solution.py:357
  15.7 0.0 copy-start.1
  15.8 0.0 copy-start.4
  15.8 0.0 collective-permute-done.1.second
  15.8 0.0 copy-done.3
  15.8 1.2 %collective-permute-start.3 = (bf16[352,128]{1,0:T(8,128)(2,1)S(1)}, bf16[352,128]{1,0:T(8,128)(2,1)S(1)}, u32[]{:S(2)}, u32[]{:S(2)}) collective-permute-start(bf16[352,128]{1,0:T(8,128)(2,1)S(1)} %get-tuple-element.51), channel_id=1, source_target_pairs={{0,1},{1,0},{2,3},{3,2},{4,5},{5,4},{6,7},{7,6},{8,9},{9,8},{10,11... | collective-permute-start | bytes 270344 | tf_op jit(solution)/shard_map/ppermute | solution.py:601
  17.0 0.9 %collective-permute-done.3.y_ref.refs_5_ = bf16[352,128]{1,0:T(8,128)(2,1)S(1)} collective-permute-done((bf16[352,128]{1,0:T(8,128)(2,1)S(1)}, bf16[352,128]{1,0:T(8,128)(2,1)S(1)}, u32[]{:S(2)}, u32[]{:S(2)}) %collective-permute-start.3) | collective-permute-done | bytes 90144 | tf_op jit(solution)/shard_map/ppermute | solution.py:601
  17.9 0.0 collective-permute-done.2.x_ref.x_came.refs_4_
  17.9 0.0 copy-done.5
  17.9 2.0 %rim_terms.1 = (f32[1728,128]{1,0:T(8,128)S(1)}, f32[1728,128]{1,0:T(8,128)S(1)}) custom-call(s32[4,27]{1,0:T(4,128)S(1)} %copy-done.5, f32[3456,128]{1,0:T(8,128)S(1)} %inner_terms.1.inner, bf16[4,512,128]{2,1,0:T(8,128)(2,1)S(1)} %copy-done, bf16[384,128]{1,0:T(8,128)(2,1)S(1)} %collective-permute-done.2.x_ref.x_came.refs_4_, ...), custom_call_target="tpu_custom_call" | custom-call | flops 301989888 | bytes 6291456 | tf_op jit(solution)/shard_map/rim_terms/pallas_call | solution.py:443
  19.9 0.4 collective-permute-start.4
  20.3 2.1 %collective-permute-done.4.refs_1_ = f32[1728,128]{1,0:T(8,128)S(1)} collective-permute-done((f32[1728,128]{1,0:T(8,128)S(1)}, f32[1728,128]{1,0:T(8,128)S(1)}, u32[]{:S(2)}, u32[]{:S(2)}) %collective-permute-start.4) | collective-permute-done | bytes 884768 | tf_op jit(solution)/shard_map/ppermute | solution.py:601
  22.4 0.3 merge.1
  22.7 0.8 %convert_element_type.15 = f16[16,112,128]{2,1,0:T(8,128)(2,1)} convert(f32[16,112,128]{2,1,0:T(8,128)S(1)} %merge.1) | non-fusion elementwise | flops 229376 | bytes 1376256 | tf_op jit(solution)/shard_map/convert_element_type | solution.py:647
  23.6 6.0 %all-to-all-start = ((f16[16,112,128]{2,1,0:T(8,128)(2,1)}), f16[16,112,128]{2,1,0:T(8,128)(2,1)S(1)}, u32[]{:S(2)}, u32[]{:S(2)}) async-start(f16[16,112,128]{2,1,0:T(8,128)(2,1)} %convert_element_type.15), calls=%async_computation | async-start | bytes 917504 | tf_op jit(solution)/shard_map/all_to_all | solution.py:625
  29.6 0.1 collective-permute-start.5
  29.8 0.6 %collective-permute-start.6 = (bf16[32,128]{1,0:T(8,128)(2,1)S(1)}, bf16[32,128]{1,0:T(8,128)(2,1)S(1)}, u32[]{:S(2)}, u32[]{:S(2)}) collective-permute-start(bf16[32,128]{1,0:T(8,128)(2,1)S(1)} %get-tuple-element.60), channel_id=1, source_target_pairs={{1,2},{2,1},{5,6},{6,5},{9,10},{10,9},{13,14},{14,13},{17,18},{18,... | collective-permute-start | bytes 24584 | tf_op jit(solution)/shard_map/ppermute | solution.py:601
  30.4 1.5 %collective-permute-start.7 = (bf16[256,128]{1,0:T(8,128)(2,1)S(1)}, bf16[256,128]{1,0:T(8,128)(2,1)S(1)}, u32[]{:S(2)}, u32[]{:S(2)}) collective-permute-start(bf16[256,128]{1,0:T(8,128)(2,1)S(1)} %get-tuple-element.61), channel_id=1, source_target_pairs={{0,4},{4,0},{8,12},{12,8},{16,20},{20,16},{24,28},{28,24},{1,5},{5... | collective-permute-start | bytes 196616 | tf_op jit(solution)/shard_map/ppermute | solution.py:601
  31.9 2.6 %collective-permute-start.8 = (bf16[256,128]{1,0:T(8,128)(2,1)S(1)}, bf16[256,128]{1,0:T(8,128)(2,1)S(1)}, u32[]{:S(2)}, u32[]{:S(2)}) collective-permute-start(bf16[256,128]{1,0:T(8,128)(2,1)S(1)} %get-tuple-element.62), channel_id=1, source_target_pairs={{0,1},{1,0},{2,3},{3,2},{4,5},{5,4},{6,7},{7,6},{8,9},{9,8},{10,11... | collective-permute-start | bytes 196616 | tf_op jit(solution)/shard_map/ppermute | solution.py:601
  34.5 0.0 collective-permute-done.5.refs_6_
  34.5 0.0 collective-permute-done.6.refs_7_
  34.5 0.0 copy-done.1
  34.5 0.0 copy-done.4
  34.5 6.5 %output_product.1 = bf16[4,512,128]{2,1,0:T(8,128)(2,1)} custom-call(s32[4,27]{1,0:T(4,128)S(1)} %copy-done.5, s32[4,512]{1,0:T(4,128)S(1)} %copy-done.4, bf16[3456,128]{1,0:T(8,128)(2,1)S(1)} %bitcast.8, bf16[48,4,512,128]{3,2,1,0:T(8,128)(2,1)} %get-tuple-element.57.act_hbm.refs_3_, bf16[384,128]{1,0:T(8,128)(2,1)S(1)} %collective-permute-done.2.x_ref.x_came.refs_4_, ...), custom_call_target="tpu_custom_call" | custom-call | flops 1811939328 | bytes 4194304 | tf_op jit(solution)/shard_map/output_product/pallas_call | solution.py:579
  41.0 0.0 collective-permute-done.7.refs_4_
  41.0 0.0 collective-permute-done.8.refs_5_
  41.1 0.3 all-to-all-done
  41.4 0.1 convert_element_type.16.refs_0_
  41.5 0.3 sum_blocks.1
  41.7 0.8 %convert_element_type.17 = f16[16,112,128]{2,1,0:T(8,128)(2,1)} convert(f32[16,112,128]{2,1,0:T(8,128)S(1)} %sum_blocks.1) | non-fusion elementwise | flops 229376 | bytes 1376256 | tf_op jit(solution)/shard_map/convert_element_type | solution.py:655
  42.6 6.1 %all-to-all-start.1 = ((f16[16,112,128]{2,1,0:T(8,128)(2,1)}), f16[16,112,128]{2,1,0:T(8,128)(2,1)S(1)}, u32[]{:S(2)}, u32[]{:S(2)}) async-start(f16[16,112,128]{2,1,0:T(8,128)(2,1)} %convert_element_type.17), calls=%async_computation.1 | async-start | bytes 917504 | tf_op jit(solution)/shard_map/all_to_all | solution.py:625
  48.6 6.1 %input_grad_product.1 = bf16[4,512,128]{2,1,0:T(8,128)(2,1)} custom-call(s32[4,27]{1,0:T(4,128)S(1)} %copy-done.5, s32[4,512]{1,0:T(4,128)S(1)} %copy-done.4, bf16[3456,128]{1,0:T(8,128)(2,1)S(1)} %bitcast.9, bf16[4,512,128]{2,1,0:T(8,128)(2,1)S(1)} %copy-done, bf16[256,128]{1,0:T(8,128)(2,1)S(1)} %collective-permute-done.7.refs_4_, ...), custom_call_target="tpu_custom_call" | custom-call | flops 1811939328 | bytes 4194304 | tf_op jit(solution)/shard_map/input_grad_product/pallas_call | solution.py:579
  54.7 5.4 %all-to-all-done.1 = f16[16,112,128]{2,1,0:T(8,128)(2,1)S(1)} async-done(((f16[16,112,128]{2,1,0:T(8,128)(2,1)}), f16[16,112,128]{2,1,0:T(8,128)(2,1)S(1)}, u32[]{:S(2)}, u32[]{:S(2)}) %all-to-all-start.1) | async-done | bytes 458784 | tf_op jit(solution)/shard_map/all_to_all | solution.py:625
  60.1 0.0 collective-permute-start.9
  60.1 0.1 convert_element_type.19.refs_0_
  60.1 1.0 %decode_own.1.refs_1_ = f32[2,1728,128]{2,1,0:T(8,128)} custom-call(f32[16,112,128]{2,1,0:T(8,128)S(1)} %convert_element_type.19.refs_0_), custom_call_target="tpu_custom_call" | custom-call | tf_op jit(solution)/shard_map/decode_own/pallas_call | solution.py:538
  61.1 0.8 %collective-permute-done.9 = f16[16,112,128]{2,1,0:T(8,128)(2,1)S(1)} collective-permute-done((f16[16,112,128]{2,1,0:T(8,128)(2,1)S(1)}, f16[16,112,128]{2,1,0:T(8,128)(2,1)S(1)}, u32[]{:S(2)}, u32[]{:S(2)}) %collective-permute-start.9) | collective-permute-done | bytes 458784 | tf_op jit(solution)/shard_map/ppermute | solution.py:601
  61.9 0.1 convert_element_type.18.refs_0_
  61.9 1.0 %decode_other.1 = f32[2,1728,128]{2,1,0:T(8,128)} custom-call(f32[16,112,128]{2,1,0:T(8,128)S(1)} %convert_element_type.18.refs_0_, f32[2,1728,128]{2,1,0:T(8,128)} %decode_own.1.refs_1_), custom_call_target="tpu_custom_call", output_to_operand_aliasing={{}: (1, {})} | custom-call | tf_op jit(solution)/shard_map/decode_other/pallas_call | solution.py:538
  (3 shorter events, 0.0 us)
Async XLA Ops:
  3.5 7.6 %collective-permute-start = (bf16[320,128]{1,0:T(8,128)(2,1)}, bf16[320,128]{1,0:T(8,128)(2,1)S(1)}, u32[]{:S(2)}, u32[]{:S(2)}) collective-permute-start(bf16[320,128]{1,0:T(8,128)(2,1)} %get-tuple-element.38), channel_id=1, source_target_pairs={{4,12},{12,20},{20,28},{8,0},{16,8},{24,16},{5,13},{13,21},{21,29}... | collective-permute-start | bytes 245768 | tf_op jit(solution)/shard_map/ppermute | solution.py:607
  4.8 11.0 %collective-permute-start.1 = (bf16[304,128]{1,0:T(8,128)(2,1)}, bf16[304,128]{1,0:T(8,128)(2,1)S(1)}, u32[]{:S(2)}, u32[]{:S(2)}) collective-permute-start(bf16[304,128]{1,0:T(8,128)(2,1)} %get-tuple-element.46), channel_id=1, source_target_pairs={{1,3},{2,0},{5,7},{6,4},{9,11},{10,8},{13,15},{14,12},{17,19},{18,... | collective-permute-start | bytes 233480 | tf_op jit(solution)/shard_map/ppermute | solution.py:607
  6.1 5.0 %copy-start.2 = (bf16[320,128]{1,0:T(8,128)(2,1)S(1)}, bf16[320,128]{1,0:T(8,128)(2,1)}, u32[]{:S(2)}) copy-start(bf16[320,128]{1,0:T(8,128)(2,1)} %get-tuple-element.37.first) | copy-start | bytes 245764
  6.1 7.3 %copy-start = (bf16[4,512,128]{2,1,0:T(8,128)(2,1)S(1)}, bf16[4,512,128]{2,1,0:T(8,128)(2,1)}, u32[]{:S(2)}) copy-start(bf16[4,512,128]{2,1,0:T(8,128)(2,1)} %get-tuple-element.66.grd.refs_3_) | copy-start | bytes 1572868
  8.1 7.6 %copy-start.3 = (bf16[304,128]{1,0:T(8,128)(2,1)S(1)}, bf16[304,128]{1,0:T(8,128)(2,1)}, u32[]{:S(2)}) copy-start(bf16[304,128]{1,0:T(8,128)(2,1)} %get-tuple-element.49.first) | copy-start | bytes 233476
  8.2 9.8 %copy-start.5 = (s32[4,27]{1,0:T(4,128)S(1)}, s32[4,27]{1,0:T(4,128)}, u32[]{:S(2)}) copy-start(s32[4,27]{1,0:T(4,128)} %refs_0_.3) | copy-start | bytes 1300
  11.1 6.9 %collective-permute-start.2 = (bf16[384,128]{1,0:T(8,128)(2,1)S(1)}, bf16[384,128]{1,0:T(8,128)(2,1)S(1)}, u32[]{:S(2)}, u32[]{:S(2)}) collective-permute-start(bf16[384,128]{1,0:T(8,128)(2,1)S(1)} %get-tuple-element.48), channel_id=1, source_target_pairs={{0,4},{4,0},{8,12},{12,8},{16,20},{20,16},{24,28},{28,24},{1,5},{5... | collective-permute-start | bytes 294920 | tf_op jit(solution)/shard_map/ppermute | solution.py:601
  15.7 18.7 %copy-start.1 = (bf16[27,128,128]{2,1,0:T(8,128)(2,1)S(1)}, bf16[27,128,128]{2,1,0:T(8,128)(2,1)}, u32[]{:S(2)}) copy-start(bf16[27,128,128]{2,1,0:T(8,128)(2,1)} %param.9) | copy-start | bytes 2654212
  15.8 18.7 %copy-start.4 = (s32[4,512]{1,0:T(4,128)S(1)}, s32[4,512]{1,0:T(4,128)}, u32[]{:S(2)}) copy-start(s32[4,512]{1,0:T(4,128)} %refs_1_.3) | copy-start | bytes 24580
  15.8 2.1 %collective-permute-start.3 = (bf16[352,128]{1,0:T(8,128)(2,1)S(1)}, bf16[352,128]{1,0:T(8,128)(2,1)S(1)}, u32[]{:S(2)}, u32[]{:S(2)}) collective-permute-start(bf16[352,128]{1,0:T(8,128)(2,1)S(1)} %get-tuple-element.51), channel_id=1, source_target_pairs={{0,1},{1,0},{2,3},{3,2},{4,5},{5,4},{6,7},{7,6},{8,9},{9,8},{10,11... | collective-permute-start | bytes 270344 | tf_op jit(solution)/shard_map/ppermute | solution.py:601
  19.9 2.5 %collective-permute-start.4 = (f32[1728,128]{1,0:T(8,128)S(1)}, f32[1728,128]{1,0:T(8,128)S(1)}, u32[]{:S(2)}, u32[]{:S(2)}) collective-permute-start(f32[1728,128]{1,0:T(8,128)S(1)} %get-tuple-element.53), channel_id=1, source_target_pairs={{0,1},{1,0},{2,3},{3,2},{4,5},{5,4},{6,7},{7,6},{8,9},{9,8},{10,11... | collective-permute-start | bytes 2654216 | tf_op jit(solution)/shard_map/ppermute | solution.py:601
  23.6 17.8 %all-to-all-start = ((f16[16,112,128]{2,1,0:T(8,128)(2,1)}), f16[16,112,128]{2,1,0:T(8,128)(2,1)S(1)}, u32[]{:S(2)}, u32[]{:S(2)}) async-start(f16[16,112,128]{2,1,0:T(8,128)(2,1)} %convert_element_type.15), calls=%async_computation | async-start | bytes 917504 | tf_op jit(solution)/shard_map/all_to_all | solution.py:625
  29.6 4.9 %collective-permute-start.5 = (bf16[32,128]{1,0:T(8,128)(2,1)S(1)}, bf16[32,128]{1,0:T(8,128)(2,1)S(1)}, u32[]{:S(2)}, u32[]{:S(2)}) collective-permute-start(bf16[32,128]{1,0:T(8,128)(2,1)S(1)} %get-tuple-element.59), channel_id=1, source_target_pairs={{0,1},{1,0},{2,3},{3,2},{4,5},{5,4},{6,7},{7,6},{8,9},{9,8},{10,11... | collective-permute-start | bytes 24584 | tf_op jit(solution)/shard_map/ppermute | solution.py:601
  29.8 4.7 %collective-permute-start.6 = (bf16[32,128]{1,0:T(8,128)(2,1)S(1)}, bf16[32,128]{1,0:T(8,128)(2,1)S(1)}, u32[]{:S(2)}, u32[]{:S(2)}) collective-permute-start(bf16[32,128]{1,0:T(8,128)(2,1)S(1)} %get-tuple-element.60), channel_id=1, source_target_pairs={{1,2},{2,1},{5,6},{6,5},{9,10},{10,9},{13,14},{14,13},{17,18},{18,... | collective-permute-start | bytes 24584 | tf_op jit(solution)/shard_map/ppermute | solution.py:601
  30.4 10.6 %collective-permute-start.7 = (bf16[256,128]{1,0:T(8,128)(2,1)S(1)}, bf16[256,128]{1,0:T(8,128)(2,1)S(1)}, u32[]{:S(2)}, u32[]{:S(2)}) collective-permute-start(bf16[256,128]{1,0:T(8,128)(2,1)S(1)} %get-tuple-element.61), channel_id=1, source_target_pairs={{0,4},{4,0},{8,12},{12,8},{16,20},{20,16},{24,28},{28,24},{1,5},{5... | collective-permute-start | bytes 196616 | tf_op jit(solution)/shard_map/ppermute | solution.py:601
  31.9 9.1 %collective-permute-start.8 = (bf16[256,128]{1,0:T(8,128)(2,1)S(1)}, bf16[256,128]{1,0:T(8,128)(2,1)S(1)}, u32[]{:S(2)}, u32[]{:S(2)}) collective-permute-start(bf16[256,128]{1,0:T(8,128)(2,1)S(1)} %get-tuple-element.62), channel_id=1, source_target_pairs={{0,1},{1,0},{2,3},{3,2},{4,5},{5,4},{6,7},{7,6},{8,9},{9,8},{10,11... | collective-permute-start | bytes 196616 | tf_op jit(solution)/shard_map/ppermute | solution.py:601
  42.6 17.5 %all-to-all-start.1 = ((f16[16,112,128]{2,1,0:T(8,128)(2,1)}), f16[16,112,128]{2,1,0:T(8,128)(2,1)S(1)}, u32[]{:S(2)}, u32[]{:S(2)}) async-start(f16[16,112,128]{2,1,0:T(8,128)(2,1)} %convert_element_type.17), calls=%async_computation.1 | async-start | bytes 917504 | tf_op jit(solution)/shard_map/all_to_all | solution.py:625
  60.1 1.8 %collective-permute-start.9 = (f16[16,112,128]{2,1,0:T(8,128)(2,1)S(1)}, f16[16,112,128]{2,1,0:T(8,128)(2,1)S(1)}, u32[]{:S(2)}, u32[]{:S(2)}) collective-permute-start(f16[16,112,128]{2,1,0:T(8,128)(2,1)S(1)} %all-to-all-done.1), channel_id=1, source_target_pairs={{0,1},{1,0},{2,3},{3,2},{4,5},{5,4},{6,7},{7,6},{8,9},{9,8},{10,11... | collective-permute-start | bytes 1376264 | tf_op jit(solution)/shard_map/ppermute | solution.py:601

commit v12 on v10

--- a/solution.py
+++ b/solution.py
@@ -514,7 +514,7 @@
     )(blocks)
 
 
-def decode_kernel(take, scale, own, blocks, *refs):
+def decode_kernel(take, scale, places, own, blocks, *refs):
     out, half, sems = refs[-3:]
     groups = blocks.shape[0]
     core = parity("gy")
@@ -524,8 +524,8 @@
     for p in range(groups):
         rows = min(take, HALF - p * take)
         if rows > 0:
-            factor = jnp.exp2(blocks[p, pl.ds(take, 1)] - 14.0) * scale
-            half[pl.ds(p * take, rows)] = blocks[p, pl.ds(0, rows)] * factor
+            factor = jnp.exp2(blocks[places[p], pl.ds(take, 1)] - 14.0) * scale
+            half[pl.ds(p * take, rows)] = blocks[places[p], pl.ds(0, rows)] * factor
         ready = min((p + 1) * take, HALF)
         if ready - done >= HALF // 4 and ready % 8 == 0 or p == groups - 1:
             piece = pl.ds(done, ready - done)
@@ -535,10 +535,10 @@
         copy.wait()
 
 
-def decode(take, scale, blocks, begun=None):
+def decode(take, scale, places, blocks, begun=None):
     rest = () if begun is None else (begun,)
     return pl.pallas_call(
-        lambda *refs: decode_kernel(take, scale, not rest, *refs),
+        lambda *refs: decode_kernel(take, scale, places, not rest, *refs),
         out_shape=jax.ShapeDtypeStruct((2, HALF, C), jnp.float32),
         in_specs=[vmem()] + [hbm()] * len(rest),
         out_specs=hbm(),
@@ -608,10 +608,15 @@
     groups = parts // 2
     take = -(-HALF // groups)
     held = -(-(take + 1) // 16) * 16
-    order = [(i + parts // 2) % parts for i in range(parts)]
-    same_core = [[i for i in order if i % size_y % 2 == core] for core in range(2)]
-
-    def spread(blocks):
+    members = [[i for i in range(parts) if i % size_y % 2 == core] for core in range(2)]
+    half, row = groups // 2, size_y // 2
+    inward = [k + j for k in range(half - row, -1, -row) for j in range(row)]
+    in_turn = [k for pair in zip(range(half, groups), inward) for k in pair]
+    onward = [(k + half) % groups for k in range(groups)]
+    places = [onward.index(k) for k in in_turn]
+
+    def spread(blocks, order):
+        same_core = [[core[k] for k in order] for core in members]
         return lax.all_to_all(blocks, ("gx", "gy"), 0, 0, axis_index_groups=same_core, tiled=True)
 
     held_act, act, grd, table, y0, y1, x0, x1 = pack(
@@ -641,15 +646,15 @@
     e0, e1 = forward_corners(x_came)
     edges = [swapped(e0, "gy", 0), swapped(e1, "gy", 1)]
     output = product(0, neighbours, voxel_mask, rows, act, x_came, y_came, edges)
-    arrived, output, x_more, y_more = lax.optimization_barrier((spread(blocks), output, x_more, y_more))
+    arrived, output, x_more, y_more = lax.optimization_barrier((spread(blocks, in_turn), output, x_more, y_more))
     copies = sum_blocks(take, arrived.astype(jnp.float32)).astype(jnp.float16)
     copies, grd = lax.optimization_barrier((copies, grd))
     input_grad = product(1, neighbours, voxel_mask, rows, grd, x_more, y_more, edges)
-    mine, input_grad = lax.optimization_barrier((spread(copies), input_grad))
+    mine, input_grad = lax.optimization_barrier((spread(copies, onward), input_grad))
     other = swapped(mine, "gy", 0)
     scale = 1.0 / math.sqrt(parts * SLOTS * 512)
-    weight = decode(take, scale, mine.astype(jnp.float32))
-    weight = decode(take, scale, other.astype(jnp.float32), weight)
+    weight = decode(take, scale, places, mine.astype(jnp.float32))
+    weight = decode(take, scale, places, other.astype(jnp.float32), weight)
     shape = (SLOTS, 8, 8, 8, C)
     return output.reshape(shape), input_grad.reshape(shape), weight.reshape(27, C, C)
 

time: 63 us -> 63.3 us (level)
  no operation moved by 1% of the time
where the time goes in v12:
time: 63.3 us; the launch traced here: 62.9 us
  Pallas kernels  24 us (38%)
  starting transfers between devices  23.4 us (37%)
  waiting for transfers between devices  12.7 us (20%)
  other arithmetic  1.84 us (3%)
  between operations  0.86 us (1%)
    pallas_call x2, Pallas kernels, product(): pl.pallas_call(lambda *refs: product_kernel(f, *refs), out_shape=jax.Shap...  12.1 us
    all_to_all x2, starting transfers between devices, spread(): lax.all_to_all(blocks, ('gx', 'gy'), 0, 0, axis_index_groups=same_core, t...  12.1 us
    ppermute x8, starting transfers between devices, swapped(): return lax.ppermute(value, axis, pairs)  8.8 us
    all_to_all x2, waiting for transfers between devices, spread(): lax.all_to_all(blocks, ('gx', 'gy'), 0, 0, axis_index_groups=same_core, t...  6.04 us
    ppermute x8, waiting for transfers between devices, swapped(): return lax.ppermute(value, axis, pairs)  3.78 us
    pallas_call x1, Pallas kernels, pack(): pl.pallas_call(pack_kernel, out_shape=[jax.ShapeDtypeStruct((ROOM_BRICKS,...  3.01 us
    ppermute x2, waiting for transfers between devices, hopped(): return lax.ppermute(value, axis, pairs)  2.89 us
    ppermute x2, starting transfers between devices, hopped(): return lax.ppermute(value, axis, pairs)  2.58 us
  transfers between devices with their start and end apart: 12, of which 6 were waited for; matrix products, arithmetic and copies ran while one was open for 0% of the time, Pallas kernels for 28%

profile of v12, /device:TPU:0, one launch (start us, length us, event | category | flops | bytes accessed | tf_op | source)
XLA Modules:
  0.0 62.9 jit_solution(17768093748785549067)
XLA Ops:
  0.6 3.0 %pack.1 = (bf16[48,4,512,128]{3,2,1,0:T(8,128)(2,1)}, bf16[4,512,128]{2,1,0:T(8,128)(2,1)}, bf16[4,512,128]{2,1,0:T(8,128)(2,1)}, s32[12288,4,27]{2,1,0:T(4,128)...) custom-call(s32[2,4]{1,0:T(2,128)} %bitcast.13, ...), custom_call_target="tpu_custom_call" | custom-call | tf_op jit(solution)/shard_map/pack/pallas_call | solution.py:144
  3.6 1.3 %collective-permute-start = (bf16[320,128]{1,0:T(8,128)(2,1)}, bf16[320,128]{1,0:T(8,128)(2,1)S(1)}, u32[]{:S(2)}, u32[]{:S(2)}) collective-permute-start(bf16[320,128]{1,0:T(8,128)(2,1)} %get-tuple-element.39), channel_id=1, source_target_pairs={{4,12},{12,20},{20,28},{8,0},{16,8},{24,16},{5,13},{13,21},{21,29}... | collective-permute-start | bytes 245768 | tf_op jit(solution)/shard_map/ppermute | solution.py:602
  4.9 1.3 %collective-permute-start.1 = (bf16[304,128]{1,0:T(8,128)(2,1)}, bf16[304,128]{1,0:T(8,128)(2,1)S(1)}, u32[]{:S(2)}, u32[]{:S(2)}) collective-permute-start(bf16[304,128]{1,0:T(8,128)(2,1)} %get-tuple-element.47), channel_id=1, source_target_pairs={{1,3},{2,0},{5,7},{6,4},{9,11},{10,8},{13,15},{14,12},{17,19},{18,... | collective-permute-start | bytes 233480 | tf_op jit(solution)/shard_map/ppermute | solution.py:602
  6.2 0.0 copy-start.1
  6.3 0.0 copy-start
  6.3 2.0 %own_columns.1.v = bf16[4,10,64,1152]{3,2,1,0:T(8,128)(2,1)S(1)} custom-call(s32[12288,4,27]{2,1,0:T(4,128)} %get-tuple-element.40.near_hbm, bf16[48,4,512,128]{3,2,1,0:T(8,128)(2,1)} %get-tuple-element.41.act_hbm), custom_call_target="tpu_custom_call" | custom-call | flops 16777216 | bytes 6291456 | tf_op jit(solution)/shard_map/own_columns/pallas_call | solution.py:334
  8.3 0.0 copy-start.2
  8.3 0.0 copy-start.4
  8.3 2.9 %collective-permute-done.second = bf16[320,128]{1,0:T(8,128)(2,1)S(1)} collective-permute-done((bf16[320,128]{1,0:T(8,128)(2,1)}, bf16[320,128]{1,0:T(8,128)(2,1)S(1)}, u32[]{:S(2)}, u32[]{:S(2)}) %collective-permute-start) | collective-permute-done | bytes 81952 | tf_op jit(solution)/shard_map/ppermute | solution.py:602
  11.2 0.0 copy-done.1
  11.2 2.3 %collective-permute-start.2 = (bf16[384,128]{1,0:T(8,128)(2,1)S(1)}, bf16[384,128]{1,0:T(8,128)(2,1)S(1)}, u32[]{:S(2)}, u32[]{:S(2)}) collective-permute-start(bf16[384,128]{1,0:T(8,128)(2,1)S(1)} %get-tuple-element.49), channel_id=1, source_target_pairs={{0,4},{4,0},{8,12},{12,8},{16,20},{20,16},{24,28},{28,24},{1,5},{5... | collective-permute-start | bytes 294920 | tf_op jit(solution)/shard_map/ppermute | solution.py:596
  13.6 0.0 copy-done
  13.6 2.3 %inner_terms.1.inner = f32[3456,128]{1,0:T(8,128)S(1)} custom-call(bf16[4,10,64,1152]{3,2,1,0:T(8,128)(2,1)S(1)} %own_columns.1.v, bf16[4,512,128]{2,1,0:T(8,128)(2,1)S(1)} %copy-done), custom_call_target="tpu_custom_call" | custom-call | flops 1811939328 | bytes 6291456 | tf_op jit(solution)/shard_map/inner_terms/pallas_call | solution.py:359
  15.9 0.0 copy-start.3
  15.9 0.0 copy-start.5
  15.9 0.0 copy-start.6
  16.0 0.0 collective-permute-done.1.second
  16.0 0.0 copy-done.2
  16.0 1.2 %collective-permute-start.3 = (bf16[352,128]{1,0:T(8,128)(2,1)S(1)}, bf16[352,128]{1,0:T(8,128)(2,1)S(1)}, u32[]{:S(2)}, u32[]{:S(2)}) collective-permute-start(bf16[352,128]{1,0:T(8,128)(2,1)S(1)} %get-tuple-element.52), channel_id=1, source_target_pairs={{0,1},{1,0},{2,3},{3,2},{4,5},{5,4},{6,7},{7,6},{8,9},{9,8},{10,11... | collective-permute-start | bytes 270344 | tf_op jit(solution)/shard_map/ppermute | solution.py:596
  17.2 0.9 %collective-permute-done.3.y_ref.refs_5_ = bf16[352,128]{1,0:T(8,128)(2,1)S(1)} collective-permute-done((bf16[352,128]{1,0:T(8,128)(2,1)S(1)}, bf16[352,128]{1,0:T(8,128)(2,1)S(1)}, u32[]{:S(2)}, u32[]{:S(2)}) %collective-permute-start.3) | collective-permute-done | bytes 90144 | tf_op jit(solution)/shard_map/ppermute | solution.py:596
  18.1 0.0 collective-permute-done.2.x_ref.x_came.refs_4_
  18.1 0.0 copy-done.4
  18.1 2.0 %rim_terms.1 = (f32[1728,128]{1,0:T(8,128)S(1)}, f32[1728,128]{1,0:T(8,128)S(1)}) custom-call(s32[4,27]{1,0:T(4,128)S(1)} %copy-done.4, f32[3456,128]{1,0:T(8,128)S(1)} %inner_terms.1.inner, bf16[4,512,128]{2,1,0:T(8,128)(2,1)S(1)} %copy-done, bf16[384,128]{1,0:T(8,128)(2,1)S(1)} %collective-permute-done.2.x_ref.x_came.refs_4_, ...), custom_call_target="tpu_custom_call" | custom-call | flops 301989888 | bytes 6291456 | tf_op jit(solution)/shard_map/rim_terms/pallas_call | solution.py:445
  20.1 0.4 collective-permute-start.4
  20.5 2.1 %collective-permute-done.4.refs_1_ = f32[1728,128]{1,0:T(8,128)S(1)} collective-permute-done((f32[1728,128]{1,0:T(8,128)S(1)}, f32[1728,128]{1,0:T(8,128)S(1)}, u32[]{:S(2)}, u32[]{:S(2)}) %collective-permute-start.4) | collective-permute-done | bytes 884768 | tf_op jit(solution)/shard_map/ppermute | solution.py:596
  22.6 0.3 merge.1
  22.9 0.8 %convert_element_type.15 = f16[16,112,128]{2,1,0:T(8,128)(2,1)} convert(f32[16,112,128]{2,1,0:T(8,128)S(1)} %merge.1) | non-fusion elementwise | flops 229376 | bytes 1376256 | tf_op jit(solution)/shard_map/convert_element_type | solution.py:642
  23.8 6.0 %all-to-all-start = ((f16[16,112,128]{2,1,0:T(8,128)(2,1)}), f16[16,112,128]{2,1,0:T(8,128)(2,1)S(1)}, u32[]{:S(2)}, u32[]{:S(2)}) async-start(f16[16,112,128]{2,1,0:T(8,128)(2,1)} %convert_element_type.15), calls=%async_computation | async-start | bytes 917504 | tf_op jit(solution)/shard_map/all_to_all | solution.py:620
  29.8 0.1 collective-permute-start.5
  29.9 0.6 %collective-permute-start.6 = (bf16[32,128]{1,0:T(8,128)(2,1)S(1)}, bf16[32,128]{1,0:T(8,128)(2,1)S(1)}, u32[]{:S(2)}, u32[]{:S(2)}) collective-permute-start(bf16[32,128]{1,0:T(8,128)(2,1)S(1)} %get-tuple-element.62), channel_id=1, source_target_pairs={{1,2},{2,1},{5,6},{6,5},{9,10},{10,9},{13,14},{14,13},{17,18},{18,... | collective-permute-start | bytes 24584 | tf_op jit(solution)/shard_map/ppermute | solution.py:596
  30.6 1.5 %collective-permute-start.7 = (bf16[256,128]{1,0:T(8,128)(2,1)S(1)}, bf16[256,128]{1,0:T(8,128)(2,1)S(1)}, u32[]{:S(2)}, u32[]{:S(2)}) collective-permute-start(bf16[256,128]{1,0:T(8,128)(2,1)S(1)} %get-tuple-element.63), channel_id=1, source_target_pairs={{0,4},{4,0},{8,12},{12,8},{16,20},{20,16},{24,28},{28,24},{1,5},{5... | collective-permute-start | bytes 196616 | tf_op jit(solution)/shard_map/ppermute | solution.py:596
  32.1 2.6 %collective-permute-start.8 = (bf16[256,128]{1,0:T(8,128)(2,1)S(1)}, bf16[256,128]{1,0:T(8,128)(2,1)S(1)}, u32[]{:S(2)}, u32[]{:S(2)}) collective-permute-start(bf16[256,128]{1,0:T(8,128)(2,1)S(1)} %get-tuple-element.64), channel_id=1, source_target_pairs={{0,1},{1,0},{2,3},{3,2},{4,5},{5,4},{6,7},{7,6},{8,9},{9,8},{10,11... | collective-permute-start | bytes 196616 | tf_op jit(solution)/shard_map/ppermute | solution.py:596
  34.7 0.0 collective-permute-done.5.refs_6_
  34.7 0.0 collective-permute-done.6.refs_7_
  34.7 0.0 copy-done.3
  34.7 0.0 copy-done.5
  34.7 0.0 copy-done.6
  34.7 6.0 %output_product.1 = bf16[4,512,128]{2,1,0:T(8,128)(2,1)} custom-call(s32[4,27]{1,0:T(4,128)S(1)} %copy-done.4, s32[4,512]{1,0:T(4,128)S(1)} %copy-done.3, bf16[3456,128]{1,0:T(8,128)(2,1)S(1)} %bitcast.8, bf16[4,512,128]{2,1,0:T(8,128)(2,1)S(1)} %copy-done.6, bf16[384,128]{1,0:T(8,128)(2,1)S(1)} %collective-permute-done.2.x_ref.x_came.refs_4_, ...), custom_call_target="tpu_custom_call" | custom-call | flops 1811939328 | bytes 4194304 | tf_op jit(solution)/shard_map/output_product/pallas_call | solution.py:578
  40.7 0.0 collective-permute-done.7.refs_4_
  40.7 0.0 collective-permute-done.8.refs_5_
  40.7 0.9 %all-to-all-done = f16[16,112,128]{2,1,0:T(8,128)(2,1)S(1)} async-done(((f16[16,112,128]{2,1,0:T(8,128)(2,1)}), f16[16,112,128]{2,1,0:T(8,128)(2,1)S(1)}, u32[]{:S(2)}, u32[]{:S(2)}) %all-to-all-start) | async-done | bytes 458784 | tf_op jit(solution)/shard_map/all_to_all | solution.py:620
  41.6 0.1 convert_element_type.16.refs_0_
  41.6 0.3 sum_blocks.1
  41.9 0.8 %convert_element_type.17 = f16[16,112,128]{2,1,0:T(8,128)(2,1)} convert(f32[16,112,128]{2,1,0:T(8,128)S(1)} %sum_blocks.1) | non-fusion elementwise | flops 229376 | bytes 1376256 | tf_op jit(solution)/shard_map/convert_element_type | solution.py:650
  42.7 6.0 %all-to-all-start.1 = ((f16[16,112,128]{2,1,0:T(8,128)(2,1)}), f16[16,112,128]{2,1,0:T(8,128)(2,1)S(1)}, u32[]{:S(2)}, u32[]{:S(2)}) async-start(f16[16,112,128]{2,1,0:T(8,128)(2,1)} %convert_element_type.17), calls=%async_computation.1 | async-start | bytes 917504 | tf_op jit(solution)/shard_map/all_to_all | solution.py:620
  48.8 6.1 %input_grad_product.1 = bf16[4,512,128]{2,1,0:T(8,128)(2,1)} custom-call(s32[4,27]{1,0:T(4,128)S(1)} %copy-done.4, s32[4,512]{1,0:T(4,128)S(1)} %copy-done.3, bf16[3456,128]{1,0:T(8,128)(2,1)S(1)} %bitcast.9, bf16[4,512,128]{2,1,0:T(8,128)(2,1)S(1)} %copy-done, bf16[256,128]{1,0:T(8,128)(2,1)S(1)} %collective-permute-done.7.refs_4_, ...), custom_call_target="tpu_custom_call" | custom-call | flops 1811939328 | bytes 4194304 | tf_op jit(solution)/shard_map/input_grad_product/pallas_call | solution.py:578
  54.8 5.2 %all-to-all-done.1 = f16[16,112,128]{2,1,0:T(8,128)(2,1)S(1)} async-done(((f16[16,112,128]{2,1,0:T(8,128)(2,1)}), f16[16,112,128]{2,1,0:T(8,128)(2,1)S(1)}, u32[]{:S(2)}, u32[]{:S(2)}) %all-to-all-start.1) | async-done | bytes 458784 | tf_op jit(solution)/shard_map/all_to_all | solution.py:620
  60.0 0.0 collective-permute-start.9
  60.0 0.1 convert_element_type.19.refs_0_
  60.1 1.0 %decode_own.1.refs_1_ = f32[2,1728,128]{2,1,0:T(8,128)} custom-call(f32[16,112,128]{2,1,0:T(8,128)S(1)} %convert_element_type.19.refs_0_), custom_call_target="tpu_custom_call" | custom-call | tf_op jit(solution)/shard_map/decode_own/pallas_call | solution.py:540
  61.1 0.8 %collective-permute-done.9 = f16[16,112,128]{2,1,0:T(8,128)(2,1)S(1)} collective-permute-done((f16[16,112,128]{2,1,0:T(8,128)(2,1)S(1)}, f16[16,112,128]{2,1,0:T(8,128)(2,1)S(1)}, u32[]{:S(2)}, u32[]{:S(2)}) %collective-permute-start.9) | collective-permute-done | bytes 458784 | tf_op jit(solution)/shard_map/ppermute | solution.py:596
  61.8 0.1 convert_element_type.18.refs_0_
  61.9 1.0 %decode_other.1 = f32[2,1728,128]{2,1,0:T(8,128)} custom-call(f32[16,112,128]{2,1,0:T(8,128)S(1)} %convert_element_type.18.refs_0_, f32[2,1728,128]{2,1,0:T(8,128)} %decode_own.1.refs_1_), custom_call_target="tpu_custom_call", output_to_operand_aliasing={{}: (1, {})} | custom-call | tf_op jit(solution)/shard_map/decode_other/pallas_call | solution.py:540
  (3 shorter events, 0.0 us)
Async XLA Ops:
  3.6 7.6 %collective-permute-start = (bf16[320,128]{1,0:T(8,128)(2,1)}, bf16[320,128]{1,0:T(8,128)(2,1)S(1)}, u32[]{:S(2)}, u32[]{:S(2)}) collective-permute-start(bf16[320,128]{1,0:T(8,128)(2,1)} %get-tuple-element.39), channel_id=1, source_target_pairs={{4,12},{12,20},{20,28},{8,0},{16,8},{24,16},{5,13},{13,21},{21,29}... | collective-permute-start | bytes 245768 | tf_op jit(solution)/shard_map/ppermute | solution.py:602
  4.9 11.0 %collective-permute-start.1 = (bf16[304,128]{1,0:T(8,128)(2,1)}, bf16[304,128]{1,0:T(8,128)(2,1)S(1)}, u32[]{:S(2)}, u32[]{:S(2)}) collective-permute-start(bf16[304,128]{1,0:T(8,128)(2,1)} %get-tuple-element.47), channel_id=1, source_target_pairs={{1,3},{2,0},{5,7},{6,4},{9,11},{10,8},{13,15},{14,12},{17,19},{18,... | collective-permute-start | bytes 233480 | tf_op jit(solution)/shard_map/ppermute | solution.py:602
  6.2 5.0 %copy-start.1 = (bf16[320,128]{1,0:T(8,128)(2,1)S(1)}, bf16[320,128]{1,0:T(8,128)(2,1)}, u32[]{:S(2)}) copy-start(bf16[320,128]{1,0:T(8,128)(2,1)} %get-tuple-element.38.first) | copy-start | bytes 245764
  6.3 7.3 %copy-start = (bf16[4,512,128]{2,1,0:T(8,128)(2,1)S(1)}, bf16[4,512,128]{2,1,0:T(8,128)(2,1)}, u32[]{:S(2)}) copy-start(bf16[4,512,128]{2,1,0:T(8,128)(2,1)} %get-tuple-element.68.grd.refs_3_) | copy-start | bytes 1572868
  8.3 7.6 %copy-start.2 = (bf16[304,128]{1,0:T(8,128)(2,1)S(1)}, bf16[304,128]{1,0:T(8,128)(2,1)}, u32[]{:S(2)}) copy-start(bf16[304,128]{1,0:T(8,128)(2,1)} %get-tuple-element.50.first) | copy-start | bytes 233476
  8.3 9.8 %copy-start.4 = (s32[4,27]{1,0:T(4,128)S(1)}, s32[4,27]{1,0:T(4,128)}, u32[]{:S(2)}) copy-start(s32[4,27]{1,0:T(4,128)} %refs_0_.3) | copy-start | bytes 1300
  11.2 6.9 %collective-permute-start.2 = (bf16[384,128]{1,0:T(8,128)(2,1)S(1)}, bf16[384,128]{1,0:T(8,128)(2,1)S(1)}, u32[]{:S(2)}, u32[]{:S(2)}) collective-permute-start(bf16[384,128]{1,0:T(8,128)(2,1)S(1)} %get-tuple-element.49), channel_id=1, source_target_pairs={{0,4},{4,0},{8,12},{12,8},{16,20},{20,16},{24,28},{28,24},{1,5},{5... | collective-permute-start | bytes 294920 | tf_op jit(solution)/shard_map/ppermute | solution.py:596
  15.9 18.7 %copy-start.3 = (s32[4,512]{1,0:T(4,128)S(1)}, s32[4,512]{1,0:T(4,128)}, u32[]{:S(2)}) copy-start(s32[4,512]{1,0:T(4,128)} %refs_1_.3) | copy-start | bytes 24580
  15.9 18.7 %copy-start.5 = (bf16[27,128,128]{2,1,0:T(8,128)(2,1)S(1)}, bf16[27,128,128]{2,1,0:T(8,128)(2,1)}, u32[]{:S(2)}) copy-start(bf16[27,128,128]{2,1,0:T(8,128)(2,1)} %param.9) | copy-start | bytes 2654212
  15.9 18.7 %copy-start.6 = (bf16[4,512,128]{2,1,0:T(8,128)(2,1)S(1)}, bf16[4,512,128]{2,1,0:T(8,128)(2,1)}, u32[]{:S(2)}) copy-start(bf16[4,512,128]{2,1,0:T(8,128)(2,1)} %get-tuple-element.59.refs_3_) | copy-start | bytes 1572868
  16.0 2.1 %collective-permute-start.3 = (bf16[352,128]{1,0:T(8,128)(2,1)S(1)}, bf16[352,128]{1,0:T(8,128)(2,1)S(1)}, u32[]{:S(2)}, u32[]{:S(2)}) collective-permute-start(bf16[352,128]{1,0:T(8,128)(2,1)S(1)} %get-tuple-element.52), channel_id=1, source_target_pairs={{0,1},{1,0},{2,3},{3,2},{4,5},{5,4},{6,7},{7,6},{8,9},{9,8},{10,11... | collective-permute-start | bytes 270344 | tf_op jit(solution)/shard_map/ppermute | solution.py:596
  20.1 2.5 %collective-permute-start.4 = (f32[1728,128]{1,0:T(8,128)S(1)}, f32[1728,128]{1,0:T(8,128)S(1)}, u32[]{:S(2)}, u32[]{:S(2)}) collective-permute-start(f32[1728,128]{1,0:T(8,128)S(1)} %get-tuple-element.54), channel_id=1, source_target_pairs={{0,1},{1,0},{2,3},{3,2},{4,5},{5,4},{6,7},{7,6},{8,9},{9,8},{10,11... | collective-permute-start | bytes 2654216 | tf_op jit(solution)/shard_map/ppermute | solution.py:596
  23.8 17.8 %all-to-all-start = ((f16[16,112,128]{2,1,0:T(8,128)(2,1)}), f16[16,112,128]{2,1,0:T(8,128)(2,1)S(1)}, u32[]{:S(2)}, u32[]{:S(2)}) async-start(f16[16,112,128]{2,1,0:T(8,128)(2,1)} %convert_element_type.15), calls=%async_computation | async-start | bytes 917504 | tf_op jit(solution)/shard_map/all_to_all | solution.py:620
  29.8 4.9 %collective-permute-start.5 = (bf16[32,128]{1,0:T(8,128)(2,1)S(1)}, bf16[32,128]{1,0:T(8,128)(2,1)S(1)}, u32[]{:S(2)}, u32[]{:S(2)}) collective-permute-start(bf16[32,128]{1,0:T(8,128)(2,1)S(1)} %get-tuple-element.61), channel_id=1, source_target_pairs={{0,1},{1,0},{2,3},{3,2},{4,5},{5,4},{6,7},{7,6},{8,9},{9,8},{10,11... | collective-permute-start | bytes 24584 | tf_op jit(solution)/shard_map/ppermute | solution.py:596
  29.9 4.7 %collective-permute-start.6 = (bf16[32,128]{1,0:T(8,128)(2,1)S(1)}, bf16[32,128]{1,0:T(8,128)(2,1)S(1)}, u32[]{:S(2)}, u32[]{:S(2)}) collective-permute-start(bf16[32,128]{1,0:T(8,128)(2,1)S(1)} %get-tuple-element.62), channel_id=1, source_target_pairs={{1,2},{2,1},{5,6},{6,5},{9,10},{10,9},{13,14},{14,13},{17,18},{18,... | collective-permute-start | bytes 24584 | tf_op jit(solution)/shard_map/ppermute | solution.py:596
  30.6 10.1 %collective-permute-start.7 = (bf16[256,128]{1,0:T(8,128)(2,1)S(1)}, bf16[256,128]{1,0:T(8,128)(2,1)S(1)}, u32[]{:S(2)}, u32[]{:S(2)}) collective-permute-start(bf16[256,128]{1,0:T(8,128)(2,1)S(1)} %get-tuple-element.63), channel_id=1, source_target_pairs={{0,4},{4,0},{8,12},{12,8},{16,20},{20,16},{24,28},{28,24},{1,5},{5... | collective-permute-start | bytes 196616 | tf_op jit(solution)/shard_map/ppermute | solution.py:596
  32.1 8.6 %collective-permute-start.8 = (bf16[256,128]{1,0:T(8,128)(2,1)S(1)}, bf16[256,128]{1,0:T(8,128)(2,1)S(1)}, u32[]{:S(2)}, u32[]{:S(2)}) collective-permute-start(bf16[256,128]{1,0:T(8,128)(2,1)S(1)} %get-tuple-element.64), channel_id=1, source_target_pairs={{0,1},{1,0},{2,3},{3,2},{4,5},{5,4},{6,7},{7,6},{8,9},{9,8},{10,11... | collective-permute-start | bytes 196616 | tf_op jit(solution)/shard_map/ppermute | solution.py:596
  42.7 17.3 %all-to-all-start.1 = ((f16[16,112,128]{2,1,0:T(8,128)(2,1)}), f16[16,112,128]{2,1,0:T(8,128)(2,1)S(1)}, u32[]{:S(2)}, u32[]{:S(2)}) async-start(f16[16,112,128]{2,1,0:T(8,128)(2,1)} %convert_element_type.17), calls=%async_computation.1 | async-start | bytes 917504 | tf_op jit(solution)/shard_map/all_to_all | solution.py:620
  60.0 1.8 %collective-permute-start.9 = (f16[16,112,128]{2,1,0:T(8,128)(2,1)S(1)}, f16[16,112,128]{2,1,0:T(8,128)(2,1)S(1)}, u32[]{:S(2)}, u32[]{:S(2)}) collective-permute-start(f16[16,112,128]{2,1,0:T(8,128)(2,1)S(1)} %all-to-all-done.1), channel_id=1, source_target_pairs={{0,1},{1,0},{2,3},{3,2},{4,5},{5,4},{6,7},{7,6},{8,9},{9,8},{10,11... | collective-permute-start | bytes 1376264 | tf_op jit(solution)/shard_map/ppermute | solution.py:596

commit v13 on v12

--- a/solution.py
+++ b/solution.py
@@ -363,7 +363,7 @@
         out_specs=vmem(),
         scratch_shapes=[pltpu.VMEM((C, SLOTS * 512), jnp.bfloat16)],
         compiler_params=pltpu.CompilerParams(vmem_limit_bytes=VMEM_LIMIT),
-        cost_estimate=pl.CostEstimate(flops=2 * 2048 * ROWS * C, bytes_accessed=6 << 20, transcendentals=0),
+        cost_estimate=pl.CostEstimate(flops=2048 * ROWS * C, bytes_accessed=3 << 20, transcendentals=0),
         name="inner_terms",
     )(v, grd)
 
@@ -635,7 +635,6 @@
     x_more, v = lax.optimization_barrier((x_more, v))
     x_came = swapped(x_came, "gx", 0)
     inner = inner_terms(v, grd)
-    inner, y1 = lax.optimization_barrier((inner, y1))
     y_came, y_more = join(y0, y1)
     y_came = swapped(y_came, "gy", 0)
     keep, send = rim_terms(neighbours, inner, grd, x_came, y_came)

time: 63.3 us -> 63 us (level)
  waiting for transfers between devices: 12.7 us -> 12 us
    all_to_all x2, starting transfers between devices: 12.1 us -> 12.9 us  [spread(): lax.all_to_all(blocks, ('gx', 'gy'), 0, 0, axis_index_groups=same_core, t...]
  transfers between devices with their start and end apart: 12 -> 12, of which waited for: 6 -> 5; matrix products, arithmetic and copies ran while one was open for 0% -> 0% of each run, Pallas kernels for 28% -> 28%
where the time goes in v13:
time: 63 us; the launch traced here: 62.6 us
  Pallas kernels  24 us (38%)
  starting transfers between devices  23.9 us (38%)
  waiting for transfers between devices  12 us (19%)
  other arithmetic  1.84 us (3%)
  between operations  0.86 us (1%)
    all_to_all x2, starting transfers between devices, spread(): lax.all_to_all(blocks, ('gx', 'gy'), 0, 0, axis_index_groups=same_core, t...  12.9 us
    pallas_call x2, Pallas kernels, product(): pl.pallas_call(lambda *refs: product_kernel(f, *refs), out_shape=jax.Shap...  12.1 us
    ppermute x8, starting transfers between devices, swapped(): return lax.ppermute(value, axis, pairs)  8.46 us
    all_to_all x2, waiting for transfers between devices, spread(): lax.all_to_all(blocks, ('gx', 'gy'), 0, 0, axis_index_groups=same_core, t...  5.92 us
    ppermute x8, waiting for transfers between devices, swapped(): return lax.ppermute(value, axis, pairs)  3.15 us
    pallas_call x1, Pallas kernels, pack(): pl.pallas_call(pack_kernel, out_shape=[jax.ShapeDtypeStruct((ROOM_BRICKS,...  3.01 us
    ppermute x2, waiting for transfers between devices, hopped(): return lax.ppermute(value, axis, pairs)  2.89 us
    ppermute x2, starting transfers between devices, hopped(): return lax.ppermute(value, axis, pairs)  2.58 us
  transfers between devices with their start and end apart: 12, of which 5 were waited for; matrix products, arithmetic and copies ran while one was open for 0% of the time, Pallas kernels for 28%

profile of v13, /device:TPU:0, one launch (start us, length us, event | category | flops | bytes accessed | tf_op | source)
XLA Modules:
  0.0 62.6 jit_solution(4694318033142621161)
XLA Ops:
  0.6 3.0 %pack.1 = (bf16[48,4,512,128]{3,2,1,0:T(8,128)(2,1)}, bf16[4,512,128]{2,1,0:T(8,128)(2,1)}, bf16[4,512,128]{2,1,0:T(8,128)(2,1)}, s32[12288,4,27]{2,1,0:T(4,128)...) custom-call(s32[2,4]{1,0:T(2,128)} %bitcast.13, ...), custom_call_target="tpu_custom_call" | custom-call | tf_op jit(solution)/shard_map/pack/pallas_call | solution.py:144
  3.6 1.3 %collective-permute-start = (bf16[320,128]{1,0:T(8,128)(2,1)}, bf16[320,128]{1,0:T(8,128)(2,1)S(1)}, u32[]{:S(2)}, u32[]{:S(2)}) collective-permute-start(bf16[320,128]{1,0:T(8,128)(2,1)} %get-tuple-element.37), channel_id=1, source_target_pairs={{4,12},{12,20},{20,28},{8,0},{16,8},{24,16},{5,13},{13,21},{21,29}... | collective-permute-start | bytes 245768 | tf_op jit(solution)/shard_map/ppermute | solution.py:602
  4.9 1.3 %collective-permute-start.2 = (bf16[304,128]{1,0:T(8,128)(2,1)}, bf16[304,128]{1,0:T(8,128)(2,1)S(1)}, u32[]{:S(2)}, u32[]{:S(2)}) collective-permute-start(bf16[304,128]{1,0:T(8,128)(2,1)} %get-tuple-element.47), channel_id=1, source_target_pairs={{1,3},{2,0},{5,7},{6,4},{9,11},{10,8},{13,15},{14,12},{17,19},{18,... | collective-permute-start | bytes 233480 | tf_op jit(solution)/shard_map/ppermute | solution.py:602
  6.2 0.0 copy-start.1
  6.3 0.0 copy-start.2
  6.3 0.0 copy-start
  6.3 2.0 %own_columns.1.v = bf16[4,10,64,1152]{3,2,1,0:T(8,128)(2,1)S(1)} custom-call(s32[12288,4,27]{2,1,0:T(4,128)} %get-tuple-element.38.near_hbm, bf16[48,4,512,128]{3,2,1,0:T(8,128)(2,1)} %get-tuple-element.39.act_hbm), custom_call_target="tpu_custom_call" | custom-call | flops 16777216 | bytes 6291456 | tf_op jit(solution)/shard_map/own_columns/pallas_call | solution.py:334
  8.3 0.0 copy-start.4
  8.3 2.9 %collective-permute-done.second = bf16[320,128]{1,0:T(8,128)(2,1)S(1)} collective-permute-done((bf16[320,128]{1,0:T(8,128)(2,1)}, bf16[320,128]{1,0:T(8,128)(2,1)S(1)}, u32[]{:S(2)}, u32[]{:S(2)}) %collective-permute-start) | collective-permute-done | bytes 81952 | tf_op jit(solution)/shard_map/ppermute | solution.py:602
  11.2 0.0 copy-done.1
  11.2 2.3 %collective-permute-start.1 = (bf16[384,128]{1,0:T(8,128)(2,1)S(1)}, bf16[384,128]{1,0:T(8,128)(2,1)S(1)}, u32[]{:S(2)}, u32[]{:S(2)}) collective-permute-start(bf16[384,128]{1,0:T(8,128)(2,1)S(1)} %get-tuple-element.45), channel_id=1, source_target_pairs={{0,4},{4,0},{8,12},{12,8},{16,20},{20,16},{24,28},{28,24},{1,5},{5... | collective-permute-start | bytes 294920 | tf_op jit(solution)/shard_map/ppermute | solution.py:596
  13.6 0.0 collective-permute-done.2.second
  13.6 0.0 copy-done.2
  13.6 1.2 %collective-permute-start.3 = (bf16[352,128]{1,0:T(8,128)(2,1)S(1)}, bf16[352,128]{1,0:T(8,128)(2,1)S(1)}, u32[]{:S(2)}, u32[]{:S(2)}) collective-permute-start(bf16[352,128]{1,0:T(8,128)(2,1)S(1)} %get-tuple-element.48), channel_id=1, source_target_pairs={{0,1},{1,0},{2,3},{3,2},{4,5},{5,4},{6,7},{7,6},{8,9},{9,8},{10,11... | collective-permute-start | bytes 270344 | tf_op jit(solution)/shard_map/ppermute | solution.py:596
  14.8 0.0 copy-done
  14.8 0.0 copy-start.3
  14.8 0.0 copy-start.5
  14.8 0.0 copy-start.6
  14.8 2.3 %inner_terms.1.inner = f32[3456,128]{1,0:T(8,128)S(1)} custom-call(bf16[4,10,64,1152]{3,2,1,0:T(8,128)(2,1)S(1)} %own_columns.1.v, bf16[4,512,128]{2,1,0:T(8,128)(2,1)S(1)} %copy-done), custom_call_target="tpu_custom_call" | custom-call | flops 905969664 | bytes 3145728 | tf_op jit(solution)/shard_map/inner_terms/pallas_call | solution.py:359
  17.1 0.0 collective-permute-done.3.y_ref.refs_5_
  17.2 0.0 collective-permute-done.1.x_ref.x_came.refs_4_
  17.2 0.0 copy-done.4
  17.2 2.0 %rim_terms.1 = (f32[1728,128]{1,0:T(8,128)S(1)}, f32[1728,128]{1,0:T(8,128)S(1)}) custom-call(s32[4,27]{1,0:T(4,128)S(1)} %copy-done.4, f32[3456,128]{1,0:T(8,128)S(1)} %inner_terms.1.inner, bf16[4,512,128]{2,1,0:T(8,128)(2,1)S(1)} %copy-done, bf16[384,128]{1,0:T(8,128)(2,1)S(1)} %collective-permute-done.1.x_ref.x_came.refs_4_, ...), custom_call_target="tpu_custom_call" | custom-call | flops 301989888 | bytes 6291456 | tf_op jit(solution)/shard_map/rim_terms/pallas_call | solution.py:445
  19.1 0.1 collective-permute-start.4
  19.3 2.4 %collective-permute-done.4.refs_1_ = f32[1728,128]{1,0:T(8,128)S(1)} collective-permute-done((f32[1728,128]{1,0:T(8,128)S(1)}, f32[1728,128]{1,0:T(8,128)S(1)}, u32[]{:S(2)}, u32[]{:S(2)}) %collective-permute-start.4) | collective-permute-done | bytes 884768 | tf_op jit(solution)/shard_map/ppermute | solution.py:596
  21.6 0.3 merge.1
  22.0 0.8 %convert_element_type.15 = f16[16,112,128]{2,1,0:T(8,128)(2,1)} convert(f32[16,112,128]{2,1,0:T(8,128)S(1)} %merge.1) | non-fusion elementwise | flops 229376 | bytes 1376256 | tf_op jit(solution)/shard_map/convert_element_type | solution.py:641
  22.8 7.0 %all-to-all-start = ((f16[16,112,128]{2,1,0:T(8,128)(2,1)}), f16[16,112,128]{2,1,0:T(8,128)(2,1)S(1)}, u32[]{:S(2)}, u32[]{:S(2)}) async-start(f16[16,112,128]{2,1,0:T(8,128)(2,1)} %convert_element_type.15), calls=%async_computation | async-start | bytes 917504 | tf_op jit(solution)/shard_map/all_to_all | solution.py:620
  29.8 0.1 collective-permute-start.5
  29.9 0.7 %collective-permute-start.6 = (bf16[32,128]{1,0:T(8,128)(2,1)S(1)}, bf16[32,128]{1,0:T(8,128)(2,1)S(1)}, u32[]{:S(2)}, u32[]{:S(2)}) collective-permute-start(bf16[32,128]{1,0:T(8,128)(2,1)S(1)} %get-tuple-element.58), channel_id=1, source_target_pairs={{1,2},{2,1},{5,6},{6,5},{9,10},{10,9},{13,14},{14,13},{17,18},{18,... | collective-permute-start | bytes 24584 | tf_op jit(solution)/shard_map/ppermute | solution.py:596
  30.5 1.5 %collective-permute-start.7 = (bf16[256,128]{1,0:T(8,128)(2,1)S(1)}, bf16[256,128]{1,0:T(8,128)(2,1)S(1)}, u32[]{:S(2)}, u32[]{:S(2)}) collective-permute-start(bf16[256,128]{1,0:T(8,128)(2,1)S(1)} %get-tuple-element.59), channel_id=1, source_target_pairs={{0,4},{4,0},{8,12},{12,8},{16,20},{20,16},{24,28},{28,24},{1,5},{5... | collective-permute-start | bytes 196616 | tf_op jit(solution)/shard_map/ppermute | solution.py:596
  32.1 2.5 %collective-permute-start.8 = (bf16[256,128]{1,0:T(8,128)(2,1)S(1)}, bf16[256,128]{1,0:T(8,128)(2,1)S(1)}, u32[]{:S(2)}, u32[]{:S(2)}) collective-permute-start(bf16[256,128]{1,0:T(8,128)(2,1)S(1)} %get-tuple-element.60), channel_id=1, source_target_pairs={{0,1},{1,0},{2,3},{3,2},{4,5},{5,4},{6,7},{7,6},{8,9},{9,8},{10,11... | collective-permute-start | bytes 196616 | tf_op jit(solution)/shard_map/ppermute | solution.py:596
  34.6 0.0 collective-permute-done.5.refs_6_
  34.6 0.0 collective-permute-done.6.refs_7_
  34.6 0.0 copy-done.3
  34.6 0.0 copy-done.5
  34.6 0.0 copy-done.6
  34.7 6.0 %output_product.1 = bf16[4,512,128]{2,1,0:T(8,128)(2,1)} custom-call(s32[4,27]{1,0:T(4,128)S(1)} %copy-done.4, s32[4,512]{1,0:T(4,128)S(1)} %copy-done.3, bf16[3456,128]{1,0:T(8,128)(2,1)S(1)} %bitcast.8, bf16[4,512,128]{2,1,0:T(8,128)(2,1)S(1)} %copy-done.6, bf16[384,128]{1,0:T(8,128)(2,1)S(1)} %collective-permute-done.1.x_ref.x_came.refs_4_, ...), custom_call_target="tpu_custom_call" | custom-call | flops 1811939328 | bytes 4194304 | tf_op jit(solution)/shard_map/output_product/pallas_call | solution.py:578
  40.7 0.0 collective-permute-done.7.refs_4_
  40.7 0.0 collective-permute-done.8.refs_5_
  40.7 0.7 %all-to-all-done = f16[16,112,128]{2,1,0:T(8,128)(2,1)S(1)} async-done(((f16[16,112,128]{2,1,0:T(8,128)(2,1)}), f16[16,112,128]{2,1,0:T(8,128)(2,1)S(1)}, u32[]{:S(2)}, u32[]{:S(2)}) %all-to-all-start) | async-done | bytes 458784 | tf_op jit(solution)/shard_map/all_to_all | solution.py:620
  41.3 0.1 convert_element_type.16.refs_0_
  41.4 0.3 sum_blocks.1
  41.7 0.8 %convert_element_type.17 = f16[16,112,128]{2,1,0:T(8,128)(2,1)} convert(f32[16,112,128]{2,1,0:T(8,128)S(1)} %sum_blocks.1) | non-fusion elementwise | flops 229376 | bytes 1376256 | tf_op jit(solution)/shard_map/convert_element_type | solution.py:649
  42.5 5.9 %all-to-all-start.1 = ((f16[16,112,128]{2,1,0:T(8,128)(2,1)}), f16[16,112,128]{2,1,0:T(8,128)(2,1)S(1)}, u32[]{:S(2)}, u32[]{:S(2)}) async-start(f16[16,112,128]{2,1,0:T(8,128)(2,1)} %convert_element_type.17), calls=%async_computation.1 | async-start | bytes 917504 | tf_op jit(solution)/shard_map/all_to_all | solution.py:620
  48.4 6.1 %input_grad_product.1 = bf16[4,512,128]{2,1,0:T(8,128)(2,1)} custom-call(s32[4,27]{1,0:T(4,128)S(1)} %copy-done.4, s32[4,512]{1,0:T(4,128)S(1)} %copy-done.3, bf16[3456,128]{1,0:T(8,128)(2,1)S(1)} %bitcast.9, bf16[4,512,128]{2,1,0:T(8,128)(2,1)S(1)} %copy-done, bf16[256,128]{1,0:T(8,128)(2,1)S(1)} %collective-permute-done.7.refs_4_, ...), custom_call_target="tpu_custom_call" | custom-call | flops 1811939328 | bytes 4194304 | tf_op jit(solution)/shard_map/input_grad_product/pallas_call | solution.py:578
  54.5 5.3 %all-to-all-done.1 = f16[16,112,128]{2,1,0:T(8,128)(2,1)S(1)} async-done(((f16[16,112,128]{2,1,0:T(8,128)(2,1)}), f16[16,112,128]{2,1,0:T(8,128)(2,1)S(1)}, u32[]{:S(2)}, u32[]{:S(2)}) %all-to-all-start.1) | async-done | bytes 458784 | tf_op jit(solution)/shard_map/all_to_all | solution.py:620
  59.8 0.0 collective-permute-start.9
  59.8 0.1 convert_element_type.19.refs_0_
  59.8 1.0 %decode_own.1.refs_1_ = f32[2,1728,128]{2,1,0:T(8,128)} custom-call(f32[16,112,128]{2,1,0:T(8,128)S(1)} %convert_element_type.19.refs_0_), custom_call_target="tpu_custom_call" | custom-call | tf_op jit(solution)/shard_map/decode_own/pallas_call | solution.py:540
  60.8 0.8 %collective-permute-done.9 = f16[16,112,128]{2,1,0:T(8,128)(2,1)S(1)} collective-permute-done((f16[16,112,128]{2,1,0:T(8,128)(2,1)S(1)}, f16[16,112,128]{2,1,0:T(8,128)(2,1)S(1)}, u32[]{:S(2)}, u32[]{:S(2)}) %collective-permute-start.9) | collective-permute-done | bytes 458784 | tf_op jit(solution)/shard_map/ppermute | solution.py:596
  61.6 0.1 convert_element_type.18.refs_0_
  61.6 1.0 %decode_other.1 = f32[2,1728,128]{2,1,0:T(8,128)} custom-call(f32[16,112,128]{2,1,0:T(8,128)S(1)} %convert_element_type.18.refs_0_, f32[2,1728,128]{2,1,0:T(8,128)} %decode_own.1.refs_1_), custom_call_target="tpu_custom_call", output_to_operand_aliasing={{}: (1, {})} | custom-call | tf_op jit(solution)/shard_map/decode_other/pallas_call | solution.py:540
  (3 shorter events, 0.0 us)
Async XLA Ops:
  3.6 7.6 %collective-permute-start = (bf16[320,128]{1,0:T(8,128)(2,1)}, bf16[320,128]{1,0:T(8,128)(2,1)S(1)}, u32[]{:S(2)}, u32[]{:S(2)}) collective-permute-start(bf16[320,128]{1,0:T(8,128)(2,1)} %get-tuple-element.37), channel_id=1, source_target_pairs={{4,12},{12,20},{20,28},{8,0},{16,8},{24,16},{5,13},{13,21},{21,29}... | collective-permute-start | bytes 245768 | tf_op jit(solution)/shard_map/ppermute | solution.py:602
  4.9 8.6 %collective-permute-start.2 = (bf16[304,128]{1,0:T(8,128)(2,1)}, bf16[304,128]{1,0:T(8,128)(2,1)S(1)}, u32[]{:S(2)}, u32[]{:S(2)}) collective-permute-start(bf16[304,128]{1,0:T(8,128)(2,1)} %get-tuple-element.47), channel_id=1, source_target_pairs={{1,3},{2,0},{5,7},{6,4},{9,11},{10,8},{13,15},{14,12},{17,19},{18,... | collective-permute-start | bytes 233480 | tf_op jit(solution)/shard_map/ppermute | solution.py:602
  6.2 5.0 %copy-start.1 = (bf16[320,128]{1,0:T(8,128)(2,1)S(1)}, bf16[320,128]{1,0:T(8,128)(2,1)}, u32[]{:S(2)}) copy-start(bf16[320,128]{1,0:T(8,128)(2,1)} %get-tuple-element.36.first) | copy-start | bytes 245764
  6.3 7.3 %copy-start.2 = (bf16[304,128]{1,0:T(8,128)(2,1)S(1)}, bf16[304,128]{1,0:T(8,128)(2,1)}, u32[]{:S(2)}) copy-start(bf16[304,128]{1,0:T(8,128)(2,1)} %get-tuple-element.46.first) | copy-start | bytes 233476
  6.3 8.5 %copy-start = (bf16[4,512,128]{2,1,0:T(8,128)(2,1)S(1)}, bf16[4,512,128]{2,1,0:T(8,128)(2,1)}, u32[]{:S(2)}) copy-start(bf16[4,512,128]{2,1,0:T(8,128)(2,1)} %get-tuple-element.64.grd.refs_3_) | copy-start | bytes 1572868
  8.3 8.8 %copy-start.4 = (s32[4,27]{1,0:T(4,128)S(1)}, s32[4,27]{1,0:T(4,128)}, u32[]{:S(2)}) copy-start(s32[4,27]{1,0:T(4,128)} %refs_0_.3) | copy-start | bytes 1300
  11.2 5.9 %collective-permute-start.1 = (bf16[384,128]{1,0:T(8,128)(2,1)S(1)}, bf16[384,128]{1,0:T(8,128)(2,1)S(1)}, u32[]{:S(2)}, u32[]{:S(2)}) collective-permute-start(bf16[384,128]{1,0:T(8,128)(2,1)S(1)} %get-tuple-element.45), channel_id=1, source_target_pairs={{0,4},{4,0},{8,12},{12,8},{16,20},{20,16},{24,28},{28,24},{1,5},{5... | collective-permute-start | bytes 294920 | tf_op jit(solution)/shard_map/ppermute | solution.py:596
  13.6 3.5 %collective-permute-start.3 = (bf16[352,128]{1,0:T(8,128)(2,1)S(1)}, bf16[352,128]{1,0:T(8,128)(2,1)S(1)}, u32[]{:S(2)}, u32[]{:S(2)}) collective-permute-start(bf16[352,128]{1,0:T(8,128)(2,1)S(1)} %get-tuple-element.48), channel_id=1, source_target_pairs={{0,1},{1,0},{2,3},{3,2},{4,5},{5,4},{6,7},{7,6},{8,9},{9,8},{10,11... | collective-permute-start | bytes 270344 | tf_op jit(solution)/shard_map/ppermute | solution.py:596
  14.8 19.8 %copy-start.3 = (s32[4,512]{1,0:T(4,128)S(1)}, s32[4,512]{1,0:T(4,128)}, u32[]{:S(2)}) copy-start(s32[4,512]{1,0:T(4,128)} %refs_1_.3) | copy-start | bytes 24580
  14.8 19.8 %copy-start.5 = (bf16[27,128,128]{2,1,0:T(8,128)(2,1)S(1)}, bf16[27,128,128]{2,1,0:T(8,128)(2,1)}, u32[]{:S(2)}) copy-start(bf16[27,128,128]{2,1,0:T(8,128)(2,1)} %param.9) | copy-start | bytes 2654212
  14.8 19.8 %copy-start.6 = (bf16[4,512,128]{2,1,0:T(8,128)(2,1)S(1)}, bf16[4,512,128]{2,1,0:T(8,128)(2,1)}, u32[]{:S(2)}) copy-start(bf16[4,512,128]{2,1,0:T(8,128)(2,1)} %get-tuple-element.55.refs_3_) | copy-start | bytes 1572868
  19.1 2.5 %collective-permute-start.4 = (f32[1728,128]{1,0:T(8,128)S(1)}, f32[1728,128]{1,0:T(8,128)S(1)}, u32[]{:S(2)}, u32[]{:S(2)}) collective-permute-start(f32[1728,128]{1,0:T(8,128)S(1)} %get-tuple-element.50), channel_id=1, source_target_pairs={{0,1},{1,0},{2,3},{3,2},{4,5},{5,4},{6,7},{7,6},{8,9},{9,8},{10,11... | collective-permute-start | bytes 2654216 | tf_op jit(solution)/shard_map/ppermute | solution.py:596
  22.8 18.5 %all-to-all-start = ((f16[16,112,128]{2,1,0:T(8,128)(2,1)}), f16[16,112,128]{2,1,0:T(8,128)(2,1)S(1)}, u32[]{:S(2)}, u32[]{:S(2)}) async-start(f16[16,112,128]{2,1,0:T(8,128)(2,1)} %convert_element_type.15), calls=%async_computation | async-start | bytes 917504 | tf_op jit(solution)/shard_map/all_to_all | solution.py:620
  29.8 4.8 %collective-permute-start.5 = (bf16[32,128]{1,0:T(8,128)(2,1)S(1)}, bf16[32,128]{1,0:T(8,128)(2,1)S(1)}, u32[]{:S(2)}, u32[]{:S(2)}) collective-permute-start(bf16[32,128]{1,0:T(8,128)(2,1)S(1)} %get-tuple-element.57), channel_id=1, source_target_pairs={{0,1},{1,0},{2,3},{3,2},{4,5},{5,4},{6,7},{7,6},{8,9},{9,8},{10,11... | collective-permute-start | bytes 24584 | tf_op jit(solution)/shard_map/ppermute | solution.py:596
  29.9 4.7 %collective-permute-start.6 = (bf16[32,128]{1,0:T(8,128)(2,1)S(1)}, bf16[32,128]{1,0:T(8,128)(2,1)S(1)}, u32[]{:S(2)}, u32[]{:S(2)}) collective-permute-start(bf16[32,128]{1,0:T(8,128)(2,1)S(1)} %get-tuple-element.58), channel_id=1, source_target_pairs={{1,2},{2,1},{5,6},{6,5},{9,10},{10,9},{13,14},{14,13},{17,18},{18,... | collective-permute-start | bytes 24584 | tf_op jit(solution)/shard_map/ppermute | solution.py:596
  30.5 10.1 %collective-permute-start.7 = (bf16[256,128]{1,0:T(8,128)(2,1)S(1)}, bf16[256,128]{1,0:T(8,128)(2,1)S(1)}, u32[]{:S(2)}, u32[]{:S(2)}) collective-permute-start(bf16[256,128]{1,0:T(8,128)(2,1)S(1)} %get-tuple-element.59), channel_id=1, source_target_pairs={{0,4},{4,0},{8,12},{12,8},{16,20},{20,16},{24,28},{28,24},{1,5},{5... | collective-permute-start | bytes 196616 | tf_op jit(solution)/shard_map/ppermute | solution.py:596
  32.1 8.6 %collective-permute-start.8 = (bf16[256,128]{1,0:T(8,128)(2,1)S(1)}, bf16[256,128]{1,0:T(8,128)(2,1)S(1)}, u32[]{:S(2)}, u32[]{:S(2)}) collective-permute-start(bf16[256,128]{1,0:T(8,128)(2,1)S(1)} %get-tuple-element.60), channel_id=1, source_target_pairs={{0,1},{1,0},{2,3},{3,2},{4,5},{5,4},{6,7},{7,6},{8,9},{9,8},{10,11... | collective-permute-start | bytes 196616 | tf_op jit(solution)/shard_map/ppermute | solution.py:596
  42.5 17.3 %all-to-all-start.1 = ((f16[16,112,128]{2,1,0:T(8,128)(2,1)}), f16[16,112,128]{2,1,0:T(8,128)(2,1)S(1)}, u32[]{:S(2)}, u32[]{:S(2)}) async-start(f16[16,112,128]{2,1,0:T(8,128)(2,1)} %convert_element_type.17), calls=%async_computation.1 | async-start | bytes 917504 | tf_op jit(solution)/shard_map/all_to_all | solution.py:620
  59.8 1.8 %collective-permute-start.9 = (f16[16,112,128]{2,1,0:T(8,128)(2,1)S(1)}, f16[16,112,128]{2,1,0:T(8,128)(2,1)S(1)}, u32[]{:S(2)}, u32[]{:S(2)}) collective-permute-start(f16[16,112,128]{2,1,0:T(8,128)(2,1)S(1)} %all-to-all-done.1), channel_id=1, source_target_pairs={{0,1},{1,0},{2,3},{3,2},{4,5},{5,4},{6,7},{7,6},{8,9},{9,8},{10,11... | collective-permute-start | bytes 1376264 | tf_op jit(solution)/shard_map/ppermute | solution.py:596

commit v14 on v12

--- a/solution.py
+++ b/solution.py
@@ -15,9 +15,10 @@
 ZERO = SLOTS + 4 * FACE + 4
 ROWS = 27 * C
 FACE_ROWS = FACE * 64
-X_ROWS = FACE_ROWS + 64
+X_ROWS = FACE_ROWS + 32
 Y_ROWS = FACE_ROWS + 48
 HALF = ROWS // 2
+SPARE_ROWS = 32
 VMEM_LIMIT = 32 * 1024 * 1024
 PACK_LIMIT = 60 * 1024 * 1024
 ROOM_BRICKS = 48
@@ -127,10 +128,9 @@
                     live & (low < ZERO),
                 )
                 lines += [down, same, up]
-            if axis == 0:
-                lines.append(jnp.zeros((32, C), jnp.float32))
             lines = jnp.concatenate(lines, axis=0).astype(jnp.bfloat16)
             outs[k][pl.ds(FACE_ROWS, lines.shape[0])] = lines
+    x_out[1][pl.ds(X_ROWS + FACE_ROWS, SPARE_ROWS)] = jnp.zeros((SPARE_ROWS, C), jnp.bfloat16)
     for i, (built, send) in enumerate(zip(refs[4:8], sends)):
         results += fetching((built, send, sems.at[10 + i]))
     for result in results:
@@ -139,7 +139,8 @@
 
 def pack(features, out_grad, mask, near, face_sends, edge_sends):
     sends = [
-        jax.ShapeDtypeStruct((rows + FACE_ROWS, C), jnp.bfloat16) for rows in (Y_ROWS, Y_ROWS, X_ROWS, X_ROWS)
+        jax.ShapeDtypeStruct((rows + FACE_ROWS, C), jnp.bfloat16)
+        for rows in (Y_ROWS, Y_ROWS, X_ROWS, X_ROWS + SPARE_ROWS)
     ]
     return pl.pallas_call(
         pack_kernel,
@@ -233,11 +234,11 @@
 
 def fill_came(f, x_came, y_came, edges, lx, ly, corners):
     odd_x, odd_y = parity("gx"), parity("gy")
-    for came, odd, dst in ((x_came, odd_x, lx), (y_came, odd_y, ly)):
-        for k, part in enumerate(parts_of(came)):
+    for came, first, odd, dst in ((parts_of(x_came), 0, odd_x, lx), (y_came, f * Y_ROWS, odd_y, ly)):
+        for k, part in enumerate(came):
             side = side_of(k, odd)
             for r in range(FACE):
-                rows = part[pl.ds(r * 64, 64)]
+                rows = part[pl.ds(first + r * 64, 64)]
                 dst[side, SLOTS + r] = rows.astype(jnp.float32).reshape(8, 8, C)
             dst[k, SLOTS + FACE] = jnp.zeros((8, 8, C), jnp.float32)
     for k, came in enumerate(edges):
@@ -368,15 +369,15 @@
     )(v, grd)
 
 
-def rim_kernel(near_hbm, inner, grd, x_ref, y_ref, keep, send, lx, ly, corners, wide, near, sem, *refs):
+def rim_kernel(near_hbm, inner, grd, x_ref, y0, y1, keep, send, lx, ly, corners, wide, near, sem, *refs):
     vx, vy, ends_a, ends_g, side_x, side_y = refs
     (table,) = fetching((near_hbm, near, sem))
-    fill_came(0, x_ref, y_ref, (), lx, ly, corners)
+    fill_came(0, x_ref, (y0, y1), (), lx, ly, corners)
     for k, came in enumerate(parts_of(x_ref)):
         side = side_of(k, parity("gx"))
         for j in range(2):
             ends_a[side, j] = came[pl.ds(FACE_ROWS + 16 * j, 16)].astype(jnp.float32)[0:8]
-    for k, came in enumerate(parts_of(y_ref)):
+    for k, came in enumerate((y0, y1)):
         side = side_of(k, parity("gy"))
         ends_g[side] = came[pl.ds(FACE_ROWS, 48)].astype(jnp.float32).reshape(2, 3, 8, C)
     table.wait()
@@ -445,7 +446,7 @@
     return pl.pallas_call(
         rim_kernel,
         out_shape=[half, half],
-        in_specs=[hbm()] + [vmem()] * 4,
+        in_specs=[hbm()] + [vmem()] * 5,
         out_specs=[vmem()] * 2,
         scratch_shapes=columns_scratch()
         + [
@@ -459,7 +460,7 @@
         compiler_params=pltpu.CompilerParams(vmem_limit_bytes=VMEM_LIMIT),
         cost_estimate=pl.CostEstimate(flops=2 * 256 * 36 * C * C, bytes_accessed=6 << 20, transcendentals=0),
         name="rim_terms",
-    )(near, inner, grd, x_came, y_came)
+    )(near, inner, grd, x_came, *y_came)
 
 
 def power_of(values):
@@ -549,7 +550,7 @@
     )(blocks, *rest)
 
 
-def product_kernel(f, near_hbm, mask_ref, kernel_ref, bricks, x_ref, y_ref, e0, e1, out, *refs):
+def product_kernel(f, near_hbm, mask_ref, kernel_ref, bricks, x_ref, y0, y1, e0, e1, out, *refs):
     lx, ly, corners, wide, near, sem, v, *flipped = refs
     (table,) = fetching((near_hbm, near, sem))
     weights = kernel_ref
@@ -558,7 +559,7 @@
         for o in range(27):
             weights[pl.ds((26 - o) * C, C)] = kernel_ref[pl.ds(o * C, C)].T
     fill_own(bricks, lx, ly, corners)
-    fill_came(f, x_ref, y_ref, (e0, e1), lx, ly, corners)
+    fill_came(f, x_ref, (y0, y1), (e0, e1), lx, ly, corners)
     table.wait()
 
     def per_slot(s, carry):
@@ -578,7 +579,7 @@
     return pl.pallas_call(
         lambda *refs: product_kernel(f, *refs),
         out_shape=jax.ShapeDtypeStruct((SLOTS, 512, C), jnp.bfloat16),
-        in_specs=[hbm()] + [vmem()] * 7,
+        in_specs=[hbm()] + [vmem()] * 8,
         out_specs=vmem(),
         scratch_shapes=columns_scratch()
         + [pltpu.VMEM((SLOTS, 10, 64, 9 * C), jnp.bfloat16)]
@@ -586,7 +587,7 @@
         compiler_params=pltpu.CompilerParams(vmem_limit_bytes=VMEM_LIMIT),
         cost_estimate=pl.CostEstimate(flops=2 * 2048 * ROWS * C, bytes_accessed=4 << 20, transcendentals=0),
         name=("output_product", "input_grad_product")[f],
-    )(near, mask, kernel, bricks, x_came, y_came, *edges)
+    )(near, mask, kernel, bricks, x_came, *y_came, *edges)
 
 
 def swapped(value, axis, k):
@@ -627,29 +628,26 @@
         face_sends,
         edge_sends,
     )
-    y1 = hopped(y1, "gy")
     x1 = hopped(x1, "gx")
+    y_came = [swapped(y0, "gy", 0), swapped(y1, "gy", 1)]
     v = own_columns(table, held_act)
     x1, v = lax.optimization_barrier((x1, v))
     x_came, x_more = join(x0, x1)
     x_more, v = lax.optimization_barrier((x_more, v))
     x_came = swapped(x_came, "gx", 0)
     inner = inner_terms(v, grd)
-    inner, y1 = lax.optimization_barrier((inner, y1))
-    y_came, y_more = join(y0, y1)
-    y_came = swapped(y_came, "gy", 0)
     keep, send = rim_terms(neighbours, inner, grd, x_came, y_came)
     blocks = merge(groups, take, held, keep, swapped(send, "gy", 0)).astype(jnp.float16)
     rows = kernel.reshape(ROWS, C)
-    blocks, act, x_came, x_more, y_more = lax.optimization_barrier((blocks, act, x_came, x_more, y_more))
-    x_more, y_more = swapped(x_more, "gx", 0), swapped(y_more, "gy", 0)
+    blocks, act, x_came, x_more = lax.optimization_barrier((blocks, act, x_came, x_more))
+    x_more = swapped(x_more, "gx", 0)
     e0, e1 = forward_corners(x_came)
     edges = [swapped(e0, "gy", 0), swapped(e1, "gy", 1)]
     output = product(0, neighbours, voxel_mask, rows, act, x_came, y_came, edges)
-    arrived, output, x_more, y_more = lax.optimization_barrier((spread(blocks, in_turn), output, x_more, y_more))
+    arrived, output, x_more = lax.optimization_barrier((spread(blocks, in_turn), output, x_more))
     copies = sum_blocks(take, arrived.astype(jnp.float32)).astype(jnp.float16)
     copies, grd = lax.optimization_barrier((copies, grd))
-    input_grad = product(1, neighbours, voxel_mask, rows, grd, x_more, y_more, edges)
+    input_grad = product(1, neighbours, voxel_mask, rows, grd, x_more, y_came, edges)
     mine, input_grad = lax.optimization_barrier((spread(copies, onward), input_grad))
     other = swapped(mine, "gy", 0)
     scale = 1.0 / math.sqrt(parts * SLOTS * 512)

time: 63.3 us -> 63 us (level)
  starting transfers between devices: 23.4 us -> 21.2 us
  waiting for transfers between devices: 12.7 us -> 14.7 us
    all_to_all x2, waiting for transfers between devices: 6.04 us -> 8.46 us  [spread(): lax.all_to_all(blocks, ('gx', 'gy'), 0, 0, axis_index_groups=same_core, t...]
    ppermute x2 -> x1, starting transfers between devices: 2.58 us -> 1.29 us  [hopped(): return lax.ppermute(value, axis, pairs)]
    ppermute x8, starting transfers between devices: 8.8 us -> 7.53 us  [swapped(): return lax.ppermute(value, axis, pairs)]
    ppermute x2 -> x1, waiting for transfers between devices: 2.89 us -> 3.02 us  [hopped(): return lax.ppermute(value, axis, pairs)]
  transfers between devices with their start and end apart: 12 -> 11, of which waited for: 6 -> 6; matrix products, arithmetic and copies ran while one was open for 0% -> 0% of each run, Pallas kernels for 28% -> 28%
where the time goes in v14:
time: 63 us; the launch traced here: 62.6 us
  Pallas kernels  24 us (38%)
  starting transfers between devices  21.2 us (34%)
  waiting for transfers between devices  14.7 us (23%)
  other arithmetic  1.84 us (3%)
  between operations  0.83 us (1%)
    all_to_all x2, starting transfers between devices, spread(): lax.all_to_all(blocks, ('gx', 'gy'), 0, 0, axis_index_groups=same_core, t...  12.4 us
    pallas_call x2, Pallas kernels, product(): pl.pallas_call(lambda *refs: product_kernel(f, *refs), out_shape=jax.Shap...  12.1 us
    all_to_all x2, waiting for transfers between devices, spread(): lax.all_to_all(blocks, ('gx', 'gy'), 0, 0, axis_index_groups=same_core, t...  8.46 us
    ppermute x8, starting transfers between devices, swapped(): return lax.ppermute(value, axis, pairs)  7.53 us
    ppermute x8, waiting for transfers between devices, swapped(): return lax.ppermute(value, axis, pairs)  3.2 us
    ppermute x1, waiting for transfers between devices, hopped(): return lax.ppermute(value, axis, pairs)  3.02 us
    pallas_call x1, Pallas kernels, pack(): pl.pallas_call(pack_kernel, out_shape=[jax.ShapeDtypeStruct((ROOM_BRICKS,...  3.01 us
    pallas_call x1, Pallas kernels, inner_terms(): pl.pallas_call(inner_kernel, out_shape=jax.ShapeDtypeStruct((ROWS, C), jn...  2.33 us
  transfers between devices with their start and end apart: 11, of which 6 were waited for; matrix products, arithmetic and copies ran while one was open for 0% of the time, Pallas kernels for 28%

profile of v14, /device:TPU:0, one launch (start us, length us, event | category | flops | bytes accessed | tf_op | source)
XLA Modules:
  0.0 62.6 jit_solution(17695380620792993714)
XLA Ops:
  0.6 3.0 %pack.1 = (bf16[48,4,512,128]{3,2,1,0:T(8,128)(2,1)}, bf16[4,512,128]{2,1,0:T(8,128)(2,1)}, bf16[4,512,128]{2,1,0:T(8,128)(2,1)}, s32[12288,4,27]{2,1,0:T(4,128)...) custom-call(s32[2,4]{1,0:T(2,128)} %bitcast.13, ...), custom_call_target="tpu_custom_call" | custom-call | tf_op jit(solution)/shard_map/pack/pallas_call | solution.py:145
  3.6 1.3 %collective-permute-start = (bf16[320,128]{1,0:T(8,128)(2,1)}, bf16[320,128]{1,0:T(8,128)(2,1)S(1)}, u32[]{:S(2)}, u32[]{:S(2)}) collective-permute-start(bf16[320,128]{1,0:T(8,128)(2,1)} %get-tuple-element.33), channel_id=1, source_target_pairs={{4,12},{12,20},{20,28},{8,0},{16,8},{24,16},{5,13},{13,21},{21,29}... | collective-permute-start | bytes 245768 | tf_op jit(solution)/shard_map/ppermute | solution.py:603
  4.9 0.5 collective-permute-start.2
  5.5 0.7 %collective-permute-start.3 = (bf16[304,128]{1,0:T(8,128)(2,1)}, bf16[304,128]{1,0:T(8,128)(2,1)S(1)}, u32[]{:S(2)}, u32[]{:S(2)}) collective-permute-start(bf16[304,128]{1,0:T(8,128)(2,1)} %get-tuple-element.43), channel_id=1, source_target_pairs={{1,2},{2,1},{5,6},{6,5},{9,10},{10,9},{13,14},{14,13},{17,18},{18,... | collective-permute-start | bytes 233480 | tf_op jit(solution)/shard_map/ppermute | solution.py:597
  6.1 0.0 copy-start.1
  6.1 0.0 copy-start
  6.1 2.0 %own_columns.1.v = bf16[4,10,64,1152]{3,2,1,0:T(8,128)(2,1)S(1)} custom-call(s32[12288,4,27]{2,1,0:T(4,128)} %get-tuple-element.34.near_hbm, bf16[48,4,512,128]{3,2,1,0:T(8,128)(2,1)} %get-tuple-element.35.act_hbm), custom_call_target="tpu_custom_call" | custom-call | flops 16777216 | bytes 6291456 | tf_op jit(solution)/shard_map/own_columns/pallas_call | solution.py:335
  8.2 0.0 copy-start.3
  8.2 3.0 %collective-permute-done.second = bf16[320,128]{1,0:T(8,128)(2,1)S(1)} collective-permute-done((bf16[320,128]{1,0:T(8,128)(2,1)}, bf16[320,128]{1,0:T(8,128)(2,1)S(1)}, u32[]{:S(2)}, u32[]{:S(2)}) %collective-permute-start) | collective-permute-done | bytes 81952 | tf_op jit(solution)/shard_map/ppermute | solution.py:603
  11.2 0.0 copy-done.1
  11.2 1.8 %collective-permute-start.1 = (bf16[320,128]{1,0:T(8,128)(2,1)S(1)}, bf16[320,128]{1,0:T(8,128)(2,1)S(1)}, u32[]{:S(2)}, u32[]{:S(2)}) collective-permute-start(bf16[320,128]{1,0:T(8,128)(2,1)S(1)} %get-tuple-element.41), channel_id=1, source_target_pairs={{0,4},{4,0},{8,12},{12,8},{16,20},{20,16},{24,28},{28,24},{1,5},{5... | collective-permute-start | bytes 245768 | tf_op jit(solution)/shard_map/ppermute | solution.py:597
  13.0 0.0 copy-done
  13.0 0.0 copy-start.2
  13.0 0.0 copy-start.4
  13.0 0.0 copy-start.5
  13.0 2.3 %inner_terms.1.inner = f32[3456,128]{1,0:T(8,128)S(1)} custom-call(bf16[4,10,64,1152]{3,2,1,0:T(8,128)(2,1)S(1)} %own_columns.1.v, bf16[4,512,128]{2,1,0:T(8,128)(2,1)S(1)} %copy-done), custom_call_target="tpu_custom_call" | custom-call | flops 1811939328 | bytes 6291456 | tf_op jit(solution)/shard_map/inner_terms/pallas_call | solution.py:360
  15.4 0.0 collective-permute-done.2.y0.refs_5_
  15.4 0.0 collective-permute-done.3.y1.refs_6_
  15.4 0.4 collective-permute-done.1.x_ref.x_came.refs_4_
  15.7 0.0 copy-done.3
  15.8 2.0 %rim_terms.1 = (f32[1728,128]{1,0:T(8,128)S(1)}, f32[1728,128]{1,0:T(8,128)S(1)}) custom-call(s32[4,27]{1,0:T(4,128)S(1)} %copy-done.3, f32[3456,128]{1,0:T(8,128)S(1)} %inner_terms.1.inner, bf16[4,512,128]{2,1,0:T(8,128)(2,1)S(1)} %copy-done, bf16[320,128]{1,0:T(8,128)(2,1)S(1)} %collective-permute-done.1.x_ref.x_came.refs_4_, ...), custom_call_target="tpu_custom_call" | custom-call | flops 301989888 | bytes 6291456 | tf_op jit(solution)/shard_map/rim_terms/pallas_call | solution.py:446
  17.7 2.3 %collective-permute-start.4 = (f32[1728,128]{1,0:T(8,128)S(1)}, f32[1728,128]{1,0:T(8,128)S(1)}, u32[]{:S(2)}, u32[]{:S(2)}) collective-permute-start(f32[1728,128]{1,0:T(8,128)S(1)} %get-tuple-element.45), channel_id=1, source_target_pairs={{0,1},{1,0},{2,3},{3,2},{4,5},{5,4},{6,7},{7,6},{8,9},{9,8},{10,11... | collective-permute-start | bytes 2654216 | tf_op jit(solution)/shard_map/ppermute | solution.py:597
  20.0 2.1 %collective-permute-done.4.refs_1_ = f32[1728,128]{1,0:T(8,128)S(1)} collective-permute-done((f32[1728,128]{1,0:T(8,128)S(1)}, f32[1728,128]{1,0:T(8,128)S(1)}, u32[]{:S(2)}, u32[]{:S(2)}) %collective-permute-start.4) | collective-permute-done | bytes 884768 | tf_op jit(solution)/shard_map/ppermute | solution.py:597
  22.1 0.3 merge.1
  22.4 0.8 %convert_element_type.15 = f16[16,112,128]{2,1,0:T(8,128)(2,1)} convert(f32[16,112,128]{2,1,0:T(8,128)S(1)} %merge.1) | non-fusion elementwise | flops 229376 | bytes 1376256 | tf_op jit(solution)/shard_map/convert_element_type | solution.py:640
  23.3 6.5 %all-to-all-start = ((f16[16,112,128]{2,1,0:T(8,128)(2,1)}), f16[16,112,128]{2,1,0:T(8,128)(2,1)S(1)}, u32[]{:S(2)}, u32[]{:S(2)}) async-start(f16[16,112,128]{2,1,0:T(8,128)(2,1)} %convert_element_type.15), calls=%async_computation | async-start | bytes 917504 | tf_op jit(solution)/shard_map/all_to_all | solution.py:621
  29.8 0.1 collective-permute-start.5
  29.9 0.7 %collective-permute-start.6 = (bf16[32,128]{1,0:T(8,128)(2,1)S(1)}, bf16[32,128]{1,0:T(8,128)(2,1)S(1)}, u32[]{:S(2)}, u32[]{:S(2)}) collective-permute-start(bf16[32,128]{1,0:T(8,128)(2,1)S(1)} %get-tuple-element.52), channel_id=1, source_target_pairs={{1,2},{2,1},{5,6},{6,5},{9,10},{10,9},{13,14},{14,13},{17,18},{18,... | collective-permute-start | bytes 24584 | tf_op jit(solution)/shard_map/ppermute | solution.py:597
  30.5 1.5 %collective-permute-start.7 = (bf16[256,128]{1,0:T(8,128)(2,1)S(1)}, bf16[256,128]{1,0:T(8,128)(2,1)S(1)}, u32[]{:S(2)}, u32[]{:S(2)}) collective-permute-start(bf16[256,128]{1,0:T(8,128)(2,1)S(1)} %get-tuple-element.53), channel_id=1, source_target_pairs={{0,4},{4,0},{8,12},{12,8},{16,20},{20,16},{24,28},{28,24},{1,5},{5... | collective-permute-start | bytes 196616 | tf_op jit(solution)/shard_map/ppermute | solution.py:597
  32.0 0.0 collective-permute-done.5.refs_7_
  32.1 0.0 collective-permute-done.6.refs_8_
  32.1 0.0 copy-done.2
  32.1 0.0 copy-done.4
  32.1 0.0 copy-done.5
  32.1 6.0 %output_product.1 = bf16[4,512,128]{2,1,0:T(8,128)(2,1)} custom-call(s32[4,27]{1,0:T(4,128)S(1)} %copy-done.3, s32[4,512]{1,0:T(4,128)S(1)} %copy-done.2, bf16[3456,128]{1,0:T(8,128)(2,1)S(1)} %bitcast.8, bf16[4,512,128]{2,1,0:T(8,128)(2,1)S(1)} %copy-done.5, bf16[320,128]{1,0:T(8,128)(2,1)S(1)} %collective-permute-done.1.x_ref.x_came.refs_4_, ...), custom_call_target="tpu_custom_call" | custom-call | flops 1811939328 | bytes 4194304 | tf_op jit(solution)/shard_map/output_product/pallas_call | solution.py:579
  38.1 0.0 collective-permute-done.7.refs_4_
  38.1 3.2 %all-to-all-done = f16[16,112,128]{2,1,0:T(8,128)(2,1)S(1)} async-done(((f16[16,112,128]{2,1,0:T(8,128)(2,1)}), f16[16,112,128]{2,1,0:T(8,128)(2,1)S(1)}, u32[]{:S(2)}, u32[]{:S(2)}) %all-to-all-start) | async-done | bytes 458784 | tf_op jit(solution)/shard_map/all_to_all | solution.py:621
  41.3 0.1 convert_element_type.16.refs_0_
  41.4 0.3 sum_blocks.1
  41.7 0.8 %convert_element_type.17 = f16[16,112,128]{2,1,0:T(8,128)(2,1)} convert(f32[16,112,128]{2,1,0:T(8,128)S(1)} %sum_blocks.1) | non-fusion elementwise | flops 229376 | bytes 1376256 | tf_op jit(solution)/shard_map/convert_element_type | solution.py:648
  42.5 5.9 %all-to-all-start.1 = ((f16[16,112,128]{2,1,0:T(8,128)(2,1)}), f16[16,112,128]{2,1,0:T(8,128)(2,1)S(1)}, u32[]{:S(2)}, u32[]{:S(2)}) async-start(f16[16,112,128]{2,1,0:T(8,128)(2,1)} %convert_element_type.17), calls=%async_computation.1 | async-start | bytes 917504 | tf_op jit(solution)/shard_map/all_to_all | solution.py:621
  48.4 6.1 %input_grad_product.1 = bf16[4,512,128]{2,1,0:T(8,128)(2,1)} custom-call(s32[4,27]{1,0:T(4,128)S(1)} %copy-done.3, s32[4,512]{1,0:T(4,128)S(1)} %copy-done.2, bf16[3456,128]{1,0:T(8,128)(2,1)S(1)} %bitcast.9, bf16[4,512,128]{2,1,0:T(8,128)(2,1)S(1)} %copy-done, bf16[256,128]{1,0:T(8,128)(2,1)S(1)} %collective-permute-done.7.refs_4_, ...), custom_call_target="tpu_custom_call" | custom-call | flops 1811939328 | bytes 4194304 | tf_op jit(solution)/shard_map/input_grad_product/pallas_call | solution.py:579
  54.5 5.2 %all-to-all-done.1 = f16[16,112,128]{2,1,0:T(8,128)(2,1)S(1)} async-done(((f16[16,112,128]{2,1,0:T(8,128)(2,1)}), f16[16,112,128]{2,1,0:T(8,128)(2,1)S(1)}, u32[]{:S(2)}, u32[]{:S(2)}) %all-to-all-start.1) | async-done | bytes 458784 | tf_op jit(solution)/shard_map/all_to_all | solution.py:621
  59.7 0.0 collective-permute-start.8
  59.7 0.1 convert_element_type.19.refs_0_
  59.8 1.0 %decode_own.1.refs_1_ = f32[2,1728,128]{2,1,0:T(8,128)} custom-call(f32[16,112,128]{2,1,0:T(8,128)S(1)} %convert_element_type.19.refs_0_), custom_call_target="tpu_custom_call" | custom-call | tf_op jit(solution)/shard_map/decode_own/pallas_call | solution.py:541
  60.8 0.8 %collective-permute-done.8 = f16[16,112,128]{2,1,0:T(8,128)(2,1)S(1)} collective-permute-done((f16[16,112,128]{2,1,0:T(8,128)(2,1)S(1)}, f16[16,112,128]{2,1,0:T(8,128)(2,1)S(1)}, u32[]{:S(2)}, u32[]{:S(2)}) %collective-permute-start.8) | collective-permute-done | bytes 458784 | tf_op jit(solution)/shard_map/ppermute | solution.py:597
  61.5 0.1 convert_element_type.18.refs_0_
  61.6 1.0 %decode_other.1 = f32[2,1728,128]{2,1,0:T(8,128)} custom-call(f32[16,112,128]{2,1,0:T(8,128)S(1)} %convert_element_type.18.refs_0_, f32[2,1728,128]{2,1,0:T(8,128)} %decode_own.1.refs_1_), custom_call_target="tpu_custom_call", output_to_operand_aliasing={{}: (1, {})} | custom-call | tf_op jit(solution)/shard_map/decode_other/pallas_call | solution.py:541
  (2 shorter events, 0.0 us)
Async XLA Ops:
  3.6 7.6 %collective-permute-start = (bf16[320,128]{1,0:T(8,128)(2,1)}, bf16[320,128]{1,0:T(8,128)(2,1)S(1)}, u32[]{:S(2)}, u32[]{:S(2)}) collective-permute-start(bf16[320,128]{1,0:T(8,128)(2,1)} %get-tuple-element.33), channel_id=1, source_target_pairs={{4,12},{12,20},{20,28},{8,0},{16,8},{24,16},{5,13},{13,21},{21,29}... | collective-permute-start | bytes 245768 | tf_op jit(solution)/shard_map/ppermute | solution.py:603
  4.9 10.4 %collective-permute-start.2 = (bf16[304,128]{1,0:T(8,128)(2,1)}, bf16[304,128]{1,0:T(8,128)(2,1)S(1)}, u32[]{:S(2)}, u32[]{:S(2)}) collective-permute-start(bf16[304,128]{1,0:T(8,128)(2,1)} %get-tuple-element.42), channel_id=1, source_target_pairs={{0,1},{1,0},{2,3},{3,2},{4,5},{5,4},{6,7},{7,6},{8,9},{9,8},{10,11... | collective-permute-start | bytes 233480 | tf_op jit(solution)/shard_map/ppermute | solution.py:597
  5.5 9.9 %collective-permute-start.3 = (bf16[304,128]{1,0:T(8,128)(2,1)}, bf16[304,128]{1,0:T(8,128)(2,1)S(1)}, u32[]{:S(2)}, u32[]{:S(2)}) collective-permute-start(bf16[304,128]{1,0:T(8,128)(2,1)} %get-tuple-element.43), channel_id=1, source_target_pairs={{1,2},{2,1},{5,6},{6,5},{9,10},{10,9},{13,14},{14,13},{17,18},{18,... | collective-permute-start | bytes 233480 | tf_op jit(solution)/shard_map/ppermute | solution.py:597
  6.1 5.1 %copy-start.1 = (bf16[288,128]{1,0:T(8,128)(2,1)S(1)}, bf16[288,128]{1,0:T(8,128)(2,1)}, u32[]{:S(2)}) copy-start(bf16[288,128]{1,0:T(8,128)(2,1)} %get-tuple-element.32.first) | copy-start | bytes 221188
  6.1 6.9 %copy-start = (bf16[4,512,128]{2,1,0:T(8,128)(2,1)S(1)}, bf16[4,512,128]{2,1,0:T(8,128)(2,1)}, u32[]{:S(2)}) copy-start(bf16[4,512,128]{2,1,0:T(8,128)(2,1)} %get-tuple-element.57.grd.refs_3_) | copy-start | bytes 1572868
  8.2 7.6 %copy-start.3 = (s32[4,27]{1,0:T(4,128)S(1)}, s32[4,27]{1,0:T(4,128)}, u32[]{:S(2)}) copy-start(s32[4,27]{1,0:T(4,128)} %refs_0_.3) | copy-start | bytes 1300
  11.2 4.5 %collective-permute-start.1 = (bf16[320,128]{1,0:T(8,128)(2,1)S(1)}, bf16[320,128]{1,0:T(8,128)(2,1)S(1)}, u32[]{:S(2)}, u32[]{:S(2)}) collective-permute-start(bf16[320,128]{1,0:T(8,128)(2,1)S(1)} %get-tuple-element.41), channel_id=1, source_target_pairs={{0,4},{4,0},{8,12},{12,8},{16,20},{20,16},{24,28},{28,24},{1,5},{5... | collective-permute-start | bytes 245768 | tf_op jit(solution)/shard_map/ppermute | solution.py:597
  13.0 19.0 %copy-start.2 = (s32[4,512]{1,0:T(4,128)S(1)}, s32[4,512]{1,0:T(4,128)}, u32[]{:S(2)}) copy-start(s32[4,512]{1,0:T(4,128)} %refs_1_.3) | copy-start | bytes 24580
  13.0 19.0 %copy-start.4 = (bf16[27,128,128]{2,1,0:T(8,128)(2,1)S(1)}, bf16[27,128,128]{2,1,0:T(8,128)(2,1)}, u32[]{:S(2)}) copy-start(bf16[27,128,128]{2,1,0:T(8,128)(2,1)} %param.9) | copy-start | bytes 2654212
  13.0 19.1 %copy-start.5 = (bf16[4,512,128]{2,1,0:T(8,128)(2,1)S(1)}, bf16[4,512,128]{2,1,0:T(8,128)(2,1)}, u32[]{:S(2)}) copy-start(bf16[4,512,128]{2,1,0:T(8,128)(2,1)} %get-tuple-element.49.refs_3_) | copy-start | bytes 1572868
  17.7 4.4 %collective-permute-start.4 = (f32[1728,128]{1,0:T(8,128)S(1)}, f32[1728,128]{1,0:T(8,128)S(1)}, u32[]{:S(2)}, u32[]{:S(2)}) collective-permute-start(f32[1728,128]{1,0:T(8,128)S(1)} %get-tuple-element.45), channel_id=1, source_target_pairs={{0,1},{1,0},{2,3},{3,2},{4,5},{5,4},{6,7},{7,6},{8,9},{9,8},{10,11... | collective-permute-start | bytes 2654216 | tf_op jit(solution)/shard_map/ppermute | solution.py:597
  23.3 18.1 %all-to-all-start = ((f16[16,112,128]{2,1,0:T(8,128)(2,1)}), f16[16,112,128]{2,1,0:T(8,128)(2,1)S(1)}, u32[]{:S(2)}, u32[]{:S(2)}) async-start(f16[16,112,128]{2,1,0:T(8,128)(2,1)} %convert_element_type.15), calls=%async_computation | async-start | bytes 917504 | tf_op jit(solution)/shard_map/all_to_all | solution.py:621
  29.8 2.3 %collective-permute-start.5 = (bf16[32,128]{1,0:T(8,128)(2,1)S(1)}, bf16[32,128]{1,0:T(8,128)(2,1)S(1)}, u32[]{:S(2)}, u32[]{:S(2)}) collective-permute-start(bf16[32,128]{1,0:T(8,128)(2,1)S(1)} %get-tuple-element.51), channel_id=1, source_target_pairs={{0,1},{1,0},{2,3},{3,2},{4,5},{5,4},{6,7},{7,6},{8,9},{9,8},{10,11... | collective-permute-start | bytes 24584 | tf_op jit(solution)/shard_map/ppermute | solution.py:597
  29.9 2.2 %collective-permute-start.6 = (bf16[32,128]{1,0:T(8,128)(2,1)S(1)}, bf16[32,128]{1,0:T(8,128)(2,1)S(1)}, u32[]{:S(2)}, u32[]{:S(2)}) collective-permute-start(bf16[32,128]{1,0:T(8,128)(2,1)S(1)} %get-tuple-element.52), channel_id=1, source_target_pairs={{1,2},{2,1},{5,6},{6,5},{9,10},{10,9},{13,14},{14,13},{17,18},{18,... | collective-permute-start | bytes 24584 | tf_op jit(solution)/shard_map/ppermute | solution.py:597
  30.5 7.6 %collective-permute-start.7 = (bf16[256,128]{1,0:T(8,128)(2,1)S(1)}, bf16[256,128]{1,0:T(8,128)(2,1)S(1)}, u32[]{:S(2)}, u32[]{:S(2)}) collective-permute-start(bf16[256,128]{1,0:T(8,128)(2,1)S(1)} %get-tuple-element.53), channel_id=1, source_target_pairs={{0,4},{4,0},{8,12},{12,8},{16,20},{20,16},{24,28},{28,24},{1,5},{5... | collective-permute-start | bytes 196616 | tf_op jit(solution)/shard_map/ppermute | solution.py:597
  42.5 17.2 %all-to-all-start.1 = ((f16[16,112,128]{2,1,0:T(8,128)(2,1)}), f16[16,112,128]{2,1,0:T(8,128)(2,1)S(1)}, u32[]{:S(2)}, u32[]{:S(2)}) async-start(f16[16,112,128]{2,1,0:T(8,128)(2,1)} %convert_element_type.17), calls=%async_computation.1 | async-start | bytes 917504 | tf_op jit(solution)/shard_map/all_to_all | solution.py:621
  59.7 1.8 %collective-permute-start.8 = (f16[16,112,128]{2,1,0:T(8,128)(2,1)S(1)}, f16[16,112,128]{2,1,0:T(8,128)(2,1)S(1)}, u32[]{:S(2)}, u32[]{:S(2)}) collective-permute-start(f16[16,112,128]{2,1,0:T(8,128)(2,1)S(1)} %all-to-all-done.1), channel_id=1, source_target_pairs={{0,1},{1,0},{2,3},{3,2},{4,5},{5,4},{6,7},{7,6},{8,9},{9,8},{10,11... | collective-permute-start | bytes 1376264 | tf_op jit(solution)/shard_map/ppermute | solution.py:597

commit v15 on v14

--- a/solution.py
+++ b/solution.py
@@ -71,31 +71,38 @@
     sends = refs[0:4]
     y_out, x_out = refs[4:6], refs[6:8]
     face_ref, edge_ref, near, raw, mask_ref, full, sems = refs[8:]
-    got_mask, got_feat, got_grad, *tables = fetching(
+    got_mask, *tables = fetching(
         (mask_hbm, mask_ref, sems.at[0]),
-        (feat_hbm, raw.at[0], sems.at[1]),
-        (grad_hbm, raw.at[1], sems.at[2]),
-        (face_hbm, face_ref, sems.at[3]),
-        (edge_hbm, edge_ref, sems.at[4]),
-        (near_hbm, near, sems.at[5]),
+        (face_hbm, face_ref, sems.at[1]),
+        (edge_hbm, edge_ref, sems.at[2]),
+        (near_hbm, near, sems.at[3]),
     )
+    got = [
+        fetching(
+            (feat_hbm.at[s], raw.at[0, s], sems.at[4 + 2 * s]),
+            (grad_hbm.at[s], raw.at[1, s], sems.at[5 + 2 * s]),
+        )
+        for s in range(SLOTS)
+    ]
     got_mask.wait()
-    got_feat.wait()
-    got_grad.wait()
+    results = []
     for s in range(SLOTS):
         rows = mask_columns(mask_ref, s)
         for f in range(2):
+            got[s][f].wait()
             masked = raw[f, s].astype(jnp.float32) * rows
             full[f, s] = masked.reshape(8, 8, 8, C)
             raw[f, s] = masked.astype(jnp.bfloat16)
-    results = fetching(
-        (raw.at[0], held_out.at[0], sems.at[7]),
-        (raw.at[0], act_out, sems.at[8]),
-        (raw.at[1], grd_out, sems.at[9]),
-    )
+        first = 4 + 2 * SLOTS + 3 * s
+        results += fetching(
+            (raw.at[0, s], held_out.at[0, s], sems.at[first]),
+            (raw.at[0, s], act_out.at[s], sems.at[first + 1]),
+            (raw.at[1, s], grd_out.at[s], sems.at[first + 2]),
+        )
     for table in tables:
         table.wait()
-    results += fetching((near, near_out.at[0], sems.at[6]))
+    last = 4 + 5 * SLOTS
+    results += fetching((near, near_out.at[0], sems.at[last]))
     for axis, outs in enumerate((x_out, y_out)):
         odd = parity("gy" if axis else "gx")
         for k in range(2):
@@ -132,7 +139,7 @@
             outs[k][pl.ds(FACE_ROWS, lines.shape[0])] = lines
     x_out[1][pl.ds(X_ROWS + FACE_ROWS, SPARE_ROWS)] = jnp.zeros((SPARE_ROWS, C), jnp.bfloat16)
     for i, (built, send) in enumerate(zip(refs[4:8], sends)):
-        results += fetching((built, send, sems.at[10 + i]))
+        results += fetching((built, send, sems.at[last + 1 + i]))
     for result in results:
         result.wait()
 
@@ -161,7 +168,7 @@
             pltpu.VMEM((2, SLOTS, 512, C), jnp.bfloat16),
             pltpu.VMEM((SLOTS, 512), jnp.int32),
             pltpu.VMEM((2, SLOTS, 8, 8, 8, C), jnp.float32),
-            pltpu.SemaphoreType.DMA((14,)),
+            pltpu.SemaphoreType.DMA((4 + 5 * SLOTS + 5,)),
         ],
         compiler_params=pltpu.CompilerParams(vmem_limit_bytes=PACK_LIMIT),
         name="pack",
@@ -370,7 +377,7 @@
 
 
 def rim_kernel(near_hbm, inner, grd, x_ref, y0, y1, keep, send, lx, ly, corners, wide, near, sem, *refs):
-    vx, vy, ends_a, ends_g, side_x, side_y = refs
+    vx, vy, ends_a, ends_g, side_x, side_y, ends = refs
     (table,) = fetching((near_hbm, near, sem))
     fill_came(0, x_ref, (y0, y1), (), lx, ly, corners)
     for k, came in enumerate(parts_of(x_ref)):
@@ -403,13 +410,18 @@
         return lax.dot_general(cells, rows, (((0,), (0,)), ((), ())), preferred_element_type=jnp.float32)
 
     def end(line):
-        return jnp.concatenate([line, jnp.zeros((8, C), jnp.float32)], axis=0).astype(jnp.bfloat16)
+        return jnp.concatenate([line, jnp.zeros(line.shape, jnp.float32)], axis=0).astype(jnp.bfloat16)
 
     for side in range(2):
         rows = grads[:, 448 * side : 448 * side + 64].reshape(SLOTS * 64, C)
         side_x[side] = term(vx[side], rows)
         rows = lines[:, :, 7 * side].reshape(SLOTS * 64, C).astype(jnp.bfloat16)
         side_y[side] = term(vy[side], rows)
+    for sx in range(2):
+        for sy in range(2):
+            lines_g = jnp.concatenate([ends_g[sy, sx, z] for z in range(3)], axis=1)
+            ends[sx, sy] = term(end(ends_a[sx, sy]), end(lines_g))
+
     def write(halves):
         for x in range(3):
             for y in range(3):
@@ -422,7 +434,7 @@
                         value += side_y[y // 2, pl.ds((3 * x + z) * C, C)]
                     if x != 1 and y != 1:
                         sx, sy = x // 2, 1 - y // 2
-                        value += term(end(ends_a[sx, sy]), end(ends_g[sy, sx, z]))
+                        value += ends[sx, sy, :, pl.ds(z * C, C)]
                     for half in range(2):
                         low = max(first, half * HALF)
                         rows = min(first + C, (half + 1) * HALF) - low
@@ -456,6 +468,7 @@
             pltpu.VMEM((2, 2, 3, 8, C), jnp.float32),
             pltpu.VMEM((2, 9 * C, C), jnp.float32),
             pltpu.VMEM((2, 9 * C, C), jnp.float32),
+            pltpu.VMEM((2, 2, C, 3 * C), jnp.float32),
         ],
         compiler_params=pltpu.CompilerParams(vmem_limit_bytes=VMEM_LIMIT),
         cost_estimate=pl.CostEstimate(flops=2 * 256 * 36 * C * C, bytes_accessed=6 << 20, transcendentals=0),

time: 63 us -> 63 us (level)
  no operation moved by 1% of the time
where the time goes in v15:
time: 63 us; the launch traced here: 62.6 us
  Pallas kernels  23.9 us (38%)
  starting transfers between devices  21.2 us (34%)
  waiting for transfers between devices  14.7 us (23%)
  other arithmetic  1.84 us (3%)
  between operations  0.83 us (1%)
    all_to_all x2, starting transfers between devices, spread(): lax.all_to_all(blocks, ('gx', 'gy'), 0, 0, axis_index_groups=same_core, t...  12.4 us
    pallas_call x2, Pallas kernels, product(): pl.pallas_call(lambda *refs: product_kernel(f, *refs), out_shape=jax.Shap...  12.1 us
    all_to_all x2, waiting for transfers between devices, spread(): lax.all_to_all(blocks, ('gx', 'gy'), 0, 0, axis_index_groups=same_core, t...  8.46 us
    ppermute x8, starting transfers between devices, swapped(): return lax.ppermute(value, axis, pairs)  7.53 us
    ppermute x8, waiting for transfers between devices, swapped(): return lax.ppermute(value, axis, pairs)  3.2 us
    ppermute x1, waiting for transfers between devices, hopped(): return lax.ppermute(value, axis, pairs)  3.02 us
    pallas_call x1, Pallas kernels, pack(): pl.pallas_call(pack_kernel, out_shape=[jax.ShapeDtypeStruct((ROOM_BRICKS,...  2.95 us
    pallas_call x1, Pallas kernels, inner_terms(): pl.pallas_call(inner_kernel, out_shape=jax.ShapeDtypeStruct((ROWS, C), jn...  2.34 us
  transfers between devices with their start and end apart: 11, of which 6 were waited for; matrix products, arithmetic and copies ran while one was open for 0% of the time, Pallas kernels for 28%

profile of v15, /device:TPU:0, one launch (start us, length us, event | category | flops | bytes accessed | tf_op | source)
XLA Modules:
  0.0 62.6 jit_solution(10913438225943221285)
XLA Ops:
  0.6 3.0 %pack.1 = (bf16[48,4,512,128]{3,2,1,0:T(8,128)(2,1)}, bf16[4,512,128]{2,1,0:T(8,128)(2,1)}, bf16[4,512,128]{2,1,0:T(8,128)(2,1)}, s32[12288,4,27]{2,1,0:T(4,128)...) custom-call(s32[2,4]{1,0:T(2,128)} %bitcast.13, ...), custom_call_target="tpu_custom_call" | custom-call | tf_op jit(solution)/shard_map/pack/pallas_call | solution.py:152
  3.6 1.3 %collective-permute-start = (bf16[320,128]{1,0:T(8,128)(2,1)}, bf16[320,128]{1,0:T(8,128)(2,1)S(1)}, u32[]{:S(2)}, u32[]{:S(2)}) collective-permute-start(bf16[320,128]{1,0:T(8,128)(2,1)} %get-tuple-element.33), channel_id=1, source_target_pairs={{4,12},{12,20},{20,28},{8,0},{16,8},{24,16},{5,13},{13,21},{21,29}... | collective-permute-start | bytes 245768 | tf_op jit(solution)/shard_map/ppermute | solution.py:616
  4.9 0.5 collective-permute-start.2
  5.4 0.7 %collective-permute-start.3 = (bf16[304,128]{1,0:T(8,128)(2,1)}, bf16[304,128]{1,0:T(8,128)(2,1)S(1)}, u32[]{:S(2)}, u32[]{:S(2)}) collective-permute-start(bf16[304,128]{1,0:T(8,128)(2,1)} %get-tuple-element.43), channel_id=1, source_target_pairs={{1,2},{2,1},{5,6},{6,5},{9,10},{10,9},{13,14},{14,13},{17,18},{18,... | collective-permute-start | bytes 233480 | tf_op jit(solution)/shard_map/ppermute | solution.py:610
  6.1 0.0 copy-start.1
  6.1 0.0 copy-start
  6.1 2.0 %own_columns.1.v = bf16[4,10,64,1152]{3,2,1,0:T(8,128)(2,1)S(1)} custom-call(s32[12288,4,27]{2,1,0:T(4,128)} %get-tuple-element.34.near_hbm, bf16[48,4,512,128]{3,2,1,0:T(8,128)(2,1)} %get-tuple-element.35.act_hbm), custom_call_target="tpu_custom_call" | custom-call | flops 16777216 | bytes 6291456 | tf_op jit(solution)/shard_map/own_columns/pallas_call | solution.py:342
  8.1 0.0 copy-start.3
  8.1 3.0 %collective-permute-done.second = bf16[320,128]{1,0:T(8,128)(2,1)S(1)} collective-permute-done((bf16[320,128]{1,0:T(8,128)(2,1)}, bf16[320,128]{1,0:T(8,128)(2,1)S(1)}, u32[]{:S(2)}, u32[]{:S(2)}) %collective-permute-start) | collective-permute-done | bytes 81952 | tf_op jit(solution)/shard_map/ppermute | solution.py:616
  11.2 0.0 copy-done.1
  11.2 1.8 %collective-permute-start.1 = (bf16[320,128]{1,0:T(8,128)(2,1)S(1)}, bf16[320,128]{1,0:T(8,128)(2,1)S(1)}, u32[]{:S(2)}, u32[]{:S(2)}) collective-permute-start(bf16[320,128]{1,0:T(8,128)(2,1)S(1)} %get-tuple-element.41), channel_id=1, source_target_pairs={{0,4},{4,0},{8,12},{12,8},{16,20},{20,16},{24,28},{28,24},{1,5},{5... | collective-permute-start | bytes 245768 | tf_op jit(solution)/shard_map/ppermute | solution.py:610
  13.0 0.0 copy-done
  13.0 0.0 copy-start.2
  13.0 0.0 copy-start.4
  13.0 0.0 copy-start.5
  13.0 2.3 %inner_terms.1.inner = f32[3456,128]{1,0:T(8,128)S(1)} custom-call(bf16[4,10,64,1152]{3,2,1,0:T(8,128)(2,1)S(1)} %own_columns.1.v, bf16[4,512,128]{2,1,0:T(8,128)(2,1)S(1)} %copy-done), custom_call_target="tpu_custom_call" | custom-call | flops 1811939328 | bytes 6291456 | tf_op jit(solution)/shard_map/inner_terms/pallas_call | solution.py:367
  15.3 0.0 collective-permute-done.2.y0.refs_5_
  15.3 0.0 collective-permute-done.3.y1.refs_6_
  15.3 0.4 collective-permute-done.1.x_ref.x_came.refs_4_
  15.7 0.0 copy-done.3
  15.7 2.0 %rim_terms.1 = (f32[1728,128]{1,0:T(8,128)S(1)}, f32[1728,128]{1,0:T(8,128)S(1)}) custom-call(s32[4,27]{1,0:T(4,128)S(1)} %copy-done.3, f32[3456,128]{1,0:T(8,128)S(1)} %inner_terms.1.inner, bf16[4,512,128]{2,1,0:T(8,128)(2,1)S(1)} %copy-done, bf16[320,128]{1,0:T(8,128)(2,1)S(1)} %collective-permute-done.1.x_ref.x_came.refs_4_, ...), custom_call_target="tpu_custom_call" | custom-call | flops 301989888 | bytes 6291456 | tf_op jit(solution)/shard_map/rim_terms/pallas_call | solution.py:458
  17.7 2.3 %collective-permute-start.4 = (f32[1728,128]{1,0:T(8,128)S(1)}, f32[1728,128]{1,0:T(8,128)S(1)}, u32[]{:S(2)}, u32[]{:S(2)}) collective-permute-start(f32[1728,128]{1,0:T(8,128)S(1)} %get-tuple-element.45), channel_id=1, source_target_pairs={{0,1},{1,0},{2,3},{3,2},{4,5},{5,4},{6,7},{7,6},{8,9},{9,8},{10,11... | collective-permute-start | bytes 2654216 | tf_op jit(solution)/shard_map/ppermute | solution.py:610
  20.0 2.1 %collective-permute-done.4.refs_1_ = f32[1728,128]{1,0:T(8,128)S(1)} collective-permute-done((f32[1728,128]{1,0:T(8,128)S(1)}, f32[1728,128]{1,0:T(8,128)S(1)}, u32[]{:S(2)}, u32[]{:S(2)}) %collective-permute-start.4) | collective-permute-done | bytes 884768 | tf_op jit(solution)/shard_map/ppermute | solution.py:610
  22.1 0.3 merge.1
  22.4 0.8 %convert_element_type.15 = f16[16,112,128]{2,1,0:T(8,128)(2,1)} convert(f32[16,112,128]{2,1,0:T(8,128)S(1)} %merge.1) | non-fusion elementwise | flops 229376 | bytes 1376256 | tf_op jit(solution)/shard_map/convert_element_type | solution.py:653
  23.2 6.5 %all-to-all-start = ((f16[16,112,128]{2,1,0:T(8,128)(2,1)}), f16[16,112,128]{2,1,0:T(8,128)(2,1)S(1)}, u32[]{:S(2)}, u32[]{:S(2)}) async-start(f16[16,112,128]{2,1,0:T(8,128)(2,1)} %convert_element_type.15), calls=%async_computation | async-start | bytes 917504 | tf_op jit(solution)/shard_map/all_to_all | solution.py:634
  29.7 0.1 collective-permute-start.5
  29.8 0.7 %collective-permute-start.6 = (bf16[32,128]{1,0:T(8,128)(2,1)S(1)}, bf16[32,128]{1,0:T(8,128)(2,1)S(1)}, u32[]{:S(2)}, u32[]{:S(2)}) collective-permute-start(bf16[32,128]{1,0:T(8,128)(2,1)S(1)} %get-tuple-element.52), channel_id=1, source_target_pairs={{1,2},{2,1},{5,6},{6,5},{9,10},{10,9},{13,14},{14,13},{17,18},{18,... | collective-permute-start | bytes 24584 | tf_op jit(solution)/shard_map/ppermute | solution.py:610
  30.5 1.5 %collective-permute-start.7 = (bf16[256,128]{1,0:T(8,128)(2,1)S(1)}, bf16[256,128]{1,0:T(8,128)(2,1)S(1)}, u32[]{:S(2)}, u32[]{:S(2)}) collective-permute-start(bf16[256,128]{1,0:T(8,128)(2,1)S(1)} %get-tuple-element.53), channel_id=1, source_target_pairs={{0,4},{4,0},{8,12},{12,8},{16,20},{20,16},{24,28},{28,24},{1,5},{5... | collective-permute-start | bytes 196616 | tf_op jit(solution)/shard_map/ppermute | solution.py:610
  32.0 0.0 collective-permute-done.5.refs_7_
  32.0 0.0 collective-permute-done.6.refs_8_
  32.0 0.0 copy-done.2
  32.0 0.0 copy-done.4
  32.0 0.0 copy-done.5
  32.0 6.0 %output_product.1 = bf16[4,512,128]{2,1,0:T(8,128)(2,1)} custom-call(s32[4,27]{1,0:T(4,128)S(1)} %copy-done.3, s32[4,512]{1,0:T(4,128)S(1)} %copy-done.2, bf16[3456,128]{1,0:T(8,128)(2,1)S(1)} %bitcast.8, bf16[4,512,128]{2,1,0:T(8,128)(2,1)S(1)} %copy-done.5, bf16[320,128]{1,0:T(8,128)(2,1)S(1)} %collective-permute-done.1.x_ref.x_came.refs_4_, ...), custom_call_target="tpu_custom_call" | custom-call | flops 1811939328 | bytes 4194304 | tf_op jit(solution)/shard_map/output_product/pallas_call | solution.py:592
  38.1 0.0 collective-permute-done.7.refs_4_
  38.1 3.2 %all-to-all-done = f16[16,112,128]{2,1,0:T(8,128)(2,1)S(1)} async-done(((f16[16,112,128]{2,1,0:T(8,128)(2,1)}), f16[16,112,128]{2,1,0:T(8,128)(2,1)S(1)}, u32[]{:S(2)}, u32[]{:S(2)}) %all-to-all-start) | async-done | bytes 458784 | tf_op jit(solution)/shard_map/all_to_all | solution.py:634
  41.3 0.1 convert_element_type.16.refs_0_
  41.4 0.3 sum_blocks.1
  41.6 0.8 %convert_element_type.17 = f16[16,112,128]{2,1,0:T(8,128)(2,1)} convert(f32[16,112,128]{2,1,0:T(8,128)S(1)} %sum_blocks.1) | non-fusion elementwise | flops 229376 | bytes 1376256 | tf_op jit(solution)/shard_map/convert_element_type | solution.py:661
  42.5 5.9 %all-to-all-start.1 = ((f16[16,112,128]{2,1,0:T(8,128)(2,1)}), f16[16,112,128]{2,1,0:T(8,128)(2,1)S(1)}, u32[]{:S(2)}, u32[]{:S(2)}) async-start(f16[16,112,128]{2,1,0:T(8,128)(2,1)} %convert_element_type.17), calls=%async_computation.1 | async-start | bytes 917504 | tf_op jit(solution)/shard_map/all_to_all | solution.py:634
  48.4 6.1 %input_grad_product.1 = bf16[4,512,128]{2,1,0:T(8,128)(2,1)} custom-call(s32[4,27]{1,0:T(4,128)S(1)} %copy-done.3, s32[4,512]{1,0:T(4,128)S(1)} %copy-done.2, bf16[3456,128]{1,0:T(8,128)(2,1)S(1)} %bitcast.9, bf16[4,512,128]{2,1,0:T(8,128)(2,1)S(1)} %copy-done, bf16[256,128]{1,0:T(8,128)(2,1)S(1)} %collective-permute-done.7.refs_4_, ...), custom_call_target="tpu_custom_call" | custom-call | flops 1811939328 | bytes 4194304 | tf_op jit(solution)/shard_map/input_grad_product/pallas_call | solution.py:592
  54.5 5.2 %all-to-all-done.1 = f16[16,112,128]{2,1,0:T(8,128)(2,1)S(1)} async-done(((f16[16,112,128]{2,1,0:T(8,128)(2,1)}), f16[16,112,128]{2,1,0:T(8,128)(2,1)S(1)}, u32[]{:S(2)}, u32[]{:S(2)}) %all-to-all-start.1) | async-done | bytes 458784 | tf_op jit(solution)/shard_map/all_to_all | solution.py:634
  59.7 0.0 collective-permute-start.8
  59.7 0.1 convert_element_type.19.refs_0_
  59.8 1.0 %decode_own.1.refs_1_ = f32[2,1728,128]{2,1,0:T(8,128)} custom-call(f32[16,112,128]{2,1,0:T(8,128)S(1)} %convert_element_type.19.refs_0_), custom_call_target="tpu_custom_call" | custom-call | tf_op jit(solution)/shard_map/decode_own/pallas_call | solution.py:554
  60.7 0.8 %collective-permute-done.8 = f16[16,112,128]{2,1,0:T(8,128)(2,1)S(1)} collective-permute-done((f16[16,112,128]{2,1,0:T(8,128)(2,1)S(1)}, f16[16,112,128]{2,1,0:T(8,128)(2,1)S(1)}, u32[]{:S(2)}, u32[]{:S(2)}) %collective-permute-start.8) | collective-permute-done | bytes 458784 | tf_op jit(solution)/shard_map/ppermute | solution.py:610
  61.5 0.1 convert_element_type.18.refs_0_
  61.6 1.0 %decode_other.1 = f32[2,1728,128]{2,1,0:T(8,128)} custom-call(f32[16,112,128]{2,1,0:T(8,128)S(1)} %convert_element_type.18.refs_0_, f32[2,1728,128]{2,1,0:T(8,128)} %decode_own.1.refs_1_), custom_call_target="tpu_custom_call", output_to_operand_aliasing={{}: (1, {})} | custom-call | tf_op jit(solution)/shard_map/decode_other/pallas_call | solution.py:554
  (2 shorter events, 0.0 us)
Async XLA Ops:
  3.6 7.6 %collective-permute-start = (bf16[320,128]{1,0:T(8,128)(2,1)}, bf16[320,128]{1,0:T(8,128)(2,1)S(1)}, u32[]{:S(2)}, u32[]{:S(2)}) collective-permute-start(bf16[320,128]{1,0:T(8,128)(2,1)} %get-tuple-element.33), channel_id=1, source_target_pairs={{4,12},{12,20},{20,28},{8,0},{16,8},{24,16},{5,13},{13,21},{21,29}... | collective-permute-start | bytes 245768 | tf_op jit(solution)/shard_map/ppermute | solution.py:616
  4.9 10.4 %collective-permute-start.2 = (bf16[304,128]{1,0:T(8,128)(2,1)}, bf16[304,128]{1,0:T(8,128)(2,1)S(1)}, u32[]{:S(2)}, u32[]{:S(2)}) collective-permute-start(bf16[304,128]{1,0:T(8,128)(2,1)} %get-tuple-element.42), channel_id=1, source_target_pairs={{0,1},{1,0},{2,3},{3,2},{4,5},{5,4},{6,7},{7,6},{8,9},{9,8},{10,11... | collective-permute-start | bytes 233480 | tf_op jit(solution)/shard_map/ppermute | solution.py:610
  5.4 9.9 %collective-permute-start.3 = (bf16[304,128]{1,0:T(8,128)(2,1)}, bf16[304,128]{1,0:T(8,128)(2,1)S(1)}, u32[]{:S(2)}, u32[]{:S(2)}) collective-permute-start(bf16[304,128]{1,0:T(8,128)(2,1)} %get-tuple-element.43), channel_id=1, source_target_pairs={{1,2},{2,1},{5,6},{6,5},{9,10},{10,9},{13,14},{14,13},{17,18},{18,... | collective-permute-start | bytes 233480 | tf_op jit(solution)/shard_map/ppermute | solution.py:610
  6.1 5.1 %copy-start.1 = (bf16[288,128]{1,0:T(8,128)(2,1)S(1)}, bf16[288,128]{1,0:T(8,128)(2,1)}, u32[]{:S(2)}) copy-start(bf16[288,128]{1,0:T(8,128)(2,1)} %get-tuple-element.32.first) | copy-start | bytes 221188
  6.1 6.9 %copy-start = (bf16[4,512,128]{2,1,0:T(8,128)(2,1)S(1)}, bf16[4,512,128]{2,1,0:T(8,128)(2,1)}, u32[]{:S(2)}) copy-start(bf16[4,512,128]{2,1,0:T(8,128)(2,1)} %get-tuple-element.57.grd.refs_3_) | copy-start | bytes 1572868
  8.1 7.6 %copy-start.3 = (s32[4,27]{1,0:T(4,128)S(1)}, s32[4,27]{1,0:T(4,128)}, u32[]{:S(2)}) copy-start(s32[4,27]{1,0:T(4,128)} %refs_0_.3) | copy-start | bytes 1300
  11.2 4.5 %collective-permute-start.1 = (bf16[320,128]{1,0:T(8,128)(2,1)S(1)}, bf16[320,128]{1,0:T(8,128)(2,1)S(1)}, u32[]{:S(2)}, u32[]{:S(2)}) collective-permute-start(bf16[320,128]{1,0:T(8,128)(2,1)S(1)} %get-tuple-element.41), channel_id=1, source_target_pairs={{0,4},{4,0},{8,12},{12,8},{16,20},{20,16},{24,28},{28,24},{1,5},{5... | collective-permute-start | bytes 245768 | tf_op jit(solution)/shard_map/ppermute | solution.py:610
  13.0 19.1 %copy-start.2 = (s32[4,512]{1,0:T(4,128)S(1)}, s32[4,512]{1,0:T(4,128)}, u32[]{:S(2)}) copy-start(s32[4,512]{1,0:T(4,128)} %refs_1_.3) | copy-start | bytes 24580
  13.0 19.1 %copy-start.4 = (bf16[27,128,128]{2,1,0:T(8,128)(2,1)S(1)}, bf16[27,128,128]{2,1,0:T(8,128)(2,1)}, u32[]{:S(2)}) copy-start(bf16[27,128,128]{2,1,0:T(8,128)(2,1)} %param.9) | copy-start | bytes 2654212
  13.0 19.1 %copy-start.5 = (bf16[4,512,128]{2,1,0:T(8,128)(2,1)S(1)}, bf16[4,512,128]{2,1,0:T(8,128)(2,1)}, u32[]{:S(2)}) copy-start(bf16[4,512,128]{2,1,0:T(8,128)(2,1)} %get-tuple-element.49.refs_3_) | copy-start | bytes 1572868
  17.7 4.4 %collective-permute-start.4 = (f32[1728,128]{1,0:T(8,128)S(1)}, f32[1728,128]{1,0:T(8,128)S(1)}, u32[]{:S(2)}, u32[]{:S(2)}) collective-permute-start(f32[1728,128]{1,0:T(8,128)S(1)} %get-tuple-element.45), channel_id=1, source_target_pairs={{0,1},{1,0},{2,3},{3,2},{4,5},{5,4},{6,7},{7,6},{8,9},{9,8},{10,11... | collective-permute-start | bytes 2654216 | tf_op jit(solution)/shard_map/ppermute | solution.py:610
  23.2 18.1 %all-to-all-start = ((f16[16,112,128]{2,1,0:T(8,128)(2,1)}), f16[16,112,128]{2,1,0:T(8,128)(2,1)S(1)}, u32[]{:S(2)}, u32[]{:S(2)}) async-start(f16[16,112,128]{2,1,0:T(8,128)(2,1)} %convert_element_type.15), calls=%async_computation | async-start | bytes 917504 | tf_op jit(solution)/shard_map/all_to_all | solution.py:634
  29.7 2.3 %collective-permute-start.5 = (bf16[32,128]{1,0:T(8,128)(2,1)S(1)}, bf16[32,128]{1,0:T(8,128)(2,1)S(1)}, u32[]{:S(2)}, u32[]{:S(2)}) collective-permute-start(bf16[32,128]{1,0:T(8,128)(2,1)S(1)} %get-tuple-element.51), channel_id=1, source_target_pairs={{0,1},{1,0},{2,3},{3,2},{4,5},{5,4},{6,7},{7,6},{8,9},{9,8},{10,11... | collective-permute-start | bytes 24584 | tf_op jit(solution)/shard_map/ppermute | solution.py:610
  29.8 2.2 %collective-permute-start.6 = (bf16[32,128]{1,0:T(8,128)(2,1)S(1)}, bf16[32,128]{1,0:T(8,128)(2,1)S(1)}, u32[]{:S(2)}, u32[]{:S(2)}) collective-permute-start(bf16[32,128]{1,0:T(8,128)(2,1)S(1)} %get-tuple-element.52), channel_id=1, source_target_pairs={{1,2},{2,1},{5,6},{6,5},{9,10},{10,9},{13,14},{14,13},{17,18},{18,... | collective-permute-start | bytes 24584 | tf_op jit(solution)/shard_map/ppermute | solution.py:610
  30.5 7.6 %collective-permute-start.7 = (bf16[256,128]{1,0:T(8,128)(2,1)S(1)}, bf16[256,128]{1,0:T(8,128)(2,1)S(1)}, u32[]{:S(2)}, u32[]{:S(2)}) collective-permute-start(bf16[256,128]{1,0:T(8,128)(2,1)S(1)} %get-tuple-element.53), channel_id=1, source_target_pairs={{0,4},{4,0},{8,12},{12,8},{16,20},{20,16},{24,28},{28,24},{1,5},{5... | collective-permute-start | bytes 196616 | tf_op jit(solution)/shard_map/ppermute | solution.py:610
  42.5 17.2 %all-to-all-start.1 = ((f16[16,112,128]{2,1,0:T(8,128)(2,1)}), f16[16,112,128]{2,1,0:T(8,128)(2,1)S(1)}, u32[]{:S(2)}, u32[]{:S(2)}) async-start(f16[16,112,128]{2,1,0:T(8,128)(2,1)} %convert_element_type.17), calls=%async_computation.1 | async-start | bytes 917504 | tf_op jit(solution)/shard_map/all_to_all | solution.py:634
  59.7 1.8 %collective-permute-start.8 = (f16[16,112,128]{2,1,0:T(8,128)(2,1)S(1)}, f16[16,112,128]{2,1,0:T(8,128)(2,1)S(1)}, u32[]{:S(2)}, u32[]{:S(2)}) collective-permute-start(f16[16,112,128]{2,1,0:T(8,128)(2,1)S(1)} %all-to-all-done.1), channel_id=1, source_target_pairs={{0,1},{1,0},{2,3},{3,2},{4,5},{5,4},{6,7},{7,6},{8,9},{9,8},{10,11... | collective-permute-start | bytes 1376264 | tf_op jit(solution)/shard_map/ppermute | solution.py:610

commit v16 on v15

--- a/solution.py
+++ b/solution.py
@@ -643,11 +643,10 @@
     )
     x1 = hopped(x1, "gx")
     y_came = [swapped(y0, "gy", 0), swapped(y1, "gy", 1)]
+    x_came, x_more = join(x0, x1)
+    x_more, table = lax.optimization_barrier((x_more, table))
+    x_came = swapped(x_came, "gx", 0)
     v = own_columns(table, held_act)
-    x1, v = lax.optimization_barrier((x1, v))
-    x_came, x_more = join(x0, x1)
-    x_more, v = lax.optimization_barrier((x_more, v))
-    x_came = swapped(x_came, "gx", 0)
     inner = inner_terms(v, grd)
     keep, send = rim_terms(neighbours, inner, grd, x_came, y_came)
     blocks = merge(groups, take, held, keep, swapped(send, "gy", 0)).astype(jnp.float16)

time: 63 us -> 63.9 us (1.014)
  starting transfers between devices: 21.2 us -> 19.5 us
  waiting for transfers between devices: 14.7 us -> 16.4 us
  local copies, waits for them, and re-layouts: 0.03 us -> 0.91 us
    ppermute x1, waiting for transfers between devices: 3.02 us -> 5.1 us  [hopped(): return lax.ppermute(value, axis, pairs)]
    ppermute x8, starting transfers between devices: 7.53 us -> 5.79 us  [swapped(): return lax.ppermute(value, axis, pairs)]
    unnamed x12, local copies, waits for them, and re-layouts: 0.03 us -> 0.91 us
  transfers between devices with their start and end apart: 11 -> 11, of which waited for: 6 -> 5; matrix products, arithmetic and copies ran while one was open for 0% -> 0% of each run, Pallas kernels for 28% -> 28%
where the time goes in v16:
time: 63.9 us; the launch traced here: 63.4 us
  Pallas kernels  23.9 us (37%)
  starting transfers between devices  19.5 us (31%)
  waiting for transfers between devices  16.4 us (26%)
  other arithmetic  1.84 us (3%)
  local copies, waits for them, and re-layouts  0.91 us (1%)
  between operations  0.85 us (1%)
    all_to_all x2, starting transfers between devices, spread(): lax.all_to_all(blocks, ('gx', 'gy'), 0, 0, axis_index_groups=same_core, t...  12.4 us
    pallas_call x2, Pallas kernels, product(): pl.pallas_call(lambda *refs: product_kernel(f, *refs), out_shape=jax.Shap...  12.1 us
    all_to_all x2, waiting for transfers between devices, spread(): lax.all_to_all(blocks, ('gx', 'gy'), 0, 0, axis_index_groups=same_core, t...  8.42 us
    ppermute x8, starting transfers between devices, swapped(): return lax.ppermute(value, axis, pairs)  5.79 us
    ppermute x1, waiting for transfers between devices, hopped(): return lax.ppermute(value, axis, pairs)  5.1 us
    pallas_call x1, Pallas kernels, pack(): pl.pallas_call(pack_kernel, out_shape=[jax.ShapeDtypeStruct((ROOM_BRICKS,...  2.95 us
    ppermute x8, waiting for transfers between devices, swapped(): return lax.ppermute(value, axis, pairs)  2.84 us
    pallas_call x1, Pallas kernels, inner_terms(): pl.pallas_call(inner_kernel, out_shape=jax.ShapeDtypeStruct((ROWS, C), jn...  2.34 us
  transfers between devices with their start and end apart: 11, of which 5 were waited for; matrix products, arithmetic and copies ran while one was open for 0% of the time, Pallas kernels for 28%

profile of v16, /device:TPU:0, one launch (start us, length us, event | category | flops | bytes accessed | tf_op | source)
XLA Modules:
  0.0 63.4 jit_solution(7176958145725949664)
XLA Ops:
  0.6 3.0 %pack.1 = (bf16[48,4,512,128]{3,2,1,0:T(8,128)(2,1)}, bf16[4,512,128]{2,1,0:T(8,128)(2,1)}, bf16[4,512,128]{2,1,0:T(8,128)(2,1)}, s32[12288,4,27]{2,1,0:T(4,128)...) custom-call(s32[2,4]{1,0:T(2,128)} %bitcast.13, ...), custom_call_target="tpu_custom_call" | custom-call | tf_op jit(solution)/shard_map/pack/pallas_call | solution.py:152
  3.6 1.3 %collective-permute-start = (bf16[320,128]{1,0:T(8,128)(2,1)}, bf16[320,128]{1,0:T(8,128)(2,1)S(1)}, u32[]{:S(2)}, u32[]{:S(2)}) collective-permute-start(bf16[320,128]{1,0:T(8,128)(2,1)} %get-tuple-element.31), channel_id=1, source_target_pairs={{4,12},{12,20},{20,28},{8,0},{16,8},{24,16},{5,13},{13,21},{21,29}... | collective-permute-start | bytes 245768 | tf_op jit(solution)/shard_map/ppermute | solution.py:616
  4.9 0.5 collective-permute-start.2
  5.4 0.7 %collective-permute-start.3 = (bf16[304,128]{1,0:T(8,128)(2,1)}, bf16[304,128]{1,0:T(8,128)(2,1)S(1)}, u32[]{:S(2)}, u32[]{:S(2)}) collective-permute-start(bf16[304,128]{1,0:T(8,128)(2,1)} %get-tuple-element.39), channel_id=1, source_target_pairs={{1,2},{2,1},{5,6},{6,5},{9,10},{10,9},{13,14},{14,13},{17,18},{18,... | collective-permute-start | bytes 233480 | tf_op jit(solution)/shard_map/ppermute | solution.py:610
  6.1 5.1 %collective-permute-done.second = bf16[320,128]{1,0:T(8,128)(2,1)S(1)} collective-permute-done((bf16[320,128]{1,0:T(8,128)(2,1)}, bf16[320,128]{1,0:T(8,128)(2,1)S(1)}, u32[]{:S(2)}, u32[]{:S(2)}) %collective-permute-start) | collective-permute-done | bytes 81952 | tf_op jit(solution)/shard_map/ppermute | solution.py:616
  11.2 0.0 copy-start.1
  11.2 0.9 %copy-done.1 = bf16[288,128]{1,0:T(8,128)(2,1)S(1)} copy-done((bf16[288,128]{1,0:T(8,128)(2,1)S(1)}, bf16[288,128]{1,0:T(8,128)(2,1)}, u32[]{:S(2)}) %copy-start.1) | copy-done | bytes 73752
  12.1 1.3 %collective-permute-start.1 = (bf16[320,128]{1,0:T(8,128)(2,1)S(1)}, bf16[320,128]{1,0:T(8,128)(2,1)S(1)}, u32[]{:S(2)}, u32[]{:S(2)}) collective-permute-start(bf16[320,128]{1,0:T(8,128)(2,1)S(1)} %get-tuple-element.37), channel_id=1, source_target_pairs={{0,4},{4,0},{8,12},{12,8},{16,20},{20,16},{24,28},{28,24},{1,5},{5... | collective-permute-start | bytes 245768 | tf_op jit(solution)/shard_map/ppermute | solution.py:610
  13.3 0.0 copy-start
  13.3 2.0 %own_columns.1.v = bf16[4,10,64,1152]{3,2,1,0:T(8,128)(2,1)S(1)} custom-call(s32[12288,4,27]{2,1,0:T(4,128)} %get-tuple-element.34.near_hbm, bf16[48,4,512,128]{3,2,1,0:T(8,128)(2,1)} %get-tuple-element.35.act_hbm), custom_call_target="tpu_custom_call" | custom-call | flops 16777216 | bytes 6291456 | tf_op jit(solution)/shard_map/own_columns/pallas_call | solution.py:342
  15.4 0.0 copy-start.3
  15.4 0.0 copy-done
  15.4 0.0 copy-start.2
  15.4 0.0 copy-start.4
  15.4 0.0 copy-start.5
  15.4 2.3 %inner_terms.1.inner = f32[3456,128]{1,0:T(8,128)S(1)} custom-call(bf16[4,10,64,1152]{3,2,1,0:T(8,128)(2,1)S(1)} %own_columns.1.v, bf16[4,512,128]{2,1,0:T(8,128)(2,1)S(1)} %copy-done), custom_call_target="tpu_custom_call" | custom-call | flops 1811939328 | bytes 6291456 | tf_op jit(solution)/shard_map/inner_terms/pallas_call | solution.py:367
  17.8 0.0 collective-permute-done.2.y0.refs_5_
  17.8 0.0 collective-permute-done.3.y1.refs_6_
  17.8 0.0 collective-permute-done.1.x_ref.x_came.refs_4_
  17.8 0.0 copy-done.3
  17.8 2.0 %rim_terms.1 = (f32[1728,128]{1,0:T(8,128)S(1)}, f32[1728,128]{1,0:T(8,128)S(1)}) custom-call(s32[4,27]{1,0:T(4,128)S(1)} %copy-done.3, f32[3456,128]{1,0:T(8,128)S(1)} %inner_terms.1.inner, bf16[4,512,128]{2,1,0:T(8,128)(2,1)S(1)} %copy-done, bf16[320,128]{1,0:T(8,128)(2,1)S(1)} %collective-permute-done.1.x_ref.x_came.refs_4_, ...), custom_call_target="tpu_custom_call" | custom-call | flops 301989888 | bytes 6291456 | tf_op jit(solution)/shard_map/rim_terms/pallas_call | solution.py:458
  19.8 1.1 %collective-permute-start.4 = (f32[1728,128]{1,0:T(8,128)S(1)}, f32[1728,128]{1,0:T(8,128)S(1)}, u32[]{:S(2)}, u32[]{:S(2)}) collective-permute-start(f32[1728,128]{1,0:T(8,128)S(1)} %get-tuple-element.41), channel_id=1, source_target_pairs={{0,1},{1,0},{2,3},{3,2},{4,5},{5,4},{6,7},{7,6},{8,9},{9,8},{10,11... | collective-permute-start | bytes 2654216 | tf_op jit(solution)/shard_map/ppermute | solution.py:610
  20.9 2.1 %collective-permute-done.4.refs_1_ = f32[1728,128]{1,0:T(8,128)S(1)} collective-permute-done((f32[1728,128]{1,0:T(8,128)S(1)}, f32[1728,128]{1,0:T(8,128)S(1)}, u32[]{:S(2)}, u32[]{:S(2)}) %collective-permute-start.4) | collective-permute-done | bytes 884768 | tf_op jit(solution)/shard_map/ppermute | solution.py:610
  22.9 0.3 merge.1
  23.3 0.8 %convert_element_type.15 = f16[16,112,128]{2,1,0:T(8,128)(2,1)} convert(f32[16,112,128]{2,1,0:T(8,128)S(1)} %merge.1) | non-fusion elementwise | flops 229376 | bytes 1376256 | tf_op jit(solution)/shard_map/convert_element_type | solution.py:652
  24.1 6.5 %all-to-all-start = ((f16[16,112,128]{2,1,0:T(8,128)(2,1)}), f16[16,112,128]{2,1,0:T(8,128)(2,1)S(1)}, u32[]{:S(2)}, u32[]{:S(2)}) async-start(f16[16,112,128]{2,1,0:T(8,128)(2,1)} %convert_element_type.15), calls=%async_computation | async-start | bytes 917504 | tf_op jit(solution)/shard_map/all_to_all | solution.py:634
  30.6 0.1 collective-permute-start.5
  30.7 0.7 %collective-permute-start.6 = (bf16[32,128]{1,0:T(8,128)(2,1)S(1)}, bf16[32,128]{1,0:T(8,128)(2,1)S(1)}, u32[]{:S(2)}, u32[]{:S(2)}) collective-permute-start(bf16[32,128]{1,0:T(8,128)(2,1)S(1)} %get-tuple-element.48), channel_id=1, source_target_pairs={{1,2},{2,1},{5,6},{6,5},{9,10},{10,9},{13,14},{14,13},{17,18},{18,... | collective-permute-start | bytes 24584 | tf_op jit(solution)/shard_map/ppermute | solution.py:610
  31.3 1.5 %collective-permute-start.7 = (bf16[256,128]{1,0:T(8,128)(2,1)S(1)}, bf16[256,128]{1,0:T(8,128)(2,1)S(1)}, u32[]{:S(2)}, u32[]{:S(2)}) collective-permute-start(bf16[256,128]{1,0:T(8,128)(2,1)S(1)} %get-tuple-element.49), channel_id=1, source_target_pairs={{0,4},{4,0},{8,12},{12,8},{16,20},{20,16},{24,28},{28,24},{1,5},{5... | collective-permute-start | bytes 196616 | tf_op jit(solution)/shard_map/ppermute | solution.py:610
  32.9 0.0 collective-permute-done.5.refs_7_
  32.9 0.0 collective-permute-done.6.refs_8_
  32.9 0.0 copy-done.2
  32.9 0.0 copy-done.4
  32.9 0.0 copy-done.5
  32.9 6.0 %output_product.1 = bf16[4,512,128]{2,1,0:T(8,128)(2,1)} custom-call(s32[4,27]{1,0:T(4,128)S(1)} %copy-done.3, s32[4,512]{1,0:T(4,128)S(1)} %copy-done.2, bf16[3456,128]{1,0:T(8,128)(2,1)S(1)} %bitcast.8, bf16[4,512,128]{2,1,0:T(8,128)(2,1)S(1)} %copy-done.5, bf16[320,128]{1,0:T(8,128)(2,1)S(1)} %collective-permute-done.1.x_ref.x_came.refs_4_, ...), custom_call_target="tpu_custom_call" | custom-call | flops 1811939328 | bytes 4194304 | tf_op jit(solution)/shard_map/output_product/pallas_call | solution.py:592
  38.9 0.0 collective-permute-done.7.refs_4_
  38.9 3.2 %all-to-all-done = f16[16,112,128]{2,1,0:T(8,128)(2,1)S(1)} async-done(((f16[16,112,128]{2,1,0:T(8,128)(2,1)}), f16[16,112,128]{2,1,0:T(8,128)(2,1)S(1)}, u32[]{:S(2)}, u32[]{:S(2)}) %all-to-all-start) | async-done | bytes 458784 | tf_op jit(solution)/shard_map/all_to_all | solution.py:634
  42.2 0.1 convert_element_type.16.refs_0_
  42.2 0.3 sum_blocks.1
  42.5 0.8 %convert_element_type.17 = f16[16,112,128]{2,1,0:T(8,128)(2,1)} convert(f32[16,112,128]{2,1,0:T(8,128)S(1)} %sum_blocks.1) | non-fusion elementwise | flops 229376 | bytes 1376256 | tf_op jit(solution)/shard_map/convert_element_type | solution.py:660
  43.3 6.0 %all-to-all-start.1 = ((f16[16,112,128]{2,1,0:T(8,128)(2,1)}), f16[16,112,128]{2,1,0:T(8,128)(2,1)S(1)}, u32[]{:S(2)}, u32[]{:S(2)}) async-start(f16[16,112,128]{2,1,0:T(8,128)(2,1)} %convert_element_type.17), calls=%async_computation.1 | async-start | bytes 917504 | tf_op jit(solution)/shard_map/all_to_all | solution.py:634
  49.3 6.1 %input_grad_product.1 = bf16[4,512,128]{2,1,0:T(8,128)(2,1)} custom-call(s32[4,27]{1,0:T(4,128)S(1)} %copy-done.3, s32[4,512]{1,0:T(4,128)S(1)} %copy-done.2, bf16[3456,128]{1,0:T(8,128)(2,1)S(1)} %bitcast.9, bf16[4,512,128]{2,1,0:T(8,128)(2,1)S(1)} %copy-done, bf16[256,128]{1,0:T(8,128)(2,1)S(1)} %collective-permute-done.7.refs_4_, ...), custom_call_target="tpu_custom_call" | custom-call | flops 1811939328 | bytes 4194304 | tf_op jit(solution)/shard_map/input_grad_product/pallas_call | solution.py:592
  55.4 5.2 %all-to-all-done.1 = f16[16,112,128]{2,1,0:T(8,128)(2,1)S(1)} async-done(((f16[16,112,128]{2,1,0:T(8,128)(2,1)}), f16[16,112,128]{2,1,0:T(8,128)(2,1)S(1)}, u32[]{:S(2)}, u32[]{:S(2)}) %all-to-all-start.1) | async-done | bytes 458784 | tf_op jit(solution)/shard_map/all_to_all | solution.py:634
  60.6 0.0 collective-permute-start.8
  60.6 0.1 convert_element_type.19.refs_0_
  60.6 1.0 %decode_own.1.refs_1_ = f32[2,1728,128]{2,1,0:T(8,128)} custom-call(f32[16,112,128]{2,1,0:T(8,128)S(1)} %convert_element_type.19.refs_0_), custom_call_target="tpu_custom_call" | custom-call | tf_op jit(solution)/shard_map/decode_own/pallas_call | solution.py:554
  61.6 0.8 %collective-permute-done.8 = f16[16,112,128]{2,1,0:T(8,128)(2,1)S(1)} collective-permute-done((f16[16,112,128]{2,1,0:T(8,128)(2,1)S(1)}, f16[16,112,128]{2,1,0:T(8,128)(2,1)S(1)}, u32[]{:S(2)}, u32[]{:S(2)}) %collective-permute-start.8) | collective-permute-done | bytes 458784 | tf_op jit(solution)/shard_map/ppermute | solution.py:610
  62.4 0.1 convert_element_type.18.refs_0_
  62.4 1.0 %decode_other.1 = f32[2,1728,128]{2,1,0:T(8,128)} custom-call(f32[16,112,128]{2,1,0:T(8,128)S(1)} %convert_element_type.18.refs_0_, f32[2,1728,128]{2,1,0:T(8,128)} %decode_own.1.refs_1_), custom_call_target="tpu_custom_call", output_to_operand_aliasing={{}: (1, {})} | custom-call | tf_op jit(solution)/shard_map/decode_other/pallas_call | solution.py:554
  (2 shorter events, 0.0 us)
Async XLA Ops:
  3.6 7.6 %collective-permute-start = (bf16[320,128]{1,0:T(8,128)(2,1)}, bf16[320,128]{1,0:T(8,128)(2,1)S(1)}, u32[]{:S(2)}, u32[]{:S(2)}) collective-permute-start(bf16[320,128]{1,0:T(8,128)(2,1)} %get-tuple-element.31), channel_id=1, source_target_pairs={{4,12},{12,20},{20,28},{8,0},{16,8},{24,16},{5,13},{13,21},{21,29}... | collective-permute-start | bytes 245768 | tf_op jit(solution)/shard_map/ppermute | solution.py:616
  4.9 12.9 %collective-permute-start.2 = (bf16[304,128]{1,0:T(8,128)(2,1)}, bf16[304,128]{1,0:T(8,128)(2,1)S(1)}, u32[]{:S(2)}, u32[]{:S(2)}) collective-permute-start(bf16[304,128]{1,0:T(8,128)(2,1)} %get-tuple-element.38), channel_id=1, source_target_pairs={{0,1},{1,0},{2,3},{3,2},{4,5},{5,4},{6,7},{7,6},{8,9},{9,8},{10,11... | collective-permute-start | bytes 233480 | tf_op jit(solution)/shard_map/ppermute | solution.py:610
  5.4 12.4 %collective-permute-start.3 = (bf16[304,128]{1,0:T(8,128)(2,1)}, bf16[304,128]{1,0:T(8,128)(2,1)S(1)}, u32[]{:S(2)}, u32[]{:S(2)}) collective-permute-start(bf16[304,128]{1,0:T(8,128)(2,1)} %get-tuple-element.39), channel_id=1, source_target_pairs={{1,2},{2,1},{5,6},{6,5},{9,10},{10,9},{13,14},{14,13},{17,18},{18,... | collective-permute-start | bytes 233480 | tf_op jit(solution)/shard_map/ppermute | solution.py:610
  11.2 0.9 %copy-start.1 = (bf16[288,128]{1,0:T(8,128)(2,1)S(1)}, bf16[288,128]{1,0:T(8,128)(2,1)}, u32[]{:S(2)}) copy-start(bf16[288,128]{1,0:T(8,128)(2,1)} %get-tuple-element.30.first) | copy-start | bytes 221188
  12.1 5.7 %collective-permute-start.1 = (bf16[320,128]{1,0:T(8,128)(2,1)S(1)}, bf16[320,128]{1,0:T(8,128)(2,1)S(1)}, u32[]{:S(2)}, u32[]{:S(2)}) collective-permute-start(bf16[320,128]{1,0:T(8,128)(2,1)S(1)} %get-tuple-element.37), channel_id=1, source_target_pairs={{0,4},{4,0},{8,12},{12,8},{16,20},{20,16},{24,28},{28,24},{1,5},{5... | collective-permute-start | bytes 245768 | tf_op jit(solution)/shard_map/ppermute | solution.py:610
  13.3 2.1 %copy-start = (bf16[4,512,128]{2,1,0:T(8,128)(2,1)S(1)}, bf16[4,512,128]{2,1,0:T(8,128)(2,1)}, u32[]{:S(2)}) copy-start(bf16[4,512,128]{2,1,0:T(8,128)(2,1)} %get-tuple-element.53.grd.refs_3_) | copy-start | bytes 1572868
  15.4 2.4 %copy-start.3 = (s32[4,27]{1,0:T(4,128)S(1)}, s32[4,27]{1,0:T(4,128)}, u32[]{:S(2)}) copy-start(s32[4,27]{1,0:T(4,128)} %refs_0_.3) | copy-start | bytes 1300
  15.4 17.5 %copy-start.2 = (s32[4,512]{1,0:T(4,128)S(1)}, s32[4,512]{1,0:T(4,128)}, u32[]{:S(2)}) copy-start(s32[4,512]{1,0:T(4,128)} %refs_1_.3) | copy-start | bytes 24580
  15.4 17.5 %copy-start.4 = (bf16[27,128,128]{2,1,0:T(8,128)(2,1)S(1)}, bf16[27,128,128]{2,1,0:T(8,128)(2,1)}, u32[]{:S(2)}) copy-start(bf16[27,128,128]{2,1,0:T(8,128)(2,1)} %param.9) | copy-start | bytes 2654212
  15.4 17.5 %copy-start.5 = (bf16[4,512,128]{2,1,0:T(8,128)(2,1)S(1)}, bf16[4,512,128]{2,1,0:T(8,128)(2,1)}, u32[]{:S(2)}) copy-start(bf16[4,512,128]{2,1,0:T(8,128)(2,1)} %get-tuple-element.45.refs_3_) | copy-start | bytes 1572868
  19.8 3.1 %collective-permute-start.4 = (f32[1728,128]{1,0:T(8,128)S(1)}, f32[1728,128]{1,0:T(8,128)S(1)}, u32[]{:S(2)}, u32[]{:S(2)}) collective-permute-start(f32[1728,128]{1,0:T(8,128)S(1)} %get-tuple-element.41), channel_id=1, source_target_pairs={{0,1},{1,0},{2,3},{3,2},{4,5},{5,4},{6,7},{7,6},{8,9},{9,8},{10,11... | collective-permute-start | bytes 2654216 | tf_op jit(solution)/shard_map/ppermute | solution.py:610
  24.1 18.0 %all-to-all-start = ((f16[16,112,128]{2,1,0:T(8,128)(2,1)}), f16[16,112,128]{2,1,0:T(8,128)(2,1)S(1)}, u32[]{:S(2)}, u32[]{:S(2)}) async-start(f16[16,112,128]{2,1,0:T(8,128)(2,1)} %convert_element_type.15), calls=%async_computation | async-start | bytes 917504 | tf_op jit(solution)/shard_map/all_to_all | solution.py:634
  30.6 2.3 %collective-permute-start.5 = (bf16[32,128]{1,0:T(8,128)(2,1)S(1)}, bf16[32,128]{1,0:T(8,128)(2,1)S(1)}, u32[]{:S(2)}, u32[]{:S(2)}) collective-permute-start(bf16[32,128]{1,0:T(8,128)(2,1)S(1)} %get-tuple-element.47), channel_id=1, source_target_pairs={{0,1},{1,0},{2,3},{3,2},{4,5},{5,4},{6,7},{7,6},{8,9},{9,8},{10,11... | collective-permute-start | bytes 24584 | tf_op jit(solution)/shard_map/ppermute | solution.py:610
  30.7 2.2 %collective-permute-start.6 = (bf16[32,128]{1,0:T(8,128)(2,1)S(1)}, bf16[32,128]{1,0:T(8,128)(2,1)S(1)}, u32[]{:S(2)}, u32[]{:S(2)}) collective-permute-start(bf16[32,128]{1,0:T(8,128)(2,1)S(1)} %get-tuple-element.48), channel_id=1, source_target_pairs={{1,2},{2,1},{5,6},{6,5},{9,10},{10,9},{13,14},{14,13},{17,18},{18,... | collective-permute-start | bytes 24584 | tf_op jit(solution)/shard_map/ppermute | solution.py:610
  31.3 7.6 %collective-permute-start.7 = (bf16[256,128]{1,0:T(8,128)(2,1)S(1)}, bf16[256,128]{1,0:T(8,128)(2,1)S(1)}, u32[]{:S(2)}, u32[]{:S(2)}) collective-permute-start(bf16[256,128]{1,0:T(8,128)(2,1)S(1)} %get-tuple-element.49), channel_id=1, source_target_pairs={{0,4},{4,0},{8,12},{12,8},{16,20},{20,16},{24,28},{28,24},{1,5},{5... | collective-permute-start | bytes 196616 | tf_op jit(solution)/shard_map/ppermute | solution.py:610
  43.3 17.2 %all-to-all-start.1 = ((f16[16,112,128]{2,1,0:T(8,128)(2,1)}), f16[16,112,128]{2,1,0:T(8,128)(2,1)S(1)}, u32[]{:S(2)}, u32[]{:S(2)}) async-start(f16[16,112,128]{2,1,0:T(8,128)(2,1)} %convert_element_type.17), calls=%async_computation.1 | async-start | bytes 917504 | tf_op jit(solution)/shard_map/all_to_all | solution.py:634
  60.6 1.8 %collective-permute-start.8 = (f16[16,112,128]{2,1,0:T(8,128)(2,1)S(1)}, f16[16,112,128]{2,1,0:T(8,128)(2,1)S(1)}, u32[]{:S(2)}, u32[]{:S(2)}) collective-permute-start(f16[16,112,128]{2,1,0:T(8,128)(2,1)S(1)} %all-to-all-done.1), channel_id=1, source_target_pairs={{0,1},{1,0},{2,3},{3,2},{4,5},{5,4},{6,7},{7,6},{8,9},{9,8},{10,11... | collective-permute-start | bytes 1376264 | tf_op jit(solution)/shard_map/ppermute | solution.py:610

commit v17 on v15

--- a/solution.py
+++ b/solution.py
@@ -626,7 +626,7 @@
     half, row = groups // 2, size_y // 2
     inward = [k + j for k in range(half - row, -1, -row) for j in range(row)]
     in_turn = [k for pair in zip(range(half, groups), inward) for k in pair]
-    onward = [(k + half) % groups for k in range(groups)]
+    onward = [(k + half // 2) % groups for k in range(groups)]
     places = [onward.index(k) for k in in_turn]
 
     def spread(blocks, order):

time: 63 us -> 63.5 us (level)
  waiting for transfers between devices: 14.7 us -> 15.8 us
    all_to_all x2, waiting for transfers between devices: 8.46 us -> 9.62 us  [spread(): lax.all_to_all(blocks, ('gx', 'gy'), 0, 0, axis_index_groups=same_core, t...]
    all_to_all x2, starting transfers between devices: 12.4 us -> 11.8 us  [spread(): lax.all_to_all(blocks, ('gx', 'gy'), 0, 0, axis_index_groups=same_core, t...]
where the time goes in v17:
time: 63.5 us; the launch traced here: 63.1 us
  Pallas kernels  23.9 us (38%)
  starting transfers between devices  20.6 us (32%)
  waiting for transfers between devices  15.8 us (25%)
  other arithmetic  1.84 us (3%)
  between operations  0.83 us (1%)
    pallas_call x2, Pallas kernels, product(): pl.pallas_call(lambda *refs: product_kernel(f, *refs), out_shape=jax.Shap...  12.1 us
    all_to_all x2, starting transfers between devices, spread(): lax.all_to_all(blocks, ('gx', 'gy'), 0, 0, axis_index_groups=same_core, t...  11.8 us
    all_to_all x2, waiting for transfers between devices, spread(): lax.all_to_all(blocks, ('gx', 'gy'), 0, 0, axis_index_groups=same_core, t...  9.62 us
    ppermute x8, starting transfers between devices, swapped(): return lax.ppermute(value, axis, pairs)  7.53 us
    ppermute x8, waiting for transfers between devices, swapped(): return lax.ppermute(value, axis, pairs)  3.2 us
    ppermute x1, waiting for transfers between devices, hopped(): return lax.ppermute(value, axis, pairs)  3.02 us
    pallas_call x1, Pallas kernels, pack(): pl.pallas_call(pack_kernel, out_shape=[jax.ShapeDtypeStruct((ROOM_BRICKS,...  2.95 us
    pallas_call x1, Pallas kernels, inner_terms(): pl.pallas_call(inner_kernel, out_shape=jax.ShapeDtypeStruct((ROWS, C), jn...  2.34 us
  transfers between devices with their start and end apart: 11, of which 6 were waited for; matrix products, arithmetic and copies ran while one was open for 0% of the time, Pallas kernels for 28%

profile of v17, /device:TPU:0, one launch (start us, length us, event | category | flops | bytes accessed | tf_op | source)
XLA Modules:
  0.0 63.1 jit_solution(16438260891734159452)
XLA Ops:
  0.6 3.0 %pack.1 = (bf16[48,4,512,128]{3,2,1,0:T(8,128)(2,1)}, bf16[4,512,128]{2,1,0:T(8,128)(2,1)}, bf16[4,512,128]{2,1,0:T(8,128)(2,1)}, s32[12288,4,27]{2,1,0:T(4,128)...) custom-call(s32[2,4]{1,0:T(2,128)} %bitcast.13, ...), custom_call_target="tpu_custom_call" | custom-call | tf_op jit(solution)/shard_map/pack/pallas_call | solution.py:152
  3.6 1.3 %collective-permute-start = (bf16[320,128]{1,0:T(8,128)(2,1)}, bf16[320,128]{1,0:T(8,128)(2,1)S(1)}, u32[]{:S(2)}, u32[]{:S(2)}) collective-permute-start(bf16[320,128]{1,0:T(8,128)(2,1)} %get-tuple-element.33), channel_id=1, source_target_pairs={{4,12},{12,20},{20,28},{8,0},{16,8},{24,16},{5,13},{13,21},{21,29}... | collective-permute-start | bytes 245768 | tf_op jit(solution)/shard_map/ppermute | solution.py:616
  4.9 0.5 collective-permute-start.2
  5.4 0.7 %collective-permute-start.3 = (bf16[304,128]{1,0:T(8,128)(2,1)}, bf16[304,128]{1,0:T(8,128)(2,1)S(1)}, u32[]{:S(2)}, u32[]{:S(2)}) collective-permute-start(bf16[304,128]{1,0:T(8,128)(2,1)} %get-tuple-element.43), channel_id=1, source_target_pairs={{1,2},{2,1},{5,6},{6,5},{9,10},{10,9},{13,14},{14,13},{17,18},{18,... | collective-permute-start | bytes 233480 | tf_op jit(solution)/shard_map/ppermute | solution.py:610
  6.1 0.0 copy-start.1
  6.1 0.0 copy-start
  6.1 2.0 %own_columns.1.v = bf16[4,10,64,1152]{3,2,1,0:T(8,128)(2,1)S(1)} custom-call(s32[12288,4,27]{2,1,0:T(4,128)} %get-tuple-element.34.near_hbm, bf16[48,4,512,128]{3,2,1,0:T(8,128)(2,1)} %get-tuple-element.35.act_hbm), custom_call_target="tpu_custom_call" | custom-call | flops 16777216 | bytes 6291456 | tf_op jit(solution)/shard_map/own_columns/pallas_call | solution.py:342
  8.1 0.0 copy-start.3
  8.1 3.0 %collective-permute-done.second = bf16[320,128]{1,0:T(8,128)(2,1)S(1)} collective-permute-done((bf16[320,128]{1,0:T(8,128)(2,1)}, bf16[320,128]{1,0:T(8,128)(2,1)S(1)}, u32[]{:S(2)}, u32[]{:S(2)}) %collective-permute-start) | collective-permute-done | bytes 81952 | tf_op jit(solution)/shard_map/ppermute | solution.py:616
  11.2 0.0 copy-done.1
  11.2 1.8 %collective-permute-start.1 = (bf16[320,128]{1,0:T(8,128)(2,1)S(1)}, bf16[320,128]{1,0:T(8,128)(2,1)S(1)}, u32[]{:S(2)}, u32[]{:S(2)}) collective-permute-start(bf16[320,128]{1,0:T(8,128)(2,1)S(1)} %get-tuple-element.41), channel_id=1, source_target_pairs={{0,4},{4,0},{8,12},{12,8},{16,20},{20,16},{24,28},{28,24},{1,5},{5... | collective-permute-start | bytes 245768 | tf_op jit(solution)/shard_map/ppermute | solution.py:610
  13.0 0.0 copy-done
  13.0 0.0 copy-start.2
  13.0 0.0 copy-start.4
  13.0 0.0 copy-start.5
  13.0 2.3 %inner_terms.1.inner = f32[3456,128]{1,0:T(8,128)S(1)} custom-call(bf16[4,10,64,1152]{3,2,1,0:T(8,128)(2,1)S(1)} %own_columns.1.v, bf16[4,512,128]{2,1,0:T(8,128)(2,1)S(1)} %copy-done), custom_call_target="tpu_custom_call" | custom-call | flops 1811939328 | bytes 6291456 | tf_op jit(solution)/shard_map/inner_terms/pallas_call | solution.py:367
  15.3 0.0 collective-permute-done.2.y0.refs_5_
  15.3 0.0 collective-permute-done.3.y1.refs_6_
  15.3 0.4 collective-permute-done.1.x_ref.x_came.refs_4_
  15.7 0.0 copy-done.3
  15.7 2.0 %rim_terms.1 = (f32[1728,128]{1,0:T(8,128)S(1)}, f32[1728,128]{1,0:T(8,128)S(1)}) custom-call(s32[4,27]{1,0:T(4,128)S(1)} %copy-done.3, f32[3456,128]{1,0:T(8,128)S(1)} %inner_terms.1.inner, bf16[4,512,128]{2,1,0:T(8,128)(2,1)S(1)} %copy-done, bf16[320,128]{1,0:T(8,128)(2,1)S(1)} %collective-permute-done.1.x_ref.x_came.refs_4_, ...), custom_call_target="tpu_custom_call" | custom-call | flops 301989888 | bytes 6291456 | tf_op jit(solution)/shard_map/rim_terms/pallas_call | solution.py:458
  17.7 2.3 %collective-permute-start.4 = (f32[1728,128]{1,0:T(8,128)S(1)}, f32[1728,128]{1,0:T(8,128)S(1)}, u32[]{:S(2)}, u32[]{:S(2)}) collective-permute-start(f32[1728,128]{1,0:T(8,128)S(1)} %get-tuple-element.45), channel_id=1, source_target_pairs={{0,1},{1,0},{2,3},{3,2},{4,5},{5,4},{6,7},{7,6},{8,9},{9,8},{10,11... | collective-permute-start | bytes 2654216 | tf_op jit(solution)/shard_map/ppermute | solution.py:610
  20.0 2.1 %collective-permute-done.4.refs_1_ = f32[1728,128]{1,0:T(8,128)S(1)} collective-permute-done((f32[1728,128]{1,0:T(8,128)S(1)}, f32[1728,128]{1,0:T(8,128)S(1)}, u32[]{:S(2)}, u32[]{:S(2)}) %collective-permute-start.4) | collective-permute-done | bytes 884768 | tf_op jit(solution)/shard_map/ppermute | solution.py:610
  22.1 0.3 merge.1
  22.4 0.8 %convert_element_type.15 = f16[16,112,128]{2,1,0:T(8,128)(2,1)} convert(f32[16,112,128]{2,1,0:T(8,128)S(1)} %merge.1) | non-fusion elementwise | flops 229376 | bytes 1376256 | tf_op jit(solution)/shard_map/convert_element_type | solution.py:653
  23.2 6.5 %all-to-all-start = ((f16[16,112,128]{2,1,0:T(8,128)(2,1)}), f16[16,112,128]{2,1,0:T(8,128)(2,1)S(1)}, u32[]{:S(2)}, u32[]{:S(2)}) async-start(f16[16,112,128]{2,1,0:T(8,128)(2,1)} %convert_element_type.15), calls=%async_computation | async-start | bytes 917504 | tf_op jit(solution)/shard_map/all_to_all | solution.py:634
  29.7 0.1 collective-permute-start.5
  29.8 0.7 %collective-permute-start.6 = (bf16[32,128]{1,0:T(8,128)(2,1)S(1)}, bf16[32,128]{1,0:T(8,128)(2,1)S(1)}, u32[]{:S(2)}, u32[]{:S(2)}) collective-permute-start(bf16[32,128]{1,0:T(8,128)(2,1)S(1)} %get-tuple-element.52), channel_id=1, source_target_pairs={{1,2},{2,1},{5,6},{6,5},{9,10},{10,9},{13,14},{14,13},{17,18},{18,... | collective-permute-start | bytes 24584 | tf_op jit(solution)/shard_map/ppermute | solution.py:610
  30.5 1.5 %collective-permute-start.7 = (bf16[256,128]{1,0:T(8,128)(2,1)S(1)}, bf16[256,128]{1,0:T(8,128)(2,1)S(1)}, u32[]{:S(2)}, u32[]{:S(2)}) collective-permute-start(bf16[256,128]{1,0:T(8,128)(2,1)S(1)} %get-tuple-element.53), channel_id=1, source_target_pairs={{0,4},{4,0},{8,12},{12,8},{16,20},{20,16},{24,28},{28,24},{1,5},{5... | collective-permute-start | bytes 196616 | tf_op jit(solution)/shard_map/ppermute | solution.py:610
  32.0 0.0 collective-permute-done.5.refs_7_
  32.0 0.0 collective-permute-done.6.refs_8_
  32.0 0.0 copy-done.2
  32.0 0.0 copy-done.4
  32.0 0.0 copy-done.5
  32.0 6.0 %output_product.1 = bf16[4,512,128]{2,1,0:T(8,128)(2,1)} custom-call(s32[4,27]{1,0:T(4,128)S(1)} %copy-done.3, s32[4,512]{1,0:T(4,128)S(1)} %copy-done.2, bf16[3456,128]{1,0:T(8,128)(2,1)S(1)} %bitcast.8, bf16[4,512,128]{2,1,0:T(8,128)(2,1)S(1)} %copy-done.5, bf16[320,128]{1,0:T(8,128)(2,1)S(1)} %collective-permute-done.1.x_ref.x_came.refs_4_, ...), custom_call_target="tpu_custom_call" | custom-call | flops 1811939328 | bytes 4194304 | tf_op jit(solution)/shard_map/output_product/pallas_call | solution.py:592
  38.1 0.0 collective-permute-done.7.refs_4_
  38.1 3.2 %all-to-all-done = f16[16,112,128]{2,1,0:T(8,128)(2,1)S(1)} async-done(((f16[16,112,128]{2,1,0:T(8,128)(2,1)}), f16[16,112,128]{2,1,0:T(8,128)(2,1)S(1)}, u32[]{:S(2)}, u32[]{:S(2)}) %all-to-all-start) | async-done | bytes 458784 | tf_op jit(solution)/shard_map/all_to_all | solution.py:634
  41.3 0.1 convert_element_type.16.refs_0_
  41.4 0.3 sum_blocks.1
  41.6 0.8 %convert_element_type.17 = f16[16,112,128]{2,1,0:T(8,128)(2,1)} convert(f32[16,112,128]{2,1,0:T(8,128)S(1)} %sum_blocks.1) | non-fusion elementwise | flops 229376 | bytes 1376256 | tf_op jit(solution)/shard_map/convert_element_type | solution.py:661
  42.5 5.3 %all-to-all-start.1 = ((f16[16,112,128]{2,1,0:T(8,128)(2,1)}), f16[16,112,128]{2,1,0:T(8,128)(2,1)S(1)}, u32[]{:S(2)}, u32[]{:S(2)}) async-start(f16[16,112,128]{2,1,0:T(8,128)(2,1)} %convert_element_type.17), calls=%async_computation.1 | async-start | bytes 917504 | tf_op jit(solution)/shard_map/all_to_all | solution.py:634
  47.7 6.1 %input_grad_product.1 = bf16[4,512,128]{2,1,0:T(8,128)(2,1)} custom-call(s32[4,27]{1,0:T(4,128)S(1)} %copy-done.3, s32[4,512]{1,0:T(4,128)S(1)} %copy-done.2, bf16[3456,128]{1,0:T(8,128)(2,1)S(1)} %bitcast.9, bf16[4,512,128]{2,1,0:T(8,128)(2,1)S(1)} %copy-done, bf16[256,128]{1,0:T(8,128)(2,1)S(1)} %collective-permute-done.7.refs_4_, ...), custom_call_target="tpu_custom_call" | custom-call | flops 1811939328 | bytes 4194304 | tf_op jit(solution)/shard_map/input_grad_product/pallas_call | solution.py:592
  53.8 6.4 %all-to-all-done.1 = f16[16,112,128]{2,1,0:T(8,128)(2,1)S(1)} async-done(((f16[16,112,128]{2,1,0:T(8,128)(2,1)}), f16[16,112,128]{2,1,0:T(8,128)(2,1)S(1)}, u32[]{:S(2)}, u32[]{:S(2)}) %all-to-all-start.1) | async-done | bytes 458784 | tf_op jit(solution)/shard_map/all_to_all | solution.py:634
  60.2 0.0 collective-permute-start.8
  60.2 0.1 convert_element_type.19.refs_0_
  60.3 1.0 %decode_own.1.refs_1_ = f32[2,1728,128]{2,1,0:T(8,128)} custom-call(f32[16,112,128]{2,1,0:T(8,128)S(1)} %convert_element_type.19.refs_0_), custom_call_target="tpu_custom_call" | custom-call | tf_op jit(solution)/shard_map/decode_own/pallas_call | solution.py:554
  61.2 0.8 %collective-permute-done.8 = f16[16,112,128]{2,1,0:T(8,128)(2,1)S(1)} collective-permute-done((f16[16,112,128]{2,1,0:T(8,128)(2,1)S(1)}, f16[16,112,128]{2,1,0:T(8,128)(2,1)S(1)}, u32[]{:S(2)}, u32[]{:S(2)}) %collective-permute-start.8) | collective-permute-done | bytes 458784 | tf_op jit(solution)/shard_map/ppermute | solution.py:610
  62.0 0.1 convert_element_type.18.refs_0_
  62.1 1.0 %decode_other.1 = f32[2,1728,128]{2,1,0:T(8,128)} custom-call(f32[16,112,128]{2,1,0:T(8,128)S(1)} %convert_element_type.18.refs_0_, f32[2,1728,128]{2,1,0:T(8,128)} %decode_own.1.refs_1_), custom_call_target="tpu_custom_call", output_to_operand_aliasing={{}: (1, {})} | custom-call | tf_op jit(solution)/shard_map/decode_other/pallas_call | solution.py:554
  (2 shorter events, 0.0 us)
Async XLA Ops:
  3.6 7.6 %collective-permute-start = (bf16[320,128]{1,0:T(8,128)(2,1)}, bf16[320,128]{1,0:T(8,128)(2,1)S(1)}, u32[]{:S(2)}, u32[]{:S(2)}) collective-permute-start(bf16[320,128]{1,0:T(8,128)(2,1)} %get-tuple-element.33), channel_id=1, source_target_pairs={{4,12},{12,20},{20,28},{8,0},{16,8},{24,16},{5,13},{13,21},{21,29}... | collective-permute-start | bytes 245768 | tf_op jit(solution)/shard_map/ppermute | solution.py:616
  4.9 10.4 %collective-permute-start.2 = (bf16[304,128]{1,0:T(8,128)(2,1)}, bf16[304,128]{1,0:T(8,128)(2,1)S(1)}, u32[]{:S(2)}, u32[]{:S(2)}) collective-permute-start(bf16[304,128]{1,0:T(8,128)(2,1)} %get-tuple-element.42), channel_id=1, source_target_pairs={{0,1},{1,0},{2,3},{3,2},{4,5},{5,4},{6,7},{7,6},{8,9},{9,8},{10,11... | collective-permute-start | bytes 233480 | tf_op jit(solution)/shard_map/ppermute | solution.py:610
  5.4 9.9 %collective-permute-start.3 = (bf16[304,128]{1,0:T(8,128)(2,1)}, bf16[304,128]{1,0:T(8,128)(2,1)S(1)}, u32[]{:S(2)}, u32[]{:S(2)}) collective-permute-start(bf16[304,128]{1,0:T(8,128)(2,1)} %get-tuple-element.43), channel_id=1, source_target_pairs={{1,2},{2,1},{5,6},{6,5},{9,10},{10,9},{13,14},{14,13},{17,18},{18,... | collective-permute-start | bytes 233480 | tf_op jit(solution)/shard_map/ppermute | solution.py:610
  6.1 5.1 %copy-start.1 = (bf16[288,128]{1,0:T(8,128)(2,1)S(1)}, bf16[288,128]{1,0:T(8,128)(2,1)}, u32[]{:S(2)}) copy-start(bf16[288,128]{1,0:T(8,128)(2,1)} %get-tuple-element.32.first) | copy-start | bytes 221188
  6.1 6.9 %copy-start = (bf16[4,512,128]{2,1,0:T(8,128)(2,1)S(1)}, bf16[4,512,128]{2,1,0:T(8,128)(2,1)}, u32[]{:S(2)}) copy-start(bf16[4,512,128]{2,1,0:T(8,128)(2,1)} %get-tuple-element.57.grd.refs_3_) | copy-start | bytes 1572868
  8.1 7.6 %copy-start.3 = (s32[4,27]{1,0:T(4,128)S(1)}, s32[4,27]{1,0:T(4,128)}, u32[]{:S(2)}) copy-start(s32[4,27]{1,0:T(4,128)} %refs_0_.3) | copy-start | bytes 1300
  11.2 4.5 %collective-permute-start.1 = (bf16[320,128]{1,0:T(8,128)(2,1)S(1)}, bf16[320,128]{1,0:T(8,128)(2,1)S(1)}, u32[]{:S(2)}, u32[]{:S(2)}) collective-permute-start(bf16[320,128]{1,0:T(8,128)(2,1)S(1)} %get-tuple-element.41), channel_id=1, source_target_pairs={{0,4},{4,0},{8,12},{12,8},{16,20},{20,16},{24,28},{28,24},{1,5},{5... | collective-permute-start | bytes 245768 | tf_op jit(solution)/shard_map/ppermute | solution.py:610
  13.0 19.1 %copy-start.2 = (s32[4,512]{1,0:T(4,128)S(1)}, s32[4,512]{1,0:T(4,128)}, u32[]{:S(2)}) copy-start(s32[4,512]{1,0:T(4,128)} %refs_1_.3) | copy-start | bytes 24580
  13.0 19.1 %copy-start.4 = (bf16[27,128,128]{2,1,0:T(8,128)(2,1)S(1)}, bf16[27,128,128]{2,1,0:T(8,128)(2,1)}, u32[]{:S(2)}) copy-start(bf16[27,128,128]{2,1,0:T(8,128)(2,1)} %param.9) | copy-start | bytes 2654212
  13.0 19.1 %copy-start.5 = (bf16[4,512,128]{2,1,0:T(8,128)(2,1)S(1)}, bf16[4,512,128]{2,1,0:T(8,128)(2,1)}, u32[]{:S(2)}) copy-start(bf16[4,512,128]{2,1,0:T(8,128)(2,1)} %get-tuple-element.49.refs_3_) | copy-start | bytes 1572868
  17.7 4.4 %collective-permute-start.4 = (f32[1728,128]{1,0:T(8,128)S(1)}, f32[1728,128]{1,0:T(8,128)S(1)}, u32[]{:S(2)}, u32[]{:S(2)}) collective-permute-start(f32[1728,128]{1,0:T(8,128)S(1)} %get-tuple-element.45), channel_id=1, source_target_pairs={{0,1},{1,0},{2,3},{3,2},{4,5},{5,4},{6,7},{7,6},{8,9},{9,8},{10,11... | collective-permute-start | bytes 2654216 | tf_op jit(solution)/shard_map/ppermute | solution.py:610
  23.2 18.1 %all-to-all-start = ((f16[16,112,128]{2,1,0:T(8,128)(2,1)}), f16[16,112,128]{2,1,0:T(8,128)(2,1)S(1)}, u32[]{:S(2)}, u32[]{:S(2)}) async-start(f16[16,112,128]{2,1,0:T(8,128)(2,1)} %convert_element_type.15), calls=%async_computation | async-start | bytes 917504 | tf_op jit(solution)/shard_map/all_to_all | solution.py:634
  29.7 2.3 %collective-permute-start.5 = (bf16[32,128]{1,0:T(8,128)(2,1)S(1)}, bf16[32,128]{1,0:T(8,128)(2,1)S(1)}, u32[]{:S(2)}, u32[]{:S(2)}) collective-permute-start(bf16[32,128]{1,0:T(8,128)(2,1)S(1)} %get-tuple-element.51), channel_id=1, source_target_pairs={{0,1},{1,0},{2,3},{3,2},{4,5},{5,4},{6,7},{7,6},{8,9},{9,8},{10,11... | collective-permute-start | bytes 24584 | tf_op jit(solution)/shard_map/ppermute | solution.py:610
  29.8 2.2 %collective-permute-start.6 = (bf16[32,128]{1,0:T(8,128)(2,1)S(1)}, bf16[32,128]{1,0:T(8,128)(2,1)S(1)}, u32[]{:S(2)}, u32[]{:S(2)}) collective-permute-start(bf16[32,128]{1,0:T(8,128)(2,1)S(1)} %get-tuple-element.52), channel_id=1, source_target_pairs={{1,2},{2,1},{5,6},{6,5},{9,10},{10,9},{13,14},{14,13},{17,18},{18,... | collective-permute-start | bytes 24584 | tf_op jit(solution)/shard_map/ppermute | solution.py:610
  30.5 7.6 %collective-permute-start.7 = (bf16[256,128]{1,0:T(8,128)(2,1)S(1)}, bf16[256,128]{1,0:T(8,128)(2,1)S(1)}, u32[]{:S(2)}, u32[]{:S(2)}) collective-permute-start(bf16[256,128]{1,0:T(8,128)(2,1)S(1)} %get-tuple-element.53), channel_id=1, source_target_pairs={{0,4},{4,0},{8,12},{12,8},{16,20},{20,16},{24,28},{28,24},{1,5},{5... | collective-permute-start | bytes 196616 | tf_op jit(solution)/shard_map/ppermute | solution.py:610
  42.5 17.7 %all-to-all-start.1 = ((f16[16,112,128]{2,1,0:T(8,128)(2,1)}), f16[16,112,128]{2,1,0:T(8,128)(2,1)S(1)}, u32[]{:S(2)}, u32[]{:S(2)}) async-start(f16[16,112,128]{2,1,0:T(8,128)(2,1)} %convert_element_type.17), calls=%async_computation.1 | async-start | bytes 917504 | tf_op jit(solution)/shard_map/all_to_all | solution.py:634
  60.2 1.8 %collective-permute-start.8 = (f16[16,112,128]{2,1,0:T(8,128)(2,1)S(1)}, f16[16,112,128]{2,1,0:T(8,128)(2,1)S(1)}, u32[]{:S(2)}, u32[]{:S(2)}) collective-permute-start(f16[16,112,128]{2,1,0:T(8,128)(2,1)S(1)} %all-to-all-done.1), channel_id=1, source_target_pairs={{0,1},{1,0},{2,3},{3,2},{4,5},{5,4},{6,7},{7,6},{8,9},{9,8},{10,11... | collective-permute-start | bytes 1376264 | tf_op jit(solution)/shard_map/ppermute | solution.py:610
